TPU v7x, 256 devices: a whole 4x4x8 slice. The times are simulated.
256 devices in a mesh: group: 32 (over z, y), tensor: 8 (over x, core).
Axes of the slice: x: 4, y: 4, z: 8, core: 2. Of those that a mesh axis runs over, the one named last changes fastest.
Arguments:
- hidden: bfloat16 [256, 8192], P(None, 'group'), may hold values from -6 to 6
- vision: bfloat16 [20480, 8192], P('group', 'tensor'), may hold values from -6 to 6
- attn_gain: float32 [8192], P('group'), may hold values from 0.1 to 1.9
- q_weight: bfloat16 [8192, 8192], P('group', 'tensor'), may hold values from -0.0625 to 0.0625
- k_weight: bfloat16 [8192, 1024], P('tensor'), may hold values from -0.0625 to 0.0625
- v_weight: bfloat16 [8192, 1024], P('tensor'), may hold values from -0.0625 to 0.0625
- q_gain: float32 [128], replicated, may hold values from 0.5 to 2
- k_gain: float32 [128], replicated, may hold values from 0.5 to 2
- o_weight: bfloat16 [8192, 8192], P('tensor', 'group'), may hold values from -0.0625 to 0.0625
- gate_logits: float32 [2], replicated, may hold values from 0.5 to 2
- mlp_gain: float32 [8192], P('group'), may hold values from 0.1 to 1.9
- gate_weight: bfloat16 [8192, 28672], P('group', 'tensor'), may hold values from -0.0625 to 0.0625
- up_weight: bfloat16 [8192, 28672], P('group', 'tensor'), may hold values from -0.0625 to 0.0625
- down_weight: bfloat16 [28672, 8192], P('tensor', 'group'), may hold values from -0.03125 to 0.03125
- image_tiles: int32 [32, 4], replicated, may hold values from 1 to 4, 10 in all within a row
- image_groups: int32 [128, 8], replicated, may hold values from 0 to 31, as said below
- image_requests: int32 [128, 8], replicated, may hold values from 0 to 3, as said below
Outputs:
- output: bfloat16 [256, 8192], P(None, 'group')
Inputs may be any that keep to these rules, and one draw needn't show every extreme that they name: `image_tiles`: row e lists the tiles of the 4 images of encoder group e in order; each row sums to 10 and holds an image of 4 tiles. `image_groups`: row i names 8 different decoder groups that receive image i. Among the rows of one encoder group (rows e * 4 to e * 4 + 3) no decoder group is named more than 2 times, and some decoder group is named exactly 2 times by some encoder group; every decoder group is named by some image. image_requests[i, c] is the request, numbered within decoder group image_groups[i, c], that sees image i; a request may see no image at all.
All inputs are finite; a program needn't handle non-finite values.
Results may differ from a plain program's by a relative error of at most 0.008.
Values may be sent and summed in bfloat16 or wider, within the bound.
No kernel may reach another device: no remote copies, remote signals or barrier semaphores. Data moves between devices by JAX's collectives and lax.ppermute only.
A program may use at most 128 MiB of HBM per device.

v0:
```python
import math

import jax
import jax.numpy as jnp
from jax import lax
from jax.sharding import PartitionSpec as P

REQ_DEV = 4
STEPS = 2
TILE_TOK = 64
MAXT = 4
CAP = 2


def rms_norm(values, gain):
    mean_square = jnp.mean(values * values, axis=-1, keepdims=True)
    return values * lax.rsqrt(mean_square + 1e-05) * gain


def row_scale(square_sums, full_width):
    return lax.rsqrt(square_sums / full_width + 1e-05)


def shards(
    hidden,
    vision,
    attn_gain,
    q_weight,
    k_weight,
    v_weight,
    q_gain,
    k_gain,
    o_weight,
    gate_logits,
    mlp_gain,
    gate_weight,
    up_weight,
    down_weight,
    image_tiles,
    image_groups,
    image_requests,
):
    num_groups = lax.axis_size("group")
    my_group = lax.axis_index("group")
    all_rows, width_part = hidden.shape
    own_rows = all_rows // num_groups
    full_width = width_part * num_groups
    head_size = q_gain.shape[0]
    kv_local = k_weight.shape[1] // head_size // lax.axis_size("tensor")
    q_local = q_weight.shape[1] // head_size
    group_share = q_local // kv_local
    copies_each = image_groups.shape[1]
    images_each = image_tiles.shape[1]
    slot_rows = MAXT * TILE_TOK
    score_scale = 1.0 / math.sqrt(head_size)
    request_ids = (image_groups * REQ_DEV + image_requests).reshape(-1)
    row_request = jnp.arange(all_rows, dtype=jnp.int32) // STEPS
    has_image = jnp.any(row_request[:, None] == request_ids[None, :], axis=1)
    hidden_f = hidden.astype(jnp.float32)
    normed = (hidden_f * attn_gain).astype(jnp.bfloat16)
    queries = lax.psum_scatter(
        jnp.dot(normed, q_weight, preferred_element_type=jnp.float32),
        "group",
        scatter_dimension=0,
        tiled=True,
    )
    queries = rms_norm(queries.reshape(own_rows, kv_local, group_share, head_size), q_gain).astype(
        jnp.bfloat16
    )
    key_part = jnp.einsum(
        "rd,dch->crh",
        vision,
        k_weight.reshape(-1, kv_local * lax.axis_size("tensor"), head_size),
        preferred_element_type=jnp.float32,
    )
    value_part = jnp.einsum(
        "rd,dch->crh",
        vision,
        v_weight.reshape(-1, kv_local * lax.axis_size("tensor"), head_size),
        preferred_element_type=jnp.float32,
    )
    projected = lax.psum_scatter(
        jnp.concatenate((key_part, value_part), axis=2), "tensor", scatter_dimension=0, tiled=True
    )
    key_local = rms_norm(projected[:, :, :head_size], k_gain).astype(jnp.bfloat16)
    value_local = projected[:, :, head_size:].astype(jnp.bfloat16)
    packed = jnp.concatenate((key_local, value_local), axis=2)
    slot_range = jnp.arange(CAP, dtype=jnp.int32)
    within = jnp.arange(slot_rows, dtype=jnp.int32)
    tile_of_row = within // TILE_TOK
    my_tiles = lax.dynamic_index_in_dim(image_tiles, my_group, 0, keepdims=False)
    my_routes = lax.dynamic_slice_in_dim(image_groups, my_group * images_each, images_each, 0)
    destinations = jnp.arange(num_groups, dtype=jnp.int32)
    bound_for = jnp.any(my_routes[:, :, None] == destinations[None, None, :], axis=1)
    slot_place = jnp.cumsum(bound_for.astype(jnp.int32), axis=0) - 1
    chosen = (bound_for[:, :, None] & (slot_place[:, :, None] == slot_range[None, None, :])).astype(
        jnp.int32
    )
    first_row = (jnp.cumsum(my_tiles) - my_tiles) * TILE_TOK
    slot_start = jnp.sum(chosen * first_row[:, None, None], axis=0)
    slot_tiles = jnp.sum(chosen * my_tiles[:, None, None], axis=0)
    sending = tile_of_row[None, None, :] < slot_tiles[:, :, None]
    source_row = jnp.where(sending, slot_start[:, :, None] + within[None, None, :], 0).reshape(
        num_groups, CAP * slot_rows
    )
    outgoing = jnp.take(packed, source_row, axis=1)
    outgoing = jnp.where(
        sending.reshape(1, num_groups, CAP * slot_rows, 1), outgoing, jnp.zeros((), jnp.bfloat16)
    )
    incoming = lax.all_to_all(outgoing, "group", split_axis=1, concat_axis=1, tiled=True)
    route_grid = image_groups.reshape(num_groups, images_each, copies_each)
    request_grid = image_requests.reshape(num_groups, images_each, copies_each)
    arrives = route_grid == my_group
    to_me = jnp.any(arrives, axis=2)
    holder = jnp.sum(jnp.where(arrives, request_grid, 0), axis=2)
    arrival_place = jnp.cumsum(to_me.astype(jnp.int32), axis=1) - 1
    picked = (to_me[:, :, None] & (arrival_place[:, :, None] == slot_range[None, None, :])).astype(
        jnp.int32
    )
    slot_count = jnp.sum(picked * image_tiles[:, :, None], axis=1)
    slot_owner = jnp.sum(picked * holder[:, :, None], axis=1)
    key_owner = jnp.where(
        tile_of_row[None, None, :] < slot_count[:, :, None], slot_owner[:, :, None], -1
    ).reshape(-1)
    local_request = jnp.arange(own_rows, dtype=jnp.int32) // STEPS
    permitted = (local_request[:, None] == key_owner[None, :])[None, None]
    keys_in = incoming[:, :, :, :head_size].reshape(kv_local, -1, head_size)
    values_in = incoming[:, :, :, head_size:].reshape(kv_local, -1, head_size)
    scores = (
        jnp.einsum("rksh,knh->ksrn", queries, keys_in, preferred_element_type=jnp.float32)
        * score_scale
    )
    highest = jnp.max(jnp.where(permitted, scores, -1e30), axis=-1, keepdims=True)
    weights = jnp.where(permitted, jnp.exp(scores - highest), 0.0)
    denominator = jnp.maximum(jnp.sum(weights, axis=-1, keepdims=True), 1.0)
    attn_probs = (weights / denominator).astype(jnp.bfloat16)
    mixed_heads = jnp.einsum(
        "ksrn,knh->rksh", attn_probs, values_in, preferred_element_type=jnp.float32
    )
    attended = mixed_heads.reshape(own_rows, q_local * head_size).astype(jnp.bfloat16)
    partial_out = jnp.dot(
        lax.all_gather(attended, "group", axis=0, tiled=True),
        o_weight,
        preferred_element_type=jnp.float32,
    )
    attn_sum = lax.psum(partial_out, "tensor")
    middle = (hidden_f + jnp.tanh(gate_logits[0]) * attn_sum).astype(jnp.bfloat16)
    middle_f = middle.astype(jnp.float32)
    square_mid = lax.psum(jnp.sum(middle_f * middle_f, axis=1), "group")
    mlp_normed = (middle_f * row_scale(square_mid, full_width)[:, None] * mlp_gain).astype(
        jnp.bfloat16
    )
    gate_part = jnp.dot(mlp_normed, gate_weight, preferred_element_type=jnp.float32)
    up_part = jnp.dot(mlp_normed, up_weight, preferred_element_type=jnp.float32)
    gate_sum, up_sum = lax.psum((gate_part, up_part), "group")
    active = (jax.nn.silu(gate_sum) * up_sum).astype(jnp.bfloat16)
    down_part = jnp.dot(active, down_weight, preferred_element_type=jnp.float32)
    down_sum = lax.psum(down_part, "tensor")
    image_mask = has_image.astype(jnp.float32)
    return (middle_f + jnp.tanh(gate_logits[1]) * image_mask[:, None] * down_sum).astype(
        jnp.bfloat16
    )


def solution(mesh):
    in_specs = (
        P(None, "group"),
        P("group", "tensor"),
        P("group"),
        P("group", "tensor"),
        P("tensor", None),
        P("tensor", None),
        P(),
        P(),
        P("tensor", "group"),
        P(),
        P("group"),
        P("group", "tensor"),
        P("group", "tensor"),
        P("tensor", "group"),
        P(),
        P(),
        P(),
    )
    out_specs = P(None, "group")
    return jax.shard_map(shards, mesh=mesh, in_specs=in_specs, out_specs=out_specs, check_vma=False)
```

profile of v0, /device:TPU:1, one launch (start us, length us, event | category | flops | bytes accessed | tf_op | source)
XLA Modules:
  0.0 936.4 jit_solution(3723865982122952579)
XLA Ops:
  7.4 4.1 copy.58
  11.5 4.0 copy.57
  15.4 3.6 convolution_bitcast_fusion
  19.0 1.8 convolution_bitcast_fusion.1
  20.8 2.7 pad_maximum_fusion
  25.7 41.7 %reduce-scatter.3.cloned.1.call-done = f32[1,640,256]{1,2,0:T(8,128)} async-done(((f32[8,640,256]{1,2,0:T(8,128)}), f32[1,640,256]{1,2,0:T(8,128)}) %reduce-scatter.3.cloned.1.call-update) | async-done | bytes 655376 | tf_op jit(solution)/shard_map/reduce_scatter | solution.py:82
  70.7 64.8 %gather_fusion = bf16[16384,256]{1,0:T(8,128)(2,1)} fusion(bf16[640,256]{1,0:T(8,128)(2,1)S(1)} %copy.47, s32[16384]{0:T(1024)S(1)} %broadcast_clamp_fusion), kind=kCustom, calls=%fused_computation | custom fusion | bytes 16842752 | tf_op jit(solution)/shard_map/jit(_take)/gather | solution.py:106
  135.5 7.8 select_select_fusion
  143.3 9.8 %all-to-all-start = ((bf16[1,32,512,256]{3,2,0,1:T(8,128)(2,1)}), bf16[1,32,512,256]{3,2,0,1:T(8,128)(2,1)}, u32[]{:S(2)}, u32[]{:S(2)}) async-start(bf16[1,32,512,256]{3,2,0,1:T(8,128)(2,1)} %select_select_fusion), calls=%async_computation.1 | async-start | bytes 16777216 | tf_op jit(solution)/shard_map/all_to_all | solution.py:110
  153.2 1.3 fusion.20
  156.1 302.2 %reduce-scatter.5.cloned.1.call-done = f32[8,1024]{1,0:T(8,128)} async-done(((f32[256,1024]{1,0:T(8,128)}), f32[8,1024]{1,0:T(8,128)}) %reduce-scatter.5.cloned.1.call-update) | async-done | bytes 32784 | tf_op jit(solution)/shard_map/reduce_scatter | solution.py:61
  460.0 3.9 fusion.40
  463.9 1.7 select_reduce_fusion
  465.6 1.3 fusion.1
  468.1 1.4 fusion.11
  469.5 35.7 %all_gather.3 = bf16[256,1024]{1,0:T(8,128)(2,1)S(1)} all-gather(bf16[8,1024]{1,0:T(8,128)(2,1)S(1)} %fusion.11), channel_id=1, replica_groups=mesh['group'=32,'tensor'=8] {'group'}, dimensions={0}, use_global_device_ids=true | all-gather | bytes 540672 | tf_op jit(solution)/shard_map/all_gather | solution.py:142
  507.5 77.8 %all-reduce.5.cloned.1.call-done = f32[256,256]{1,0:T(8,128)} async-done(((f32[256,256]{1,0:T(8,128)}), f32[256,256]{1,0:T(8,128)}) %all-reduce.5.cloned.1.call-update) | async-done | bytes 262160 | tf_op jit(solution)/shard_map/psum | solution.py:146
  586.4 61.1 %psum.36 = f32[256]{0:T(256)S(1)} all-reduce(f32[256]{0:T(256)S(1)} %get-tuple-element.11), channel_id=1, replica_groups=mesh['group'=32,'tensor'=8] {'group'}, use_global_device_ids=true, to_apply=%region_19.20 | all-reduce | flops 256 | bytes 2048 | tf_op jit(solution)/shard_map/psum | solution.py:149
  647.6 2.6 fusion.27
  650.2 2.6 fusion.25
  654.0 206.4 %all-reduce.9.cloned.1.call-done = (f32[256,3584]{1,0:T(8,128)}, f32[256,3584]{1,0:T(8,128)}) async-done(((f32[256,3584]{1,0:T(8,128)}, f32[256,3584]{1,0:T(8,128)}), (f32[256,3584]{1,0:T(8,128)}, f32[256,3584]{1,0:T(8,128)})) %all-reduce.9.cloned.1.call-update) | async-done | bytes 7340048 | tf_op jit(solution)/shard_map/psum | solution.py:155
  860.3 5.5 fusion.5
  865.8 61.8 %all-reduce.7.cloned.1.call-done = f32[256,256]{1,0:T(8,128)} async-done(((f32[256,256]{1,0:T(8,128)}), f32[256,256]{1,0:T(8,128)}) %all-reduce.7.cloned.1.call-update) | async-done | bytes 262160 | tf_op jit(solution)/shard_map/psum | solution.py:158
  927.6 1.7 fusion.19
  (106 shorter events, 13.0 us)
Async XLA Ops:
  7.4 640.2 %copy-start = (bf16[256,3584]{1,0:T(8,128)(2,1)S(1)}, bf16[256,3584]{1,0:T(8,128)(2,1)}, u32[]{:S(2)}) copy-start(bf16[256,3584]{1,0:T(8,128)(2,1)} %param.28) | copy-start | bytes 5505028
  7.4 8.1 copy-start.14
  7.4 60.0 %reduce-scatter.3.cloned.1.call-start = ((), (), s32[]{:S(2)}) async-start(), calls=%async_computation.3 | async-start | bytes 5898240 | tf_op jit(solution)/shard_map/reduce_scatter | solution.py:82
  15.4 3.6 copy-start.1
  23.5 0.7 copy-start.8
  23.5 1.0 copy-start.7
  23.5 45.8 %copy-start.12 = (f32[128]{0:T(128)S(1)}, f32[128]{0:T(128)}, u32[]{:S(2)}) copy-start(f32[128]{0:T(128)} %param.24) | copy-start | bytes 1540
  143.3 9.9 %copy-start.3 = (bf16[256,1024]{1,0:T(8,128)(2,1)S(1)}, bf16[256,1024]{1,0:T(8,128)(2,1)}, u32[]{:S(2)}) copy-start(bf16[256,1024]{1,0:T(8,128)(2,1)} %param.20) | copy-start | bytes 1572868
  143.3 9.9 %copy-start.4 = (bf16[256,256]{1,0:T(8,128)(2,1)S(1)}, bf16[256,256]{1,0:T(8,128)(2,1)}, u32[]{:S(2)}) copy-start(bf16[256,256]{1,0:T(8,128)(2,1)} %param.17) | copy-start | bytes 393220
  143.3 9.9 %copy-start.11 = (f32[256]{0:T(256)S(1)}, f32[256]{0:T(256)}, u32[]{:S(2)}) copy-start(f32[256]{0:T(256)} %param.19) | copy-start | bytes 3076
  143.3 11.5 %copy-start.9 = (s32[128,8]{0,1:T(8,128)S(1)}, s32[128,8]{0,1:T(8,128)}, u32[]{:S(2)}) copy-start(s32[128,8]{0,1:T(8,128)} %param.33) | copy-start | bytes 12292
  143.3 12.6 %copy-start.13 = (f32[128]{0:T(128)S(1)}, f32[128]{0:T(128)}, u32[]{:S(2)}) copy-start(f32[128]{0:T(128)} %param.23) | copy-start | bytes 1540
  143.3 316.7 %all-to-all-start = ((bf16[1,32,512,256]{3,2,0,1:T(8,128)(2,1)}), bf16[1,32,512,256]{3,2,0,1:T(8,128)(2,1)}, u32[]{:S(2)}, u32[]{:S(2)}) async-start(bf16[1,32,512,256]{3,2,0,1:T(8,128)(2,1)} %select_select_fusion), calls=%async_computation.1 | async-start | bytes 16777216 | tf_op jit(solution)/shard_map/all_to_all | solution.py:110
  153.1 305.2 %reduce-scatter.5.cloned.1.call-start = ((), (), s32[]{:S(2)}) async-start(), calls=%async_computation.4 | async-start | bytes 1081344 | tf_op jit(solution)/shard_map/reduce_scatter | solution.py:61
  154.6 430.8 %all-reduce.5.cloned.1.call-start = ((), (), s32[]{:S(2)}) async-start(), calls=%async_computation.5 | async-start | bytes 524288 | tf_op jit(solution)/shard_map/psum | solution.py:146
  468.0 37.2 %copy-start.5 = (bf16[1024,256]{1,0:T(8,128)(2,1)S(1)}, bf16[1024,256]{1,0:T(8,128)(2,1)}, u32[]{:S(2)}) copy-start(bf16[1024,256]{1,0:T(8,128)(2,1)} %param.25) | copy-start | bytes 1572868
  468.1 38.2 %copy-start.10 = (f32[2]{0:T(128)S(1)}, f32[2]{0:T(128)}, u32[]{:S(2)}) copy-start(f32[2]{0:T(128)} %param.26) | copy-start | bytes 28
  468.1 179.5 %copy-start.6 = (f32[256]{0:T(256)S(1)}, f32[256]{0:T(256)}, u32[]{:S(2)}) copy-start(f32[256]{0:T(256)} %param.27) | copy-start | bytes 3076
  506.3 354.1 %all-reduce.9.cloned.1.call-start = ((), (), s32[]{:S(2)}) async-start(), calls=%async_computation.7 | async-start | bytes 14680064 | tf_op jit(solution)/shard_map/psum | solution.py:155
  647.5 2.6 copy-start.2
  652.8 274.8 %all-reduce.7.cloned.1.call-start = ((), (), s32[]{:S(2)}) async-start(), calls=%async_computation.6 | async-start | bytes 524288 | tf_op jit(solution)/shard_map/psum | solution.py:158
Sparse Core Ops, SparseCore 0:
  23.7 43.6 reduce-scatter.2
  506.4 78.9 all-reduce.4
  865.9 61.6 all-reduce.6
Sparse Core Ops, SparseCore 1:
  157.4 300.8 reduce-scatter.4
  652.9 207.4 all-reduce.8
where the time goes:
time: 938 us; the launch traced here: 936 us
  waiting for transfers between devices  690 us (74%)
  blocking collectives  96.8 us (10%)
  local copies, waits for them, and re-layouts  81 us (9%)
  matrix products  21.4 us (2%)
  other arithmetic  20.8 us (2%)
  between operations  16.3 us (2%)
  starting transfers between devices  10.2 us (1%)
    reduce_scatter x1, waiting for transfers between devices, shards(): lax.psum_scatter(jnp.dot(normed, q_weight, preferred_element_type=jnp.flo...  302 us
    psum x1, waiting for transfers between devices, shards(): gate_sum, up_sum = lax.psum((gate_part, up_part), 'group')  206 us
    psum x1, waiting for transfers between devices, shards(): attn_sum = lax.psum(partial_out, 'tensor')  77.8 us
    gather x1, local copies, waits for them, and re-layouts, shards(): outgoing = jnp.take(packed, source_row, axis=1)  64.8 us
    psum x1, waiting for transfers between devices, shards(): down_sum = lax.psum(down_part, 'tensor')  61.8 us
    psum x1, blocking collectives, shards(): square_mid = lax.psum(jnp.sum(middle_f * middle_f, axis=1), 'group')  61.1 us
    reduce_scatter x1, waiting for transfers between devices, shards(): lax.psum_scatter(jnp.concatenate((key_part, value_part), axis=2), 'tensor...  41.7 us
    all_gather x1, blocking collectives, shards(): lax.all_gather(attended, 'group', axis=0, tiled=True)  35.7 us
  transfers between devices with their start and end apart: 6, of which 5 were waited for; matrix products, arithmetic and copies ran while one was open for 1% of the time, Pallas kernels for 0%

commit v1 on v0

v1 whole, which is shorter than its diff:
```python
import math

import jax
import jax.numpy as jnp
from jax import lax
from jax.experimental import pallas as pl
from jax.experimental.pallas import tpu as pltpu
from jax.sharding import Mesh
from jax.sharding import PartitionSpec as P

GROUP = ("z", "y")
TENSOR = ("x", "c")
HEAD = 128
SLOTS = 2
STEPS = 2
EPS = 1e-05
VMEM_BYTES = 40 * 1024 * 1024
BF = jnp.bfloat16
F32 = jnp.float32


def params():
    return pltpu.CompilerParams(vmem_limit_bytes=VMEM_BYTES)


def dot(a, b):
    return jnp.dot(a, b, preferred_element_type=F32)


def vmem():
    return pl.BlockSpec(memory_space=pltpu.VMEM)


def smem():
    return pl.BlockSpec(memory_space=pltpu.SMEM)


def route_kernel(me_ref, routes_ref, requests_ref, sel_ref, image_ref):
    me = me_ref[0]
    groups, links = routes_ref.shape
    rows = groups * SLOTS * STEPS
    row = lax.broadcasted_iota(jnp.int32, (rows, links), 0)
    lane = lax.broadcasted_iota(jnp.int32, (rows, links), 1)
    group_of_row = row >> 2
    slot = (row >> 1) & 1
    step = row & 1
    spread = (group_of_row == lane).astype(F32)
    link = lax.broadcasted_iota(jnp.int32, (groups, links), 1)
    code = (link * 4 + requests_ref[...]).astype(F32)
    route_rows = dot(spread, routes_ref[...].astype(F32))
    code_rows = dot(spread, code)
    hit = route_rows == me.astype(F32)
    first = jnp.min(jnp.where(hit, code_rows, 1e4), axis=1, keepdims=True)
    last = jnp.max(jnp.where(hit, code_rows, -1.0), axis=1, keepdims=True)
    slot1, step1 = slot[:, :1], step[:, :1]
    chosen = jnp.where(slot1 == 0, first, last).astype(jnp.int32)
    found_first = jnp.where(first < 1e3, 1, 0)
    found_last = jnp.where(last > first, 1, 0)
    found = jnp.where(slot1 == 0, found_first, found_last)
    wanted = jnp.where(found == 1, (chosen & 3) * STEPS + step1, -1)
    sel_ref[...] = jnp.where(lane[:, :8] == wanted, 1.0, 0.0).astype(BF)
    mine = routes_ref[pl.ds(me, 1), :]
    here = mine == group_of_row
    first_link = jnp.min(jnp.where(here, lane, 1000), axis=1, keepdims=True)
    last_link = jnp.max(jnp.where(here, lane, -1), axis=1, keepdims=True)
    first_image = jnp.where(first_link < 1000, first_link >> 3, -1)
    last_image = jnp.where(last_link > first_link, last_link >> 3, -1)
    image_ref[...] = jnp.where(slot1 == 0, first_image, last_image)


def kv_kernel(place_ref, vision_ref, k_ref, v_ref, out_ref):
    weight = jnp.concatenate((k_ref[...], v_ref[...]), axis=1)
    out_ref[0] = dot(vision_ref[...], weight).astype(BF)


def kv_project(place, vision, k_weight, v_weight, other):
    rows, depth = vision.shape
    chips = 4

    def head(d, place_ref):
        core = place_ref[1]
        return 0, lax.rem(place_ref[0] + d, chips) * 2 + (1 - core if other else core)

    return pl.pallas_call(
        kv_kernel,
        grid_spec=pltpu.PrefetchScalarGridSpec(
            num_scalar_prefetch=1,
            grid=(chips,),
            in_specs=[
                pl.BlockSpec((rows, depth), lambda d, p: (0, 0)),
                pl.BlockSpec((depth, HEAD), head),
                pl.BlockSpec((depth, HEAD), head),
            ],
            out_specs=pl.BlockSpec((1, rows, 2 * HEAD), lambda d, p: (d, 0, 0)),
        ),
        out_shape=jax.ShapeDtypeStruct((chips, rows, 2 * HEAD), BF),
        compiler_params=params(),
        cost_estimate=pl.CostEstimate(
            flops=2 * chips * rows * depth * 2 * HEAD,
            bytes_accessed=2 * (rows * depth + chips * 2 * HEAD * (depth + rows)),
            transcendentals=0,
        ),
    )(place, vision, k_weight, v_weight)


def query_kernel(parts_ref, sel_ref, gain_ref, out_ref):
    total = jnp.sum(parts_ref[...].astype(F32), axis=0)
    gain = gain_ref[...]
    sel = sel_ref[...]
    for h in range(total.shape[1] // HEAD):
        span = slice(h * HEAD, (h + 1) * HEAD)
        v = total[:, span]
        scale = lax.rsqrt(jnp.mean(v * v, axis=1, keepdims=True) + EPS)
        q = (v * scale * gain).astype(BF)
        out_ref[:, span] = dot(sel, q).astype(BF)


def attention_kernel(me_ref, tiles_ref, own_ref, left_ref, right_ref, gain_ref, q_ref, image_ref, out_ref):
    me = me_ref[0]
    total = own_ref[...].astype(F32) + left_ref[...].astype(F32) + right_ref[...].astype(F32)
    k = total[:, :HEAD]
    scale = lax.rsqrt(jnp.mean(k * k, axis=1, keepdims=True) + EPS)
    k = (k * scale * gain_ref[...]).astype(BF)
    v = total[:, HEAD:].astype(BF)
    rows, keys = q_ref.shape[0], k.shape[0]
    tile = lax.broadcasted_iota(jnp.int32, (1, keys), 1) >> 6
    owner = jnp.zeros((1, keys), jnp.int32)
    end = jnp.int32(0)
    for j in range(4):
        end = end + tiles_ref[me, j]
        owner = owner + (tile >= end).astype(jnp.int32)
    allowed = owner == image_ref[...]
    lane = lax.broadcasted_iota(jnp.int32, (rows, HEAD), 1)
    sums = jnp.zeros((rows, HEAD), F32)
    heads = q_ref.shape[1] // HEAD
    for h in range(heads):
        span = slice(h * HEAD, (h + 1) * HEAD)
        score = lax.dot_general(
            q_ref[:, span], k, (((1,), (1,)), ((), ())), preferred_element_type=F32
        )
        weight = jnp.where(allowed, jnp.exp(score * (1.0 / math.sqrt(HEAD))), 0.0)
        den = jnp.sum(weight, axis=1, keepdims=True)
        high = den.astype(BF).astype(F32)
        sums = sums + jnp.where(lane == h, high, 0.0) + jnp.where(lane == heads + h, den - high, 0.0)
        out_ref[:, span] = dot(weight.astype(BF), v).astype(BF)
    out_ref[:, heads * HEAD :] = sums.astype(BF)


def combine_kernel(parts_ref, sel_ref, out_ref):
    total = lax.dot_general(
        sel_ref[...], parts_ref[...], (((0,), (0,)), ((), ())), preferred_element_type=F32
    )
    heads = out_ref.shape[2] // HEAD
    sums = total[:, heads * HEAD :]
    for h in range(heads):
        span = slice(h * HEAD, (h + 1) * HEAD)
        den = sums[:, h : h + 1] + sums[:, heads + h : heads + h + 1]
        mixed = (total[:, span] / jnp.where(den > 0.0, den, 1.0)).astype(BF)
        out_ref[:, :, span] = jnp.broadcast_to(mixed[None], (out_ref.shape[0],) + mixed.shape)


def shift(value, axis, by):
    n = lax.axis_size(axis)
    return lax.ppermute(value, axis, [(i, (i + by) % n) for i in range(n)])


def exchange(value, axis):
    n = lax.axis_size(axis)
    out = lax.all_to_all(value, axis, 0, 0, tiled=True)
    return out.reshape((n, value.shape[0] // n) + value.shape[1:])


def gather(value, axis):
    n = lax.axis_size(axis)
    wide = jnp.broadcast_to(value[None], (n,) + value.shape)
    out = lax.all_to_all(wide, axis, 0, 0, tiled=True)
    return out.reshape((n * value.shape[0],) + value.shape[1:])


def tensor_sum(part):
    part = part.astype(BF)
    pair = (part.astype(F32) + shift(part, "c", 1).astype(F32)).astype(BF)
    ahead, behind, across = shift(pair, "x", 1), shift(pair, "x", -1), shift(pair, "x", 2)
    return (pair.astype(F32) + across.astype(F32)) + (ahead.astype(F32) + behind.astype(F32))


def shards(
    hidden,
    vision,
    attn_gain,
    q_weight,
    k_weight,
    v_weight,
    q_gain,
    k_gain,
    o_weight,
    gate_logits,
    mlp_gain,
    gate_weight,
    up_weight,
    down_weight,
    image_tiles,
    image_groups,
    image_requests,
):
    groups = lax.axis_size("z") * lax.axis_size("y")
    me = (lax.axis_index("z") * lax.axis_size("y") + lax.axis_index("y")).astype(jnp.int32).reshape(1)
    place = jnp.stack((lax.axis_index("x"), lax.axis_index("c"))).astype(jnp.int32)
    all_rows, width_part = hidden.shape
    own_rows = all_rows // groups
    full_width = width_part * groups
    local_heads = q_weight.shape[1]
    hidden_part = gate_weight.shape[1]
    slot_rows = groups * SLOTS * STEPS
    key_rows = vision.shape[0]

    sel, row_image = pl.pallas_call(
        route_kernel,
        in_specs=[smem(), vmem(), vmem()],
        out_specs=[vmem(), vmem()],
        out_shape=[
            jax.ShapeDtypeStruct((slot_rows, own_rows), BF),
            jax.ShapeDtypeStruct((slot_rows, 1), jnp.int32),
        ],
        compiler_params=params(),
    )(me, image_groups.reshape(groups, -1), image_requests.reshape(groups, -1))

    hidden_f = hidden.astype(F32)
    normed = (hidden_f * attn_gain).astype(BF)
    q_parts = exchange(dot(normed, q_weight).astype(BF), GROUP)

    there = kv_project(place, vision, k_weight, v_weight, True)
    from_core = shift(there, "c", 1)
    here = kv_project(place, vision, k_weight, v_weight, False)
    pieces = (here.astype(F32) + from_core.astype(F32)).astype(BF)
    half = key_rows // 2
    low = shift(pieces[2, :half], "x", 1)
    high = shift(pieces[2, half:], "x", -1)
    forward = jnp.concatenate(
        ((pieces[1, :half].astype(F32) + low.astype(F32)).astype(BF), pieces[1, half:]), axis=0
    )
    backward = jnp.concatenate(
        (pieces[3, :half], (pieces[3, half:].astype(F32) + high.astype(F32)).astype(BF)), axis=0
    )
    kv_left = shift(forward, "x", 1)
    kv_right = shift(backward, "x", -1)

    queries = pl.pallas_call(
        query_kernel,
        in_specs=[vmem()] * 3,
        out_specs=vmem(),
        out_shape=jax.ShapeDtypeStruct((slot_rows, local_heads), BF),
        compiler_params=params(),
    )(q_parts, sel, q_gain.reshape(1, HEAD))
    queries = lax.all_to_all(queries, GROUP, 0, 0, tiled=True)

    mixed = pl.pallas_call(
        attention_kernel,
        in_specs=[smem(), smem()] + [vmem()] * 6,
        out_specs=vmem(),
        out_shape=jax.ShapeDtypeStruct((slot_rows, local_heads + HEAD), BF),
        compiler_params=params(),
    )(me, image_tiles, pieces[0], kv_left, kv_right, k_gain.reshape(1, HEAD), queries, row_image)
    mixed = lax.all_to_all(mixed, GROUP, 0, 0, tiled=True)

    attended = pl.pallas_call(
        combine_kernel,
        in_specs=[vmem()] * 2,
        out_specs=vmem(),
        out_shape=jax.ShapeDtypeStruct((groups, own_rows, local_heads), BF),
        compiler_params=params(),
    )(mixed, sel)
    attended = lax.all_to_all(attended, GROUP, 0, 0, tiled=True).reshape(all_rows, local_heads)

    attn_sum = tensor_sum(dot(attended, o_weight))
    middle = (hidden_f + jnp.tanh(gate_logits[0]) * attn_sum).astype(BF)
    middle_f = middle.astype(F32)
    scaled = (middle_f * mlp_gain).astype(BF)
    square = jnp.sum(middle_f * middle_f, axis=1, keepdims=True)
    square_high = square.astype(BF)
    square_low = (square - square_high.astype(F32)).astype(BF)
    lane = lax.broadcasted_iota(jnp.int32, (all_rows, HEAD), 1)
    extra = jnp.where(lane == 0, square_high, jnp.where(lane == 1, square_low, jnp.zeros((), BF)))
    gate_up = jnp.concatenate(
        (dot(scaled, gate_weight).astype(BF), dot(scaled, up_weight).astype(BF), extra), axis=1
    )
    by_y = jnp.sum(exchange(gate_up, "y").astype(F32), axis=0).astype(BF)
    summed = jnp.sum(exchange(by_y, "z").astype(F32), axis=0)
    square = summed[:, 2 * hidden_part : 2 * hidden_part + 1] + summed[:, 2 * hidden_part + 1 : 2 * hidden_part + 2]
    row_scale = lax.rsqrt(square / full_width + EPS)
    gate = summed[:, :hidden_part] * row_scale
    up = summed[:, hidden_part : 2 * hidden_part] * row_scale
    active = (jax.nn.silu(gate) * up).astype(BF)
    active = gather(gather(active, "z"), "y")
    down_sum = tensor_sum(dot(active, down_weight))
    row_request = jnp.arange(all_rows, dtype=jnp.int32) // STEPS
    request_ids = (image_groups * (own_rows // STEPS) + image_requests).reshape(-1)
    has_image = jnp.any(row_request[:, None] == request_ids[None, :], axis=1).astype(F32)
    return (middle_f + jnp.tanh(gate_logits[1]) * has_image[:, None] * down_sum).astype(BF)


def solution(mesh):
    fine = Mesh(mesh.devices.reshape(8, 4, 4, 2), GROUP + TENSOR)
    in_specs = (
        P(None, GROUP),
        P(GROUP, TENSOR),
        P(GROUP),
        P(GROUP, TENSOR),
        P(TENSOR, None),
        P(TENSOR, None),
        P(),
        P(),
        P(TENSOR, GROUP),
        P(),
        P(GROUP),
        P(GROUP, TENSOR),
        P(GROUP, TENSOR),
        P(TENSOR, GROUP),
        P(),
        P(),
        P(),
    )
    return jax.shard_map(shards, mesh=fine, in_specs=in_specs, out_specs=P(None, GROUP), check_vma=False)
```

time: 938 us -> 261 us (0.28)
  waiting for transfers between devices: 690 us -> 44.2 us
  local copies, waits for them, and re-layouts: 81 us -> 15.1 us
  starting transfers between devices: 10.2 us -> 45.2 us
  blocking collectives: 96.8 us -> 125 us
  between operations: 16.3 us -> 1.77 us
  matrix products: 21.4 us -> 7.02 us
  Pallas kernels: 0 us -> 12.1 us
  other arithmetic: 20.8 us -> 10.3 us
    psum x3 -> x0, waiting for transfers between devices: 346 us -> none  [the longest x1 206 us: shards(): gate_sum, up_sum = lax.psum((gate_part, up_part), 'group')]
    reduce_scatter x2 -> x0, waiting for transfers between devices: 344 us -> none  [the longest x1 302 us: shards(): lax.psum_scatter(jnp.dot(normed, q_weight, preferred_element_type=jnp.flo...]
    all_to_all x0 -> x5, blocking collectives: none -> 125 us  [the longest x2 73.7 us: exchange(): out = lax.all_to_all(value, axis, 0, 0, tiled=True)]
    gather x1 -> x0, local copies, waits for them, and re-layouts: 64.8 us -> none  [shards(): outgoing = jnp.take(packed, source_row, axis=1)]
    psum x1 -> x0, blocking collectives: 61.1 us -> none  [shards(): square_mid = lax.psum(jnp.sum(middle_f * middle_f, axis=1), 'group')]
    all_gather x1 -> x0, blocking collectives: 35.7 us -> none  [shards(): lax.all_gather(attended, 'group', axis=0, tiled=True)]
    ppermute x0 -> x13, starting transfers between devices: none -> 26.2 us  [shift(): return lax.ppermute(value, axis, [(i, (i + by) % n) for i in range(n)])]
    all_to_all x1 -> x3, waiting for transfers between devices: 0.01 us -> 26 us  [the longest x1 19.2 us: gather(): out = lax.all_to_all(wide, axis, 0, 0, tiled=True)]
  transfers between devices with their start and end apart: 6 -> 16, of which waited for: 5 -> 10; matrix products, arithmetic and copies ran while one was open for 1% -> 5% of each run, Pallas kernels for 0% -> 2%
where the time goes in v1:
time: 261 us
  blocking collectives  125 us (48%)
  starting transfers between devices  45.2 us (17%)
  waiting for transfers between devices  44.2 us (17%)
  local copies, waits for them, and re-layouts  15.1 us (6%)
  Pallas kernels  12.1 us (5%)
  other arithmetic  10.3 us (4%)
  matrix products  7.02 us (3%)
    all_to_all x2, blocking collectives, exchange(): out = lax.all_to_all(value, axis, 0, 0, tiled=True)  73.7 us
    ppermute x13, starting transfers between devices, shift(): return lax.ppermute(value, axis, [(i, (i + by) % n) for i in range(n)])  26.2 us
    all_to_all x1, blocking collectives, shards(): mixed = lax.all_to_all(mixed, GROUP, 0, 0, tiled=True)  19.5 us
    all_to_all x1, waiting for transfers between devices, gather(): out = lax.all_to_all(wide, axis, 0, 0, tiled=True)  19.2 us
    ppermute x13, waiting for transfers between devices, shift(): return lax.ppermute(value, axis, [(i, (i + by) % n) for i in range(n)])  18.2 us
    all_to_all x1, blocking collectives, shards(): lax.all_to_all(attended, GROUP, 0, 0, tiled=True)  16.6 us
    all_to_all x1, blocking collectives, gather(): out = lax.all_to_all(wide, axis, 0, 0, tiled=True)  15.2 us
    all_to_all x1, starting transfers between devices, exchange(): out = lax.all_to_all(value, axis, 0, 0, tiled=True)  9.61 us
  transfers between devices with their start and end apart: 16, of which 10 were waited for; matrix products, arithmetic and copies ran while one was open for 5% of the time, Pallas kernels for 2%

profile of v1, /device:TPU:1, one launch (start us, length us, event | category | flops | bytes accessed | tf_op | source)
XLA Modules:
  0.0 260.5 jit_solution(14725490464034907472)
XLA Ops:
  4.7 4.0 %shard_map.164 = bf16[4,640,256]{2,1,0:T(8,128)(2,1)} custom-call(s32[2]{0:T(128)S(1)} %pad_add_fusion.place_ref, bf16[640,1024]{1,0:T(8,128)(2,1)S(1)} %copy-done.5, bf16[1024,1024]{1,0:T(8,128)(2,1)S(1)} %copy-done.1, bf16[1024,1024]{1,0:T(8,128)(2,1)S(1)} %copy-done.3), custom_call_target="tpu_custom_call" | custom-call | flops 1342177280 | bytes 4718592 | tf_op jit(solution)/shard_map/pallas_call | solution.py:84
  8.7 3.2 %collective-permute-start = (bf16[4,640,256]{2,1,0:T(8,128)(2,1)}, bf16[4,640,256]{2,1,0:T(8,128)(2,1)}, u32[]{:S(2)}, u32[]{:S(2)}) collective-permute-start(bf16[4,640,256]{2,1,0:T(8,128)(2,1)} %shard_map.164), channel_id=1, source_target_pairs={{0,1},{1,0},{2,3},{3,2},{4,5},{5,4},{6,7},{7,6},{8,9},{9,8},{10,11... | collective-permute-start | bytes 3932168 | tf_op jit(solution)/shard_map/ppermute | solution.py:164
  14.4 9.6 %all-to-all-start = ((bf16[32,8,1024]{2,1,0:T(8,128)(2,1)}), bf16[32,8,1024]{2,1,0:T(8,128)(2,1)}, u32[]{:S(2)}, u32[]{:S(2)}) async-start(bf16[32,8,1024]{2,1,0:T(8,128)(2,1)} %fusion), calls=%async_computation | async-start | bytes 1048576 | tf_op jit(solution)/shard_map/all_to_all | solution.py:169
  27.3 3.3 %shard_map.163 = bf16[4,640,256]{2,1,0:T(8,128)(2,1)S(1)} custom-call(s32[2]{0:T(128)S(1)} %pad_add_fusion.place_ref, bf16[640,1024]{1,0:T(8,128)(2,1)S(1)} %copy-done.6, bf16[1024,1024]{1,0:T(8,128)(2,1)S(1)} %copy-done.2, bf16[1024,1024]{1,0:T(8,128)(2,1)S(1)} %copy-done.4), custom_call_target="tpu_custom_call" | custom-call | flops 1342177280 | bytes 4718592 | tf_op jit(solution)/shard_map/pallas_call | solution.py:84
  36.5 4.3 %all-to-all-done.parts_ref = bf16[32,8,1024]{2,1,0:T(8,128)(2,1)} async-done(((bf16[32,8,1024]{2,1,0:T(8,128)(2,1)}), bf16[32,8,1024]{2,1,0:T(8,128)(2,1)}, u32[]{:S(2)}, u32[]{:S(2)}) %all-to-all-start) | async-done | bytes 524320 | tf_op jit(solution)/shard_map/all_to_all | solution.py:169
  43.0 5.0 %all-to-all-start.1 = ((bf16[32,4,1024]{2,1,0:T(4,128)(2,1)}), bf16[32,4,1024]{2,1,0:T(4,128)(2,1)S(1)}, u32[]{:S(2)}, u32[]{:S(2)}) async-start(bf16[32,4,1024]{2,1,0:T(4,128)(2,1)} %all_to_all.43), calls=%async_computation.1 | async-start | bytes 524288 | tf_op jit(solution)/shard_map/all_to_all | solution.py:255
  59.0 4.7 %collective-permute-done.2.left_ref = bf16[640,256]{1,0:T(8,128)(2,1)S(1)} collective-permute-done((bf16[640,256]{1,0:T(8,128)(2,1)}, bf16[640,256]{1,0:T(8,128)(2,1)S(1)}, u32[]{:S(2)}, u32[]{:S(2)}) %collective-permute-start.2) | collective-permute-done | bytes 327712 | tf_op jit(solution)/shard_map/ppermute | solution.py:164
  63.7 2.7 %shard_map.167 = bf16[128,1152]{1,0:T(8,128)(2,1)S(1)} custom-call(s32[1]{0:T(128)} %bitcast.1.me_ref, s32[32,4]{1,0:T(8,128)S(1)} %copy.43.tiles_ref, bf16[640,256]{1,0:T(8,128)(2,1)S(1)} %slice_bitcast_fusion.own_ref, bf16[640,256]{1,0:T(8,128)(2,1)S(1)} %collective-permute-done.2.left_ref, bf16[640,256]{1,0:T(8,128)(2,1)S(1)} %collective-permute-done.4.right_ref, ...), custom_call_target="tpu_custom_call" | custom-call | tf_op jit(solution)/shard_map/pallas_call | solution.py:257
  66.4 19.5 %all_to_all.64 = bf16[32,4,1152]{2,1,0:T(4,128)(2,1)S(1)} all-to-all(bf16[32,4,1152]{2,1,0:T(4,128)(2,1)S(1)} %all_to_all.46), channel_id=1, replica_groups=mesh['z'=8,'y'=4,'x'=4,'c'=2] {'z','y'}, dimensions={0} | all-to-all | bytes 589824 | tf_op jit(solution)/shard_map/all_to_all | solution.py:264
  86.5 16.6 %all_to_all.65 = bf16[32,8,1024]{2,1,0:T(8,128)(2,1)S(1)} all-to-all(bf16[32,8,1024]{2,1,0:T(8,128)(2,1)S(1)} %shard_map.168), channel_id=1, replica_groups=mesh['z'=8,'y'=4,'x'=4,'c'=2] {'z','y'}, dimensions={0} | all-to-all | bytes 1048576 | tf_op jit(solution)/shard_map/all_to_all | solution.py:273
  103.5 6.6 %collective-permute-start.5 = (bf16[256,256]{0,1:T(8,128)(2,1)S(1)}, bf16[256,256]{0,1:T(8,128)(2,1)S(1)}, u32[]{:S(2)}, u32[]{:S(2)}) collective-permute-start(bf16[256,256]{0,1:T(8,128)(2,1)S(1)} %convolution_convert_fusion.3), channel_id=1, source_target_pairs={{0,1},{1,0},{2,3},{3,2},{4,5},{5,4},{6,7},{7,6},{8,9},{9,8},{10,11... | collective-permute-start | bytes 393224 | tf_op jit(solution)/shard_map/ppermute | solution.py:164
  111.4 2.7 %collective-permute-start.8 = (bf16[256,256]{0,1:T(8,128)(2,1)S(1)}, bf16[256,256]{0,1:T(8,128)(2,1)S(1)}, u32[]{:S(2)}, u32[]{:S(2)}) collective-permute-start(bf16[256,256]{0,1:T(8,128)(2,1)S(1)} %add_convert_fusion.2), channel_id=1, source_target_pairs={{0,6},{2,0},{4,2},{6,4},{1,7},{3,1},{5,3},{7,5},{8,14},{10,8},{12,... | collective-permute-start | bytes 393224 | tf_op jit(solution)/shard_map/ppermute | solution.py:164
  117.4 3.4 %collective-permute-done.7 = bf16[256,256]{0,1:T(8,128)(2,1)S(1)} collective-permute-done((bf16[256,256]{0,1:T(8,128)(2,1)S(1)}, bf16[256,256]{0,1:T(8,128)(2,1)S(1)}, u32[]{:S(2)}, u32[]{:S(2)}) %collective-permute-start.7) | collective-permute-done | bytes 131104 | tf_op jit(solution)/shard_map/ppermute | solution.py:164
  123.7 46.7 %all_to_all.66 = bf16[4,64,7296]{2,1,0:T(8,128)(2,1)} all-to-all(bf16[4,64,7296]{2,1,0:T(8,128)(2,1)S(1)} %bitcast.44), channel_id=1, replica_groups=mesh['z'=8,'y'=4,'x'=4,'c'=2] {'y'}, dimensions={0} | all-to-all | bytes 7471104 | tf_op jit(solution)/shard_map/all_to_all | solution.py:169
  170.4 2.7 %reduce_sum.31 = bf16[64,7296]{1,0:T(8,128)(2,1)S(1)} reduce(bf16[4,64,7296]{2,1,0:T(8,128)(2,1)} %all_to_all.66, bf16[]{:T(256)} %constant.49.clone.1), dimensions={0}, to_apply=%region_2.3 | reduce | flops 1400832 | bytes 4669442 | tf_op jit(solution)/shard_map/reduce_sum | solution.py:287
  173.1 27.0 %all_to_all.67 = bf16[8,8,7296]{2,1,0:T(8,128)(2,1)S(1)} all-to-all(bf16[8,8,7296]{2,1,0:T(8,128)(2,1)S(1)} %bitcast.45), channel_id=1, replica_groups=mesh['z'=8,'y'=4,'x'=4,'c'=2] {'z'}, dimensions={0} | all-to-all | bytes 1867776 | tf_op jit(solution)/shard_map/all_to_all | solution.py:169
  200.6 15.2 %all_to_all.68 = bf16[8,8,3584]{2,1,0:T(8,128)(2,1)S(1)} all-to-all(bf16[8,8,3584]{2,1,0:T(8,128)(2,1)S(1)} %broadcast_in_dim.41), channel_id=1, replica_groups=mesh['z'=8,'y'=4,'x'=4,'c'=2] {'z'}, dimensions={0} | all-to-all | bytes 917504 | tf_op jit(solution)/shard_map/all_to_all | solution.py:176
  217.1 4.4 %all-to-all-start.7 = ((bf16[4,64,3584]{2,1,0:T(8,128)(2,1)}), bf16[4,64,3584]{2,1,0:T(8,128)(2,1)}, u32[]{:S(2)}, u32[]{:S(2)}) async-start(bf16[4,64,3584]{2,1,0:T(8,128)(2,1)} %broadcast_in_dim.43), calls=%async_computation.7 | async-start | bytes 3670016 | tf_op jit(solution)/shard_map/all_to_all | solution.py:176
  221.5 19.2 %all-to-all-done.7 = bf16[4,64,3584]{2,1,0:T(8,128)(2,1)} async-done(((bf16[4,64,3584]{2,1,0:T(8,128)(2,1)}), bf16[4,64,3584]{2,1,0:T(8,128)(2,1)}, u32[]{:S(2)}, u32[]{:S(2)}) %all-to-all-start.7) | async-done | bytes 1835040 | tf_op jit(solution)/shard_map/all_to_all | solution.py:176
  240.8 2.9 %convolution_convert_fusion.4 = bf16[256,256]{0,1:T(8,128)(2,1)S(1)} fusion(bf16[256,3584]{1,0:T(8,128)(2,1)} %bitcast.19, bf16[3584,256]{1,0:T(8,128)(2,1)} %param.30), kind=kOutput, calls=%fused_computation.8 | convolution fusion | flops 469827584 | bytes 3801088 | tf_op jit(solution)/shard_map/dot_general | solution.py:27
  243.7 5.4 %collective-permute-start.9 = (bf16[256,256]{0,1:T(8,128)(2,1)S(1)}, bf16[256,256]{0,1:T(8,128)(2,1)S(1)}, u32[]{:S(2)}, u32[]{:S(2)}) collective-permute-start(bf16[256,256]{0,1:T(8,128)(2,1)S(1)} %convolution_convert_fusion.4), channel_id=1, source_target_pairs={{0,1},{1,0},{2,3},{3,2},{4,5},{5,4},{6,7},{7,6},{8,9},{9,8},{10,11... | collective-permute-start | bytes 393224 | tf_op jit(solution)/shard_map/ppermute | solution.py:164
  250.5 2.7 %collective-permute-start.12 = (bf16[256,256]{0,1:T(8,128)(2,1)S(1)}, bf16[256,256]{0,1:T(8,128)(2,1)S(1)}, u32[]{:S(2)}, u32[]{:S(2)}) collective-permute-start(bf16[256,256]{0,1:T(8,128)(2,1)S(1)} %add_convert_fusion.1), channel_id=1, source_target_pairs={{0,6},{2,0},{4,2},{6,4},{1,7},{3,1},{5,3},{7,5},{8,14},{10,8},{12,... | collective-permute-start | bytes 393224 | tf_op jit(solution)/shard_map/ppermute | solution.py:164
  253.1 3.7 %collective-permute-done.10 = bf16[256,256]{0,1:T(8,128)(2,1)S(1)} collective-permute-done((bf16[256,256]{0,1:T(8,128)(2,1)S(1)}, bf16[256,256]{0,1:T(8,128)(2,1)S(1)}, u32[]{:S(2)}, u32[]{:S(2)}) %collective-permute-start.10) | collective-permute-done | bytes 131104 | tf_op jit(solution)/shard_map/ppermute | solution.py:164
  256.8 2.8 %collective-permute-done.11 = bf16[256,256]{0,1:T(8,128)(2,1)S(1)} collective-permute-done((bf16[256,256]{0,1:T(8,128)(2,1)S(1)}, bf16[256,256]{0,1:T(8,128)(2,1)S(1)}, u32[]{:S(2)}, u32[]{:S(2)}) %collective-permute-start.11) | collective-permute-done | bytes 131104 | tf_op jit(solution)/shard_map/ppermute | solution.py:164
  (105 shorter events, 40.5 us)
Async XLA Ops:
  0.0 121.0 %copy-start = (bf16[256,3584]{1,0:T(8,128)(2,1)S(1)}, bf16[256,3584]{1,0:T(8,128)(2,1)}, u32[]{:S(2)}) copy-start(bf16[256,3584]{1,0:T(8,128)(2,1)} %param.29) | copy-start | bytes 5505028
  8.7 15.3 %copy-start.6 = (bf16[640,1024]{1,0:T(8,128)(2,1)S(1)}, bf16[640,1024]{1,0:T(8,128)(2,1)}, u32[]{:S(2)}) copy-start(bf16[640,1024]{1,0:T(8,128)(2,1)} %vision_ref.3) | copy-start | bytes 3932164
  8.7 21.8 %collective-permute-start = (bf16[4,640,256]{2,1,0:T(8,128)(2,1)}, bf16[4,640,256]{2,1,0:T(8,128)(2,1)}, u32[]{:S(2)}, u32[]{:S(2)}) collective-permute-start(bf16[4,640,256]{2,1,0:T(8,128)(2,1)} %shard_map.164), channel_id=1, source_target_pairs={{0,1},{1,0},{2,3},{3,2},{4,5},{5,4},{6,7},{7,6},{8,9},{9,8},{10,11... | collective-permute-start | bytes 3932168 | tf_op jit(solution)/shard_map/ppermute | solution.py:164
  14.4 26.4 %all-to-all-start = ((bf16[32,8,1024]{2,1,0:T(8,128)(2,1)}), bf16[32,8,1024]{2,1,0:T(8,128)(2,1)}, u32[]{:S(2)}, u32[]{:S(2)}) async-start(bf16[32,8,1024]{2,1,0:T(8,128)(2,1)} %fusion), calls=%async_computation | async-start | bytes 1048576 | tf_op jit(solution)/shard_map/all_to_all | solution.py:169
  32.2 16.9 %copy-start.9 = (bf16[4,640,256]{2,1,0:T(8,128)(2,1)}, bf16[4,640,256]{2,1,0:T(8,128)(2,1)S(1)}, u32[]{:S(2)}) copy-start(bf16[4,640,256]{2,1,0:T(8,128)(2,1)S(1)} %add_convert_fusion) | copy-start | bytes 3932164
  33.1 14.9 %collective-permute-start.1 = (bf16[320,256]{1,0:T(8,128)(2,1)}, bf16[320,256]{1,0:T(8,128)(2,1)}, u32[]{:S(2)}, u32[]{:S(2)}) collective-permute-start(bf16[320,256]{1,0:T(8,128)(2,1)} %get-tuple-element.16), channel_id=1, source_target_pairs={{0,2},{2,4},{4,6},{6,0},{1,3},{3,5},{5,7},{7,1},{8,10},{10,12},{12... | collective-permute-start | bytes 491528 | tf_op jit(solution)/shard_map/ppermute | solution.py:164
  34.4 13.7 %collective-permute-start.3 = (bf16[320,256]{1,0:T(8,128)(2,1)}, bf16[320,256]{1,0:T(8,128)(2,1)}, u32[]{:S(2)}, u32[]{:S(2)}) collective-permute-start(bf16[320,256]{1,0:T(8,128)(2,1)} %get-tuple-element.14), channel_id=1, source_target_pairs={{0,6},{2,0},{4,2},{6,4},{1,7},{3,1},{5,3},{7,5},{8,14},{10,8},{12,... | collective-permute-start | bytes 491528 | tf_op jit(solution)/shard_map/ppermute | solution.py:164
  43.0 15.4 %all-to-all-start.1 = ((bf16[32,4,1024]{2,1,0:T(4,128)(2,1)}), bf16[32,4,1024]{2,1,0:T(4,128)(2,1)S(1)}, u32[]{:S(2)}, u32[]{:S(2)}) async-start(bf16[32,4,1024]{2,1,0:T(4,128)(2,1)} %all_to_all.43), calls=%async_computation.1 | async-start | bytes 524288 | tf_op jit(solution)/shard_map/all_to_all | solution.py:255
  48.0 15.7 %copy-start.7 = (f32[128]{0:T(128)S(1)}, f32[128]{0:T(128)}, u32[]{:S(2)}) copy-start(f32[128]{0:T(128)} %param.24) | copy-start | bytes 1540
  50.8 8.2 %collective-permute-start.4 = (bf16[640,256]{1,0:T(8,128)(2,1)}, bf16[640,256]{1,0:T(8,128)(2,1)S(1)}, u32[]{:S(2)}, u32[]{:S(2)}) collective-permute-start(bf16[640,256]{1,0:T(8,128)(2,1)} %pad_maximum_fusion.2), channel_id=1, source_target_pairs={{0,6},{2,0},{4,2},{6,4},{1,7},{3,1},{5,3},{7,5},{8,14},{10,8},{12,... | collective-permute-start | bytes 983048 | tf_op jit(solution)/shard_map/ppermute | solution.py:164
  54.9 8.7 %collective-permute-start.2 = (bf16[640,256]{1,0:T(8,128)(2,1)}, bf16[640,256]{1,0:T(8,128)(2,1)S(1)}, u32[]{:S(2)}, u32[]{:S(2)}) collective-permute-start(bf16[640,256]{1,0:T(8,128)(2,1)} %pad_maximum_fusion.1), channel_id=1, source_target_pairs={{0,2},{2,4},{4,6},{6,0},{1,3},{3,5},{5,7},{7,1},{8,10},{10,12},{12... | collective-permute-start | bytes 983048 | tf_op jit(solution)/shard_map/ppermute | solution.py:164
  66.3 36.8 %copy-start.13 = (bf16[1024,256]{1,0:T(8,128)(2,1)S(1)}, bf16[1024,256]{1,0:T(8,128)(2,1)}, u32[]{:S(2)}) copy-start(bf16[1024,256]{1,0:T(8,128)(2,1)} %param.25) | copy-start | bytes 1572868
  86.0 28.1 %copy-start.19 = (f32[2]{0:T(128)S(1)}, f32[2]{0:T(128)}, u32[]{:S(2)}) copy-start(f32[2]{0:T(128)} %param.26) | copy-start | bytes 28
  86.1 34.8 %copy-start.12 = (bf16[256,256]{0,1:T(8,128)(2,1)S(1)}, bf16[256,256]{0,1:T(8,128)(2,1)}, u32[]{:S(2)}) copy-start(bf16[256,256]{0,1:T(8,128)(2,1)} %copy-done.11) | copy-start | bytes 393220
  86.5 34.4 %copy-start.15 = (f32[256]{0:T(256)S(1)}, f32[256]{0:T(256)}, u32[]{:S(2)}) copy-start(f32[256]{0:T(256)} %param.27) | copy-start | bytes 3076
  103.5 7.6 %collective-permute-start.5 = (bf16[256,256]{0,1:T(8,128)(2,1)S(1)}, bf16[256,256]{0,1:T(8,128)(2,1)S(1)}, u32[]{:S(2)}, u32[]{:S(2)}) collective-permute-start(bf16[256,256]{0,1:T(8,128)(2,1)S(1)} %convolution_convert_fusion.3), channel_id=1, source_target_pairs={{0,1},{1,0},{2,3},{3,2},{4,5},{5,4},{6,7},{7,6},{8,9},{9,8},{10,11... | collective-permute-start | bytes 393224 | tf_op jit(solution)/shard_map/ppermute | solution.py:164
  111.1 6.4 %collective-permute-start.6 = (bf16[256,256]{0,1:T(8,128)(2,1)S(1)}, bf16[256,256]{0,1:T(8,128)(2,1)S(1)}, u32[]{:S(2)}, u32[]{:S(2)}) collective-permute-start(bf16[256,256]{0,1:T(8,128)(2,1)S(1)} %add_convert_fusion.2), channel_id=1, source_target_pairs={{0,4},{2,6},{4,0},{6,2},{1,5},{3,7},{5,1},{7,3},{8,12},{10,14},{12... | collective-permute-start | bytes 393224 | tf_op jit(solution)/shard_map/ppermute | solution.py:164
  111.2 9.7 %collective-permute-start.7 = (bf16[256,256]{0,1:T(8,128)(2,1)S(1)}, bf16[256,256]{0,1:T(8,128)(2,1)S(1)}, u32[]{:S(2)}, u32[]{:S(2)}) collective-permute-start(bf16[256,256]{0,1:T(8,128)(2,1)S(1)} %add_convert_fusion.2), channel_id=1, source_target_pairs={{0,2},{2,4},{4,6},{6,0},{1,3},{3,5},{5,7},{7,1},{8,10},{10,12},{12... | collective-permute-start | bytes 393224 | tf_op jit(solution)/shard_map/ppermute | solution.py:164
  111.4 9.4 %collective-permute-start.8 = (bf16[256,256]{0,1:T(8,128)(2,1)S(1)}, bf16[256,256]{0,1:T(8,128)(2,1)S(1)}, u32[]{:S(2)}, u32[]{:S(2)}) collective-permute-start(bf16[256,256]{0,1:T(8,128)(2,1)S(1)} %add_convert_fusion.2), channel_id=1, source_target_pairs={{0,6},{2,0},{4,2},{6,4},{1,7},{3,1},{5,3},{7,5},{8,14},{10,8},{12,... | collective-permute-start | bytes 393224 | tf_op jit(solution)/shard_map/ppermute | solution.py:164
  217.1 23.7 %all-to-all-start.7 = ((bf16[4,64,3584]{2,1,0:T(8,128)(2,1)}), bf16[4,64,3584]{2,1,0:T(8,128)(2,1)}, u32[]{:S(2)}, u32[]{:S(2)}) async-start(bf16[4,64,3584]{2,1,0:T(8,128)(2,1)} %broadcast_in_dim.43), calls=%async_computation.7 | async-start | bytes 3670016 | tf_op jit(solution)/shard_map/all_to_all | solution.py:176
  243.7 6.6 %collective-permute-start.9 = (bf16[256,256]{0,1:T(8,128)(2,1)S(1)}, bf16[256,256]{0,1:T(8,128)(2,1)S(1)}, u32[]{:S(2)}, u32[]{:S(2)}) collective-permute-start(bf16[256,256]{0,1:T(8,128)(2,1)S(1)} %convolution_convert_fusion.4), channel_id=1, source_target_pairs={{0,1},{1,0},{2,3},{3,2},{4,5},{5,4},{6,7},{7,6},{8,9},{9,8},{10,11... | collective-permute-start | bytes 393224 | tf_op jit(solution)/shard_map/ppermute | solution.py:164
  250.3 6.6 %collective-permute-start.10 = (bf16[256,256]{0,1:T(8,128)(2,1)S(1)}, bf16[256,256]{0,1:T(8,128)(2,1)S(1)}, u32[]{:S(2)}, u32[]{:S(2)}) collective-permute-start(bf16[256,256]{0,1:T(8,128)(2,1)S(1)} %add_convert_fusion.1), channel_id=1, source_target_pairs={{0,4},{2,6},{4,0},{6,2},{1,5},{3,7},{5,1},{7,3},{8,12},{10,14},{12... | collective-permute-start | bytes 393224 | tf_op jit(solution)/shard_map/ppermute | solution.py:164
  250.4 9.3 %collective-permute-start.11 = (bf16[256,256]{0,1:T(8,128)(2,1)S(1)}, bf16[256,256]{0,1:T(8,128)(2,1)S(1)}, u32[]{:S(2)}, u32[]{:S(2)}) collective-permute-start(bf16[256,256]{0,1:T(8,128)(2,1)S(1)} %add_convert_fusion.1), channel_id=1, source_target_pairs={{0,2},{2,4},{4,6},{6,0},{1,3},{3,5},{5,7},{7,1},{8,10},{10,12},{12... | collective-permute-start | bytes 393224 | tf_op jit(solution)/shard_map/ppermute | solution.py:164
  250.5 9.2 %collective-permute-start.12 = (bf16[256,256]{0,1:T(8,128)(2,1)S(1)}, bf16[256,256]{0,1:T(8,128)(2,1)S(1)}, u32[]{:S(2)}, u32[]{:S(2)}) collective-permute-start(bf16[256,256]{0,1:T(8,128)(2,1)S(1)} %add_convert_fusion.1), channel_id=1, source_target_pairs={{0,6},{2,0},{4,2},{6,4},{1,7},{3,1},{5,3},{7,5},{8,14},{10,8},{12,... | collective-permute-start | bytes 393224 | tf_op jit(solution)/shard_map/ppermute | solution.py:164
  (13 other events, 69.6 us)

commit v2 on v1

--- a/solution.py
+++ b/solution.py
@@ -1,3 +1,4 @@
+import functools
 import math
 
 import jax
@@ -68,21 +69,50 @@
     image_ref[...] = jnp.where(slot1 == 0, first_image, last_image)
 
 
-def kv_kernel(place_ref, vision_ref, k_ref, v_ref, out_ref):
+def kv_there_kernel(place_ref, vision_ref, k_ref, v_ref, out_ref):
     weight = jnp.concatenate((k_ref[...], v_ref[...]), axis=1)
     out_ref[0] = dot(vision_ref[...], weight).astype(BF)
 
 
-def kv_project(place, vision, k_weight, v_weight, other):
+def kv_here_kernel(place_ref, vision_ref, k_ref, v_ref, core_ref, low_ref, high_ref, ahead_ref, behind_ref, own_ref):
+    weight = jnp.concatenate((k_ref[...], v_ref[...]), axis=1)
+    total = (dot(vision_ref[...], weight) + core_ref[0].astype(F32)).astype(BF)
+    half = low_ref.shape[0]
+    step = pl.program_id(0)
+
+    @pl.when(step == 0)
+    def _():
+        low_ref[...] = total[:half]
+        high_ref[...] = total[half:]
+
+    @pl.when(step == 1)
+    def _():
+        ahead_ref[...] = total
+
+    @pl.when(step == 2)
+    def _():
+        behind_ref[...] = total
+
+    @pl.when(step == 3)
+    def _():
+        own_ref[...] = total
+
+
+def kv_project(place, vision, k_weight, v_weight, from_core=None):
     rows, depth = vision.shape
     chips = 4
+    other = from_core is None
 
     def head(d, place_ref):
         core = place_ref[1]
-        return 0, lax.rem(place_ref[0] + d, chips) * 2 + (1 - core if other else core)
-
+        ahead = jnp.where(d == 0, 2, jnp.where(d == 1, 1, jnp.where(d == 2, 3, 0)))
+        return 0, lax.rem(place_ref[0] + ahead, chips) * 2 + (1 - core if other else core)
+
+    one = pl.BlockSpec((1, rows, 2 * HEAD), lambda d, p: (d, 0, 0))
+    sizes = [rows // 2, rows // 2, rows, rows, rows]
+    whole = [pl.BlockSpec((n, 2 * HEAD), lambda d, p: (0, 0)) for n in sizes]
     return pl.pallas_call(
-        kv_kernel,
+        kv_there_kernel if other else kv_here_kernel,
         grid_spec=pltpu.PrefetchScalarGridSpec(
             num_scalar_prefetch=1,
             grid=(chips,),
@@ -90,17 +120,28 @@
                 pl.BlockSpec((rows, depth), lambda d, p: (0, 0)),
                 pl.BlockSpec((depth, HEAD), head),
                 pl.BlockSpec((depth, HEAD), head),
-            ],
-            out_specs=pl.BlockSpec((1, rows, 2 * HEAD), lambda d, p: (d, 0, 0)),
+            ]
+            + ([] if other else [one]),
+            out_specs=one if other else whole,
         ),
-        out_shape=jax.ShapeDtypeStruct((chips, rows, 2 * HEAD), BF),
+        out_shape=jax.ShapeDtypeStruct((chips, rows, 2 * HEAD), BF)
+        if other
+        else [jax.ShapeDtypeStruct((n, 2 * HEAD), BF) for n in sizes],
         compiler_params=params(),
         cost_estimate=pl.CostEstimate(
             flops=2 * chips * rows * depth * 2 * HEAD,
             bytes_accessed=2 * (rows * depth + chips * 2 * HEAD * (depth + rows)),
             transcendentals=0,
         ),
-    )(place, vision, k_weight, v_weight)
+    )(place, vision, k_weight, v_weight, *(() if other else (from_core,)))
+
+
+def kv_merge_kernel(ahead_ref, behind_ref, low_ref, high_ref, forward_ref, backward_ref):
+    half = low_ref.shape[0]
+    forward_ref[:half] = (ahead_ref[:half].astype(F32) + low_ref[...].astype(F32)).astype(BF)
+    forward_ref[half:] = ahead_ref[half:]
+    backward_ref[:half] = behind_ref[:half]
+    backward_ref[half:] = (behind_ref[half:].astype(F32) + high_ref[...].astype(F32)).astype(BF)
 
 
 def query_kernel(parts_ref, sel_ref, gain_ref, out_ref):
@@ -159,22 +200,51 @@
         out_ref[:, :, span] = jnp.broadcast_to(mixed[None], (out_ref.shape[0],) + mixed.shape)
 
 
+def gate_up_kernel(m0, m1, m2, m3, w0, w1, gate2, up2, w3, out_ref):
+    blocks = (m0, m1, m2, m3)
+    units = gate2.shape[1]
+    columns = 2 * units
+    for start in range(0, columns, HEAD):
+        span = slice(start, start + HEAD)
+        part = slice(start % units, start % units + HEAD)
+        w2 = gate2 if start < units else up2
+        total = dot(m0[...], w0[:, span]) + dot(m1[...], w1[:, span])
+        total = total + dot(m2[...], w2[:, part]) + dot(m3[...], w3[:, span])
+        out_ref[:, span] = total.astype(BF)
+    square = jnp.zeros((m0.shape[0], 1), F32)
+    for m in blocks:
+        value = m[...].astype(F32)
+        square = square + jnp.sum(value * value, axis=1, keepdims=True)
+    high = square.astype(BF).astype(F32)
+    lane = lax.broadcasted_iota(jnp.int32, (m0.shape[0], HEAD), 1)
+    extra = jnp.where(lane == 0, high, jnp.where(lane == 1, square - high, 0.0))
+    out_ref[:, columns:] = extra.astype(BF)
+
+
+def active_kernel(full_width, parts_ref, out_ref):
+    total = jnp.sum(parts_ref[...].astype(F32), axis=0)
+    units = out_ref.shape[2]
+    square = total[:, 2 * units : 2 * units + 1] + total[:, 2 * units + 1 : 2 * units + 2]
+    scale = lax.rsqrt(square * (1.0 / full_width) + EPS)
+    gate = total[:, :units] * scale
+    up = total[:, units : 2 * units] * scale
+    active = (gate / (1.0 + jnp.exp(-gate)) * up).astype(BF)
+    out_ref[...] = jnp.broadcast_to(active[None], out_ref.shape)
+
+
 def shift(value, axis, by):
     n = lax.axis_size(axis)
     return lax.ppermute(value, axis, [(i, (i + by) % n) for i in range(n)])
+
+
+def after(value, *others):
+    return lax.optimization_barrier((value,) + others)[0]
 
 
 def exchange(value, axis):
     n = lax.axis_size(axis)
     out = lax.all_to_all(value, axis, 0, 0, tiled=True)
     return out.reshape((n, value.shape[0] // n) + value.shape[1:])
-
-
-def gather(value, axis):
-    n = lax.axis_size(axis)
-    wide = jnp.broadcast_to(value[None], (n,) + value.shape)
-    out = lax.all_to_all(wide, axis, 0, 0, tiled=True)
-    return out.reshape((n * value.shape[0],) + value.shape[1:])
 
 
 def tensor_sum(part):
@@ -227,23 +297,49 @@
 
     hidden_f = hidden.astype(F32)
     normed = (hidden_f * attn_gain).astype(BF)
-    q_parts = exchange(dot(normed, q_weight).astype(BF), GROUP)
-
-    there = kv_project(place, vision, k_weight, v_weight, True)
-    from_core = shift(there, "c", 1)
-    here = kv_project(place, vision, k_weight, v_weight, False)
-    pieces = (here.astype(F32) + from_core.astype(F32)).astype(BF)
-    half = key_rows // 2
-    low = shift(pieces[2, :half], "x", 1)
-    high = shift(pieces[2, half:], "x", -1)
-    forward = jnp.concatenate(
-        ((pieces[1, :half].astype(F32) + low.astype(F32)).astype(BF), pieces[1, half:]), axis=0
-    )
-    backward = jnp.concatenate(
-        (pieces[3, :half], (pieces[3, half:].astype(F32) + high.astype(F32)).astype(BF)), axis=0
-    )
+    q_part = dot(normed, q_weight).astype(BF)
+    q_part, vision = lax.optimization_barrier((q_part, vision))
+    q_parts = exchange(q_part, GROUP)
+
+    there = kv_project(place, vision, k_weight, v_weight)
+    low, high, ahead, behind, own = kv_project(place, vision, k_weight, v_weight, shift(there, "c", 1))
+    q_parts = after(q_parts, own)
+    forward, backward = pl.pallas_call(
+        kv_merge_kernel,
+        in_specs=[vmem()] * 4,
+        out_specs=[vmem()] * 2,
+        out_shape=[jax.ShapeDtypeStruct(ahead.shape, BF)] * 2,
+        compiler_params=params(),
+    )(ahead, behind, shift(low, "x", 1), shift(high, "x", -1))
     kv_left = shift(forward, "x", 1)
     kv_right = shift(backward, "x", -1)
+
+    chips_y = lax.axis_size("y")
+    units = hidden_part // chips_y
+    gain = mlp_gain[:, None]
+
+    def columns(weight, d):
+        at = lax.rem(lax.axis_index("y") + d, chips_y) * units
+        return lax.dynamic_slice_in_dim(weight, at, units, 1).astype(F32)
+
+    def rows(weight, d, start, size):
+        at = lax.rem(lax.axis_index("y") + d, chips_y) * units + start
+        return lax.dynamic_slice_in_dim(weight, at, size, 0)
+
+    def wide(*parts):
+        return (jnp.concatenate(parts, axis=1) * gain).astype(BF)
+
+    wide_0 = wide(columns(gate_weight, 0), columns(up_weight, 0))
+    wide_1 = wide(columns(gate_weight, 1), columns(up_weight, 1), columns(gate_weight, 2))
+    wide_3 = wide(columns(gate_weight, 3), columns(up_weight, 3), columns(up_weight, 2))
+    wide_1 = shift(wide_1, "y", 1)
+    wide_3 = shift(wide_3, "y", -1)
+    gate_2 = shift(wide_1[:, 2 * units :], "y", 1)
+    up_2 = shift(wide_3[:, 2 * units :], "y", -1)
+    half = units // 2
+    down_0 = rows(down_weight, 0, 0, units)
+    down_1 = jnp.concatenate((rows(down_weight, 1, 0, units), rows(down_weight, 2, 0, half)), axis=0)
+    down_3 = jnp.concatenate((rows(down_weight, 3, 0, units), rows(down_weight, 2, half, half)), axis=0)
 
     queries = pl.pallas_call(
         query_kernel,
@@ -254,15 +350,17 @@
     )(q_parts, sel, q_gain.reshape(1, HEAD))
     queries = lax.all_to_all(queries, GROUP, 0, 0, tiled=True)
 
+    queries = after(queries, wide_1, wide_3)
     mixed = pl.pallas_call(
         attention_kernel,
         in_specs=[smem(), smem()] + [vmem()] * 6,
         out_specs=vmem(),
         out_shape=jax.ShapeDtypeStruct((slot_rows, local_heads + HEAD), BF),
         compiler_params=params(),
-    )(me, image_tiles, pieces[0], kv_left, kv_right, k_gain.reshape(1, HEAD), queries, row_image)
+    )(me, image_tiles, own, kv_left, kv_right, k_gain.reshape(1, HEAD), queries, row_image)
     mixed = lax.all_to_all(mixed, GROUP, 0, 0, tiled=True)
 
+    mixed = after(mixed, gate_2, up_2)
     attended = pl.pallas_call(
         combine_kernel,
         in_specs=[vmem()] * 2,
@@ -270,29 +368,38 @@
         out_shape=jax.ShapeDtypeStruct((groups, own_rows, local_heads), BF),
         compiler_params=params(),
     )(mixed, sel)
+    down_1 = shift(after(down_1, queries), "y", 1)
+    down_3 = shift(after(down_3, queries), "y", -1)
     attended = lax.all_to_all(attended, GROUP, 0, 0, tiled=True).reshape(all_rows, local_heads)
 
+    attended = after(attended, down_1, down_3)
     attn_sum = tensor_sum(dot(attended, o_weight))
     middle = (hidden_f + jnp.tanh(gate_logits[0]) * attn_sum).astype(BF)
     middle_f = middle.astype(F32)
-    scaled = (middle_f * mlp_gain).astype(BF)
-    square = jnp.sum(middle_f * middle_f, axis=1, keepdims=True)
-    square_high = square.astype(BF)
-    square_low = (square - square_high.astype(F32)).astype(BF)
-    lane = lax.broadcasted_iota(jnp.int32, (all_rows, HEAD), 1)
-    extra = jnp.where(lane == 0, square_high, jnp.where(lane == 1, square_low, jnp.zeros((), BF)))
-    gate_up = jnp.concatenate(
-        (dot(scaled, gate_weight).astype(BF), dot(scaled, up_weight).astype(BF), extra), axis=1
-    )
-    by_y = jnp.sum(exchange(gate_up, "y").astype(F32), axis=0).astype(BF)
-    summed = jnp.sum(exchange(by_y, "z").astype(F32), axis=0)
-    square = summed[:, 2 * hidden_part : 2 * hidden_part + 1] + summed[:, 2 * hidden_part + 1 : 2 * hidden_part + 2]
-    row_scale = lax.rsqrt(square / full_width + EPS)
-    gate = summed[:, :hidden_part] * row_scale
-    up = summed[:, hidden_part : 2 * hidden_part] * row_scale
-    active = (jax.nn.silu(gate) * up).astype(BF)
-    active = gather(gather(active, "z"), "y")
-    down_sum = tensor_sum(dot(active, down_weight))
+    middles = [middle] + [shift(middle, "y", d) for d in (1, 2, 3)]
+    gate_up = pl.pallas_call(
+        gate_up_kernel,
+        in_specs=[vmem()] * 9,
+        out_specs=vmem(),
+        out_shape=jax.ShapeDtypeStruct((all_rows, 2 * units + HEAD), BF),
+        compiler_params=params(),
+    )(*middles, wide_0, wide_1, gate_2, up_2, wide_3)
+    down_2 = (shift(down_1[units:], "y", 1), shift(down_3[units:], "y", -1))
+    parts = exchange(gate_up, "z")
+    active = pl.pallas_call(
+        functools.partial(active_kernel, full_width),
+        in_specs=[vmem()],
+        out_specs=vmem(),
+        out_shape=jax.ShapeDtypeStruct(parts.shape[:2] + (units,), BF),
+        compiler_params=params(),
+    )(parts)
+    active = lax.all_to_all(active, "z", 0, 0, tiled=True).reshape(all_rows, units)
+    across = dot(active[:, :half], down_2[0]) + dot(active[:, half:], down_2[1])
+    across = shift(across.astype(BF), "y", 2)
+    behind = shift(dot(active, down_1[:units]).astype(BF), "y", -1)
+    ahead = shift(dot(active, down_3[:units]).astype(BF), "y", 1)
+    down_part = dot(active, down_0) + across.astype(F32) + behind.astype(F32) + ahead.astype(F32)
+    down_sum = tensor_sum(down_part)
     row_request = jnp.arange(all_rows, dtype=jnp.int32) // STEPS
     request_ids = (image_groups * (own_rows // STEPS) + image_requests).reshape(-1)
     has_image = jnp.any(row_request[:, None] == request_ids[None, :], axis=1).astype(F32)

time: 261 us -> 234 us (0.90)
  blocking collectives: 125 us -> 29.8 us
  starting transfers between devices: 45.2 us -> 85.2 us
  waiting for transfers between devices: 44.2 us -> 62.8 us
  local copies, waits for them, and re-layouts: 15.1 us -> 24.7 us
  other arithmetic: 10.3 us -> 3.53 us
  Pallas kernels: 12.1 us -> 18.3 us
    all_to_all x3 -> x0, blocking collectives: 51.3 us -> none  [the longest x1 19.5 us: shards(): mixed = lax.all_to_all(mixed, GROUP, 0, 0, tiled=True)]
    all_to_all x2 -> x1, blocking collectives: 73.7 us -> 29.8 us  [exchange(): out = lax.all_to_all(value, axis, 0, 0, tiled=True)]
    ppermute x13 -> x27, waiting for transfers between devices: 18.2 us -> 48.5 us  [shift(): return lax.ppermute(value, axis, [(i, (i + by) % n) for i in range(n)])]
    ppermute x13 -> x27, starting transfers between devices: 26.2 us -> 49.5 us  [shift(): return lax.ppermute(value, axis, [(i, (i + by) % n) for i in range(n)])]
    all_to_all x1 -> x3, starting transfers between devices: 4.4 us -> 18.2 us  [the longest x1 7.69 us: shards(): lax.all_to_all(attended, GROUP, 0, 0, tiled=True)]
    all_to_all x1 -> x3, waiting for transfers between devices: 19.2 us -> 6.87 us  [the longest x1 3.69 us: shards(): mixed = lax.all_to_all(mixed, GROUP, 0, 0, tiled=True)]
    pallas_call x2 -> x5, Pallas kernels: 7.33 us -> 13.8 us  [the longest x2 8.83 us: kv_project(): pl.pallas_call(kv_there_kernel if other else kv_here_kernel, grid_spec=pl...]
    dynamic_slice x0 -> x3, local copies, waits for them, and re-layouts: none -> 5.09 us  [the longest x1 2.79 us: columns(): return lax.dynamic_slice_in_dim(weight, at, units, 1).astype(F32)]
  transfers between devices with their start and end apart: 16 -> 32, of which waited for: 10 -> 19; matrix products, arithmetic and copies ran while one was open for 5% -> 7% of each run, Pallas kernels for 2% -> 2%
where the time goes in v2:
time: 234 us; the launch traced here: 233 us
  starting transfers between devices  85.2 us (36%)
  waiting for transfers between devices  62.8 us (27%)
  blocking collectives  29.8 us (13%)
  local copies, waits for them, and re-layouts  24.7 us (11%)
  Pallas kernels  18.3 us (8%)
  matrix products  6.8 us (3%)
  other arithmetic  3.53 us (2%)
    ppermute x27, starting transfers between devices, shift(): return lax.ppermute(value, axis, [(i, (i + by) % n) for i in range(n)])  49.5 us
    ppermute x27, waiting for transfers between devices, shift(): return lax.ppermute(value, axis, [(i, (i + by) % n) for i in range(n)])  48.5 us
    all_to_all x1, blocking collectives, exchange(): out = lax.all_to_all(value, axis, 0, 0, tiled=True)  29.8 us
    unnamed x63, local copies, waits for them, and re-layouts  13.1 us
    all_to_all x1, starting transfers between devices, exchange(): out = lax.all_to_all(value, axis, 0, 0, tiled=True)  9.47 us
    pallas_call x2, Pallas kernels, kv_project(): pl.pallas_call(kv_there_kernel if other else kv_here_kernel, grid_spec=pl...  8.83 us
    all_to_all x1, starting transfers between devices, shards(): queries = lax.all_to_all(queries, GROUP, 0, 0, tiled=True)  8.01 us
    all_to_all x1, starting transfers between devices, shards(): lax.all_to_all(attended, GROUP, 0, 0, tiled=True)  7.69 us
  transfers between devices with their start and end apart: 32, of which 19 were waited for; matrix products, arithmetic and copies ran while one was open for 7% of the time, Pallas kernels for 2%

profile of v2, /device:TPU:1, one launch (start us, length us, event | category | flops | bytes accessed | tf_op | source)
XLA Modules:
  0.0 232.9 jit_solution(14499109572490850208)
XLA Ops:
  7.6 4.1 %shard_map.163 = bf16[4,640,256]{2,1,0:T(8,128)(2,1)} custom-call(s32[2]{0:T(128)S(1)} %pad_add_fusion.place_ref, bf16[640,1024]{1,0:T(8,128)(2,1)S(1)} %copy-done.5, bf16[1024,1024]{1,0:T(8,128)(2,1)S(1)} %copy-done.1, bf16[1024,1024]{1,0:T(8,128)(2,1)S(1)} %copy-done.3), custom_call_target="tpu_custom_call" | custom-call | flops 1342177280 | bytes 4718592 | tf_op jit(solution)/shard_map/pallas_call | solution.py:114
  11.7 3.2 %collective-permute-start = (bf16[4,640,256]{2,1,0:T(8,128)(2,1)}, bf16[4,640,256]{2,1,0:T(8,128)(2,1)}, u32[]{:S(2)}, u32[]{:S(2)}) collective-permute-start(bf16[4,640,256]{2,1,0:T(8,128)(2,1)} %shard_map.163), channel_id=1, source_target_pairs={{0,1},{1,0},{2,3},{3,2},{4,5},{5,4},{6,7},{7,6},{8,9},{9,8},{10,11... | collective-permute-start | bytes 3932168 | tf_op jit(solution)/shard_map/ppermute | solution.py:237
  15.0 9.5 %all-to-all-start = ((bf16[32,8,1024]{2,1,0:T(8,128)(2,1)}), bf16[32,8,1024]{2,1,0:T(8,128)(2,1)S(1)}, u32[]{:S(2)}, u32[]{:S(2)}) async-start(bf16[32,8,1024]{2,1,0:T(8,128)(2,1)} %bitcast.5), calls=%async_computation | async-start | bytes 1048576 | tf_op jit(solution)/shard_map/all_to_all | solution.py:246
  24.5 2.8 %constant_dynamic-slice_fusion = (bf16[256,896]{1,0:T(8,128)(2,1)}, bf16[256,896]{1,0:T(8,128)(2,1)S(1)}, bf16[256,896]{1,0:T(8,128)(2,1)S(1)}, bf16[256,896]{1,...) fusion(bf16[256,3584]{1,0:T(8,128)(2,1)S(1)} %copy-done.21, ...), kind=kLoop, calls=%fused_computation.30 | loop fusion | bytes 7340048 | tf_op jit(solution)/shard_map/dynamic_slice | solution.py:323
  36.0 4.7 %shard_map.164 = (bf16[320,256]{1,0:T(8,128)(2,1)S(1)}, bf16[320,256]{1,0:T(8,128)(2,1)S(1)}, bf16[640,256]{1,0:T(8,128)(2,1)S(1)}, bf16[640,256]{1,0:T(8,128)(2,1)S(1)}, bf16[640,256]{1,0:T(8,128)(2,1)S(1)}) custom-call(s32[2]{0:T(128)S(1)} %pad_add_fusion.place_ref, bf16[640,1024]{1,0:T(8,128)(2,1)S(1)} %copy-done.6, bf16[1024,1024]{1,0:T(8,128)(2,1)S(1)} %copy-done.2, ...), custom_call_target="tpu_custom_call" | custom-call | flops 1342177280 | bytes 4718592 | tf_op jit(solution)/shard_map/pallas_call | solution.py:114
  44.7 8.0 %all-to-all-start.1 = ((bf16[32,4,1024]{2,1,0:T(4,128)(2,1)}), bf16[32,4,1024]{2,1,0:T(4,128)(2,1)S(1)}, u32[]{:S(2)}, u32[]{:S(2)}) async-start(bf16[32,4,1024]{2,1,0:T(4,128)(2,1)} %all_to_all.36), calls=%async_computation.1 | async-start | bytes 524288 | tf_op jit(solution)/shard_map/all_to_all | solution.py:351
  55.5 3.1 %collective-permute-done.1.low_ref = bf16[320,256]{1,0:T(8,128)(2,1)S(1)} collective-permute-done((bf16[320,256]{1,0:T(8,128)(2,1)S(1)}, bf16[320,256]{1,0:T(8,128)(2,1)S(1)}, u32[]{:S(2)}, u32[]{:S(2)}) %collective-permute-start.1) | collective-permute-done | bytes 163872 | tf_op jit(solution)/shard_map/ppermute | solution.py:237
  61.7 7.5 %all-to-all-done.1 = bf16[32,4,1024]{2,1,0:T(4,128)(2,1)S(1)} async-done(((bf16[32,4,1024]{2,1,0:T(4,128)(2,1)}), bf16[32,4,1024]{2,1,0:T(4,128)(2,1)S(1)}, u32[]{:S(2)}, u32[]{:S(2)}) %all-to-all-start.1) | async-done | bytes 262176 | tf_op jit(solution)/shard_map/all_to_all | solution.py:351
  72.7 7.0 %all-to-all-start.2 = ((bf16[32,4,1152]{2,1,0:T(4,128)(2,1)}), bf16[32,4,1152]{2,1,0:T(4,128)(2,1)S(1)}, u32[]{:S(2)}, u32[]{:S(2)}) async-start(bf16[32,4,1152]{2,1,0:T(4,128)(2,1)} %all_to_all.39), calls=%async_computation.2 | async-start | bytes 589824 | tf_op jit(solution)/shard_map/all_to_all | solution.py:361
  86.8 3.7 %all-to-all-done.2 = bf16[32,4,1152]{2,1,0:T(4,128)(2,1)S(1)} async-done(((bf16[32,4,1152]{2,1,0:T(4,128)(2,1)}), bf16[32,4,1152]{2,1,0:T(4,128)(2,1)S(1)}, u32[]{:S(2)}, u32[]{:S(2)}) %all-to-all-start.2) | async-done | bytes 294944 | tf_op jit(solution)/shard_map/all_to_all | solution.py:361
  90.5 4.7 %collective-permute-done.7.gate2 = bf16[256,896]{1,0:T(8,128)(2,1)S(1)} collective-permute-done((bf16[256,896]{1,0:T(8,128)(2,1)S(1)}, bf16[256,896]{1,0:T(8,128)(2,1)S(1)}, u32[]{:S(2)}, u32[]{:S(2)}) %collective-permute-start.7) | collective-permute-done | bytes 458784 | tf_op jit(solution)/shard_map/ppermute | solution.py:237
  96.6 7.7 %all-to-all-start.3 = ((bf16[32,8,1024]{2,1,0:T(8,128)(2,1)}), bf16[32,8,1024]{2,1,0:T(8,128)(2,1)S(1)}, u32[]{:S(2)}, u32[]{:S(2)}) async-start(bf16[32,8,1024]{2,1,0:T(8,128)(2,1)} %shard_map.169), calls=%async_computation.3 | async-start | bytes 1048576 | tf_op jit(solution)/shard_map/all_to_all | solution.py:373
  108.1 17.8 %collective-permute-done.10 = bf16[1344,256]{1,0:T(8,128)(2,1)S(1)} collective-permute-done((bf16[1344,256]{1,0:T(8,128)(2,1)S(1)}, bf16[1344,256]{1,0:T(8,128)(2,1)S(1)}, u32[]{:S(2)}, u32[]{:S(2)}) %collective-permute-start.10) | collective-permute-done | bytes 688160 | tf_op jit(solution)/shard_map/ppermute | solution.py:237
  129.9 3.2 %collective-permute-start.11 = (bf16[256,256]{1,0:T(8,128)(2,1)S(1)}, bf16[256,256]{1,0:T(8,128)(2,1)S(1)}, u32[]{:S(2)}, u32[]{:S(2)}) collective-permute-start(bf16[256,256]{1,0:T(8,128)(2,1)S(1)} %convolution_convert_fusion.3), channel_id=1, source_target_pairs={{0,1},{1,0},{2,3},{3,2},{4,5},{5,4},{6,7},{7,6},{8,9},{9,8},{10,11... | collective-permute-start | bytes 393224 | tf_op jit(solution)/shard_map/ppermute | solution.py:237
  134.1 2.9 %collective-permute-start.12 = (bf16[256,256]{1,0:T(8,128)(2,1)S(1)}, bf16[256,256]{1,0:T(8,128)(2,1)S(1)}, u32[]{:S(2)}, u32[]{:S(2)}) collective-permute-start(bf16[256,256]{1,0:T(8,128)(2,1)S(1)} %add_convert_fusion.3), channel_id=1, source_target_pairs={{0,4},{2,6},{4,0},{6,2},{1,5},{3,7},{5,1},{7,3},{8,12},{10,14},{12... | collective-permute-start | bytes 393224 | tf_op jit(solution)/shard_map/ppermute | solution.py:237
  146.8 3.7 %collective-permute-done.15.m1 = bf16[256,256]{1,0:T(8,128)(2,1)S(1)} collective-permute-done((bf16[256,256]{1,0:T(8,128)(2,1)S(1)}, bf16[256,256]{1,0:T(8,128)(2,1)S(1)}, u32[]{:S(2)}, u32[]{:S(2)}) %collective-permute-start.15) | collective-permute-done | bytes 131104 | tf_op jit(solution)/shard_map/ppermute | solution.py:237
  152.3 3.8 %shard_map.170 = bf16[256,1920]{1,0:T(8,128)(2,1)S(1)} custom-call(bf16[256,256]{1,0:T(8,128)(2,1)S(1)} %fusion.6.m0, bf16[256,256]{1,0:T(8,128)(2,1)S(1)} %collective-permute-done.15.m1, bf16[256,256]{1,0:T(8,128)(2,1)S(1)} %collective-permute-done.16.m2, bf16[256,256]{1,0:T(8,128)(2,1)S(1)} %collective-permute-done.17.m3, ...), custom_call_target="tpu_custom_call" | custom-call | tf_op jit(solution)/shard_map/pallas_call | solution.py:380
  156.2 29.8 %all_to_all.52.parts_ref = bf16[8,32,1920]{2,1,0:T(8,128)(2,1)S(1)} all-to-all(bf16[8,32,1920]{2,1,0:T(8,128)(2,1)S(1)} %bitcast.19), channel_id=1, replica_groups=mesh['z'=8,'y'=4,'x'=4,'c'=2] {'z'}, dimensions={0} | all-to-all | bytes 1966080 | tf_op jit(solution)/shard_map/all_to_all | solution.py:246
  187.0 3.5 %all-to-all-start.5 = ((bf16[8,32,896]{2,1,0:T(8,128)(2,1)}), bf16[8,32,896]{2,1,0:T(8,128)(2,1)S(1)}, u32[]{:S(2)}, u32[]{:S(2)}) async-start(bf16[8,32,896]{2,1,0:T(8,128)(2,1)} %shard_map.171), calls=%async_computation.5 | async-start | bytes 917504 | tf_op jit(solution)/shard_map/all_to_all | solution.py:396
  190.6 4.7 %collective-permute-start.19 = (bf16[448,256]{1,0:T(8,128)(2,1)S(1)}, bf16[448,256]{1,0:T(8,128)(2,1)S(1)}, u32[]{:S(2)}, u32[]{:S(2)}) collective-permute-start(bf16[448,256]{1,0:T(8,128)(2,1)S(1)} %slice.45), channel_id=1, source_target_pairs={{0,24},{8,0},{16,8},{24,16},{1,25},{9,1},{17,9},{25,17},{2,26},{10... | collective-permute-start | bytes 688136 | tf_op jit(solution)/shard_map/ppermute | solution.py:237
  198.2 3.2 %all-to-all-done.5 = bf16[8,32,896]{2,1,0:T(8,128)(2,1)S(1)} async-done(((bf16[8,32,896]{2,1,0:T(8,128)(2,1)}), bf16[8,32,896]{2,1,0:T(8,128)(2,1)S(1)}, u32[]{:S(2)}, u32[]{:S(2)}) %all-to-all-start.5) | async-done | bytes 458784 | tf_op jit(solution)/shard_map/all_to_all | solution.py:396
  205.6 4.4 %collective-permute-start.21 = (bf16[256,256]{1,0:T(8,128)(2,1)S(1)}, bf16[256,256]{1,0:T(8,128)(2,1)S(1)}, u32[]{:S(2)}, u32[]{:S(2)}) collective-permute-start(bf16[256,256]{1,0:T(8,128)(2,1)S(1)} %convolution_convert_fusion.2), channel_id=1, source_target_pairs={{0,24},{8,0},{16,8},{24,16},{1,25},{9,1},{17,9},{25,17},{2,26},{10... | collective-permute-start | bytes 393224 | tf_op jit(solution)/shard_map/ppermute | solution.py:237
  215.7 5.4 %collective-permute-start.23 = (bf16[256,256]{1,0:T(8,128)(2,1)S(1)}, bf16[256,256]{1,0:T(8,128)(2,1)S(1)}, u32[]{:S(2)}, u32[]{:S(2)}) collective-permute-start(bf16[256,256]{1,0:T(8,128)(2,1)S(1)} %add_convert_fusion.2), channel_id=1, source_target_pairs={{0,1},{1,0},{2,3},{3,2},{4,5},{5,4},{6,7},{7,6},{8,9},{9,8},{10,11... | collective-permute-start | bytes 393224 | tf_op jit(solution)/shard_map/ppermute | solution.py:237
  228.8 3.3 %collective-permute-done.25 = bf16[256,256]{1,0:T(8,128)(2,1)S(1)} collective-permute-done((bf16[256,256]{1,0:T(8,128)(2,1)S(1)}, bf16[256,256]{1,0:T(8,128)(2,1)S(1)}, u32[]{:S(2)}, u32[]{:S(2)}) %collective-permute-start.25) | collective-permute-done | bytes 131104 | tf_op jit(solution)/shard_map/ppermute | solution.py:237
  (149 shorter events, 79.5 us)
Async XLA Ops:
  11.7 21.4 %collective-permute-start = (bf16[4,640,256]{2,1,0:T(8,128)(2,1)}, bf16[4,640,256]{2,1,0:T(8,128)(2,1)}, u32[]{:S(2)}, u32[]{:S(2)}) collective-permute-start(bf16[4,640,256]{2,1,0:T(8,128)(2,1)} %shard_map.163), channel_id=1, source_target_pairs={{0,1},{1,0},{2,3},{3,2},{4,5},{5,4},{6,7},{7,6},{8,9},{9,8},{10,11... | collective-permute-start | bytes 3932168 | tf_op jit(solution)/shard_map/ppermute | solution.py:237
  15.0 28.6 %all-to-all-start = ((bf16[32,8,1024]{2,1,0:T(8,128)(2,1)}), bf16[32,8,1024]{2,1,0:T(8,128)(2,1)S(1)}, u32[]{:S(2)}, u32[]{:S(2)}) async-start(bf16[32,8,1024]{2,1,0:T(8,128)(2,1)} %bitcast.5), calls=%async_computation | async-start | bytes 1048576 | tf_op jit(solution)/shard_map/all_to_all | solution.py:246
  29.2 40.0 %collective-permute-start.5 = (bf16[256,2688]{1,0:T(8,128)(2,1)}, bf16[256,2688]{1,0:T(8,128)(2,1)}, u32[]{:S(2)}, u32[]{:S(2)}) collective-permute-start(bf16[256,2688]{1,0:T(8,128)(2,1)} %get-tuple-element.52), channel_id=1, source_target_pairs={{0,8},{8,16},{16,24},{24,0},{1,9},{9,17},{17,25},{25,1},{2,10},{10... | collective-permute-start | bytes 4128776 | tf_op jit(solution)/shard_map/ppermute | solution.py:237
  30.4 38.8 %collective-permute-start.6 = (bf16[256,2688]{1,0:T(8,128)(2,1)}, bf16[256,2688]{1,0:T(8,128)(2,1)}, u32[]{:S(2)}, u32[]{:S(2)}) collective-permute-start(bf16[256,2688]{1,0:T(8,128)(2,1)} %get-tuple-element.51), channel_id=1, source_target_pairs={{0,24},{8,0},{16,8},{24,16},{1,25},{9,1},{17,9},{25,17},{2,26},{10... | collective-permute-start | bytes 4128776 | tf_op jit(solution)/shard_map/ppermute | solution.py:237
  44.7 24.4 %all-to-all-start.1 = ((bf16[32,4,1024]{2,1,0:T(4,128)(2,1)}), bf16[32,4,1024]{2,1,0:T(4,128)(2,1)S(1)}, u32[]{:S(2)}, u32[]{:S(2)}) async-start(bf16[32,4,1024]{2,1,0:T(4,128)(2,1)} %all_to_all.36), calls=%async_computation.1 | async-start | bytes 524288 | tf_op jit(solution)/shard_map/all_to_all | solution.py:351
  58.7 10.5 %collective-permute-start.3 = (bf16[640,256]{1,0:T(8,128)(2,1)S(1)}, bf16[640,256]{1,0:T(8,128)(2,1)S(1)}, u32[]{:S(2)}, u32[]{:S(2)}) collective-permute-start(bf16[640,256]{1,0:T(8,128)(2,1)S(1)} %get-tuple-element.28), channel_id=1, source_target_pairs={{0,2},{2,4},{4,6},{6,0},{1,3},{3,5},{5,7},{7,1},{8,10},{10,12},{12... | collective-permute-start | bytes 983048 | tf_op jit(solution)/shard_map/ppermute | solution.py:237
  60.0 9.2 %collective-permute-start.4 = (bf16[640,256]{1,0:T(8,128)(2,1)S(1)}, bf16[640,256]{1,0:T(8,128)(2,1)S(1)}, u32[]{:S(2)}, u32[]{:S(2)}) collective-permute-start(bf16[640,256]{1,0:T(8,128)(2,1)S(1)} %get-tuple-element.29), channel_id=1, source_target_pairs={{0,6},{2,0},{4,2},{6,4},{1,7},{3,1},{5,3},{7,5},{8,14},{10,8},{12,... | collective-permute-start | bytes 983048 | tf_op jit(solution)/shard_map/ppermute | solution.py:237
  72.7 17.7 %all-to-all-start.2 = ((bf16[32,4,1152]{2,1,0:T(4,128)(2,1)}), bf16[32,4,1152]{2,1,0:T(4,128)(2,1)S(1)}, u32[]{:S(2)}, u32[]{:S(2)}) async-start(bf16[32,4,1152]{2,1,0:T(4,128)(2,1)} %all_to_all.39), calls=%async_computation.2 | async-start | bytes 589824 | tf_op jit(solution)/shard_map/all_to_all | solution.py:361
  80.8 14.4 %collective-permute-start.7 = (bf16[256,896]{1,0:T(8,128)(2,1)S(1)}, bf16[256,896]{1,0:T(8,128)(2,1)S(1)}, u32[]{:S(2)}, u32[]{:S(2)}) collective-permute-start(bf16[256,896]{1,0:T(8,128)(2,1)S(1)} %slice.40), channel_id=1, source_target_pairs={{0,8},{8,16},{16,24},{24,0},{1,9},{9,17},{17,25},{25,1},{2,10},{10... | collective-permute-start | bytes 1376264 | tf_op jit(solution)/shard_map/ppermute | solution.py:237
  84.1 11.2 %collective-permute-start.8 = (bf16[256,896]{1,0:T(8,128)(2,1)}, bf16[256,896]{1,0:T(8,128)(2,1)S(1)}, u32[]{:S(2)}, u32[]{:S(2)}) collective-permute-start(bf16[256,896]{1,0:T(8,128)(2,1)} %slice.41), channel_id=1, source_target_pairs={{0,24},{8,0},{16,8},{24,16},{1,25},{9,1},{17,9},{25,17},{2,26},{10... | collective-permute-start | bytes 1376264 | tf_op jit(solution)/shard_map/ppermute | solution.py:237
  96.6 31.9 %all-to-all-start.3 = ((bf16[32,8,1024]{2,1,0:T(8,128)(2,1)}), bf16[32,8,1024]{2,1,0:T(8,128)(2,1)S(1)}, u32[]{:S(2)}, u32[]{:S(2)}) async-start(bf16[32,8,1024]{2,1,0:T(8,128)(2,1)} %shard_map.169), calls=%async_computation.3 | async-start | bytes 1048576 | tf_op jit(solution)/shard_map/all_to_all | solution.py:373
  105.6 20.3 %collective-permute-start.10 = (bf16[1344,256]{1,0:T(8,128)(2,1)S(1)}, bf16[1344,256]{1,0:T(8,128)(2,1)S(1)}, u32[]{:S(2)}, u32[]{:S(2)}) collective-permute-start(bf16[1344,256]{1,0:T(8,128)(2,1)S(1)} %get-tuple-element.37), channel_id=1, source_target_pairs={{0,24},{8,0},{16,8},{24,16},{1,25},{9,1},{17,9},{25,17},{2,26},{10... | collective-permute-start | bytes 2064392 | tf_op jit(solution)/shard_map/ppermute | solution.py:237
  108.1 20.4 %collective-permute-start.9 = (bf16[1344,256]{1,0:T(8,128)(2,1)S(1)}, bf16[1344,256]{1,0:T(8,128)(2,1)}, u32[]{:S(2)}, u32[]{:S(2)}) collective-permute-start(bf16[1344,256]{1,0:T(8,128)(2,1)S(1)} %get-tuple-element.36), channel_id=1, source_target_pairs={{0,8},{8,16},{16,24},{24,0},{1,9},{9,17},{17,25},{25,1},{2,10},{10... | collective-permute-start | bytes 2064392 | tf_op jit(solution)/shard_map/ppermute | solution.py:237
  134.1 6.8 %collective-permute-start.12 = (bf16[256,256]{1,0:T(8,128)(2,1)S(1)}, bf16[256,256]{1,0:T(8,128)(2,1)S(1)}, u32[]{:S(2)}, u32[]{:S(2)}) collective-permute-start(bf16[256,256]{1,0:T(8,128)(2,1)S(1)} %add_convert_fusion.3), channel_id=1, source_target_pairs={{0,4},{2,6},{4,0},{6,2},{1,5},{3,7},{5,1},{7,3},{8,12},{10,14},{12... | collective-permute-start | bytes 393224 | tf_op jit(solution)/shard_map/ppermute | solution.py:237
  137.1 6.7 %collective-permute-start.13 = (bf16[256,256]{1,0:T(8,128)(2,1)S(1)}, bf16[256,256]{1,0:T(8,128)(2,1)S(1)}, u32[]{:S(2)}, u32[]{:S(2)}) collective-permute-start(bf16[256,256]{1,0:T(8,128)(2,1)S(1)} %add_convert_fusion.3), channel_id=1, source_target_pairs={{0,2},{2,4},{4,6},{6,0},{1,3},{3,5},{5,7},{7,1},{8,10},{10,12},{12... | collective-permute-start | bytes 393224 | tf_op jit(solution)/shard_map/ppermute | solution.py:237
  143.8 6.6 %collective-permute-start.15 = (bf16[256,256]{1,0:T(8,128)(2,1)S(1)}, bf16[256,256]{1,0:T(8,128)(2,1)S(1)}, u32[]{:S(2)}, u32[]{:S(2)}) collective-permute-start(bf16[256,256]{1,0:T(8,128)(2,1)S(1)} %fusion.6.m0), channel_id=1, source_target_pairs={{0,8},{8,16},{16,24},{24,0},{1,9},{9,17},{17,25},{25,1},{2,10},{10... | collective-permute-start | bytes 393224 | tf_op jit(solution)/shard_map/ppermute | solution.py:237
  143.9 7.1 %collective-permute-start.16 = (bf16[256,256]{1,0:T(8,128)(2,1)S(1)}, bf16[256,256]{1,0:T(8,128)(2,1)S(1)}, u32[]{:S(2)}, u32[]{:S(2)}) collective-permute-start(bf16[256,256]{1,0:T(8,128)(2,1)S(1)} %fusion.6.m0), channel_id=1, source_target_pairs={{0,16},{8,24},{16,0},{24,8},{1,17},{9,25},{17,1},{25,9},{2,18},{10... | collective-permute-start | bytes 393224 | tf_op jit(solution)/shard_map/ppermute | solution.py:237
  187.0 14.3 %all-to-all-start.5 = ((bf16[8,32,896]{2,1,0:T(8,128)(2,1)}), bf16[8,32,896]{2,1,0:T(8,128)(2,1)S(1)}, u32[]{:S(2)}, u32[]{:S(2)}) async-start(bf16[8,32,896]{2,1,0:T(8,128)(2,1)} %shard_map.171), calls=%async_computation.5 | async-start | bytes 917504 | tf_op jit(solution)/shard_map/all_to_all | solution.py:396
  190.6 7.6 %collective-permute-start.19 = (bf16[448,256]{1,0:T(8,128)(2,1)S(1)}, bf16[448,256]{1,0:T(8,128)(2,1)S(1)}, u32[]{:S(2)}, u32[]{:S(2)}) collective-permute-start(bf16[448,256]{1,0:T(8,128)(2,1)S(1)} %slice.45), channel_id=1, source_target_pairs={{0,24},{8,0},{16,8},{24,16},{1,25},{9,1},{17,9},{25,17},{2,26},{10... | collective-permute-start | bytes 688136 | tf_op jit(solution)/shard_map/ppermute | solution.py:237
  196.2 6.7 %collective-permute-start.18 = (bf16[448,256]{1,0:T(8,128)(2,1)S(1)}, bf16[448,256]{1,0:T(8,128)(2,1)S(1)}, u32[]{:S(2)}, u32[]{:S(2)}) collective-permute-start(bf16[448,256]{1,0:T(8,128)(2,1)S(1)} %slice.43), channel_id=1, source_target_pairs={{0,8},{8,16},{16,24},{24,0},{1,9},{9,17},{17,25},{25,1},{2,10},{10... | collective-permute-start | bytes 688136 | tf_op jit(solution)/shard_map/ppermute | solution.py:237
  203.1 9.2 %collective-permute-start.20 = (bf16[256,256]{1,0:T(8,128)(2,1)S(1)}, bf16[256,256]{1,0:T(8,128)(2,1)S(1)}, u32[]{:S(2)}, u32[]{:S(2)}) collective-permute-start(bf16[256,256]{1,0:T(8,128)(2,1)S(1)} %fusion), channel_id=1, source_target_pairs={{0,16},{8,24},{16,0},{24,8},{1,17},{9,25},{17,1},{25,9},{2,18},{10... | collective-permute-start | bytes 393224 | tf_op jit(solution)/shard_map/ppermute | solution.py:237
  205.6 7.6 %collective-permute-start.21 = (bf16[256,256]{1,0:T(8,128)(2,1)S(1)}, bf16[256,256]{1,0:T(8,128)(2,1)S(1)}, u32[]{:S(2)}, u32[]{:S(2)}) collective-permute-start(bf16[256,256]{1,0:T(8,128)(2,1)S(1)} %convolution_convert_fusion.2), channel_id=1, source_target_pairs={{0,24},{8,0},{16,8},{24,16},{1,25},{9,1},{17,9},{25,17},{2,26},{10... | collective-permute-start | bytes 393224 | tf_op jit(solution)/shard_map/ppermute | solution.py:237
  223.8 8.4 %collective-permute-start.25 = (bf16[256,256]{1,0:T(8,128)(2,1)S(1)}, bf16[256,256]{1,0:T(8,128)(2,1)S(1)}, u32[]{:S(2)}, u32[]{:S(2)}) collective-permute-start(bf16[256,256]{1,0:T(8,128)(2,1)S(1)} %add_convert_fusion.1), channel_id=1, source_target_pairs={{0,2},{2,4},{4,6},{6,0},{1,3},{3,5},{5,7},{7,1},{8,10},{10,12},{12... | collective-permute-start | bytes 393224 | tf_op jit(solution)/shard_map/ppermute | solution.py:237
  224.6 7.6 %collective-permute-start.26 = (bf16[256,256]{1,0:T(8,128)(2,1)S(1)}, bf16[256,256]{1,0:T(8,128)(2,1)S(1)}, u32[]{:S(2)}, u32[]{:S(2)}) collective-permute-start(bf16[256,256]{1,0:T(8,128)(2,1)S(1)} %add_convert_fusion.1), channel_id=1, source_target_pairs={{0,6},{2,0},{4,2},{6,4},{1,7},{3,1},{5,3},{7,5},{8,14},{10,8},{12,... | collective-permute-start | bytes 393224 | tf_op jit(solution)/shard_map/ppermute | solution.py:237
  (38 other events, 409.2 us)

commit v3 on v2

--- a/solution.py
+++ b/solution.py
@@ -16,12 +16,13 @@
 STEPS = 2
 EPS = 1e-05
 VMEM_BYTES = 40 * 1024 * 1024
+KV_VMEM_BYTES = 58 * 1024 * 1024
 BF = jnp.bfloat16
 F32 = jnp.float32
 
 
-def params():
-    return pltpu.CompilerParams(vmem_limit_bytes=VMEM_BYTES)
+def params(limit=VMEM_BYTES):
+    return pltpu.CompilerParams(vmem_limit_bytes=limit)
 
 
 def dot(a, b):
@@ -39,10 +40,10 @@
 def route_kernel(me_ref, routes_ref, requests_ref, sel_ref, image_ref):
     me = me_ref[0]
     groups, links = routes_ref.shape
-    rows = groups * SLOTS * STEPS
+    rows = groups * 2 * SLOTS * STEPS
     row = lax.broadcasted_iota(jnp.int32, (rows, links), 0)
     lane = lax.broadcasted_iota(jnp.int32, (rows, links), 1)
-    group_of_row = row >> 2
+    group_of_row = row >> 3
     slot = (row >> 1) & 1
     step = row & 1
     spread = (group_of_row == lane).astype(F32)
@@ -127,12 +128,7 @@
         out_shape=jax.ShapeDtypeStruct((chips, rows, 2 * HEAD), BF)
         if other
         else [jax.ShapeDtypeStruct((n, 2 * HEAD), BF) for n in sizes],
-        compiler_params=params(),
-        cost_estimate=pl.CostEstimate(
-            flops=2 * chips * rows * depth * 2 * HEAD,
-            bytes_accessed=2 * (rows * depth + chips * 2 * HEAD * (depth + rows)),
-            transcendentals=0,
-        ),
+        compiler_params=params(KV_VMEM_BYTES),
     )(place, vision, k_weight, v_weight, *(() if other else (from_core,)))
 
 
@@ -144,16 +140,24 @@
     backward_ref[half:] = (behind_ref[half:].astype(F32) + high_ref[...].astype(F32)).astype(BF)
 
 
+def half_of(shape):
+    return (lax.broadcasted_iota(jnp.int32, shape, 0) >> 2) & 1
+
+
 def query_kernel(parts_ref, sel_ref, gain_ref, out_ref):
     total = jnp.sum(parts_ref[...].astype(F32), axis=0)
     gain = gain_ref[...]
     sel = sel_ref[...]
-    for h in range(total.shape[1] // HEAD):
-        span = slice(h * HEAD, (h + 1) * HEAD)
-        v = total[:, span]
+    heads = total.shape[1] // HEAD // 2
+    upper = half_of((sel.shape[0], HEAD)) == 1
+
+    def chosen(h):
+        v = total[:, h * HEAD : (h + 1) * HEAD]
         scale = lax.rsqrt(jnp.mean(v * v, axis=1, keepdims=True) + EPS)
-        q = (v * scale * gain).astype(BF)
-        out_ref[:, span] = dot(sel, q).astype(BF)
+        return dot(sel, (v * scale * gain).astype(BF))
+
+    for h in range(heads):
+        out_ref[:, h * HEAD : (h + 1) * HEAD] = jnp.where(upper, chosen(heads + h), chosen(h)).astype(BF)
 
 
 def attention_kernel(me_ref, tiles_ref, own_ref, left_ref, right_ref, gain_ref, q_ref, image_ref, out_ref):
@@ -188,16 +192,19 @@
 
 
 def combine_kernel(parts_ref, sel_ref, out_ref):
-    total = lax.dot_general(
-        sel_ref[...], parts_ref[...], (((0,), (0,)), ((), ())), preferred_element_type=F32
-    )
-    heads = out_ref.shape[2] // HEAD
-    sums = total[:, heads * HEAD :]
-    for h in range(heads):
-        span = slice(h * HEAD, (h + 1) * HEAD)
-        den = sums[:, h : h + 1] + sums[:, heads + h : heads + h + 1]
-        mixed = (total[:, span] / jnp.where(den > 0.0, den, 1.0)).astype(BF)
-        out_ref[:, :, span] = jnp.broadcast_to(mixed[None], (out_ref.shape[0],) + mixed.shape)
+    sel = sel_ref[...].astype(F32)
+    parts = parts_ref[...]
+    heads = out_ref.shape[2] // HEAD // 2
+    for part in range(2):
+        mine = jnp.where(half_of(sel.shape) == part, sel, 0.0).astype(BF)
+        total = lax.dot_general(mine, parts, (((0,), (0,)), ((), ())), preferred_element_type=F32)
+        sums = total[:, heads * HEAD :]
+        for h in range(heads):
+            den = sums[:, h : h + 1] + sums[:, heads + h : heads + h + 1]
+            mixed = total[:, h * HEAD : (h + 1) * HEAD] / jnp.where(den > 0.0, den, 1.0)
+            mixed = jnp.broadcast_to(mixed.astype(BF)[None], (out_ref.shape[0],) + mixed.shape)
+            at = (part * heads + h) * HEAD
+            out_ref[:, :, at : at + HEAD] = mixed
 
 
 def gate_up_kernel(m0, m1, m2, m3, w0, w1, gate2, up2, w3, out_ref):
@@ -281,7 +288,7 @@
     full_width = width_part * groups
     local_heads = q_weight.shape[1]
     hidden_part = gate_weight.shape[1]
-    slot_rows = groups * SLOTS * STEPS
+    slot_rows = groups * 2 * SLOTS * STEPS
     key_rows = vision.shape[0]
 
     sel, row_image = pl.pallas_call(
@@ -314,53 +321,56 @@
     kv_left = shift(forward, "x", 1)
     kv_right = shift(backward, "x", -1)
 
-    chips_y = lax.axis_size("y")
-    units = hidden_part // chips_y
-    gain = mlp_gain[:, None]
-
-    def columns(weight, d):
-        at = lax.rem(lax.axis_index("y") + d, chips_y) * units
-        return lax.dynamic_slice_in_dim(weight, at, units, 1).astype(F32)
-
-    def rows(weight, d, start, size):
-        at = lax.rem(lax.axis_index("y") + d, chips_y) * units + start
-        return lax.dynamic_slice_in_dim(weight, at, size, 0)
-
-    def wide(*parts):
-        return (jnp.concatenate(parts, axis=1) * gain).astype(BF)
-
-    wide_0 = wide(columns(gate_weight, 0), columns(up_weight, 0))
-    wide_1 = wide(columns(gate_weight, 1), columns(up_weight, 1), columns(gate_weight, 2))
-    wide_3 = wide(columns(gate_weight, 3), columns(up_weight, 3), columns(up_weight, 2))
-    wide_1 = shift(wide_1, "y", 1)
-    wide_3 = shift(wide_3, "y", -1)
-    gate_2 = shift(wide_1[:, 2 * units :], "y", 1)
-    up_2 = shift(wide_3[:, 2 * units :], "y", -1)
-    half = units // 2
-    down_0 = rows(down_weight, 0, 0, units)
-    down_1 = jnp.concatenate((rows(down_weight, 1, 0, units), rows(down_weight, 2, 0, half)), axis=0)
-    down_3 = jnp.concatenate((rows(down_weight, 3, 0, units), rows(down_weight, 2, half, half)), axis=0)
-
     queries = pl.pallas_call(
         query_kernel,
         in_specs=[vmem()] * 3,
         out_specs=vmem(),
-        out_shape=jax.ShapeDtypeStruct((slot_rows, local_heads), BF),
+        out_shape=jax.ShapeDtypeStruct((slot_rows, local_heads // 2), BF),
         compiler_params=params(),
     )(q_parts, sel, q_gain.reshape(1, HEAD))
+    chips_y = lax.axis_size("y")
+    units = hidden_part // chips_y
+    half = units // 2
+    gain = mlp_gain[:, None]
+    queries = after(queries, forward, backward)
+    gate_weight, up_weight = lax.optimization_barrier((gate_weight, up_weight, queries))[:2]
+
+    def columns(weight, d):
+        at = lax.rem(lax.axis_index("y") + d, chips_y) * units
+        return lax.dynamic_slice_in_dim(weight, at, units, 1).astype(F32)
+
+    def wide(*parts):
+        return (jnp.concatenate(parts, axis=1) * gain).astype(BF)
+
+    wide_0 = wide(columns(gate_weight, 0), columns(up_weight, 0))
+    wide_1 = shift(wide(columns(gate_weight, 1), columns(up_weight, 1)), "y", 1)
+    wide_3 = shift(wide(columns(gate_weight, 3), columns(up_weight, 3)), "y", -1)
+    gate_2 = shift(wide(columns(gate_weight, 2)), "y", 1)
+    up_2 = shift(wide(columns(up_weight, 2)), "y", -1)
+
     queries = lax.all_to_all(queries, GROUP, 0, 0, tiled=True)
 
-    queries = after(queries, wide_1, wide_3)
     mixed = pl.pallas_call(
         attention_kernel,
         in_specs=[smem(), smem()] + [vmem()] * 6,
         out_specs=vmem(),
-        out_shape=jax.ShapeDtypeStruct((slot_rows, local_heads + HEAD), BF),
+        out_shape=jax.ShapeDtypeStruct((slot_rows, local_heads // 2 + HEAD), BF),
         compiler_params=params(),
     )(me, image_tiles, own, kv_left, kv_right, k_gain.reshape(1, HEAD), queries, row_image)
+    down_weight = after(down_weight, mixed)
+
+    def rows(d, start, size):
+        at = lax.rem(lax.axis_index("y") + d, chips_y) * units + start
+        return lax.dynamic_slice_in_dim(down_weight, at, size, 0)
+
+    down_0 = rows(0, 0, units)
+    down_1 = shift(rows(1, 0, units), "y", 1)
+    down_3 = shift(rows(3, 0, units), "y", -1)
+    down_2 = (shift(rows(2, 0, half), "y", 1), shift(rows(2, half, half), "y", -1))
     mixed = lax.all_to_all(mixed, GROUP, 0, 0, tiled=True)
-
-    mixed = after(mixed, gate_2, up_2)
+    mixed = after(mixed, wide_1, wide_3, gate_2, up_2)
+    gate_2, up_2 = shift(gate_2, "y", 1), shift(up_2, "y", -1)
+
     attended = pl.pallas_call(
         combine_kernel,
         in_specs=[vmem()] * 2,
@@ -368,14 +378,14 @@
         out_shape=jax.ShapeDtypeStruct((groups, own_rows, local_heads), BF),
         compiler_params=params(),
     )(mixed, sel)
-    down_1 = shift(after(down_1, queries), "y", 1)
-    down_3 = shift(after(down_3, queries), "y", -1)
     attended = lax.all_to_all(attended, GROUP, 0, 0, tiled=True).reshape(all_rows, local_heads)
 
-    attended = after(attended, down_1, down_3)
+    attended = after(attended, gate_2, up_2, *down_2)
     attn_sum = tensor_sum(dot(attended, o_weight))
     middle = (hidden_f + jnp.tanh(gate_logits[0]) * attn_sum).astype(BF)
     middle_f = middle.astype(F32)
+    middle = after(middle, down_1, down_3)
+    down_2 = (shift(down_2[0], "y", 1), shift(down_2[1], "y", -1))
     middles = [middle] + [shift(middle, "y", d) for d in (1, 2, 3)]
     gate_up = pl.pallas_call(
         gate_up_kernel,
@@ -384,8 +394,7 @@
         out_shape=jax.ShapeDtypeStruct((all_rows, 2 * units + HEAD), BF),
         compiler_params=params(),
     )(*middles, wide_0, wide_1, gate_2, up_2, wide_3)
-    down_2 = (shift(down_1[units:], "y", 1), shift(down_3[units:], "y", -1))
-    parts = exchange(gate_up, "z")
+    parts = after(exchange(gate_up, "z"), *down_2)
     active = pl.pallas_call(
         functools.partial(active_kernel, full_width),
         in_specs=[vmem()],
@@ -396,8 +405,8 @@
     active = lax.all_to_all(active, "z", 0, 0, tiled=True).reshape(all_rows, units)
     across = dot(active[:, :half], down_2[0]) + dot(active[:, half:], down_2[1])
     across = shift(across.astype(BF), "y", 2)
-    behind = shift(dot(active, down_1[:units]).astype(BF), "y", -1)
-    ahead = shift(dot(active, down_3[:units]).astype(BF), "y", 1)
+    behind = shift(dot(active, down_1).astype(BF), "y", -1)
+    ahead = shift(dot(active, down_3).astype(BF), "y", 1)
     down_part = dot(active, down_0) + across.astype(F32) + behind.astype(F32) + ahead.astype(F32)
     down_sum = tensor_sum(down_part)
     row_request = jnp.arange(all_rows, dtype=jnp.int32) // STEPS

time: 234 us -> 235 us (level)
  waiting for transfers between devices: 62.8 us -> 86.8 us
  blocking collectives: 29.8 us -> 15.2 us
  local copies, waits for them, and re-layouts: 24.7 us -> 11.9 us
  Pallas kernels: 18.3 us -> 23.6 us
  starting transfers between devices: 85.2 us -> 82.6 us
  other arithmetic: 3.53 us -> 6 us
    all_to_all x1 -> x2, waiting for transfers between devices: 0.01 us -> 24.2 us  [exchange(): out = lax.all_to_all(value, axis, 0, 0, tiled=True)]
    all_to_all x1, blocking collectives: 29.8 us -> 15.2 us  [shards(): lax.all_to_all(active, 'z', 0, 0, tiled=True).reshape(all_rows, units)]
    ppermute x27 -> x31, waiting for transfers between devices: 48.5 us -> 58.8 us  [shift(): return lax.ppermute(value, axis, [(i, (i + by) % n) for i in range(n)])]
    all_to_all x1 -> x2, starting transfers between devices: 9.47 us -> 16 us  [exchange(): out = lax.all_to_all(value, axis, 0, 0, tiled=True)]
    unnamed x63 -> x47, local copies, waits for them, and re-layouts: 13.1 us -> 6.69 us
    slice x4 -> x0, local copies, waits for them, and re-layouts: 3.85 us -> none  [the longest x1 1.82 us: shards(): up_2 = shift(wide_3[:, 2 * units:], 'y', -1)]
    all_to_all x1, waiting for transfers between devices: 7.46 us -> 3.73 us  [shards(): queries = lax.all_to_all(queries, GROUP, 0, 0, tiled=True)]
    all_to_all x1, waiting for transfers between devices: 3.69 us -> 0.01 us  [shards(): mixed = lax.all_to_all(mixed, GROUP, 0, 0, tiled=True)]
  transfers between devices with their start and end apart: 32 -> 36, of which waited for: 19 -> 17; matrix products, arithmetic and copies ran while one was open for 7% -> 5% of each run, Pallas kernels for 2% -> 5%
where the time goes in v3:
time: 235 us; the launch traced here: 233 us
  waiting for transfers between devices  86.8 us (37%)
  starting transfers between devices  82.6 us (35%)
  Pallas kernels  23.6 us (10%)
  blocking collectives  15.2 us (6%)
  local copies, waits for them, and re-layouts  11.9 us (5%)
  other arithmetic  6 us (3%)
  matrix products  5.79 us (2%)
    ppermute x31, waiting for transfers between devices, shift(): return lax.ppermute(value, axis, [(i, (i + by) % n) for i in range(n)])  58.8 us
    ppermute x31, starting transfers between devices, shift(): return lax.ppermute(value, axis, [(i, (i + by) % n) for i in range(n)])  50.9 us
    all_to_all x2, waiting for transfers between devices, exchange(): out = lax.all_to_all(value, axis, 0, 0, tiled=True)  24.2 us
    all_to_all x2, starting transfers between devices, exchange(): out = lax.all_to_all(value, axis, 0, 0, tiled=True)  16 us
    all_to_all x1, blocking collectives, shards(): lax.all_to_all(active, 'z', 0, 0, tiled=True).reshape(all_rows, units)  15.2 us
    pallas_call x2, Pallas kernels, kv_project(): pl.pallas_call(kv_there_kernel if other else kv_here_kernel, grid_spec=pl...  12.1 us
    unnamed x47, local copies, waits for them, and re-layouts  6.69 us
    all_to_all x1, starting transfers between devices, shards(): lax.all_to_all(attended, GROUP, 0, 0, tiled=True)  5.88 us
  transfers between devices with their start and end apart: 36, of which 17 were waited for; matrix products, arithmetic and copies ran while one was open for 5% of the time, Pallas kernels for 5%

profile of v3, /device:TPU:1, one launch (start us, length us, event | category | flops | bytes accessed | tf_op | source)
XLA Modules:
  0.0 233.4 jit_solution(9651914347181289089)
XLA Ops:
  3.7 5.7 %shard_map.163 = bf16[4,640,256]{2,1,0:T(8,128)(2,1)} custom-call(s32[2]{0:T(128)} %pad_add_fusion.place_ref, bf16[640,1024]{1,0:T(8,128)(2,1)} %vision_ref.1, bf16[1024,1024]{1,0:T(8,128)(2,1)} %k_ref.3, bf16[1024,1024]{1,0:T(8,128)(2,1)} %v_ref.3), custom_call_target="tpu_custom_call" | custom-call | tf_op jit(solution)/shard_map/pallas_call | solution.py:115
  9.4 3.2 %collective-permute-start = (bf16[4,640,256]{2,1,0:T(8,128)(2,1)}, bf16[4,640,256]{2,1,0:T(8,128)(2,1)S(1)}, u32[]{:S(2)}, u32[]{:S(2)}) collective-permute-start(bf16[4,640,256]{2,1,0:T(8,128)(2,1)} %shard_map.163), channel_id=1, source_target_pairs={{0,1},{1,0},{2,3},{3,2},{4,5},{5,4},{6,7},{7,6},{8,9},{9,8},{10,11... | collective-permute-start | bytes 3932168 | tf_op jit(solution)/shard_map/ppermute | solution.py:244
  12.7 9.5 %all-to-all-start = ((bf16[32,8,1024]{2,1,0:T(8,128)(2,1)}), bf16[32,8,1024]{2,1,0:T(8,128)(2,1)S(1)}, u32[]{:S(2)}, u32[]{:S(2)}) async-start(bf16[32,8,1024]{2,1,0:T(8,128)(2,1)} %bitcast.5), calls=%async_computation | async-start | bytes 1048576 | tf_op jit(solution)/shard_map/all_to_all | solution.py:253
  23.2 6.4 %shard_map.164 = (bf16[320,256]{1,0:T(8,128)(2,1)}, bf16[320,256]{1,0:T(8,128)(2,1)}, bf16[640,256]{1,0:T(8,128)(2,1)}, bf16[640,256]{1,0:T(8,128)(2,1)}, bf16[640,256]{1,0:T(8,128)(2,1)}) custom-call(s32[2]{0:T(128)} %pad_add_fusion.place_ref, bf16[640,1024]{1,0:T(8,128)(2,1)} %vision_ref.1, bf16[1024,1024]{1,0:T(8,128)(2,1)} %k_ref.3, ...), custom_call_target="tpu_custom_call" | custom-call | tf_op jit(solution)/shard_map/pallas_call | solution.py:115
  33.1 5.8 %all-to-all-done.parts_ref = bf16[32,8,1024]{2,1,0:T(8,128)(2,1)S(1)} async-done(((bf16[32,8,1024]{2,1,0:T(8,128)(2,1)}), bf16[32,8,1024]{2,1,0:T(8,128)(2,1)S(1)}, u32[]{:S(2)}, u32[]{:S(2)}) %all-to-all-start) | async-done | bytes 524320 | tf_op jit(solution)/shard_map/all_to_all | solution.py:253
  45.6 5.4 %all-to-all-start.1 = ((bf16[32,8,512]{2,1,0:T(8,128)(2,1)}), bf16[32,8,512]{2,1,0:T(8,128)(2,1)S(1)}, u32[]{:S(2)}, u32[]{:S(2)}) async-start(bf16[32,8,512]{2,1,0:T(8,128)(2,1)} %bitcast.7), calls=%async_computation.1 | async-start | bytes 524288 | tf_op jit(solution)/shard_map/all_to_all | solution.py:351
  57.7 3.7 %all-to-all-done.1 = bf16[32,8,512]{2,1,0:T(8,128)(2,1)S(1)} async-done(((bf16[32,8,512]{2,1,0:T(8,128)(2,1)}), bf16[32,8,512]{2,1,0:T(8,128)(2,1)S(1)}, u32[]{:S(2)}, u32[]{:S(2)}) %all-to-all-start.1) | async-done | bytes 262176 | tf_op jit(solution)/shard_map/all_to_all | solution.py:351
  61.4 3.1 %shard_map.168 = bf16[256,640]{1,0:T(8,128)(2,1)} custom-call(s32[1]{0:T(128)} %bitcast.1.me_ref, s32[32,4]{1,0:T(8,128)S(1)} %copy.27.tiles_ref, bf16[640,256]{1,0:T(8,128)(2,1)S(1)} %copy-done.1, bf16[640,256]{1,0:T(8,128)(2,1)S(1)} %collective-permute-done.3.left_ref, bf16[640,256]{1,0:T(8,128)(2,1)} %collective-permute-done.4.right_ref, ...), custom_call_target="tpu_custom_call" | custom-call | tf_op jit(solution)/shard_map/pallas_call | solution.py:353
  64.6 4.3 %all-to-all-start.2 = ((bf16[32,8,640]{2,1,0:T(8,128)(2,1)}), bf16[32,8,640]{2,1,0:T(8,128)(2,1)S(1)}, u32[]{:S(2)}, u32[]{:S(2)}) async-start(bf16[32,8,640]{2,1,0:T(8,128)(2,1)} %bitcast.9), calls=%async_computation.2 | async-start | bytes 655360 | tf_op jit(solution)/shard_map/all_to_all | solution.py:370
  73.2 18.8 %collective-permute-done.7 = bf16[256,896]{1,0:T(8,128)(2,1)S(1)} collective-permute-done((bf16[256,896]{1,0:T(8,128)(2,1)S(1)}, bf16[256,896]{1,0:T(8,128)(2,1)S(1)}, u32[]{:S(2)}, u32[]{:S(2)}) %collective-permute-start.7) | collective-permute-done | bytes 458784 | tf_op jit(solution)/shard_map/ppermute | solution.py:244
  94.2 5.9 %all-to-all-start.3 = ((bf16[32,8,1024]{2,1,0:T(8,128)(2,1)}), bf16[32,8,1024]{2,1,0:T(8,128)(2,1)}, u32[]{:S(2)}, u32[]{:S(2)}) async-start(bf16[32,8,1024]{2,1,0:T(8,128)(2,1)} %shard_map.169), calls=%async_computation.3 | async-start | bytes 1048576 | tf_op jit(solution)/shard_map/all_to_all | solution.py:381
  106.6 14.5 %collective-permute-done.11 = bf16[448,256]{1,0:T(8,128)(2,1)S(1)} collective-permute-done((bf16[448,256]{1,0:T(8,128)(2,1)S(1)}, bf16[448,256]{1,0:T(8,128)(2,1)S(1)}, u32[]{:S(2)}, u32[]{:S(2)}) %collective-permute-start.11) | collective-permute-done | bytes 229408 | tf_op jit(solution)/shard_map/ppermute | solution.py:244
  123.4 3.6 %collective-permute-start.13 = (bf16[256,256]{1,0:T(8,128)(2,1)S(1)}, bf16[256,256]{1,0:T(8,128)(2,1)S(1)}, u32[]{:S(2)}, u32[]{:S(2)}) collective-permute-start(bf16[256,256]{1,0:T(8,128)(2,1)S(1)} %convolution_convert_fusion.3), channel_id=1, source_target_pairs={{0,1},{1,0},{2,3},{3,2},{4,5},{5,4},{6,7},{7,6},{8,9},{9,8},{10,11... | collective-permute-start | bytes 393224 | tf_op jit(solution)/shard_map/ppermute | solution.py:244
  141.9 3.3 %collective-permute-start.20 = (bf16[256,256]{1,0:T(8,128)(2,1)S(1)}, bf16[256,256]{1,0:T(8,128)(2,1)S(1)}, u32[]{:S(2)}, u32[]{:S(2)}) collective-permute-start(bf16[256,256]{1,0:T(8,128)(2,1)S(1)} %fusion.16.m0), channel_id=1, source_target_pairs={{0,16},{8,24},{16,0},{24,8},{1,17},{9,25},{17,1},{25,9},{2,18},{10... | collective-permute-start | bytes 393224 | tf_op jit(solution)/shard_map/ppermute | solution.py:244
  146.6 3.4 %collective-permute-done.20.m2 = bf16[256,256]{1,0:T(8,128)(2,1)S(1)} collective-permute-done((bf16[256,256]{1,0:T(8,128)(2,1)S(1)}, bf16[256,256]{1,0:T(8,128)(2,1)S(1)}, u32[]{:S(2)}, u32[]{:S(2)}) %collective-permute-start.20) | collective-permute-done | bytes 131104 | tf_op jit(solution)/shard_map/ppermute | solution.py:244
  150.1 4.4 %shard_map.170 = bf16[256,1920]{1,0:T(8,128)(2,1)} custom-call(bf16[256,256]{1,0:T(8,128)(2,1)S(1)} %fusion.16.m0, bf16[256,256]{1,0:T(8,128)(2,1)S(1)} %collective-permute-done.19.m1, bf16[256,256]{1,0:T(8,128)(2,1)S(1)} %collective-permute-done.20.m2, bf16[256,256]{1,0:T(8,128)(2,1)S(1)} %collective-permute-done.21.m3, ...), custom_call_target="tpu_custom_call" | custom-call | tf_op jit(solution)/shard_map/pallas_call | solution.py:390
  154.4 6.6 %all-to-all-start.4 = ((bf16[8,32,1920]{2,1,0:T(8,128)(2,1)}), bf16[8,32,1920]{2,1,0:T(8,128)(2,1)S(1)}, u32[]{:S(2)}, u32[]{:S(2)}) async-start(bf16[8,32,1920]{2,1,0:T(8,128)(2,1)} %bitcast.13), calls=%async_computation.4 | async-start | bytes 1966080 | tf_op jit(solution)/shard_map/all_to_all | solution.py:253
  161.2 3.1 %collective-permute-start.23 = (bf16[448,256]{1,0:T(8,128)(2,1)}, bf16[448,256]{1,0:T(8,128)(2,1)S(1)}, u32[]{:S(2)}, u32[]{:S(2)}) collective-permute-start(bf16[448,256]{1,0:T(8,128)(2,1)} %copy-done.21), channel_id=1, source_target_pairs={{0,24},{8,0},{16,8},{24,16},{1,25},{9,1},{17,9},{25,17},{2,26},{10... | collective-permute-start | bytes 688136 | tf_op jit(solution)/shard_map/ppermute | solution.py:244
  164.3 3.3 %collective-permute-done.22 = bf16[448,256]{1,0:T(8,128)(2,1)S(1)} collective-permute-done((bf16[448,256]{1,0:T(8,128)(2,1)S(1)}, bf16[448,256]{1,0:T(8,128)(2,1)S(1)}, u32[]{:S(2)}, u32[]{:S(2)}) %collective-permute-start.22) | collective-permute-done | bytes 229408 | tf_op jit(solution)/shard_map/ppermute | solution.py:244
  168.3 18.4 %all-to-all-done.4.parts_ref = bf16[8,32,1920]{2,1,0:T(8,128)(2,1)S(1)} async-done(((bf16[8,32,1920]{2,1,0:T(8,128)(2,1)}), bf16[8,32,1920]{2,1,0:T(8,128)(2,1)S(1)}, u32[]{:S(2)}, u32[]{:S(2)}) %all-to-all-start.4) | async-done | bytes 983072 | tf_op jit(solution)/shard_map/all_to_all | solution.py:253
  187.0 15.2 %all_to_all.51 = bf16[8,32,896]{2,1,0:T(8,128)(2,1)S(1)} all-to-all(bf16[8,32,896]{2,1,0:T(8,128)(2,1)S(1)} %shard_map.171), channel_id=1, replica_groups=mesh['z'=8,'y'=4,'x'=4,'c'=2] {'z'}, dimensions={0} | all-to-all | bytes 917504 | tf_op jit(solution)/shard_map/all_to_all | solution.py:405
  203.2 8.7 %collective-permute-start.25 = (bf16[256,256]{1,0:T(8,128)(2,1)S(1)}, bf16[256,256]{1,0:T(8,128)(2,1)S(1)}, u32[]{:S(2)}, u32[]{:S(2)}) collective-permute-start(bf16[256,256]{1,0:T(8,128)(2,1)S(1)} %convolution_convert_fusion.2), channel_id=1, source_target_pairs={{0,24},{8,0},{16,8},{24,16},{1,25},{9,1},{17,9},{25,17},{2,26},{10... | collective-permute-start | bytes 393224 | tf_op jit(solution)/shard_map/ppermute | solution.py:244
  214.8 3.1 %collective-permute-done.24 = bf16[256,256]{1,0:T(8,128)(2,1)S(1)} collective-permute-done((bf16[256,256]{1,0:T(8,128)(2,1)S(1)}, bf16[256,256]{1,0:T(8,128)(2,1)S(1)}, u32[]{:S(2)}, u32[]{:S(2)}) %collective-permute-start.24) | collective-permute-done | bytes 131104 | tf_op jit(solution)/shard_map/ppermute | solution.py:244
  227.6 5.0 %collective-permute-done.29 = bf16[256,256]{1,0:T(8,128)(2,1)S(1)} collective-permute-done((bf16[256,256]{1,0:T(8,128)(2,1)S(1)}, bf16[256,256]{1,0:T(8,128)(2,1)S(1)}, u32[]{:S(2)}, u32[]{:S(2)}) %collective-permute-start.29) | collective-permute-done | bytes 131104 | tf_op jit(solution)/shard_map/ppermute | solution.py:244
  (131 shorter events, 67.2 us)
Async XLA Ops:
  9.4 12.8 %collective-permute-start = (bf16[4,640,256]{2,1,0:T(8,128)(2,1)}, bf16[4,640,256]{2,1,0:T(8,128)(2,1)S(1)}, u32[]{:S(2)}, u32[]{:S(2)}) collective-permute-start(bf16[4,640,256]{2,1,0:T(8,128)(2,1)} %shard_map.163), channel_id=1, source_target_pairs={{0,1},{1,0},{2,3},{3,2},{4,5},{5,4},{6,7},{7,6},{8,9},{9,8},{10,11... | collective-permute-start | bytes 3932168 | tf_op jit(solution)/shard_map/ppermute | solution.py:244
  12.7 26.3 %all-to-all-start = ((bf16[32,8,1024]{2,1,0:T(8,128)(2,1)}), bf16[32,8,1024]{2,1,0:T(8,128)(2,1)S(1)}, u32[]{:S(2)}, u32[]{:S(2)}) async-start(bf16[32,8,1024]{2,1,0:T(8,128)(2,1)} %bitcast.5), calls=%async_computation | async-start | bytes 1048576 | tf_op jit(solution)/shard_map/all_to_all | solution.py:253
  29.6 10.4 %collective-permute-start.1 = (bf16[320,256]{1,0:T(8,128)(2,1)}, bf16[320,256]{1,0:T(8,128)(2,1)S(1)}, u32[]{:S(2)}, u32[]{:S(2)}) collective-permute-start(bf16[320,256]{1,0:T(8,128)(2,1)} %get-tuple-element.29), channel_id=1, source_target_pairs={{0,2},{2,4},{4,6},{6,0},{1,3},{3,5},{5,7},{7,1},{8,10},{10,12},{12... | collective-permute-start | bytes 491528 | tf_op jit(solution)/shard_map/ppermute | solution.py:244
  30.9 9.2 %collective-permute-start.2 = (bf16[320,256]{1,0:T(8,128)(2,1)}, bf16[320,256]{1,0:T(8,128)(2,1)S(1)}, u32[]{:S(2)}, u32[]{:S(2)}) collective-permute-start(bf16[320,256]{1,0:T(8,128)(2,1)} %get-tuple-element.30), channel_id=1, source_target_pairs={{0,6},{2,0},{4,2},{6,4},{1,7},{3,1},{5,3},{7,5},{8,14},{10,8},{12,... | collective-permute-start | bytes 491528 | tf_op jit(solution)/shard_map/ppermute | solution.py:244
  42.9 14.8 %collective-permute-start.3 = (bf16[640,256]{1,0:T(8,128)(2,1)}, bf16[640,256]{1,0:T(8,128)(2,1)S(1)}, u32[]{:S(2)}, u32[]{:S(2)}) collective-permute-start(bf16[640,256]{1,0:T(8,128)(2,1)} %get-tuple-element.31), channel_id=1, source_target_pairs={{0,2},{2,4},{4,6},{6,0},{1,3},{3,5},{5,7},{7,1},{8,10},{10,12},{12... | collective-permute-start | bytes 983048 | tf_op jit(solution)/shard_map/ppermute | solution.py:244
  44.1 13.6 %collective-permute-start.4 = (bf16[640,256]{1,0:T(8,128)(2,1)}, bf16[640,256]{1,0:T(8,128)(2,1)}, u32[]{:S(2)}, u32[]{:S(2)}) collective-permute-start(bf16[640,256]{1,0:T(8,128)(2,1)} %get-tuple-element.32), channel_id=1, source_target_pairs={{0,6},{2,0},{4,2},{6,4},{1,7},{3,1},{5,3},{7,5},{8,14},{10,8},{12,... | collective-permute-start | bytes 983048 | tf_op jit(solution)/shard_map/ppermute | solution.py:244
  45.6 15.8 %all-to-all-start.1 = ((bf16[32,8,512]{2,1,0:T(8,128)(2,1)}), bf16[32,8,512]{2,1,0:T(8,128)(2,1)S(1)}, u32[]{:S(2)}, u32[]{:S(2)}) async-start(bf16[32,8,512]{2,1,0:T(8,128)(2,1)} %bitcast.7), calls=%async_computation.1 | async-start | bytes 524288 | tf_op jit(solution)/shard_map/all_to_all | solution.py:351
  54.9 37.1 %collective-permute-start.5 = (bf16[256,1792]{1,0:T(8,128)(2,1)}, bf16[256,1792]{1,0:T(8,128)(2,1)S(1)}, u32[]{:S(2)}, u32[]{:S(2)}) collective-permute-start(bf16[256,1792]{1,0:T(8,128)(2,1)} %get-tuple-element.57), channel_id=1, source_target_pairs={{0,8},{8,16},{16,24},{24,0},{1,9},{9,17},{17,25},{25,1},{2,10},{10... | collective-permute-start | bytes 2752520 | tf_op jit(solution)/shard_map/ppermute | solution.py:244
  56.1 36.8 %collective-permute-start.6 = (bf16[256,1792]{1,0:T(8,128)(2,1)}, bf16[256,1792]{1,0:T(8,128)(2,1)}, u32[]{:S(2)}, u32[]{:S(2)}) collective-permute-start(bf16[256,1792]{1,0:T(8,128)(2,1)} %get-tuple-element.56), channel_id=1, source_target_pairs={{0,24},{8,0},{16,8},{24,16},{1,25},{9,1},{17,9},{25,17},{2,26},{10... | collective-permute-start | bytes 2752520 | tf_op jit(solution)/shard_map/ppermute | solution.py:244
  64.6 28.3 %all-to-all-start.2 = ((bf16[32,8,640]{2,1,0:T(8,128)(2,1)}), bf16[32,8,640]{2,1,0:T(8,128)(2,1)S(1)}, u32[]{:S(2)}, u32[]{:S(2)}) async-start(bf16[32,8,640]{2,1,0:T(8,128)(2,1)} %bitcast.9), calls=%async_computation.2 | async-start | bytes 655360 | tf_op jit(solution)/shard_map/all_to_all | solution.py:370
  70.3 21.7 %collective-permute-start.7 = (bf16[256,896]{1,0:T(8,128)(2,1)S(1)}, bf16[256,896]{1,0:T(8,128)(2,1)S(1)}, u32[]{:S(2)}, u32[]{:S(2)}) collective-permute-start(bf16[256,896]{1,0:T(8,128)(2,1)S(1)} %get-tuple-element.59), channel_id=1, source_target_pairs={{0,8},{8,16},{16,24},{24,0},{1,9},{9,17},{17,25},{25,1},{2,10},{10... | collective-permute-start | bytes 1376264 | tf_op jit(solution)/shard_map/ppermute | solution.py:244
  71.8 20.2 %collective-permute-start.8 = (bf16[256,896]{1,0:T(8,128)(2,1)S(1)}, bf16[256,896]{1,0:T(8,128)(2,1)S(1)}, u32[]{:S(2)}, u32[]{:S(2)}) collective-permute-start(bf16[256,896]{1,0:T(8,128)(2,1)S(1)} %get-tuple-element.58), channel_id=1, source_target_pairs={{0,24},{8,0},{16,8},{24,16},{1,25},{9,1},{17,9},{25,17},{2,26},{10... | collective-permute-start | bytes 1376264 | tf_op jit(solution)/shard_map/ppermute | solution.py:244
  94.2 27.9 %all-to-all-start.3 = ((bf16[32,8,1024]{2,1,0:T(8,128)(2,1)}), bf16[32,8,1024]{2,1,0:T(8,128)(2,1)}, u32[]{:S(2)}, u32[]{:S(2)}) async-start(bf16[32,8,1024]{2,1,0:T(8,128)(2,1)} %shard_map.169), calls=%async_computation.3 | async-start | bytes 1048576 | tf_op jit(solution)/shard_map/all_to_all | solution.py:381
  100.0 21.3 %collective-permute-start.9 = (bf16[256,896]{1,0:T(8,128)(2,1)}, bf16[256,896]{1,0:T(8,128)(2,1)S(1)}, u32[]{:S(2)}, u32[]{:S(2)}) collective-permute-start(bf16[256,896]{1,0:T(8,128)(2,1)} %copy-done.17), channel_id=1, source_target_pairs={{0,8},{8,16},{16,24},{24,0},{1,9},{9,17},{17,25},{25,1},{2,10},{10... | collective-permute-start | bytes 1376264 | tf_op jit(solution)/shard_map/ppermute | solution.py:244
  101.3 20.7 %collective-permute-start.10 = (bf16[256,896]{1,0:T(8,128)(2,1)}, bf16[256,896]{1,0:T(8,128)(2,1)}, u32[]{:S(2)}, u32[]{:S(2)}) collective-permute-start(bf16[256,896]{1,0:T(8,128)(2,1)} %copy-done.18), channel_id=1, source_target_pairs={{0,24},{8,0},{16,8},{24,16},{1,25},{9,1},{17,9},{25,17},{2,26},{10... | collective-permute-start | bytes 1376264 | tf_op jit(solution)/shard_map/ppermute | solution.py:244
  103.9 17.3 %collective-permute-start.11 = (bf16[448,256]{1,0:T(8,128)(2,1)S(1)}, bf16[448,256]{1,0:T(8,128)(2,1)S(1)}, u32[]{:S(2)}, u32[]{:S(2)}) collective-permute-start(bf16[448,256]{1,0:T(8,128)(2,1)S(1)} %get-tuple-element.54), channel_id=1, source_target_pairs={{0,8},{8,16},{16,24},{24,0},{1,9},{9,17},{17,25},{25,1},{2,10},{10... | collective-permute-start | bytes 688136 | tf_op jit(solution)/shard_map/ppermute | solution.py:244
  104.0 17.3 %collective-permute-start.12 = (bf16[448,256]{1,0:T(8,128)(2,1)S(1)}, bf16[448,256]{1,0:T(8,128)(2,1)S(1)}, u32[]{:S(2)}, u32[]{:S(2)}) collective-permute-start(bf16[448,256]{1,0:T(8,128)(2,1)S(1)} %get-tuple-element.53), channel_id=1, source_target_pairs={{0,24},{8,0},{16,8},{24,16},{1,25},{9,1},{17,9},{25,17},{2,26},{10... | collective-permute-start | bytes 688136 | tf_op jit(solution)/shard_map/ppermute | solution.py:244
  128.2 13.4 %collective-permute-start.17 = (bf16[896,256]{1,0:T(8,128)(2,1)S(1)}, bf16[896,256]{1,0:T(8,128)(2,1)S(1)}, u32[]{:S(2)}, u32[]{:S(2)}) collective-permute-start(bf16[896,256]{1,0:T(8,128)(2,1)S(1)} %get-tuple-element.52), channel_id=1, source_target_pairs={{0,8},{8,16},{16,24},{24,0},{1,9},{9,17},{17,25},{25,1},{2,10},{10... | collective-permute-start | bytes 1376264 | tf_op jit(solution)/shard_map/ppermute | solution.py:244
  129.1 12.5 %collective-permute-start.18 = (bf16[896,256]{1,0:T(8,128)(2,1)S(1)}, bf16[896,256]{1,0:T(8,128)(2,1)S(1)}, u32[]{:S(2)}, u32[]{:S(2)}) collective-permute-start(bf16[896,256]{1,0:T(8,128)(2,1)S(1)} %get-tuple-element.51), channel_id=1, source_target_pairs={{0,24},{8,0},{16,8},{24,16},{1,25},{9,1},{17,9},{25,17},{2,26},{10... | collective-permute-start | bytes 1376264 | tf_op jit(solution)/shard_map/ppermute | solution.py:244
  154.4 32.3 %all-to-all-start.4 = ((bf16[8,32,1920]{2,1,0:T(8,128)(2,1)}), bf16[8,32,1920]{2,1,0:T(8,128)(2,1)S(1)}, u32[]{:S(2)}, u32[]{:S(2)}) async-start(bf16[8,32,1920]{2,1,0:T(8,128)(2,1)} %bitcast.13), calls=%async_computation.4 | async-start | bytes 1966080 | tf_op jit(solution)/shard_map/all_to_all | solution.py:253
  202.6 12.3 %collective-permute-start.26 = (bf16[256,256]{1,0:T(8,128)(2,1)S(1)}, bf16[256,256]{1,0:T(8,128)(2,1)S(1)}, u32[]{:S(2)}, u32[]{:S(2)}) collective-permute-start(bf16[256,256]{1,0:T(8,128)(2,1)S(1)} %convolution_convert_fusion.1), channel_id=1, source_target_pairs={{0,8},{8,16},{16,24},{24,0},{1,9},{9,17},{17,25},{25,1},{2,10},{10... | collective-permute-start | bytes 393224 | tf_op jit(solution)/shard_map/ppermute | solution.py:244
  203.2 11.6 %collective-permute-start.25 = (bf16[256,256]{1,0:T(8,128)(2,1)S(1)}, bf16[256,256]{1,0:T(8,128)(2,1)S(1)}, u32[]{:S(2)}, u32[]{:S(2)}) collective-permute-start(bf16[256,256]{1,0:T(8,128)(2,1)S(1)} %convolution_convert_fusion.2), channel_id=1, source_target_pairs={{0,24},{8,0},{16,8},{24,16},{1,25},{9,1},{17,9},{25,17},{2,26},{10... | collective-permute-start | bytes 393224 | tf_op jit(solution)/shard_map/ppermute | solution.py:244
  223.9 8.8 %collective-permute-start.29 = (bf16[256,256]{1,0:T(8,128)(2,1)S(1)}, bf16[256,256]{1,0:T(8,128)(2,1)S(1)}, u32[]{:S(2)}, u32[]{:S(2)}) collective-permute-start(bf16[256,256]{1,0:T(8,128)(2,1)S(1)} %add_convert_fusion.1), channel_id=1, source_target_pairs={{0,2},{2,4},{4,6},{6,0},{1,3},{3,5},{5,7},{7,1},{8,10},{10,12},{12... | collective-permute-start | bytes 393224 | tf_op jit(solution)/shard_map/ppermute | solution.py:244
  224.2 8.5 %collective-permute-start.28 = (bf16[256,256]{1,0:T(8,128)(2,1)S(1)}, bf16[256,256]{1,0:T(8,128)(2,1)S(1)}, u32[]{:S(2)}, u32[]{:S(2)}) collective-permute-start(bf16[256,256]{1,0:T(8,128)(2,1)S(1)} %add_convert_fusion.1), channel_id=1, source_target_pairs={{0,4},{2,6},{4,0},{6,2},{1,5},{3,7},{5,1},{7,3},{8,12},{10,14},{12... | collective-permute-start | bytes 393224 | tf_op jit(solution)/shard_map/ppermute | solution.py:244
  (34 other events, 308.0 us)

commit v4 on v3

--- a/solution.py
+++ b/solution.py
@@ -15,8 +15,8 @@
 SLOTS = 2
 STEPS = 2
 EPS = 1e-05
-VMEM_BYTES = 40 * 1024 * 1024
-KV_VMEM_BYTES = 58 * 1024 * 1024
+VMEM_BYTES = 16 * 1024 * 1024
+LARGE_VMEM_BYTES = 58 * 1024 * 1024
 BF = jnp.bfloat16
 F32 = jnp.float32
 
@@ -70,14 +70,14 @@
     image_ref[...] = jnp.where(slot1 == 0, first_image, last_image)
 
 
-def kv_there_kernel(place_ref, vision_ref, k_ref, v_ref, out_ref):
-    weight = jnp.concatenate((k_ref[...], v_ref[...]), axis=1)
-    out_ref[0] = dot(vision_ref[...], weight).astype(BF)
-
-
-def kv_here_kernel(place_ref, vision_ref, k_ref, v_ref, core_ref, low_ref, high_ref, ahead_ref, behind_ref, own_ref):
-    weight = jnp.concatenate((k_ref[...], v_ref[...]), axis=1)
-    total = (dot(vision_ref[...], weight) + core_ref[0].astype(F32)).astype(BF)
+def kv_there_kernel(place_ref, k_ref, v_ref, out_ref):
+    out_ref[0, :, :HEAD] = k_ref[...]
+    out_ref[0, :, HEAD:] = v_ref[...]
+
+
+def kv_here_kernel(place_ref, k_ref, v_ref, core_ref, low_ref, high_ref, ahead_ref, behind_ref, own_ref):
+    total = jnp.concatenate((k_ref[...], v_ref[...]), axis=1).astype(F32)
+    total = (total + core_ref[0].astype(F32)).astype(BF)
     half = low_ref.shape[0]
     step = pl.program_id(0)
 
@@ -99,8 +99,8 @@
         own_ref[...] = total
 
 
-def kv_project(place, vision, k_weight, v_weight, from_core=None):
-    rows, depth = vision.shape
+def kv_split(place, k_part, v_part, from_core=None):
+    rows = k_part.shape[0]
     chips = 4
     other = from_core is None
 
@@ -117,19 +117,14 @@
         grid_spec=pltpu.PrefetchScalarGridSpec(
             num_scalar_prefetch=1,
             grid=(chips,),
-            in_specs=[
-                pl.BlockSpec((rows, depth), lambda d, p: (0, 0)),
-                pl.BlockSpec((depth, HEAD), head),
-                pl.BlockSpec((depth, HEAD), head),
-            ]
-            + ([] if other else [one]),
+            in_specs=[pl.BlockSpec((rows, HEAD), head)] * 2 + ([] if other else [one]),
             out_specs=one if other else whole,
         ),
         out_shape=jax.ShapeDtypeStruct((chips, rows, 2 * HEAD), BF)
         if other
         else [jax.ShapeDtypeStruct((n, 2 * HEAD), BF) for n in sizes],
-        compiler_params=params(KV_VMEM_BYTES),
-    )(place, vision, k_weight, v_weight, *(() if other else (from_core,)))
+        compiler_params=params(LARGE_VMEM_BYTES),
+    )(place, k_part, v_part, *(() if other else (from_core,)))
 
 
 def kv_merge_kernel(ahead_ref, behind_ref, low_ref, high_ref, forward_ref, backward_ref):
@@ -308,8 +303,10 @@
     q_part, vision = lax.optimization_barrier((q_part, vision))
     q_parts = exchange(q_part, GROUP)
 
-    there = kv_project(place, vision, k_weight, v_weight)
-    low, high, ahead, behind, own = kv_project(place, vision, k_weight, v_weight, shift(there, "c", 1))
+    k_part = dot(vision, k_weight).astype(BF)
+    v_part = dot(vision, v_weight).astype(BF)
+    there = kv_split(place, k_part, v_part)
+    low, high, ahead, behind, own = kv_split(place, k_part, v_part, shift(there, "c", 1))
     q_parts = after(q_parts, own)
     forward, backward = pl.pallas_call(
         kv_merge_kernel,
@@ -321,6 +318,22 @@
     kv_left = shift(forward, "x", 1)
     kv_right = shift(backward, "x", -1)
 
+    chips_y = lax.axis_size("y")
+    units = hidden_part // chips_y
+    half = units // 2
+    gain = mlp_gain[:, None]
+
+    def columns(weight, d):
+        at = lax.rem(lax.axis_index("y") + d, chips_y) * units
+        return lax.dynamic_slice_in_dim(weight, at, units, 1).astype(F32)
+
+    def wide(*parts):
+        return (jnp.concatenate(parts, axis=1) * gain).astype(BF)
+
+    first_gate, first_up = lax.optimization_barrier((gate_weight, up_weight, own))[:2]
+    gate_2 = shift(wide(columns(first_gate, 2)), "y", 1)
+    up_2 = shift(wide(columns(first_up, 2)), "y", -1)
+
     queries = pl.pallas_call(
         query_kernel,
         in_specs=[vmem()] * 3,
@@ -328,27 +341,14 @@
         out_shape=jax.ShapeDtypeStruct((slot_rows, local_heads // 2), BF),
         compiler_params=params(),
     )(q_parts, sel, q_gain.reshape(1, HEAD))
-    chips_y = lax.axis_size("y")
-    units = hidden_part // chips_y
-    half = units // 2
-    gain = mlp_gain[:, None]
     queries = after(queries, forward, backward)
-    gate_weight, up_weight = lax.optimization_barrier((gate_weight, up_weight, queries))[:2]
-
-    def columns(weight, d):
-        at = lax.rem(lax.axis_index("y") + d, chips_y) * units
-        return lax.dynamic_slice_in_dim(weight, at, units, 1).astype(F32)
-
-    def wide(*parts):
-        return (jnp.concatenate(parts, axis=1) * gain).astype(BF)
-
-    wide_0 = wide(columns(gate_weight, 0), columns(up_weight, 0))
-    wide_1 = shift(wide(columns(gate_weight, 1), columns(up_weight, 1)), "y", 1)
-    wide_3 = shift(wide(columns(gate_weight, 3), columns(up_weight, 3)), "y", -1)
-    gate_2 = shift(wide(columns(gate_weight, 2)), "y", 1)
-    up_2 = shift(wide(columns(up_weight, 2)), "y", -1)
-
+    later_gate, later_up = lax.optimization_barrier((gate_weight, up_weight, queries))[:2]
+    wide_0 = wide(columns(later_gate, 0), columns(later_up, 0))
+    wide_1 = shift(wide(columns(later_gate, 1), columns(later_up, 1)), "y", 1)
+    wide_3 = shift(wide(columns(later_gate, 3), columns(later_up, 3)), "y", -1)
     queries = lax.all_to_all(queries, GROUP, 0, 0, tiled=True)
+    queries = after(queries, gate_2, up_2)
+    gate_2, up_2 = shift(gate_2, "y", 1), shift(up_2, "y", -1)
 
     mixed = pl.pallas_call(
         attention_kernel,
@@ -368,8 +368,7 @@
     down_3 = shift(rows(3, 0, units), "y", -1)
     down_2 = (shift(rows(2, 0, half), "y", 1), shift(rows(2, half, half), "y", -1))
     mixed = lax.all_to_all(mixed, GROUP, 0, 0, tiled=True)
-    mixed = after(mixed, wide_1, wide_3, gate_2, up_2)
-    gate_2, up_2 = shift(gate_2, "y", 1), shift(up_2, "y", -1)
+    mixed = after(mixed, wide_1, wide_3)
 
     attended = pl.pallas_call(
         combine_kernel,
@@ -380,11 +379,11 @@
     )(mixed, sel)
     attended = lax.all_to_all(attended, GROUP, 0, 0, tiled=True).reshape(all_rows, local_heads)
 
-    attended = after(attended, gate_2, up_2, *down_2)
+    attended = after(attended, gate_2, up_2)
     attn_sum = tensor_sum(dot(attended, o_weight))
     middle = (hidden_f + jnp.tanh(gate_logits[0]) * attn_sum).astype(BF)
     middle_f = middle.astype(F32)
-    middle = after(middle, down_1, down_3)
+    middle = after(middle, down_1, down_3, *down_2)
     down_2 = (shift(down_2[0], "y", 1), shift(down_2[1], "y", -1))
     middles = [middle] + [shift(middle, "y", d) for d in (1, 2, 3)]
     gate_up = pl.pallas_call(

time: 235 us -> 234 us (level)
  matrix products: 5.79 us -> 15.8 us
  waiting for transfers between devices: 86.8 us -> 82 us
  starting transfers between devices: 82.6 us -> 79.2 us
  Pallas kernels: 23.6 us -> 21 us
    dot_general x7 -> x9, matrix products: 5.79 us -> 15.8 us  [dot(): return jnp.dot(a, b, preferred_element_type=F32)]
    ppermute x31, waiting for transfers between devices: 58.8 us -> 49.3 us  [shift(): return lax.ppermute(value, axis, [(i, (i + by) % n) for i in range(n)])]
    all_to_all x2, waiting for transfers between devices: 24.2 us -> 27.6 us  [exchange(): out = lax.all_to_all(value, axis, 0, 0, tiled=True)]
    pallas_call x2, Pallas kernels: 12.1 us -> 9.05 us  [kv_split(): pl.pallas_call(kv_there_kernel if other else kv_here_kernel, grid_spec=pl...]
  transfers between devices with their start and end apart: 36 -> 36, of which waited for: 17 -> 17; matrix products, arithmetic and copies ran while one was open for 5% -> 6% of each run, Pallas kernels for 5% -> 5%
where the time goes in v4:
time: 234 us; the launch traced here: 233 us
  waiting for transfers between devices  82 us (35%)
  starting transfers between devices  79.2 us (34%)
  Pallas kernels  21 us (9%)
  matrix products  15.8 us (7%)
  blocking collectives  14.5 us (6%)
  local copies, waits for them, and re-layouts  11.8 us (5%)
  other arithmetic  7.12 us (3%)
    ppermute x31, starting transfers between devices, shift(): return lax.ppermute(value, axis, [(i, (i + by) % n) for i in range(n)])  50.5 us
    ppermute x31, waiting for transfers between devices, shift(): return lax.ppermute(value, axis, [(i, (i + by) % n) for i in range(n)])  49.3 us
    all_to_all x2, waiting for transfers between devices, exchange(): out = lax.all_to_all(value, axis, 0, 0, tiled=True)  27.6 us
    dot_general x9, matrix products, dot(): return jnp.dot(a, b, preferred_element_type=F32)  15.8 us
    all_to_all x2, starting transfers between devices, exchange(): out = lax.all_to_all(value, axis, 0, 0, tiled=True)  14.8 us
    all_to_all x1, blocking collectives, shards(): lax.all_to_all(active, 'z', 0, 0, tiled=True).reshape(all_rows, units)  14.5 us
    pallas_call x2, Pallas kernels, kv_split(): pl.pallas_call(kv_there_kernel if other else kv_here_kernel, grid_spec=pl...  9.05 us
    unnamed x47, local copies, waits for them, and re-layouts  5.63 us
  transfers between devices with their start and end apart: 36, of which 17 were waited for; matrix products, arithmetic and copies ran while one was open for 6% of the time, Pallas kernels for 5%

profile of v4, /device:TPU:1, one launch (start us, length us, event | category | flops | bytes accessed | tf_op | source)
XLA Modules:
  0.0 233.1 jit_solution(3983656407249659275)
XLA Ops:
  2.4 4.1 %convolution_convert_fusion.v_ref = bf16[640,1024]{1,0:T(8,128)(2,1)} fusion(bf16[640,1024]{1,0:T(8,128)(2,1)} %param.18, bf16[1024,1024]{1,0:T(8,128)(2,1)S(1)} %copy-done), kind=kOutput, calls=%fused_computation.3 | convolution fusion | flops 1342832640 | bytes 4718592 | tf_op jit(solution)/shard_map/dot_general | solution.py:29
  9.6 4.4 %shard_map.163 = bf16[4,640,256]{2,1,0:T(8,128)(2,1)} custom-call(s32[2]{0:T(128)} %pad_add_fusion.place_ref, bf16[640,1024]{1,0:T(8,128)(2,1)} %convolution_convert_fusion.1.k_ref, bf16[640,1024]{1,0:T(8,128)(2,1)} %convolution_convert_fusion.v_ref), custom_call_target="tpu_custom_call" | custom-call | tf_op jit(solution)/shard_map/pallas_call | solution.py:115
  14.0 3.2 %collective-permute-start = (bf16[4,640,256]{2,1,0:T(8,128)(2,1)}, bf16[4,640,256]{2,1,0:T(8,128)(2,1)}, u32[]{:S(2)}, u32[]{:S(2)}) collective-permute-start(bf16[4,640,256]{2,1,0:T(8,128)(2,1)} %shard_map.163), channel_id=1, source_target_pairs={{0,1},{1,0},{2,3},{3,2},{4,5},{5,4},{6,7},{7,6},{8,9},{9,8},{10,11... | collective-permute-start | bytes 3932168 | tf_op jit(solution)/shard_map/ppermute | solution.py:239
  17.3 9.5 %all-to-all-start = ((bf16[32,8,1024]{2,1,0:T(8,128)(2,1)}), bf16[32,8,1024]{2,1,0:T(8,128)(2,1)S(1)}, u32[]{:S(2)}, u32[]{:S(2)}) async-start(bf16[32,8,1024]{2,1,0:T(8,128)(2,1)} %bitcast.5), calls=%async_computation | async-start | bytes 1048576 | tf_op jit(solution)/shard_map/all_to_all | solution.py:248
  27.6 4.7 %shard_map.164 = (bf16[320,256]{1,0:T(8,128)(2,1)}, bf16[320,256]{1,0:T(8,128)(2,1)}, bf16[640,256]{1,0:T(8,128)(2,1)}, bf16[640,256]{1,0:T(8,128)(2,1)}, bf16[640,256]{1,0:T(8,128)(2,1)}) custom-call(s32[2]{0:T(128)} %pad_add_fusion.place_ref, bf16[640,1024]{1,0:T(8,128)(2,1)} %convolution_convert_fusion.1.k_ref, ...), custom_call_target="tpu_custom_call" | custom-call | tf_op jit(solution)/shard_map/pallas_call | solution.py:115
  35.0 8.6 %all-to-all-done.parts_ref = bf16[32,8,1024]{2,1,0:T(8,128)(2,1)S(1)} async-done(((bf16[32,8,1024]{2,1,0:T(8,128)(2,1)}), bf16[32,8,1024]{2,1,0:T(8,128)(2,1)S(1)}, u32[]{:S(2)}, u32[]{:S(2)}) %all-to-all-start) | async-done | bytes 524320 | tf_op jit(solution)/shard_map/all_to_all | solution.py:248
  54.2 4.0 %all-to-all-start.1 = ((bf16[32,8,512]{2,1,0:T(8,128)(2,1)}), bf16[32,8,512]{2,1,0:T(8,128)(2,1)S(1)}, u32[]{:S(2)}, u32[]{:S(2)}) async-start(bf16[32,8,512]{2,1,0:T(8,128)(2,1)} %bitcast.7), calls=%async_computation.1 | async-start | bytes 524288 | tf_op jit(solution)/shard_map/all_to_all | solution.py:349
  65.0 3.7 %all-to-all-done.1 = bf16[32,8,512]{2,1,0:T(8,128)(2,1)S(1)} async-done(((bf16[32,8,512]{2,1,0:T(8,128)(2,1)}), bf16[32,8,512]{2,1,0:T(8,128)(2,1)S(1)}, u32[]{:S(2)}, u32[]{:S(2)}) %all-to-all-start.1) | async-done | bytes 262176 | tf_op jit(solution)/shard_map/all_to_all | solution.py:349
  72.9 4.3 %all-to-all-start.2 = ((bf16[32,8,640]{2,1,0:T(8,128)(2,1)}), bf16[32,8,640]{2,1,0:T(8,128)(2,1)S(1)}, u32[]{:S(2)}, u32[]{:S(2)}) async-start(bf16[32,8,640]{2,1,0:T(8,128)(2,1)} %bitcast.30), calls=%async_computation.2 | async-start | bytes 655360 | tf_op jit(solution)/shard_map/all_to_all | solution.py:370
  77.2 9.3 %collective-permute-done.7.w1 = bf16[256,1792]{1,0:T(8,128)(2,1)} collective-permute-done((bf16[256,1792]{1,0:T(8,128)(2,1)}, bf16[256,1792]{1,0:T(8,128)(2,1)}, u32[]{:S(2)}, u32[]{:S(2)}) %collective-permute-start.7) | collective-permute-done | bytes 917536 | tf_op jit(solution)/shard_map/ppermute | solution.py:239
  89.2 5.6 %all-to-all-start.3 = ((bf16[32,8,1024]{2,1,0:T(8,128)(2,1)}), bf16[32,8,1024]{2,1,0:T(8,128)(2,1)S(1)}, u32[]{:S(2)}, u32[]{:S(2)}) async-start(bf16[32,8,1024]{2,1,0:T(8,128)(2,1)} %shard_map.169), calls=%async_computation.3 | async-start | bytes 1048576 | tf_op jit(solution)/shard_map/all_to_all | solution.py:380
  97.3 10.9 %collective-permute-done.10.up2 = bf16[256,896]{1,0:T(8,128)(2,1)S(1)} collective-permute-done((bf16[256,896]{1,0:T(8,128)(2,1)}, bf16[256,896]{1,0:T(8,128)(2,1)S(1)}, u32[]{:S(2)}, u32[]{:S(2)}) %collective-permute-start.10) | collective-permute-done | bytes 458784 | tf_op jit(solution)/shard_map/ppermute | solution.py:239
  109.0 3.1 %collective-permute-done.9.gate2 = bf16[256,896]{1,0:T(8,128)(2,1)S(1)} collective-permute-done((bf16[256,896]{1,0:T(8,128)(2,1)}, bf16[256,896]{1,0:T(8,128)(2,1)S(1)}, u32[]{:S(2)}, u32[]{:S(2)}) %collective-permute-start.9) | collective-permute-done | bytes 458784 | tf_op jit(solution)/shard_map/ppermute | solution.py:239
  114.2 4.6 %collective-permute-start.11 = (bf16[256,256]{1,0:T(8,128)(2,1)S(1)}, bf16[256,256]{1,0:T(8,128)(2,1)S(1)}, u32[]{:S(2)}, u32[]{:S(2)}) collective-permute-start(bf16[256,256]{1,0:T(8,128)(2,1)S(1)} %convolution_convert_fusion.5), channel_id=1, source_target_pairs={{0,1},{1,0},{2,3},{3,2},{4,5},{5,4},{6,7},{7,6},{8,9},{9,8},{10,11... | collective-permute-start | bytes 393224 | tf_op jit(solution)/shard_map/ppermute | solution.py:239
  134.7 3.3 %collective-permute-done.17 = bf16[448,256]{1,0:T(8,128)(2,1)S(1)} collective-permute-done((bf16[448,256]{1,0:T(8,128)(2,1)S(1)}, bf16[448,256]{1,0:T(8,128)(2,1)S(1)}, u32[]{:S(2)}, u32[]{:S(2)}) %collective-permute-start.17) | collective-permute-done | bytes 229408 | tf_op jit(solution)/shard_map/ppermute | solution.py:239
  142.3 4.4 %collective-permute-done.19.m1 = bf16[256,256]{1,0:T(8,128)(2,1)S(1)} collective-permute-done((bf16[256,256]{1,0:T(8,128)(2,1)S(1)}, bf16[256,256]{1,0:T(8,128)(2,1)S(1)}, u32[]{:S(2)}, u32[]{:S(2)}) %collective-permute-start.19) | collective-permute-done | bytes 131104 | tf_op jit(solution)/shard_map/ppermute | solution.py:239
  149.4 4.5 %shard_map.170 = bf16[256,1920]{1,0:T(8,128)(2,1)} custom-call(bf16[256,256]{1,0:T(8,128)(2,1)S(1)} %fusion.16.m0, bf16[256,256]{1,0:T(8,128)(2,1)S(1)} %collective-permute-done.19.m1, bf16[256,256]{1,0:T(8,128)(2,1)S(1)} %collective-permute-done.20.m2, bf16[256,256]{1,0:T(8,128)(2,1)S(1)} %collective-permute-done.21.m3, ...), custom_call_target="tpu_custom_call" | custom-call | tf_op jit(solution)/shard_map/pallas_call | solution.py:389
  153.9 5.3 %all-to-all-start.4 = ((bf16[8,32,1920]{2,1,0:T(8,128)(2,1)}), bf16[8,32,1920]{2,1,0:T(8,128)(2,1)S(1)}, u32[]{:S(2)}, u32[]{:S(2)}) async-start(bf16[8,32,1920]{2,1,0:T(8,128)(2,1)} %bitcast.13), calls=%async_computation.4 | async-start | bytes 1966080 | tf_op jit(solution)/shard_map/all_to_all | solution.py:248
  161.9 3.6 %collective-permute-done.22 = bf16[448,256]{1,0:T(8,128)(2,1)S(1)} collective-permute-done((bf16[448,256]{1,0:T(8,128)(2,1)}, bf16[448,256]{1,0:T(8,128)(2,1)S(1)}, u32[]{:S(2)}, u32[]{:S(2)}) %collective-permute-start.22) | collective-permute-done | bytes 229408 | tf_op jit(solution)/shard_map/ppermute | solution.py:239
  165.5 19.0 %all-to-all-done.4.parts_ref = bf16[8,32,1920]{2,1,0:T(8,128)(2,1)S(1)} async-done(((bf16[8,32,1920]{2,1,0:T(8,128)(2,1)}), bf16[8,32,1920]{2,1,0:T(8,128)(2,1)S(1)}, u32[]{:S(2)}, u32[]{:S(2)}) %all-to-all-start.4) | async-done | bytes 983072 | tf_op jit(solution)/shard_map/all_to_all | solution.py:248
  184.8 14.5 %all_to_all.52 = bf16[8,32,896]{2,1,0:T(8,128)(2,1)S(1)} all-to-all(bf16[8,32,896]{2,1,0:T(8,128)(2,1)S(1)} %shard_map.171), channel_id=1, replica_groups=mesh['z'=8,'y'=4,'x'=4,'c'=2] {'z'}, dimensions={0} | all-to-all | bytes 917504 | tf_op jit(solution)/shard_map/all_to_all | solution.py:404
  207.6 5.6 %collective-permute-done.26 = bf16[256,256]{1,0:T(8,128)(2,1)S(1)} collective-permute-done((bf16[256,256]{1,0:T(8,128)(2,1)S(1)}, bf16[256,256]{1,0:T(8,128)(2,1)S(1)}, u32[]{:S(2)}, u32[]{:S(2)}) %collective-permute-start.26) | collective-permute-done | bytes 131104 | tf_op jit(solution)/shard_map/ppermute | solution.py:239
  214.5 5.1 %collective-permute-start.27 = (bf16[256,256]{1,0:T(8,128)(2,1)S(1)}, bf16[256,256]{1,0:T(8,128)(2,1)S(1)}, u32[]{:S(2)}, u32[]{:S(2)}) collective-permute-start(bf16[256,256]{1,0:T(8,128)(2,1)S(1)} %fusion.12), channel_id=1, source_target_pairs={{0,1},{1,0},{2,3},{3,2},{4,5},{5,4},{6,7},{7,6},{8,9},{9,8},{10,11... | collective-permute-start | bytes 393224 | tf_op jit(solution)/shard_map/ppermute | solution.py:239
  220.8 5.3 %collective-permute-start.28 = (bf16[256,256]{1,0:T(8,128)(2,1)S(1)}, bf16[256,256]{1,0:T(8,128)(2,1)S(1)}, u32[]{:S(2)}, u32[]{:S(2)}) collective-permute-start(bf16[256,256]{1,0:T(8,128)(2,1)S(1)} %add_convert_fusion.1), channel_id=1, source_target_pairs={{0,4},{2,6},{4,0},{6,2},{1,5},{3,7},{5,1},{7,3},{8,12},{10,14},{12... | collective-permute-start | bytes 393224 | tf_op jit(solution)/shard_map/ppermute | solution.py:239
  (133 shorter events, 80.7 us)
Async XLA Ops:
  14.0 13.5 %collective-permute-start = (bf16[4,640,256]{2,1,0:T(8,128)(2,1)}, bf16[4,640,256]{2,1,0:T(8,128)(2,1)}, u32[]{:S(2)}, u32[]{:S(2)}) collective-permute-start(bf16[4,640,256]{2,1,0:T(8,128)(2,1)} %shard_map.163), channel_id=1, source_target_pairs={{0,1},{1,0},{2,3},{3,2},{4,5},{5,4},{6,7},{7,6},{8,9},{9,8},{10,11... | collective-permute-start | bytes 3932168 | tf_op jit(solution)/shard_map/ppermute | solution.py:239
  17.3 26.3 %all-to-all-start = ((bf16[32,8,1024]{2,1,0:T(8,128)(2,1)}), bf16[32,8,1024]{2,1,0:T(8,128)(2,1)S(1)}, u32[]{:S(2)}, u32[]{:S(2)}) async-start(bf16[32,8,1024]{2,1,0:T(8,128)(2,1)} %bitcast.5), calls=%async_computation | async-start | bytes 1048576 | tf_op jit(solution)/shard_map/all_to_all | solution.py:248
  32.2 17.4 %collective-permute-start.1 = (bf16[320,256]{1,0:T(8,128)(2,1)}, bf16[320,256]{1,0:T(8,128)(2,1)}, u32[]{:S(2)}, u32[]{:S(2)}) collective-permute-start(bf16[320,256]{1,0:T(8,128)(2,1)} %get-tuple-element.32), channel_id=1, source_target_pairs={{0,2},{2,4},{4,6},{6,0},{1,3},{3,5},{5,7},{7,1},{8,10},{10,12},{12... | collective-permute-start | bytes 491528 | tf_op jit(solution)/shard_map/ppermute | solution.py:239
  33.5 16.1 %collective-permute-start.2 = (bf16[320,256]{1,0:T(8,128)(2,1)}, bf16[320,256]{1,0:T(8,128)(2,1)}, u32[]{:S(2)}, u32[]{:S(2)}) collective-permute-start(bf16[320,256]{1,0:T(8,128)(2,1)} %get-tuple-element.33), channel_id=1, source_target_pairs={{0,6},{2,0},{4,2},{6,4},{1,7},{3,1},{5,3},{7,5},{8,14},{10,8},{12,... | collective-permute-start | bytes 491528 | tf_op jit(solution)/shard_map/ppermute | solution.py:239
  45.9 17.5 %collective-permute-start.5 = (bf16[256,896]{1,0:T(8,128)(2,1)}, bf16[256,896]{1,0:T(8,128)(2,1)}, u32[]{:S(2)}, u32[]{:S(2)}) collective-permute-start(bf16[256,896]{1,0:T(8,128)(2,1)} %get-tuple-element.65), channel_id=1, source_target_pairs={{0,8},{8,16},{16,24},{24,0},{1,9},{9,17},{17,25},{25,1},{2,10},{10... | collective-permute-start | bytes 1376264 | tf_op jit(solution)/shard_map/ppermute | solution.py:239
  46.9 18.0 %collective-permute-start.6 = (bf16[256,896]{1,0:T(8,128)(2,1)}, bf16[256,896]{1,0:T(8,128)(2,1)}, u32[]{:S(2)}, u32[]{:S(2)}) collective-permute-start(bf16[256,896]{1,0:T(8,128)(2,1)} %get-tuple-element.64), channel_id=1, source_target_pairs={{0,24},{8,0},{16,8},{24,16},{1,25},{9,1},{17,9},{25,17},{2,26},{10... | collective-permute-start | bytes 1376264 | tf_op jit(solution)/shard_map/ppermute | solution.py:239
  51.6 17.1 %collective-permute-start.3 = (bf16[640,256]{1,0:T(8,128)(2,1)}, bf16[640,256]{1,0:T(8,128)(2,1)}, u32[]{:S(2)}, u32[]{:S(2)}) collective-permute-start(bf16[640,256]{1,0:T(8,128)(2,1)} %get-tuple-element.34), channel_id=1, source_target_pairs={{0,2},{2,4},{4,6},{6,0},{1,3},{3,5},{5,7},{7,1},{8,10},{10,12},{12... | collective-permute-start | bytes 983048 | tf_op jit(solution)/shard_map/ppermute | solution.py:239
  52.8 15.9 %collective-permute-start.4 = (bf16[640,256]{1,0:T(8,128)(2,1)}, bf16[640,256]{1,0:T(8,128)(2,1)}, u32[]{:S(2)}, u32[]{:S(2)}) collective-permute-start(bf16[640,256]{1,0:T(8,128)(2,1)} %get-tuple-element.35), channel_id=1, source_target_pairs={{0,6},{2,0},{4,2},{6,4},{1,7},{3,1},{5,3},{7,5},{8,14},{10,8},{12,... | collective-permute-start | bytes 983048 | tf_op jit(solution)/shard_map/ppermute | solution.py:239
  54.2 14.4 %all-to-all-start.1 = ((bf16[32,8,512]{2,1,0:T(8,128)(2,1)}), bf16[32,8,512]{2,1,0:T(8,128)(2,1)S(1)}, u32[]{:S(2)}, u32[]{:S(2)}) async-start(bf16[32,8,512]{2,1,0:T(8,128)(2,1)} %bitcast.7), calls=%async_computation.1 | async-start | bytes 524288 | tf_op jit(solution)/shard_map/all_to_all | solution.py:349
  62.2 24.3 %collective-permute-start.7 = (bf16[256,1792]{1,0:T(8,128)(2,1)}, bf16[256,1792]{1,0:T(8,128)(2,1)}, u32[]{:S(2)}, u32[]{:S(2)}) collective-permute-start(bf16[256,1792]{1,0:T(8,128)(2,1)} %get-tuple-element.63), channel_id=1, source_target_pairs={{0,8},{8,16},{16,24},{24,0},{1,9},{9,17},{17,25},{25,1},{2,10},{10... | collective-permute-start | bytes 2752520 | tf_op jit(solution)/shard_map/ppermute | solution.py:239
  63.4 23.1 %collective-permute-start.8 = (bf16[256,1792]{1,0:T(8,128)(2,1)}, bf16[256,1792]{1,0:T(8,128)(2,1)}, u32[]{:S(2)}, u32[]{:S(2)}) collective-permute-start(bf16[256,1792]{1,0:T(8,128)(2,1)} %get-tuple-element.62), channel_id=1, source_target_pairs={{0,24},{8,0},{16,8},{24,16},{1,25},{9,1},{17,9},{25,17},{2,26},{10... | collective-permute-start | bytes 2752520 | tf_op jit(solution)/shard_map/ppermute | solution.py:239
  72.9 15.1 %all-to-all-start.2 = ((bf16[32,8,640]{2,1,0:T(8,128)(2,1)}), bf16[32,8,640]{2,1,0:T(8,128)(2,1)S(1)}, u32[]{:S(2)}, u32[]{:S(2)}) async-start(bf16[32,8,640]{2,1,0:T(8,128)(2,1)} %bitcast.30), calls=%async_computation.2 | async-start | bytes 655360 | tf_op jit(solution)/shard_map/all_to_all | solution.py:370
  89.2 23.6 %all-to-all-start.3 = ((bf16[32,8,1024]{2,1,0:T(8,128)(2,1)}), bf16[32,8,1024]{2,1,0:T(8,128)(2,1)S(1)}, u32[]{:S(2)}, u32[]{:S(2)}) async-start(bf16[32,8,1024]{2,1,0:T(8,128)(2,1)} %shard_map.169), calls=%async_computation.3 | async-start | bytes 1048576 | tf_op jit(solution)/shard_map/all_to_all | solution.py:380
  94.8 13.4 %collective-permute-start.10 = (bf16[256,896]{1,0:T(8,128)(2,1)}, bf16[256,896]{1,0:T(8,128)(2,1)S(1)}, u32[]{:S(2)}, u32[]{:S(2)}) collective-permute-start(bf16[256,896]{1,0:T(8,128)(2,1)} %collective-permute-done.6), channel_id=1, source_target_pairs={{0,24},{8,0},{16,8},{24,16},{1,25},{9,1},{17,9},{25,17},{2,26},{10... | collective-permute-start | bytes 1376264 | tf_op jit(solution)/shard_map/ppermute | solution.py:239
  97.3 14.7 %collective-permute-start.9 = (bf16[256,896]{1,0:T(8,128)(2,1)}, bf16[256,896]{1,0:T(8,128)(2,1)S(1)}, u32[]{:S(2)}, u32[]{:S(2)}) collective-permute-start(bf16[256,896]{1,0:T(8,128)(2,1)} %collective-permute-done.5), channel_id=1, source_target_pairs={{0,8},{8,16},{16,24},{24,0},{1,9},{9,17},{17,25},{25,1},{2,10},{10... | collective-permute-start | bytes 1376264 | tf_op jit(solution)/shard_map/ppermute | solution.py:239
  114.2 9.4 %collective-permute-start.11 = (bf16[256,256]{1,0:T(8,128)(2,1)S(1)}, bf16[256,256]{1,0:T(8,128)(2,1)S(1)}, u32[]{:S(2)}, u32[]{:S(2)}) collective-permute-start(bf16[256,256]{1,0:T(8,128)(2,1)S(1)} %convolution_convert_fusion.5), channel_id=1, source_target_pairs={{0,1},{1,0},{2,3},{3,2},{4,5},{5,4},{6,7},{7,6},{8,9},{9,8},{10,11... | collective-permute-start | bytes 393224 | tf_op jit(solution)/shard_map/ppermute | solution.py:239
  121.0 18.6 %collective-permute-start.15 = (bf16[896,256]{1,0:T(8,128)(2,1)}, bf16[896,256]{1,0:T(8,128)(2,1)}, u32[]{:S(2)}, u32[]{:S(2)}) collective-permute-start(bf16[896,256]{1,0:T(8,128)(2,1)} %get-tuple-element.60), channel_id=1, source_target_pairs={{0,8},{8,16},{16,24},{24,0},{1,9},{9,17},{17,25},{25,1},{2,10},{10... | collective-permute-start | bytes 1376264 | tf_op jit(solution)/shard_map/ppermute | solution.py:239
  121.0 18.6 %collective-permute-start.16 = (bf16[896,256]{1,0:T(8,128)(2,1)}, bf16[896,256]{1,0:T(8,128)(2,1)}, u32[]{:S(2)}, u32[]{:S(2)}) collective-permute-start(bf16[896,256]{1,0:T(8,128)(2,1)} %get-tuple-element.59), channel_id=1, source_target_pairs={{0,24},{8,0},{16,8},{24,16},{1,25},{9,1},{17,9},{25,17},{2,26},{10... | collective-permute-start | bytes 1376264 | tf_op jit(solution)/shard_map/ppermute | solution.py:239
  125.3 8.0 %collective-permute-start.13 = (bf16[256,256]{1,0:T(8,128)(2,1)S(1)}, bf16[256,256]{1,0:T(8,128)(2,1)}, u32[]{:S(2)}, u32[]{:S(2)}) collective-permute-start(bf16[256,256]{1,0:T(8,128)(2,1)S(1)} %add_convert_fusion.2), channel_id=1, source_target_pairs={{0,2},{2,4},{4,6},{6,0},{1,3},{3,5},{5,7},{7,1},{8,10},{10,12},{12... | collective-permute-start | bytes 393224 | tf_op jit(solution)/shard_map/ppermute | solution.py:239
  125.6 8.0 %collective-permute-start.14 = (bf16[256,256]{1,0:T(8,128)(2,1)S(1)}, bf16[256,256]{1,0:T(8,128)(2,1)}, u32[]{:S(2)}, u32[]{:S(2)}) collective-permute-start(bf16[256,256]{1,0:T(8,128)(2,1)S(1)} %add_convert_fusion.2), channel_id=1, source_target_pairs={{0,6},{2,0},{4,2},{6,4},{1,7},{3,1},{5,3},{7,5},{8,14},{10,8},{12,... | collective-permute-start | bytes 393224 | tf_op jit(solution)/shard_map/ppermute | solution.py:239
  130.4 7.7 %collective-permute-start.17 = (bf16[448,256]{1,0:T(8,128)(2,1)S(1)}, bf16[448,256]{1,0:T(8,128)(2,1)S(1)}, u32[]{:S(2)}, u32[]{:S(2)}) collective-permute-start(bf16[448,256]{1,0:T(8,128)(2,1)S(1)} %get-tuple-element.58), channel_id=1, source_target_pairs={{0,8},{8,16},{16,24},{24,0},{1,9},{9,17},{17,25},{25,1},{2,10},{10... | collective-permute-start | bytes 688136 | tf_op jit(solution)/shard_map/ppermute | solution.py:239
  139.6 7.2 %collective-permute-start.19 = (bf16[256,256]{1,0:T(8,128)(2,1)S(1)}, bf16[256,256]{1,0:T(8,128)(2,1)S(1)}, u32[]{:S(2)}, u32[]{:S(2)}) collective-permute-start(bf16[256,256]{1,0:T(8,128)(2,1)S(1)} %fusion.16.m0), channel_id=1, source_target_pairs={{0,8},{8,16},{16,24},{24,0},{1,9},{9,17},{17,25},{25,1},{2,10},{10... | collective-permute-start | bytes 393224 | tf_op jit(solution)/shard_map/ppermute | solution.py:239
  153.9 30.6 %all-to-all-start.4 = ((bf16[8,32,1920]{2,1,0:T(8,128)(2,1)}), bf16[8,32,1920]{2,1,0:T(8,128)(2,1)S(1)}, u32[]{:S(2)}, u32[]{:S(2)}) async-start(bf16[8,32,1920]{2,1,0:T(8,128)(2,1)} %bitcast.13), calls=%async_computation.4 | async-start | bytes 1966080 | tf_op jit(solution)/shard_map/all_to_all | solution.py:248
  220.8 9.1 %collective-permute-start.28 = (bf16[256,256]{1,0:T(8,128)(2,1)S(1)}, bf16[256,256]{1,0:T(8,128)(2,1)S(1)}, u32[]{:S(2)}, u32[]{:S(2)}) collective-permute-start(bf16[256,256]{1,0:T(8,128)(2,1)S(1)} %add_convert_fusion.1), channel_id=1, source_target_pairs={{0,4},{2,6},{4,0},{6,2},{1,5},{3,7},{5,1},{7,3},{8,12},{10,14},{12... | collective-permute-start | bytes 393224 | tf_op jit(solution)/shard_map/ppermute | solution.py:239
  (34 other events, 276.6 us)

commit v5 on v4

--- a/solution.py
+++ b/solution.py
@@ -70,14 +70,10 @@
     image_ref[...] = jnp.where(slot1 == 0, first_image, last_image)
 
 
-def kv_there_kernel(place_ref, k_ref, v_ref, out_ref):
-    out_ref[0, :, :HEAD] = k_ref[...]
-    out_ref[0, :, HEAD:] = v_ref[...]
-
-
-def kv_here_kernel(place_ref, k_ref, v_ref, core_ref, low_ref, high_ref, ahead_ref, behind_ref, own_ref):
-    total = jnp.concatenate((k_ref[...], v_ref[...]), axis=1).astype(F32)
-    total = (total + core_ref[0].astype(F32)).astype(BF)
+def kv_kernel(place_ref, x0, x1, k0, v0, k1, v1, low_ref, high_ref, ahead_ref, behind_ref, own_ref):
+    total = dot(x0[...], jnp.concatenate((k0[...], v0[...]), axis=1))
+    total = total + dot(x1[...], jnp.concatenate((k1[...], v1[...]), axis=1))
+    total = total.astype(BF)
     half = low_ref.shape[0]
     step = pl.program_id(0)
 
@@ -99,32 +95,36 @@
         own_ref[...] = total
 
 
-def kv_split(place, k_part, v_part, from_core=None):
-    rows = k_part.shape[0]
+def kv_project(place, vision, k_weight, v_weight):
+    rows, depth = vision.shape
     chips = 4
-    other = from_core is None
 
     def head(d, place_ref):
-        core = place_ref[1]
         ahead = jnp.where(d == 0, 2, jnp.where(d == 1, 1, jnp.where(d == 2, 3, 0)))
-        return 0, lax.rem(place_ref[0] + ahead, chips) * 2 + (1 - core if other else core)
-
-    one = pl.BlockSpec((1, rows, 2 * HEAD), lambda d, p: (d, 0, 0))
+        return 0, lax.rem(place_ref[0] + ahead, chips) * 2 + place_ref[1]
+
+    states = pl.BlockSpec((rows, depth), lambda d, p: (0, 0))
+    weights = pl.BlockSpec((depth, HEAD), head)
     sizes = [rows // 2, rows // 2, rows, rows, rows]
-    whole = [pl.BlockSpec((n, 2 * HEAD), lambda d, p: (0, 0)) for n in sizes]
     return pl.pallas_call(
-        kv_there_kernel if other else kv_here_kernel,
+        kv_kernel,
         grid_spec=pltpu.PrefetchScalarGridSpec(
             num_scalar_prefetch=1,
             grid=(chips,),
-            in_specs=[pl.BlockSpec((rows, HEAD), head)] * 2 + ([] if other else [one]),
-            out_specs=one if other else whole,
+            in_specs=[states] * 2 + [weights] * 4,
+            out_specs=[pl.BlockSpec((n, 2 * HEAD), lambda d, p: (0, 0)) for n in sizes],
         ),
-        out_shape=jax.ShapeDtypeStruct((chips, rows, 2 * HEAD), BF)
-        if other
-        else [jax.ShapeDtypeStruct((n, 2 * HEAD), BF) for n in sizes],
+        out_shape=[jax.ShapeDtypeStruct((n, 2 * HEAD), BF) for n in sizes],
         compiler_params=params(LARGE_VMEM_BYTES),
-    )(place, k_part, v_part, *(() if other else (from_core,)))
+    )(
+        place,
+        vision,
+        shift(vision, "c", 1),
+        k_weight,
+        v_weight,
+        shift(k_weight, "c", 1),
+        shift(v_weight, "c", 1),
+    )
 
 
 def kv_merge_kernel(ahead_ref, behind_ref, low_ref, high_ref, forward_ref, backward_ref):
@@ -203,24 +203,38 @@
 
 
 def gate_up_kernel(m0, m1, m2, m3, w0, w1, gate2, up2, w3, out_ref):
-    blocks = (m0, m1, m2, m3)
     units = gate2.shape[1]
-    columns = 2 * units
-    for start in range(0, columns, HEAD):
-        span = slice(start, start + HEAD)
-        part = slice(start % units, start % units + HEAD)
-        w2 = gate2 if start < units else up2
-        total = dot(m0[...], w0[:, span]) + dot(m1[...], w1[:, span])
-        total = total + dot(m2[...], w2[:, part]) + dot(m3[...], w3[:, span])
-        out_ref[:, span] = total.astype(BF)
-    square = jnp.zeros((m0.shape[0], 1), F32)
-    for m in blocks:
-        value = m[...].astype(F32)
-        square = square + jnp.sum(value * value, axis=1, keepdims=True)
-    high = square.astype(BF).astype(F32)
-    lane = lax.broadcasted_iota(jnp.int32, (m0.shape[0], HEAD), 1)
-    extra = jnp.where(lane == 0, high, jnp.where(lane == 1, square - high, 0.0))
-    out_ref[:, columns:] = extra.astype(BF)
+    step = pl.program_id(0)
+
+    def product(w2):
+        total = dot(m0[...], w0[...]) + dot(m1[...], w1[...])
+        return (total + dot(m2[...], w2[...]) + dot(m3[...], w3[...])).astype(BF)
+
+    @pl.when(step == 0)
+    def _():
+        out_ref[:, :units] = product(gate2)
+
+    @pl.when(step == 1)
+    def _():
+        out_ref[:, units : 2 * units] = product(up2)
+        square = jnp.zeros((m0.shape[0], 1), F32)
+        for m in (m0, m1, m2, m3):
+            value = m[...].astype(F32)
+            square = square + jnp.sum(value * value, axis=1, keepdims=True)
+        high = square.astype(BF).astype(F32)
+        lane = lax.broadcasted_iota(jnp.int32, (m0.shape[0], HEAD), 1)
+        extra = jnp.where(lane == 0, high, jnp.where(lane == 1, square - high, 0.0))
+        out_ref[:, 2 * units :] = extra.astype(BF)
+
+
+def down_kernel(a_ref, d0, d1, low2, high2, d3, own_ref, behind_ref, across_ref, ahead_ref):
+    active = a_ref[...]
+    half = low2.shape[0]
+    total = dot(active[:, :half], low2[...]) + dot(active[:, half:], high2[...])
+    across_ref[...] = total.astype(BF)
+    behind_ref[...] = dot(active, d1[...]).astype(BF)
+    ahead_ref[...] = dot(active, d3[...]).astype(BF)
+    own_ref[...] = dot(active, d0[...])
 
 
 def active_kernel(full_width, parts_ref, out_ref):
@@ -300,13 +314,9 @@
     hidden_f = hidden.astype(F32)
     normed = (hidden_f * attn_gain).astype(BF)
     q_part = dot(normed, q_weight).astype(BF)
-    q_part, vision = lax.optimization_barrier((q_part, vision))
     q_parts = exchange(q_part, GROUP)
 
-    k_part = dot(vision, k_weight).astype(BF)
-    v_part = dot(vision, v_weight).astype(BF)
-    there = kv_split(place, k_part, v_part)
-    low, high, ahead, behind, own = kv_split(place, k_part, v_part, shift(there, "c", 1))
+    low, high, ahead, behind, own = kv_project(place, vision, k_weight, v_weight)
     q_parts = after(q_parts, own)
     forward, backward = pl.pallas_call(
         kv_merge_kernel,
@@ -363,12 +373,12 @@
         at = lax.rem(lax.axis_index("y") + d, chips_y) * units + start
         return lax.dynamic_slice_in_dim(down_weight, at, size, 0)
 
-    down_0 = rows(0, 0, units)
-    down_1 = shift(rows(1, 0, units), "y", 1)
-    down_3 = shift(rows(3, 0, units), "y", -1)
-    down_2 = (shift(rows(2, 0, half), "y", 1), shift(rows(2, half, half), "y", -1))
+    down_0, down_1, down_3 = rows(0, 0, units), rows(1, 0, units), rows(3, 0, units)
+    down_2 = rows(2, 0, half), rows(2, half, half)
     mixed = lax.all_to_all(mixed, GROUP, 0, 0, tiled=True)
-    mixed = after(mixed, wide_1, wide_3)
+    mixed = after(mixed, wide_1, wide_3, down_1, down_3, *down_2)
+    down_1, down_3 = shift(down_1, "y", 1), shift(down_3, "y", -1)
+    down_2 = shift(down_2[0], "y", 1), shift(down_2[1], "y", -1)
 
     attended = pl.pallas_call(
         combine_kernel,
@@ -379,19 +389,23 @@
     )(mixed, sel)
     attended = lax.all_to_all(attended, GROUP, 0, 0, tiled=True).reshape(all_rows, local_heads)
 
-    attended = after(attended, gate_2, up_2)
+    attended = after(attended, gate_2, up_2, *down_2)
     attn_sum = tensor_sum(dot(attended, o_weight))
     middle = (hidden_f + jnp.tanh(gate_logits[0]) * attn_sum).astype(BF)
     middle_f = middle.astype(F32)
-    middle = after(middle, down_1, down_3, *down_2)
+    middle = after(middle, down_1, down_3)
     down_2 = (shift(down_2[0], "y", 1), shift(down_2[1], "y", -1))
     middles = [middle] + [shift(middle, "y", d) for d in (1, 2, 3)]
+    block = pl.BlockSpec((all_rows, width_part), lambda i: (0, 0))
+    direct = pl.BlockSpec((width_part, units), lambda i: (0, i))
+    passed = pl.BlockSpec((width_part, units), lambda i: (0, 0))
     gate_up = pl.pallas_call(
         gate_up_kernel,
-        in_specs=[vmem()] * 9,
-        out_specs=vmem(),
+        grid=(2,),
+        in_specs=[block] * 4 + [direct] * 2 + [passed] * 2 + [direct],
+        out_specs=pl.BlockSpec((all_rows, 2 * units + HEAD), lambda i: (0, 0)),
         out_shape=jax.ShapeDtypeStruct((all_rows, 2 * units + HEAD), BF),
-        compiler_params=params(),
+        compiler_params=params(LARGE_VMEM_BYTES),
     )(*middles, wide_0, wide_1, gate_2, up_2, wide_3)
     parts = after(exchange(gate_up, "z"), *down_2)
     active = pl.pallas_call(
@@ -402,11 +416,16 @@
         compiler_params=params(),
     )(parts)
     active = lax.all_to_all(active, "z", 0, 0, tiled=True).reshape(all_rows, units)
-    across = dot(active[:, :half], down_2[0]) + dot(active[:, half:], down_2[1])
-    across = shift(across.astype(BF), "y", 2)
-    behind = shift(dot(active, down_1).astype(BF), "y", -1)
-    ahead = shift(dot(active, down_3).astype(BF), "y", 1)
-    down_part = dot(active, down_0) + across.astype(F32) + behind.astype(F32) + ahead.astype(F32)
+    own_down, behind, across, ahead = pl.pallas_call(
+        down_kernel,
+        in_specs=[vmem()] * 6,
+        out_specs=[vmem()] * 4,
+        out_shape=[jax.ShapeDtypeStruct((all_rows, width_part), F32)]
+        + [jax.ShapeDtypeStruct((all_rows, width_part), BF)] * 3,
+        compiler_params=params(LARGE_VMEM_BYTES),
+    )(active, down_0, down_1, *down_2, down_3)
+    across, behind, ahead = shift(across, "y", 2), shift(behind, "y", -1), shift(ahead, "y", 1)
+    down_part = own_down + across.astype(F32) + behind.astype(F32) + ahead.astype(F32)
     down_sum = tensor_sum(down_part)
     row_request = jnp.arange(all_rows, dtype=jnp.int32) // STEPS
     request_ids = (image_groups * (own_rows // STEPS) + image_requests).reshape(-1)

time: 234 us -> 219 us (0.936)
  matrix products: 15.8 us -> 2.33 us
  waiting for transfers between devices: 82 us -> 74.6 us
  starting transfers between devices: 79.2 us -> 84.8 us
    dot_general x9 -> x2, matrix products: 15.8 us -> 2.33 us  [dot(): return jnp.dot(a, b, preferred_element_type=F32)]
    all_to_all x2, waiting for transfers between devices: 27.6 us -> 21.3 us  [exchange(): out = lax.all_to_all(value, axis, 0, 0, tiled=True)]
    unnamed x47 -> x63, local copies, waits for them, and re-layouts: 5.63 us -> 3.1 us
    ppermute x31 -> x33, starting transfers between devices: 50.5 us -> 52.4 us  [shift(): return lax.ppermute(value, axis, [(i, (i + by) % n) for i in range(n)])]
    ppermute x31 -> x33, waiting for transfers between devices: 49.3 us -> 48.5 us  [shift(): return lax.ppermute(value, axis, [(i, (i + by) % n) for i in range(n)])]
  transfers between devices with their start and end apart: 36 -> 38, of which waited for: 17 -> 17; matrix products, arithmetic and copies ran while one was open for 6% -> 7% of each run, Pallas kernels for 5% -> 6%
where the time goes in v5:
time: 219 us; the launch traced here: 218 us
  starting transfers between devices  84.8 us (39%)
  waiting for transfers between devices  74.6 us (34%)
  Pallas kernels  21.5 us (10%)
  blocking collectives  15.9 us (7%)
  local copies, waits for them, and re-layouts  10.4 us (5%)
  other arithmetic  7.05 us (3%)
  matrix products  2.33 us (1%)
    ppermute x33, starting transfers between devices, shift(): return lax.ppermute(value, axis, [(i, (i + by) % n) for i in range(n)])  52.4 us
    ppermute x33, waiting for transfers between devices, shift(): return lax.ppermute(value, axis, [(i, (i + by) % n) for i in range(n)])  48.5 us
    all_to_all x2, waiting for transfers between devices, exchange(): out = lax.all_to_all(value, axis, 0, 0, tiled=True)  21.3 us
    all_to_all x2, starting transfers between devices, exchange(): out = lax.all_to_all(value, axis, 0, 0, tiled=True)  16.2 us
    all_to_all x1, blocking collectives, shards(): lax.all_to_all(active, 'z', 0, 0, tiled=True).reshape(all_rows, units)  15.9 us
    pallas_call x1, Pallas kernels, kv_project(): pl.pallas_call(kv_kernel, grid_spec=pltpu.PrefetchScalarGridSpec(num_scal...  7.95 us
    all_to_all x1, starting transfers between devices, shards(): lax.all_to_all(attended, GROUP, 0, 0, tiled=True)  6.14 us
    all_to_all x1, starting transfers between devices, shards(): mixed = lax.all_to_all(mixed, GROUP, 0, 0, tiled=True)  5.08 us
  transfers between devices with their start and end apart: 38, of which 17 were waited for; matrix products, arithmetic and copies ran while one was open for 7% of the time, Pallas kernels for 6%

profile of v5, /device:TPU:1, one launch (start us, length us, event | category | flops | bytes accessed | tf_op | source)
XLA Modules:
  0.0 218.1 jit_solution(4859150974644618067)
XLA Ops:
  0.0 3.2 %collective-permute-start.1 = (bf16[1024,1024]{1,0:T(8,128)(2,1)}, bf16[1024,1024]{1,0:T(8,128)(2,1)S(1)}, u32[]{:S(2)}, u32[]{:S(2)}) collective-permute-start(bf16[1024,1024]{1,0:T(8,128)(2,1)} %k0.1), channel_id=1, source_target_pairs={{0,1},{1,0},{2,3},{3,2},{4,5},{5,4},{6,7},{7,6},{8,9},{9,8},{10,11... | collective-permute-start | bytes 6291464 | tf_op jit(solution)/shard_map/ppermute | solution.py:253
  5.8 9.6 %all-to-all-start = ((bf16[32,8,1024]{2,1,0:T(8,128)(2,1)}), bf16[32,8,1024]{2,1,0:T(8,128)(2,1)S(1)}, u32[]{:S(2)}, u32[]{:S(2)}) async-start(bf16[32,8,1024]{2,1,0:T(8,128)(2,1)} %fusion), calls=%async_computation | async-start | bytes 1048576 | tf_op jit(solution)/shard_map/all_to_all | solution.py:262
  18.2 7.9 %shard_map.163 = (bf16[320,256]{1,0:T(8,128)(2,1)}, bf16[320,256]{1,0:T(8,128)(2,1)}, bf16[640,256]{1,0:T(8,128)(2,1)}, bf16[640,256]{1,0:T(8,128)(2,1)}, bf16[640,256]{1,0:T(8,128)(2,1)}) custom-call(s32[2]{0:T(128)} %pad_add_fusion.place_ref, bf16[640,1024]{1,0:T(8,128)(2,1)} %x0.1, bf16[640,1024]{1,0:T(8,128)(2,1)} %collective-permute-done.x1, ...), custom_call_target="tpu_custom_call" | custom-call | tf_op jit(solution)/shard_map/pallas_call | solution.py:109
  28.9 3.0 %all-to-all-done.parts_ref = bf16[32,8,1024]{2,1,0:T(8,128)(2,1)S(1)} async-done(((bf16[32,8,1024]{2,1,0:T(8,128)(2,1)}), bf16[32,8,1024]{2,1,0:T(8,128)(2,1)S(1)}, u32[]{:S(2)}, u32[]{:S(2)}) %all-to-all-start) | async-done | bytes 524320 | tf_op jit(solution)/shard_map/all_to_all | solution.py:262
  40.9 5.0 %all-to-all-start.1 = ((bf16[32,8,512]{2,1,0:T(8,128)(2,1)}), bf16[32,8,512]{2,1,0:T(8,128)(2,1)S(1)}, u32[]{:S(2)}, u32[]{:S(2)}) async-start(bf16[32,8,512]{2,1,0:T(8,128)(2,1)} %bitcast.7), calls=%async_computation.1 | async-start | bytes 524288 | tf_op jit(solution)/shard_map/all_to_all | solution.py:359
  52.3 4.1 %all-to-all-done.1 = bf16[32,8,512]{2,1,0:T(8,128)(2,1)S(1)} async-done(((bf16[32,8,512]{2,1,0:T(8,128)(2,1)}), bf16[32,8,512]{2,1,0:T(8,128)(2,1)S(1)}, u32[]{:S(2)}, u32[]{:S(2)}) %all-to-all-start.1) | async-done | bytes 262176 | tf_op jit(solution)/shard_map/all_to_all | solution.py:359
  56.4 3.0 %shard_map.167 = bf16[256,640]{1,0:T(8,128)(2,1)} custom-call(s32[1]{0:T(128)} %bitcast.1.me_ref, s32[32,4]{1,0:T(8,128)S(1)} %copy.27.tiles_ref, bf16[640,256]{1,0:T(8,128)(2,1)S(1)} %copy-done.1, bf16[640,256]{1,0:T(8,128)(2,1)S(1)} %collective-permute-done.5.left_ref, bf16[640,256]{1,0:T(8,128)(2,1)S(1)} %collective-permute-done.6.right_ref, ...), custom_call_target="tpu_custom_call" | custom-call | tf_op jit(solution)/shard_map/pallas_call | solution.py:363
  59.4 5.1 %all-to-all-start.2 = ((bf16[32,8,640]{2,1,0:T(8,128)(2,1)}), bf16[32,8,640]{2,1,0:T(8,128)(2,1)S(1)}, u32[]{:S(2)}, u32[]{:S(2)}) async-start(bf16[32,8,640]{2,1,0:T(8,128)(2,1)} %bitcast.9), calls=%async_computation.2 | async-start | bytes 655360 | tf_op jit(solution)/shard_map/all_to_all | solution.py:378
  68.9 3.8 %collective-permute-done.10.w3 = bf16[256,1792]{1,0:T(8,128)(2,1)} collective-permute-done((bf16[256,1792]{1,0:T(8,128)(2,1)}, bf16[256,1792]{1,0:T(8,128)(2,1)}, u32[]{:S(2)}, u32[]{:S(2)}) %collective-permute-start.10) | collective-permute-done | bytes 917536 | tf_op jit(solution)/shard_map/ppermute | solution.py:253
  77.3 6.1 %all-to-all-start.3 = ((bf16[32,8,1024]{2,1,0:T(8,128)(2,1)}), bf16[32,8,1024]{2,1,0:T(8,128)(2,1)S(1)}, u32[]{:S(2)}, u32[]{:S(2)}) async-start(bf16[32,8,1024]{2,1,0:T(8,128)(2,1)} %shard_map.168), calls=%async_computation.3 | async-start | bytes 1048576 | tf_op jit(solution)/shard_map/all_to_all | solution.py:390
  88.9 15.3 %collective-permute-done.13 = bf16[448,256]{1,0:T(8,128)(2,1)S(1)} collective-permute-done((bf16[448,256]{1,0:T(8,128)(2,1)}, bf16[448,256]{1,0:T(8,128)(2,1)S(1)}, u32[]{:S(2)}, u32[]{:S(2)}) %collective-permute-start.13) | collective-permute-done | bytes 229408 | tf_op jit(solution)/shard_map/ppermute | solution.py:253
  105.3 4.1 %collective-permute-start.15 = (bf16[256,256]{1,0:T(8,128)(2,1)S(1)}, bf16[256,256]{1,0:T(8,128)(2,1)S(1)}, u32[]{:S(2)}, u32[]{:S(2)}) collective-permute-start(bf16[256,256]{1,0:T(8,128)(2,1)S(1)} %convolution_convert_fusion.1), channel_id=1, source_target_pairs={{0,1},{1,0},{2,3},{3,2},{4,5},{5,4},{6,7},{7,6},{8,9},{9,8},{10,11... | collective-permute-start | bytes 393224 | tf_op jit(solution)/shard_map/ppermute | solution.py:253
  118.2 3.8 %collective-permute-done.17 = bf16[256,256]{1,0:T(8,128)(2,1)S(1)} collective-permute-done((bf16[256,256]{1,0:T(8,128)(2,1)S(1)}, bf16[256,256]{1,0:T(8,128)(2,1)S(1)}, u32[]{:S(2)}, u32[]{:S(2)}) %collective-permute-start.17) | collective-permute-done | bytes 131104 | tf_op jit(solution)/shard_map/ppermute | solution.py:253
  123.0 3.2 %collective-permute-start.22 = (bf16[256,256]{1,0:T(8,128)(2,1)S(1)}, bf16[256,256]{1,0:T(8,128)(2,1)S(1)}, u32[]{:S(2)}, u32[]{:S(2)}) collective-permute-start(bf16[256,256]{1,0:T(8,128)(2,1)S(1)} %fusion.2.m0), channel_id=1, source_target_pairs={{0,16},{8,24},{16,0},{24,8},{1,17},{9,25},{17,1},{25,9},{2,18},{10... | collective-permute-start | bytes 393224 | tf_op jit(solution)/shard_map/ppermute | solution.py:253
  132.0 4.3 %shard_map.169 = bf16[256,1920]{1,0:T(8,128)(2,1)} custom-call(bf16[256,256]{1,0:T(8,128)(2,1)} %copy-done.7, bf16[256,256]{1,0:T(8,128)(2,1)} %copy-done.18, bf16[256,256]{1,0:T(8,128)(2,1)} %copy-done.19, bf16[256,256]{1,0:T(8,128)(2,1)} %copy-done.20, bf16[256,1792]{1,0:T(8,128)(2,1)} %get-tuple-element.66.w0, ...), custom_call_target="tpu_custom_call" | custom-call | tf_op jit(solution)/shard_map/pallas_call | solution.py:402
  136.3 6.6 %all-to-all-start.4 = ((bf16[8,32,1920]{2,1,0:T(8,128)(2,1)}), bf16[8,32,1920]{2,1,0:T(8,128)(2,1)S(1)}, u32[]{:S(2)}, u32[]{:S(2)}) async-start(bf16[8,32,1920]{2,1,0:T(8,128)(2,1)} %bitcast.23), calls=%async_computation.4 | async-start | bytes 1966080 | tf_op jit(solution)/shard_map/all_to_all | solution.py:262
  143.6 3.0 %collective-permute-start.25 = (bf16[448,256]{1,0:T(8,128)(2,1)S(1)}, bf16[448,256]{1,0:T(8,128)(2,1)S(1)}, u32[]{:S(2)}, u32[]{:S(2)}) collective-permute-start(bf16[448,256]{1,0:T(8,128)(2,1)S(1)} %copy-done.29), channel_id=1, source_target_pairs={{0,24},{8,0},{16,8},{24,16},{1,25},{9,1},{17,9},{25,17},{2,26},{10... | collective-permute-start | bytes 688136 | tf_op jit(solution)/shard_map/ppermute | solution.py:253
  146.7 3.9 %collective-permute-done.24.low2 = bf16[448,256]{1,0:T(8,128)(2,1)S(1)} collective-permute-done((bf16[448,256]{1,0:T(8,128)(2,1)S(1)}, bf16[448,256]{1,0:T(8,128)(2,1)S(1)}, u32[]{:S(2)}, u32[]{:S(2)}) %collective-permute-start.24) | collective-permute-done | bytes 229408 | tf_op jit(solution)/shard_map/ppermute | solution.py:253
  150.6 18.2 %all-to-all-done.4.parts_ref = bf16[8,32,1920]{2,1,0:T(8,128)(2,1)S(1)} async-done(((bf16[8,32,1920]{2,1,0:T(8,128)(2,1)}), bf16[8,32,1920]{2,1,0:T(8,128)(2,1)S(1)}, u32[]{:S(2)}, u32[]{:S(2)}) %all-to-all-start.4) | async-done | bytes 983072 | tf_op jit(solution)/shard_map/all_to_all | solution.py:262
  169.1 15.9 %all_to_all.52 = bf16[8,32,896]{2,1,0:T(8,128)(2,1)} all-to-all(bf16[8,32,896]{2,1,0:T(8,128)(2,1)S(1)} %shard_map.170), channel_id=1, replica_groups=mesh['z'=8,'y'=4,'x'=4,'c'=2] {'z'}, dimensions={0} | all-to-all | bytes 917504 | tf_op jit(solution)/shard_map/all_to_all | solution.py:418
  185.0 3.1 %shard_map.171 = (f32[256,256]{1,0:T(8,128)}, bf16[256,256]{1,0:T(8,128)(2,1)}, bf16[256,256]{1,0:T(8,128)(2,1)}, bf16[256,256]{1,0:T(8,128)(2,1)}) custom-call(bf16[256,896]{1,0:T(8,128)(2,1)} %bitcast.25, bf16[896,256]{1,0:T(8,128)(2,1)} %get-tuple-element.55.d0, bf16[896,256]{1,0:T(8,128)(2,1)} %copy-done.14, bf16[448,256]{1,0:T(8,128)(2,1)} %copy-done.16, ...), custom_call_target="tpu_custom_call" | custom-call | tf_op jit(solution)/shard_map/pallas_call | solution.py:419
  188.1 9.1 %collective-permute-start.27 = (bf16[256,256]{1,0:T(8,128)(2,1)}, bf16[256,256]{1,0:T(8,128)(2,1)S(1)}, u32[]{:S(2)}, u32[]{:S(2)}) collective-permute-start(bf16[256,256]{1,0:T(8,128)(2,1)} %get-tuple-element.53), channel_id=1, source_target_pairs={{0,24},{8,0},{16,8},{24,16},{1,25},{9,1},{17,9},{25,17},{2,26},{10... | collective-permute-start | bytes 393224 | tf_op jit(solution)/shard_map/ppermute | solution.py:253
  197.7 6.1 %collective-permute-done.27 = bf16[256,256]{1,0:T(8,128)(2,1)S(1)} collective-permute-done((bf16[256,256]{1,0:T(8,128)(2,1)}, bf16[256,256]{1,0:T(8,128)(2,1)S(1)}, u32[]{:S(2)}, u32[]{:S(2)}) %collective-permute-start.27) | collective-permute-done | bytes 131104 | tf_op jit(solution)/shard_map/ppermute | solution.py:253
  214.0 3.4 %collective-permute-done.31 = bf16[256,256]{1,0:T(8,128)(2,1)S(1)} collective-permute-done((bf16[256,256]{1,0:T(8,128)(2,1)S(1)}, bf16[256,256]{1,0:T(8,128)(2,1)S(1)}, u32[]{:S(2)}, u32[]{:S(2)}) %collective-permute-start.31) | collective-permute-done | bytes 131104 | tf_op jit(solution)/shard_map/ppermute | solution.py:253
  (147 shorter events, 65.4 us)
Async XLA Ops:
  0.0 16.8 %collective-permute-start.1 = (bf16[1024,1024]{1,0:T(8,128)(2,1)}, bf16[1024,1024]{1,0:T(8,128)(2,1)S(1)}, u32[]{:S(2)}, u32[]{:S(2)}) collective-permute-start(bf16[1024,1024]{1,0:T(8,128)(2,1)} %k0.1), channel_id=1, source_target_pairs={{0,1},{1,0},{2,3},{3,2},{4,5},{5,4},{6,7},{7,6},{8,9},{9,8},{10,11... | collective-permute-start | bytes 6291464 | tf_op jit(solution)/shard_map/ppermute | solution.py:253
  3.2 13.6 %collective-permute-start.2 = (bf16[1024,1024]{1,0:T(8,128)(2,1)}, bf16[1024,1024]{1,0:T(8,128)(2,1)}, u32[]{:S(2)}, u32[]{:S(2)}) collective-permute-start(bf16[1024,1024]{1,0:T(8,128)(2,1)} %v0.1), channel_id=1, source_target_pairs={{0,1},{1,0},{2,3},{3,2},{4,5},{5,4},{6,7},{7,6},{8,9},{9,8},{10,11... | collective-permute-start | bytes 6291464 | tf_op jit(solution)/shard_map/ppermute | solution.py:253
  3.3 13.5 %collective-permute-start = (bf16[640,1024]{1,0:T(8,128)(2,1)}, bf16[640,1024]{1,0:T(8,128)(2,1)}, u32[]{:S(2)}, u32[]{:S(2)}) collective-permute-start(bf16[640,1024]{1,0:T(8,128)(2,1)} %x0.1), channel_id=1, source_target_pairs={{0,1},{1,0},{2,3},{3,2},{4,5},{5,4},{6,7},{7,6},{8,9},{9,8},{10,11... | collective-permute-start | bytes 3932168 | tf_op jit(solution)/shard_map/ppermute | solution.py:253
  5.8 26.1 %all-to-all-start = ((bf16[32,8,1024]{2,1,0:T(8,128)(2,1)}), bf16[32,8,1024]{2,1,0:T(8,128)(2,1)S(1)}, u32[]{:S(2)}, u32[]{:S(2)}) async-start(bf16[32,8,1024]{2,1,0:T(8,128)(2,1)} %fusion), calls=%async_computation | async-start | bytes 1048576 | tf_op jit(solution)/shard_map/all_to_all | solution.py:262
  26.1 11.9 %collective-permute-start.3 = (bf16[320,256]{1,0:T(8,128)(2,1)}, bf16[320,256]{1,0:T(8,128)(2,1)S(1)}, u32[]{:S(2)}, u32[]{:S(2)}) collective-permute-start(bf16[320,256]{1,0:T(8,128)(2,1)} %get-tuple-element.33), channel_id=1, source_target_pairs={{0,2},{2,4},{4,6},{6,0},{1,3},{3,5},{5,7},{7,1},{8,10},{10,12},{12... | collective-permute-start | bytes 491528 | tf_op jit(solution)/shard_map/ppermute | solution.py:253
  27.4 10.6 %collective-permute-start.4 = (bf16[320,256]{1,0:T(8,128)(2,1)}, bf16[320,256]{1,0:T(8,128)(2,1)S(1)}, u32[]{:S(2)}, u32[]{:S(2)}) collective-permute-start(bf16[320,256]{1,0:T(8,128)(2,1)} %get-tuple-element.34), channel_id=1, source_target_pairs={{0,6},{2,0},{4,2},{6,4},{1,7},{3,1},{5,3},{7,5},{8,14},{10,8},{12,... | collective-permute-start | bytes 491528 | tf_op jit(solution)/shard_map/ppermute | solution.py:253
  34.2 18.0 %collective-permute-start.7 = (bf16[256,896]{1,0:T(8,128)(2,1)}, bf16[256,896]{1,0:T(8,128)(2,1)}, u32[]{:S(2)}, u32[]{:S(2)}) collective-permute-start(bf16[256,896]{1,0:T(8,128)(2,1)} %get-tuple-element.70), channel_id=1, source_target_pairs={{0,8},{8,16},{16,24},{24,0},{1,9},{9,17},{17,25},{25,1},{2,10},{10... | collective-permute-start | bytes 1376264 | tf_op jit(solution)/shard_map/ppermute | solution.py:253
  35.0 17.3 %collective-permute-start.8 = (bf16[256,896]{1,0:T(8,128)(2,1)}, bf16[256,896]{1,0:T(8,128)(2,1)}, u32[]{:S(2)}, u32[]{:S(2)}) collective-permute-start(bf16[256,896]{1,0:T(8,128)(2,1)} %get-tuple-element.69), channel_id=1, source_target_pairs={{0,24},{8,0},{16,8},{24,16},{1,25},{9,1},{17,9},{25,17},{2,26},{10... | collective-permute-start | bytes 1376264 | tf_op jit(solution)/shard_map/ppermute | solution.py:253
  38.1 18.3 %collective-permute-start.5 = (bf16[640,256]{1,0:T(8,128)(2,1)S(1)}, bf16[640,256]{1,0:T(8,128)(2,1)S(1)}, u32[]{:S(2)}, u32[]{:S(2)}) collective-permute-start(bf16[640,256]{1,0:T(8,128)(2,1)S(1)} %get-tuple-element.35), channel_id=1, source_target_pairs={{0,2},{2,4},{4,6},{6,0},{1,3},{3,5},{5,7},{7,1},{8,10},{10,12},{12... | collective-permute-start | bytes 983048 | tf_op jit(solution)/shard_map/ppermute | solution.py:253
  39.4 17.0 %collective-permute-start.6 = (bf16[640,256]{1,0:T(8,128)(2,1)S(1)}, bf16[640,256]{1,0:T(8,128)(2,1)S(1)}, u32[]{:S(2)}, u32[]{:S(2)}) collective-permute-start(bf16[640,256]{1,0:T(8,128)(2,1)S(1)} %get-tuple-element.36), channel_id=1, source_target_pairs={{0,6},{2,0},{4,2},{6,4},{1,7},{3,1},{5,3},{7,5},{8,14},{10,8},{12,... | collective-permute-start | bytes 983048 | tf_op jit(solution)/shard_map/ppermute | solution.py:253
  40.9 15.5 %all-to-all-start.1 = ((bf16[32,8,512]{2,1,0:T(8,128)(2,1)}), bf16[32,8,512]{2,1,0:T(8,128)(2,1)S(1)}, u32[]{:S(2)}, u32[]{:S(2)}) async-start(bf16[32,8,512]{2,1,0:T(8,128)(2,1)} %bitcast.7), calls=%async_computation.1 | async-start | bytes 524288 | tf_op jit(solution)/shard_map/all_to_all | solution.py:359
  49.8 22.9 %collective-permute-start.10 = (bf16[256,1792]{1,0:T(8,128)(2,1)}, bf16[256,1792]{1,0:T(8,128)(2,1)}, u32[]{:S(2)}, u32[]{:S(2)}) collective-permute-start(bf16[256,1792]{1,0:T(8,128)(2,1)} %get-tuple-element.67), channel_id=1, source_target_pairs={{0,24},{8,0},{16,8},{24,16},{1,25},{9,1},{17,9},{25,17},{2,26},{10... | collective-permute-start | bytes 2752520 | tf_op jit(solution)/shard_map/ppermute | solution.py:253
  52.2 23.2 %collective-permute-start.9 = (bf16[256,1792]{1,0:T(8,128)(2,1)}, bf16[256,1792]{1,0:T(8,128)(2,1)}, u32[]{:S(2)}, u32[]{:S(2)}) collective-permute-start(bf16[256,1792]{1,0:T(8,128)(2,1)} %get-tuple-element.68), channel_id=1, source_target_pairs={{0,8},{8,16},{16,24},{24,0},{1,9},{9,17},{17,25},{25,1},{2,10},{10... | collective-permute-start | bytes 2752520 | tf_op jit(solution)/shard_map/ppermute | solution.py:253
  59.4 16.6 %all-to-all-start.2 = ((bf16[32,8,640]{2,1,0:T(8,128)(2,1)}), bf16[32,8,640]{2,1,0:T(8,128)(2,1)S(1)}, u32[]{:S(2)}, u32[]{:S(2)}) async-start(bf16[32,8,640]{2,1,0:T(8,128)(2,1)} %bitcast.9), calls=%async_computation.2 | async-start | bytes 655360 | tf_op jit(solution)/shard_map/all_to_all | solution.py:378
  77.3 27.7 %all-to-all-start.3 = ((bf16[32,8,1024]{2,1,0:T(8,128)(2,1)}), bf16[32,8,1024]{2,1,0:T(8,128)(2,1)S(1)}, u32[]{:S(2)}, u32[]{:S(2)}) async-start(bf16[32,8,1024]{2,1,0:T(8,128)(2,1)} %shard_map.168), calls=%async_computation.3 | async-start | bytes 1048576 | tf_op jit(solution)/shard_map/all_to_all | solution.py:390
  83.5 20.8 %collective-permute-start.11 = (bf16[256,896]{1,0:T(8,128)(2,1)}, bf16[256,896]{1,0:T(8,128)(2,1)S(1)}, u32[]{:S(2)}, u32[]{:S(2)}) collective-permute-start(bf16[256,896]{1,0:T(8,128)(2,1)} %collective-permute-done.7), channel_id=1, source_target_pairs={{0,8},{8,16},{16,24},{24,0},{1,9},{9,17},{17,25},{25,1},{2,10},{10... | collective-permute-start | bytes 1376264 | tf_op jit(solution)/shard_map/ppermute | solution.py:253
  84.8 20.2 %collective-permute-start.12 = (bf16[256,896]{1,0:T(8,128)(2,1)}, bf16[256,896]{1,0:T(8,128)(2,1)S(1)}, u32[]{:S(2)}, u32[]{:S(2)}) collective-permute-start(bf16[256,896]{1,0:T(8,128)(2,1)} %collective-permute-done.8), channel_id=1, source_target_pairs={{0,24},{8,0},{16,8},{24,16},{1,25},{9,1},{17,9},{25,17},{2,26},{10... | collective-permute-start | bytes 1376264 | tf_op jit(solution)/shard_map/ppermute | solution.py:253
  86.2 18.0 %collective-permute-start.13 = (bf16[448,256]{1,0:T(8,128)(2,1)}, bf16[448,256]{1,0:T(8,128)(2,1)S(1)}, u32[]{:S(2)}, u32[]{:S(2)}) collective-permute-start(bf16[448,256]{1,0:T(8,128)(2,1)} %get-tuple-element.65), channel_id=1, source_target_pairs={{0,8},{8,16},{16,24},{24,0},{1,9},{9,17},{17,25},{25,1},{2,10},{10... | collective-permute-start | bytes 688136 | tf_op jit(solution)/shard_map/ppermute | solution.py:253
  86.2 18.0 %collective-permute-start.14 = (bf16[448,256]{1,0:T(8,128)(2,1)}, bf16[448,256]{1,0:T(8,128)(2,1)S(1)}, u32[]{:S(2)}, u32[]{:S(2)}) collective-permute-start(bf16[448,256]{1,0:T(8,128)(2,1)} %get-tuple-element.64), channel_id=1, source_target_pairs={{0,24},{8,0},{16,8},{24,16},{1,25},{9,1},{17,9},{25,17},{2,26},{10... | collective-permute-start | bytes 688136 | tf_op jit(solution)/shard_map/ppermute | solution.py:253
  109.4 13.5 %collective-permute-start.19 = (bf16[896,256]{1,0:T(8,128)(2,1)}, bf16[896,256]{1,0:T(8,128)(2,1)S(1)}, u32[]{:S(2)}, u32[]{:S(2)}) collective-permute-start(bf16[896,256]{1,0:T(8,128)(2,1)} %get-tuple-element.57), channel_id=1, source_target_pairs={{0,8},{8,16},{16,24},{24,0},{1,9},{9,17},{17,25},{25,1},{2,10},{10... | collective-permute-start | bytes 1376264 | tf_op jit(solution)/shard_map/ppermute | solution.py:253
  110.4 12.6 %collective-permute-start.20 = (bf16[896,256]{1,0:T(8,128)(2,1)S(1)}, bf16[896,256]{1,0:T(8,128)(2,1)S(1)}, u32[]{:S(2)}, u32[]{:S(2)}) collective-permute-start(bf16[896,256]{1,0:T(8,128)(2,1)S(1)} %copy-done.13), channel_id=1, source_target_pairs={{0,24},{8,0},{16,8},{24,16},{1,25},{9,1},{17,9},{25,17},{2,26},{10... | collective-permute-start | bytes 1376264 | tf_op jit(solution)/shard_map/ppermute | solution.py:253
  136.3 32.5 %all-to-all-start.4 = ((bf16[8,32,1920]{2,1,0:T(8,128)(2,1)}), bf16[8,32,1920]{2,1,0:T(8,128)(2,1)S(1)}, u32[]{:S(2)}, u32[]{:S(2)}) async-start(bf16[8,32,1920]{2,1,0:T(8,128)(2,1)} %bitcast.23), calls=%async_computation.4 | async-start | bytes 1966080 | tf_op jit(solution)/shard_map/all_to_all | solution.py:262
  188.1 9.6 %collective-permute-start.26 = (bf16[256,256]{1,0:T(8,128)(2,1)}, bf16[256,256]{1,0:T(8,128)(2,1)S(1)}, u32[]{:S(2)}, u32[]{:S(2)}) collective-permute-start(bf16[256,256]{1,0:T(8,128)(2,1)} %get-tuple-element.52), channel_id=1, source_target_pairs={{0,16},{8,24},{16,0},{24,8},{1,17},{9,25},{17,1},{25,9},{2,18},{10... | collective-permute-start | bytes 393224 | tf_op jit(solution)/shard_map/ppermute | solution.py:253
  188.1 15.7 %collective-permute-start.27 = (bf16[256,256]{1,0:T(8,128)(2,1)}, bf16[256,256]{1,0:T(8,128)(2,1)S(1)}, u32[]{:S(2)}, u32[]{:S(2)}) collective-permute-start(bf16[256,256]{1,0:T(8,128)(2,1)} %get-tuple-element.53), channel_id=1, source_target_pairs={{0,24},{8,0},{16,8},{24,16},{1,25},{9,1},{17,9},{25,17},{2,26},{10... | collective-permute-start | bytes 393224 | tf_op jit(solution)/shard_map/ppermute | solution.py:253
  (44 other events, 606.9 us)

commit v6 on v5

--- a/solution.py
+++ b/solution.py
@@ -340,10 +340,6 @@
     def wide(*parts):
         return (jnp.concatenate(parts, axis=1) * gain).astype(BF)
 
-    first_gate, first_up = lax.optimization_barrier((gate_weight, up_weight, own))[:2]
-    gate_2 = shift(wide(columns(first_gate, 2)), "y", 1)
-    up_2 = shift(wide(columns(first_up, 2)), "y", -1)
-
     queries = pl.pallas_call(
         query_kernel,
         in_specs=[vmem()] * 3,
@@ -357,8 +353,6 @@
     wide_1 = shift(wide(columns(later_gate, 1), columns(later_up, 1)), "y", 1)
     wide_3 = shift(wide(columns(later_gate, 3), columns(later_up, 3)), "y", -1)
     queries = lax.all_to_all(queries, GROUP, 0, 0, tiled=True)
-    queries = after(queries, gate_2, up_2)
-    gate_2, up_2 = shift(gate_2, "y", 1), shift(up_2, "y", -1)
 
     mixed = pl.pallas_call(
         attention_kernel,
@@ -367,7 +361,8 @@
         out_shape=jax.ShapeDtypeStruct((slot_rows, local_heads // 2 + HEAD), BF),
         compiler_params=params(),
     )(me, image_tiles, own, kv_left, kv_right, k_gain.reshape(1, HEAD), queries, row_image)
-    down_weight = after(down_weight, mixed)
+    gate_weight, up_weight, down_weight = lax.optimization_barrier((gate_weight, up_weight, down_weight, mixed))[:3]
+    gate_2, up_2 = wide(columns(gate_weight, 2)), wide(columns(up_weight, 2))
 
     def rows(d, start, size):
         at = lax.rem(lax.axis_index("y") + d, chips_y) * units + start
@@ -376,9 +371,8 @@
     down_0, down_1, down_3 = rows(0, 0, units), rows(1, 0, units), rows(3, 0, units)
     down_2 = rows(2, 0, half), rows(2, half, half)
     mixed = lax.all_to_all(mixed, GROUP, 0, 0, tiled=True)
-    mixed = after(mixed, wide_1, wide_3, down_1, down_3, *down_2)
-    down_1, down_3 = shift(down_1, "y", 1), shift(down_3, "y", -1)
-    down_2 = shift(down_2[0], "y", 1), shift(down_2[1], "y", -1)
+    mixed = after(mixed, gate_2, up_2, down_1, down_3, *down_2)
+    gate_2, up_2 = shift(gate_2, "y", 1), shift(up_2, "y", -1)
 
     attended = pl.pallas_call(
         combine_kernel,
@@ -387,14 +381,14 @@
         out_shape=jax.ShapeDtypeStruct((groups, own_rows, local_heads), BF),
         compiler_params=params(),
     )(mixed, sel)
+    attended = after(attended, wide_1, wide_3)
     attended = lax.all_to_all(attended, GROUP, 0, 0, tiled=True).reshape(all_rows, local_heads)
-
-    attended = after(attended, gate_2, up_2, *down_2)
+    attended = after(attended, gate_2, up_2)
+    gate_2, up_2 = shift(gate_2, "y", 1), shift(up_2, "y", -1)
     attn_sum = tensor_sum(dot(attended, o_weight))
     middle = (hidden_f + jnp.tanh(gate_logits[0]) * attn_sum).astype(BF)
     middle_f = middle.astype(F32)
-    middle = after(middle, down_1, down_3)
-    down_2 = (shift(down_2[0], "y", 1), shift(down_2[1], "y", -1))
+    middle = after(middle, gate_2, up_2)
     middles = [middle] + [shift(middle, "y", d) for d in (1, 2, 3)]
     block = pl.BlockSpec((all_rows, width_part), lambda i: (0, 0))
     direct = pl.BlockSpec((width_part, units), lambda i: (0, i))
@@ -407,7 +401,11 @@
         out_shape=jax.ShapeDtypeStruct((all_rows, 2 * units + HEAD), BF),
         compiler_params=params(LARGE_VMEM_BYTES),
     )(*middles, wide_0, wide_1, gate_2, up_2, wide_3)
-    parts = after(exchange(gate_up, "z"), *down_2)
+    down_1, down_3, *down_2 = lax.optimization_barrier((down_1, down_3, *down_2, gate_up))[:4]
+    down_1, down_3 = shift(down_1, "y", 1), shift(down_3, "y", -1)
+    down_2 = shift(down_2[0], "y", 1), shift(down_2[1], "y", -1)
+    parts = after(exchange(gate_up, "z"), down_1, down_3, *down_2)
+    down_2 = shift(down_2[0], "y", 1), shift(down_2[1], "y", -1)
     active = pl.pallas_call(
         functools.partial(active_kernel, full_width),
         in_specs=[vmem()],

time: 219 us -> 216 us (0.986)
  blocking collectives: 15.9 us -> 0 us
  waiting for transfers between devices: 74.6 us -> 86.2 us
  local copies, waits for them, and re-layouts: 10.4 us -> 13.5 us
  starting transfers between devices: 84.8 us -> 81.8 us
    all_to_all x1 -> x0, blocking collectives: 15.9 us -> none  [shards(): lax.all_to_all(active, 'z', 0, 0, tiled=True).reshape(all_rows, units)]
    all_to_all x0 -> x1, waiting for transfers between devices: none -> 8.01 us  [shards(): lax.all_to_all(active, 'z', 0, 0, tiled=True).reshape(all_rows, units)]
    all_to_all x2, waiting for transfers between devices: 21.3 us -> 13.5 us  [exchange(): out = lax.all_to_all(value, axis, 0, 0, tiled=True)]
    ppermute x33, starting transfers between devices: 52.4 us -> 45.3 us  [shift(): return lax.ppermute(value, axis, [(i, (i + by) % n) for i in range(n)])]
    ppermute x33, waiting for transfers between devices: 48.5 us -> 54.6 us  [shift(): return lax.ppermute(value, axis, [(i, (i + by) % n) for i in range(n)])]
    all_to_all x1, waiting for transfers between devices: 0.66 us -> 6.34 us  [shards(): mixed = lax.all_to_all(mixed, GROUP, 0, 0, tiled=True)]
    unnamed x63 -> x65, local copies, waits for them, and re-layouts: 3.1 us -> 6.64 us
    all_to_all x0 -> x1, starting transfers between devices: none -> 3.47 us  [shards(): lax.all_to_all(active, 'z', 0, 0, tiled=True).reshape(all_rows, units)]
  transfers between devices with their start and end apart: 38 -> 39, of which waited for: 17 -> 19; matrix products, arithmetic and copies ran while one was open for 7% -> 7% of each run, Pallas kernels for 6% -> 6%
where the time goes in v6:
time: 216 us; the launch traced here: 215 us
  waiting for transfers between devices  86.2 us (40%)
  starting transfers between devices  81.8 us (38%)
  Pallas kernels  22.3 us (10%)
  local copies, waits for them, and re-layouts  13.5 us (6%)
  other arithmetic  6.97 us (3%)
  matrix products  2.32 us (1%)
    ppermute x33, waiting for transfers between devices, shift(): return lax.ppermute(value, axis, [(i, (i + by) % n) for i in range(n)])  54.6 us
    ppermute x33, starting transfers between devices, shift(): return lax.ppermute(value, axis, [(i, (i + by) % n) for i in range(n)])  45.3 us
    all_to_all x2, starting transfers between devices, exchange(): out = lax.all_to_all(value, axis, 0, 0, tiled=True)  14.8 us
    all_to_all x2, waiting for transfers between devices, exchange(): out = lax.all_to_all(value, axis, 0, 0, tiled=True)  13.5 us
    all_to_all x1, waiting for transfers between devices, shards(): lax.all_to_all(active, 'z', 0, 0, tiled=True).reshape(all_rows, units)  8.01 us
    pallas_call x1, Pallas kernels, kv_project(): pl.pallas_call(kv_kernel, grid_spec=pltpu.PrefetchScalarGridSpec(num_scal...  7.97 us
    all_to_all x1, starting transfers between devices, shards(): queries = lax.all_to_all(queries, GROUP, 0, 0, tiled=True)  7.67 us
    unnamed x65, local copies, waits for them, and re-layouts  6.64 us
  transfers between devices with their start and end apart: 39, of which 19 were waited for; matrix products, arithmetic and copies ran while one was open for 7% of the time, Pallas kernels for 6%

profile of v6, /device:TPU:1, one launch (start us, length us, event | category | flops | bytes accessed | tf_op | source)
XLA Modules:
  0.0 214.7 jit_solution(3111733131553325459)
XLA Ops:
  0.0 3.2 %collective-permute-start.1 = (bf16[1024,1024]{1,0:T(8,128)(2,1)}, bf16[1024,1024]{1,0:T(8,128)(2,1)S(1)}, u32[]{:S(2)}, u32[]{:S(2)}) collective-permute-start(bf16[1024,1024]{1,0:T(8,128)(2,1)} %k0.1), channel_id=1, source_target_pairs={{0,1},{1,0},{2,3},{3,2},{4,5},{5,4},{6,7},{7,6},{8,9},{9,8},{10,11... | collective-permute-start | bytes 6291464 | tf_op jit(solution)/shard_map/ppermute | solution.py:253
  5.8 9.5 %all-to-all-start = ((bf16[32,8,1024]{2,1,0:T(8,128)(2,1)}), bf16[32,8,1024]{2,1,0:T(8,128)(2,1)S(1)}, u32[]{:S(2)}, u32[]{:S(2)}) async-start(bf16[32,8,1024]{2,1,0:T(8,128)(2,1)} %fusion), calls=%async_computation | async-start | bytes 1048576 | tf_op jit(solution)/shard_map/all_to_all | solution.py:262
  17.2 8.0 %shard_map.163 = (bf16[320,256]{1,0:T(8,128)(2,1)}, bf16[320,256]{1,0:T(8,128)(2,1)}, bf16[640,256]{1,0:T(8,128)(2,1)}, bf16[640,256]{1,0:T(8,128)(2,1)}, bf16[640,256]{1,0:T(8,128)(2,1)}) custom-call(s32[2]{0:T(128)} %pad_add_fusion.place_ref, bf16[640,1024]{1,0:T(8,128)(2,1)} %x0.1, bf16[640,1024]{1,0:T(8,128)(2,1)} %collective-permute-done.x1, ...), custom_call_target="tpu_custom_call" | custom-call | tf_op jit(solution)/shard_map/pallas_call | solution.py:109
  28.7 3.0 %all-to-all-done.parts_ref = bf16[32,8,1024]{2,1,0:T(8,128)(2,1)S(1)} async-done(((bf16[32,8,1024]{2,1,0:T(8,128)(2,1)}), bf16[32,8,1024]{2,1,0:T(8,128)(2,1)S(1)}, u32[]{:S(2)}, u32[]{:S(2)}) %all-to-all-start) | async-done | bytes 524320 | tf_op jit(solution)/shard_map/all_to_all | solution.py:262
  37.6 7.7 %all-to-all-start.1 = ((bf16[32,8,512]{2,1,0:T(8,128)(2,1)}), bf16[32,8,512]{2,1,0:T(8,128)(2,1)S(1)}, u32[]{:S(2)}, u32[]{:S(2)}) async-start(bf16[32,8,512]{2,1,0:T(8,128)(2,1)} %bitcast.7), calls=%async_computation.1 | async-start | bytes 524288 | tf_op jit(solution)/shard_map/all_to_all | solution.py:355
  52.0 3.7 %all-to-all-done.1 = bf16[32,8,512]{2,1,0:T(8,128)(2,1)S(1)} async-done(((bf16[32,8,512]{2,1,0:T(8,128)(2,1)}), bf16[32,8,512]{2,1,0:T(8,128)(2,1)S(1)}, u32[]{:S(2)}, u32[]{:S(2)}) %all-to-all-start.1) | async-done | bytes 262176 | tf_op jit(solution)/shard_map/all_to_all | solution.py:355
  55.7 3.0 %shard_map.167 = bf16[256,640]{1,0:T(8,128)(2,1)} custom-call(s32[1]{0:T(128)} %bitcast.1.me_ref, s32[32,4]{1,0:T(8,128)S(1)} %copy.27.tiles_ref, bf16[640,256]{1,0:T(8,128)(2,1)S(1)} %copy-done.1, bf16[640,256]{1,0:T(8,128)(2,1)S(1)} %collective-permute-done.5.left_ref, bf16[640,256]{1,0:T(8,128)(2,1)S(1)} %collective-permute-done.6.right_ref, ...), custom_call_target="tpu_custom_call" | custom-call | tf_op jit(solution)/shard_map/pallas_call | solution.py:357
  58.7 4.3 %all-to-all-start.2 = ((bf16[32,8,640]{2,1,0:T(8,128)(2,1)}), bf16[32,8,640]{2,1,0:T(8,128)(2,1)S(1)}, u32[]{:S(2)}, u32[]{:S(2)}) async-start(bf16[32,8,640]{2,1,0:T(8,128)(2,1)} %bitcast.9), calls=%async_computation.2 | async-start | bytes 655360 | tf_op jit(solution)/shard_map/all_to_all | solution.py:373
  69.2 6.3 %all-to-all-done.2 = bf16[32,8,640]{2,1,0:T(8,128)(2,1)S(1)} async-done(((bf16[32,8,640]{2,1,0:T(8,128)(2,1)}), bf16[32,8,640]{2,1,0:T(8,128)(2,1)S(1)}, u32[]{:S(2)}, u32[]{:S(2)}) %all-to-all-start.2) | async-done | bytes 327712 | tf_op jit(solution)/shard_map/all_to_all | solution.py:373
  76.8 6.2 %all-to-all-start.3 = ((bf16[32,8,1024]{2,1,0:T(8,128)(2,1)}), bf16[32,8,1024]{2,1,0:T(8,128)(2,1)S(1)}, u32[]{:S(2)}, u32[]{:S(2)}) async-start(bf16[32,8,1024]{2,1,0:T(8,128)(2,1)} %shard_map.168), calls=%async_computation.3 | async-start | bytes 1048576 | tf_op jit(solution)/shard_map/all_to_all | solution.py:385
  85.6 12.7 %collective-permute-done.10 = bf16[256,896]{1,0:T(8,128)(2,1)S(1)} collective-permute-done((bf16[256,896]{1,0:T(8,128)(2,1)}, bf16[256,896]{1,0:T(8,128)(2,1)S(1)}, u32[]{:S(2)}, u32[]{:S(2)}) %collective-permute-start.10) | collective-permute-done | bytes 458784 | tf_op jit(solution)/shard_map/ppermute | solution.py:253
  101.8 3.6 %collective-permute-start.11 = (bf16[256,256]{1,0:T(8,128)(2,1)S(1)}, bf16[256,256]{1,0:T(8,128)(2,1)S(1)}, u32[]{:S(2)}, u32[]{:S(2)}) collective-permute-start(bf16[256,256]{1,0:T(8,128)(2,1)S(1)} %convolution_convert_fusion.1), channel_id=1, source_target_pairs={{0,1},{1,0},{2,3},{3,2},{4,5},{5,4},{6,7},{7,6},{8,9},{9,8},{10,11... | collective-permute-start | bytes 393224 | tf_op jit(solution)/shard_map/ppermute | solution.py:253
  114.1 3.8 %collective-permute-done.13 = bf16[256,256]{1,0:T(8,128)(2,1)S(1)} collective-permute-done((bf16[256,256]{1,0:T(8,128)(2,1)S(1)}, bf16[256,256]{1,0:T(8,128)(2,1)S(1)}, u32[]{:S(2)}, u32[]{:S(2)}) %collective-permute-start.13) | collective-permute-done | bytes 131104 | tf_op jit(solution)/shard_map/ppermute | solution.py:253
  118.9 3.5 %collective-permute-start.18 = (bf16[256,256]{1,0:T(8,128)(2,1)S(1)}, bf16[256,256]{1,0:T(8,128)(2,1)S(1)}, u32[]{:S(2)}, u32[]{:S(2)}) collective-permute-start(bf16[256,256]{1,0:T(8,128)(2,1)S(1)} %fusion.2.m0), channel_id=1, source_target_pairs={{0,16},{8,24},{16,0},{24,8},{1,17},{9,25},{17,1},{25,9},{2,18},{10... | collective-permute-start | bytes 393224 | tf_op jit(solution)/shard_map/ppermute | solution.py:253
  128.6 4.3 %shard_map.169 = bf16[256,1920]{1,0:T(8,128)(2,1)} custom-call(bf16[256,256]{1,0:T(8,128)(2,1)} %copy-done.8, bf16[256,256]{1,0:T(8,128)(2,1)} %copy-done.18, bf16[256,256]{1,0:T(8,128)(2,1)} %copy-done.19, bf16[256,256]{1,0:T(8,128)(2,1)} %copy-done.20, bf16[256,1792]{1,0:T(8,128)(2,1)} %get-tuple-element.74.w0, ...), custom_call_target="tpu_custom_call" | custom-call | tf_op jit(solution)/shard_map/pallas_call | solution.py:396
  132.9 5.3 %all-to-all-start.4 = ((bf16[8,32,1920]{2,1,0:T(8,128)(2,1)}), bf16[8,32,1920]{2,1,0:T(8,128)(2,1)S(1)}, u32[]{:S(2)}, u32[]{:S(2)}) async-start(bf16[8,32,1920]{2,1,0:T(8,128)(2,1)} %bitcast.23), calls=%async_computation.4 | async-start | bytes 1966080 | tf_op jit(solution)/shard_map/all_to_all | solution.py:262
  144.0 10.6 %collective-permute-done.22 = bf16[448,256]{1,0:T(8,128)(2,1)S(1)} collective-permute-done((bf16[448,256]{1,0:T(8,128)(2,1)S(1)}, bf16[448,256]{1,0:T(8,128)(2,1)S(1)}, u32[]{:S(2)}, u32[]{:S(2)}) %collective-permute-start.22) | collective-permute-done | bytes 229408 | tf_op jit(solution)/shard_map/ppermute | solution.py:253
  155.4 10.5 %all-to-all-done.4.parts_ref = bf16[8,32,1920]{2,1,0:T(8,128)(2,1)S(1)} async-done(((bf16[8,32,1920]{2,1,0:T(8,128)(2,1)}), bf16[8,32,1920]{2,1,0:T(8,128)(2,1)S(1)}, u32[]{:S(2)}, u32[]{:S(2)}) %all-to-all-start.4) | async-done | bytes 983072 | tf_op jit(solution)/shard_map/all_to_all | solution.py:262
  167.0 3.5 %all-to-all-start.5 = ((bf16[8,32,896]{2,1,0:T(8,128)(2,1)}), bf16[8,32,896]{2,1,0:T(8,128)(2,1)S(1)}, u32[]{:S(2)}, u32[]{:S(2)}) async-start(bf16[8,32,896]{2,1,0:T(8,128)(2,1)} %shard_map.170), calls=%async_computation.5 | async-start | bytes 917504 | tf_op jit(solution)/shard_map/all_to_all | solution.py:416
  173.6 5.4 %collective-permute-done.24.low2 = bf16[448,256]{1,0:T(8,128)(2,1)S(1)} collective-permute-done((bf16[448,256]{1,0:T(8,128)(2,1)S(1)}, bf16[448,256]{1,0:T(8,128)(2,1)S(1)}, u32[]{:S(2)}, u32[]{:S(2)}) %collective-permute-start.24) | collective-permute-done | bytes 229408 | tf_op jit(solution)/shard_map/ppermute | solution.py:253
  179.0 8.0 %all-to-all-done.5 = bf16[8,32,896]{2,1,0:T(8,128)(2,1)S(1)} async-done(((bf16[8,32,896]{2,1,0:T(8,128)(2,1)}), bf16[8,32,896]{2,1,0:T(8,128)(2,1)S(1)}, u32[]{:S(2)}, u32[]{:S(2)}) %all-to-all-start.5) | async-done | bytes 458784 | tf_op jit(solution)/shard_map/all_to_all | solution.py:416
  187.8 3.1 %shard_map.171 = (f32[256,256]{1,0:T(8,128)}, bf16[256,256]{1,0:T(8,128)(2,1)}, bf16[256,256]{1,0:T(8,128)(2,1)}, bf16[256,256]{1,0:T(8,128)(2,1)}) custom-call(bf16[256,896]{1,0:T(8,128)(2,1)} %bitcast.25, bf16[896,256]{1,0:T(8,128)(2,1)} %get-tuple-element.63.d0, bf16[896,256]{1,0:T(8,128)(2,1)} %copy-done.14, bf16[448,256]{1,0:T(8,128)(2,1)} %copy-done.15, ...), custom_call_target="tpu_custom_call" | custom-call | tf_op jit(solution)/shard_map/pallas_call | solution.py:417
  197.1 3.4 %collective-permute-done.27 = bf16[256,256]{1,0:T(8,128)(2,1)S(1)} collective-permute-done((bf16[256,256]{1,0:T(8,128)(2,1)}, bf16[256,256]{1,0:T(8,128)(2,1)S(1)}, u32[]{:S(2)}, u32[]{:S(2)}) %collective-permute-start.27) | collective-permute-done | bytes 131104 | tf_op jit(solution)/shard_map/ppermute | solution.py:253
  210.7 3.3 %collective-permute-done.31 = bf16[256,256]{1,0:T(8,128)(2,1)S(1)} collective-permute-done((bf16[256,256]{1,0:T(8,128)(2,1)S(1)}, bf16[256,256]{1,0:T(8,128)(2,1)S(1)}, u32[]{:S(2)}, u32[]{:S(2)}) %collective-permute-start.31) | collective-permute-done | bytes 131104 | tf_op jit(solution)/shard_map/ppermute | solution.py:253
  (150 shorter events, 77.3 us)
Async XLA Ops:
  0.0 15.9 %collective-permute-start.1 = (bf16[1024,1024]{1,0:T(8,128)(2,1)}, bf16[1024,1024]{1,0:T(8,128)(2,1)S(1)}, u32[]{:S(2)}, u32[]{:S(2)}) collective-permute-start(bf16[1024,1024]{1,0:T(8,128)(2,1)} %k0.1), channel_id=1, source_target_pairs={{0,1},{1,0},{2,3},{3,2},{4,5},{5,4},{6,7},{7,6},{8,9},{9,8},{10,11... | collective-permute-start | bytes 6291464 | tf_op jit(solution)/shard_map/ppermute | solution.py:253
  3.2 12.7 %collective-permute-start.2 = (bf16[1024,1024]{1,0:T(8,128)(2,1)}, bf16[1024,1024]{1,0:T(8,128)(2,1)}, u32[]{:S(2)}, u32[]{:S(2)}) collective-permute-start(bf16[1024,1024]{1,0:T(8,128)(2,1)} %v0.1), channel_id=1, source_target_pairs={{0,1},{1,0},{2,3},{3,2},{4,5},{5,4},{6,7},{7,6},{8,9},{9,8},{10,11... | collective-permute-start | bytes 6291464 | tf_op jit(solution)/shard_map/ppermute | solution.py:253
  3.2 12.6 %collective-permute-start = (bf16[640,1024]{1,0:T(8,128)(2,1)}, bf16[640,1024]{1,0:T(8,128)(2,1)}, u32[]{:S(2)}, u32[]{:S(2)}) collective-permute-start(bf16[640,1024]{1,0:T(8,128)(2,1)} %x0.1), channel_id=1, source_target_pairs={{0,1},{1,0},{2,3},{3,2},{4,5},{5,4},{6,7},{7,6},{8,9},{9,8},{10,11... | collective-permute-start | bytes 3932168 | tf_op jit(solution)/shard_map/ppermute | solution.py:253
  5.8 25.9 %all-to-all-start = ((bf16[32,8,1024]{2,1,0:T(8,128)(2,1)}), bf16[32,8,1024]{2,1,0:T(8,128)(2,1)S(1)}, u32[]{:S(2)}, u32[]{:S(2)}) async-start(bf16[32,8,1024]{2,1,0:T(8,128)(2,1)} %fusion), calls=%async_computation | async-start | bytes 1048576 | tf_op jit(solution)/shard_map/all_to_all | solution.py:262
  34.8 17.1 %collective-permute-start.5 = (bf16[640,256]{1,0:T(8,128)(2,1)S(1)}, bf16[640,256]{1,0:T(8,128)(2,1)S(1)}, u32[]{:S(2)}, u32[]{:S(2)}) collective-permute-start(bf16[640,256]{1,0:T(8,128)(2,1)S(1)} %get-tuple-element.39), channel_id=1, source_target_pairs={{0,2},{2,4},{4,6},{6,0},{1,3},{3,5},{5,7},{7,1},{8,10},{10,12},{12... | collective-permute-start | bytes 983048 | tf_op jit(solution)/shard_map/ppermute | solution.py:253
  36.1 15.8 %collective-permute-start.6 = (bf16[640,256]{1,0:T(8,128)(2,1)S(1)}, bf16[640,256]{1,0:T(8,128)(2,1)S(1)}, u32[]{:S(2)}, u32[]{:S(2)}) collective-permute-start(bf16[640,256]{1,0:T(8,128)(2,1)S(1)} %get-tuple-element.40), channel_id=1, source_target_pairs={{0,6},{2,0},{4,2},{6,4},{1,7},{3,1},{5,3},{7,5},{8,14},{10,8},{12,... | collective-permute-start | bytes 983048 | tf_op jit(solution)/shard_map/ppermute | solution.py:253
  37.6 18.1 %all-to-all-start.1 = ((bf16[32,8,512]{2,1,0:T(8,128)(2,1)}), bf16[32,8,512]{2,1,0:T(8,128)(2,1)S(1)}, u32[]{:S(2)}, u32[]{:S(2)}) async-start(bf16[32,8,512]{2,1,0:T(8,128)(2,1)} %bitcast.7), calls=%async_computation.1 | async-start | bytes 524288 | tf_op jit(solution)/shard_map/all_to_all | solution.py:355
  49.2 27.6 %collective-permute-start.7 = (bf16[256,1792]{1,0:T(8,128)(2,1)}, bf16[256,1792]{1,0:T(8,128)(2,1)}, u32[]{:S(2)}, u32[]{:S(2)}) collective-permute-start(bf16[256,1792]{1,0:T(8,128)(2,1)} %get-tuple-element.76), channel_id=1, source_target_pairs={{0,8},{8,16},{16,24},{24,0},{1,9},{9,17},{17,25},{25,1},{2,10},{10... | collective-permute-start | bytes 2752520 | tf_op jit(solution)/shard_map/ppermute | solution.py:253
  50.4 26.3 %collective-permute-start.8 = (bf16[256,1792]{1,0:T(8,128)(2,1)}, bf16[256,1792]{1,0:T(8,128)(2,1)}, u32[]{:S(2)}, u32[]{:S(2)}) collective-permute-start(bf16[256,1792]{1,0:T(8,128)(2,1)} %get-tuple-element.75), channel_id=1, source_target_pairs={{0,24},{8,0},{16,8},{24,16},{1,25},{9,1},{17,9},{25,17},{2,26},{10... | collective-permute-start | bytes 2752520 | tf_op jit(solution)/shard_map/ppermute | solution.py:253
  58.7 16.8 %all-to-all-start.2 = ((bf16[32,8,640]{2,1,0:T(8,128)(2,1)}), bf16[32,8,640]{2,1,0:T(8,128)(2,1)S(1)}, u32[]{:S(2)}, u32[]{:S(2)}) async-start(bf16[32,8,640]{2,1,0:T(8,128)(2,1)} %bitcast.9), calls=%async_computation.2 | async-start | bytes 655360 | tf_op jit(solution)/shard_map/all_to_all | solution.py:373
  76.8 24.7 %all-to-all-start.3 = ((bf16[32,8,1024]{2,1,0:T(8,128)(2,1)}), bf16[32,8,1024]{2,1,0:T(8,128)(2,1)S(1)}, u32[]{:S(2)}, u32[]{:S(2)}) async-start(bf16[32,8,1024]{2,1,0:T(8,128)(2,1)} %shard_map.168), calls=%async_computation.3 | async-start | bytes 1048576 | tf_op jit(solution)/shard_map/all_to_all | solution.py:385
  83.0 15.3 %collective-permute-start.10 = (bf16[256,896]{1,0:T(8,128)(2,1)}, bf16[256,896]{1,0:T(8,128)(2,1)S(1)}, u32[]{:S(2)}, u32[]{:S(2)}) collective-permute-start(bf16[256,896]{1,0:T(8,128)(2,1)} %get-tuple-element.77), channel_id=1, source_target_pairs={{0,24},{8,0},{16,8},{24,16},{1,25},{9,1},{17,9},{25,17},{2,26},{10... | collective-permute-start | bytes 1376264 | tf_op jit(solution)/shard_map/ppermute | solution.py:253
  85.6 15.9 %collective-permute-start.9 = (bf16[256,896]{1,0:T(8,128)(2,1)S(1)}, bf16[256,896]{1,0:T(8,128)(2,1)}, u32[]{:S(2)}, u32[]{:S(2)}) collective-permute-start(bf16[256,896]{1,0:T(8,128)(2,1)S(1)} %get-tuple-element.78), channel_id=1, source_target_pairs={{0,8},{8,16},{16,24},{24,0},{1,9},{9,17},{17,25},{25,1},{2,10},{10... | collective-permute-start | bytes 1376264 | tf_op jit(solution)/shard_map/ppermute | solution.py:253
  105.3 13.5 %collective-permute-start.15 = (bf16[256,896]{1,0:T(8,128)(2,1)}, bf16[256,896]{1,0:T(8,128)(2,1)S(1)}, u32[]{:S(2)}, u32[]{:S(2)}) collective-permute-start(bf16[256,896]{1,0:T(8,128)(2,1)} %collective-permute-done.9), channel_id=1, source_target_pairs={{0,8},{8,16},{16,24},{24,0},{1,9},{9,17},{17,25},{25,1},{2,10},{10... | collective-permute-start | bytes 1376264 | tf_op jit(solution)/shard_map/ppermute | solution.py:253
  105.3 13.5 %collective-permute-start.16 = (bf16[256,896]{1,0:T(8,128)(2,1)}, bf16[256,896]{1,0:T(8,128)(2,1)S(1)}, u32[]{:S(2)}, u32[]{:S(2)}) collective-permute-start(bf16[256,896]{1,0:T(8,128)(2,1)} %copy-done.26), channel_id=1, source_target_pairs={{0,24},{8,0},{16,8},{24,16},{1,25},{9,1},{17,9},{25,17},{2,26},{10... | collective-permute-start | bytes 1376264 | tf_op jit(solution)/shard_map/ppermute | solution.py:253
  109.1 8.8 %collective-permute-start.13 = (bf16[256,256]{1,0:T(8,128)(2,1)S(1)}, bf16[256,256]{1,0:T(8,128)(2,1)S(1)}, u32[]{:S(2)}, u32[]{:S(2)}) collective-permute-start(bf16[256,256]{1,0:T(8,128)(2,1)S(1)} %add_convert_fusion.3), channel_id=1, source_target_pairs={{0,2},{2,4},{4,6},{6,0},{1,3},{3,5},{5,7},{7,1},{8,10},{10,12},{12... | collective-permute-start | bytes 393224 | tf_op jit(solution)/shard_map/ppermute | solution.py:253
  132.9 33.1 %all-to-all-start.4 = ((bf16[8,32,1920]{2,1,0:T(8,128)(2,1)}), bf16[8,32,1920]{2,1,0:T(8,128)(2,1)S(1)}, u32[]{:S(2)}, u32[]{:S(2)}) async-start(bf16[8,32,1920]{2,1,0:T(8,128)(2,1)} %bitcast.23), calls=%async_computation.4 | async-start | bytes 1966080 | tf_op jit(solution)/shard_map/all_to_all | solution.py:262
  138.2 16.5 %collective-permute-start.20 = (bf16[896,256]{1,0:T(8,128)(2,1)S(1)}, bf16[896,256]{1,0:T(8,128)(2,1)S(1)}, u32[]{:S(2)}, u32[]{:S(2)}) collective-permute-start(bf16[896,256]{1,0:T(8,128)(2,1)S(1)} %get-tuple-element.54), channel_id=1, source_target_pairs={{0,8},{8,16},{16,24},{24,0},{1,9},{9,17},{17,25},{25,1},{2,10},{10... | collective-permute-start | bytes 1376264 | tf_op jit(solution)/shard_map/ppermute | solution.py:253
  138.5 16.9 %collective-permute-start.21 = (bf16[896,256]{1,0:T(8,128)(2,1)S(1)}, bf16[896,256]{1,0:T(8,128)(2,1)}, u32[]{:S(2)}, u32[]{:S(2)}) collective-permute-start(bf16[896,256]{1,0:T(8,128)(2,1)S(1)} %get-tuple-element.55), channel_id=1, source_target_pairs={{0,24},{8,0},{16,8},{24,16},{1,25},{9,1},{17,9},{25,17},{2,26},{10... | collective-permute-start | bytes 1376264 | tf_op jit(solution)/shard_map/ppermute | solution.py:253
  141.4 13.3 %collective-permute-start.22 = (bf16[448,256]{1,0:T(8,128)(2,1)S(1)}, bf16[448,256]{1,0:T(8,128)(2,1)S(1)}, u32[]{:S(2)}, u32[]{:S(2)}) collective-permute-start(bf16[448,256]{1,0:T(8,128)(2,1)S(1)} %copy-done.17), channel_id=1, source_target_pairs={{0,8},{8,16},{16,24},{24,0},{1,9},{9,17},{17,25},{25,1},{2,10},{10... | collective-permute-start | bytes 688136 | tf_op jit(solution)/shard_map/ppermute | solution.py:253
  141.4 13.3 %collective-permute-start.23 = (bf16[448,256]{1,0:T(8,128)(2,1)S(1)}, bf16[448,256]{1,0:T(8,128)(2,1)S(1)}, u32[]{:S(2)}, u32[]{:S(2)}) collective-permute-start(bf16[448,256]{1,0:T(8,128)(2,1)S(1)} %get-tuple-element.57), channel_id=1, source_target_pairs={{0,24},{8,0},{16,8},{24,16},{1,25},{9,1},{17,9},{25,17},{2,26},{10... | collective-permute-start | bytes 688136 | tf_op jit(solution)/shard_map/ppermute | solution.py:253
  167.0 19.9 %all-to-all-start.5 = ((bf16[8,32,896]{2,1,0:T(8,128)(2,1)}), bf16[8,32,896]{2,1,0:T(8,128)(2,1)S(1)}, u32[]{:S(2)}, u32[]{:S(2)}) async-start(bf16[8,32,896]{2,1,0:T(8,128)(2,1)} %shard_map.170), calls=%async_computation.5 | async-start | bytes 917504 | tf_op jit(solution)/shard_map/all_to_all | solution.py:416
  190.8 9.6 %collective-permute-start.27 = (bf16[256,256]{1,0:T(8,128)(2,1)}, bf16[256,256]{1,0:T(8,128)(2,1)S(1)}, u32[]{:S(2)}, u32[]{:S(2)}) collective-permute-start(bf16[256,256]{1,0:T(8,128)(2,1)} %get-tuple-element.61), channel_id=1, source_target_pairs={{0,24},{8,0},{16,8},{24,16},{1,25},{9,1},{17,9},{25,17},{2,26},{10... | collective-permute-start | bytes 393224 | tf_op jit(solution)/shard_map/ppermute | solution.py:253
  205.1 8.8 %collective-permute-start.31 = (bf16[256,256]{1,0:T(8,128)(2,1)S(1)}, bf16[256,256]{1,0:T(8,128)(2,1)S(1)}, u32[]{:S(2)}, u32[]{:S(2)}) collective-permute-start(bf16[256,256]{1,0:T(8,128)(2,1)S(1)} %add_convert_fusion.1), channel_id=1, source_target_pairs={{0,2},{2,4},{4,6},{6,0},{1,3},{3,5},{5,7},{7,1},{8,10},{10,12},{12... | collective-permute-start | bytes 393224 | tf_op jit(solution)/shard_map/ppermute | solution.py:253
  (46 other events, 463.7 us)

commit v7 on v6

--- a/solution.py
+++ b/solution.py
@@ -16,7 +16,7 @@
 STEPS = 2
 EPS = 1e-05
 VMEM_BYTES = 16 * 1024 * 1024
-LARGE_VMEM_BYTES = 58 * 1024 * 1024
+LARGE_VMEM_BYTES = 60 * 1024 * 1024
 BF = jnp.bfloat16
 F32 = jnp.float32
 
@@ -263,9 +263,10 @@
     return out.reshape((n, value.shape[0] // n) + value.shape[1:])
 
 
-def tensor_sum(part):
+def tensor_sum(part, *others):
     part = part.astype(BF)
     pair = (part.astype(F32) + shift(part, "c", 1).astype(F32)).astype(BF)
+    pair = after(pair, *others)
     ahead, behind, across = shift(pair, "x", 1), shift(pair, "x", -1), shift(pair, "x", 2)
     return (pair.astype(F32) + across.astype(F32)) + (ahead.astype(F32) + behind.astype(F32))
 
@@ -383,12 +384,10 @@
     )(mixed, sel)
     attended = after(attended, wide_1, wide_3)
     attended = lax.all_to_all(attended, GROUP, 0, 0, tiled=True).reshape(all_rows, local_heads)
-    attended = after(attended, gate_2, up_2)
+    attn_sum = tensor_sum(dot(attended, o_weight), gate_2, up_2)
     gate_2, up_2 = shift(gate_2, "y", 1), shift(up_2, "y", -1)
-    attn_sum = tensor_sum(dot(attended, o_weight))
     middle = (hidden_f + jnp.tanh(gate_logits[0]) * attn_sum).astype(BF)
     middle_f = middle.astype(F32)
-    middle = after(middle, gate_2, up_2)
     middles = [middle] + [shift(middle, "y", d) for d in (1, 2, 3)]
     block = pl.BlockSpec((all_rows, width_part), lambda i: (0, 0))
     direct = pl.BlockSpec((width_part, units), lambda i: (0, i))

time: 216 us -> 208 us (0.963)
  waiting for transfers between devices: 86.2 us -> 74.2 us
  starting transfers between devices: 81.8 us -> 86.8 us
    ppermute x33, waiting for transfers between devices: 54.6 us -> 34.7 us  [shift(): return lax.ppermute(value, axis, [(i, (i + by) % n) for i in range(n)])]
    all_to_all x1, waiting for transfers between devices: 0.01 us -> 10.1 us  [shards(): lax.all_to_all(attended, GROUP, 0, 0, tiled=True)]
    ppermute x33, starting transfers between devices: 45.3 us -> 52 us  [shift(): return lax.ppermute(value, axis, [(i, (i + by) % n) for i in range(n)])]
    unnamed x65 -> x63, local copies, waits for them, and re-layouts: 6.64 us -> 5.92 us
  transfers between devices with their start and end apart: 39 -> 39, of which waited for: 19 -> 18; matrix products, arithmetic and copies ran while one was open for 7% -> 7% of each run, Pallas kernels for 6% -> 7%
where the time goes in v7:
time: 208 us; the launch traced here: 207 us
  starting transfers between devices  86.8 us (42%)
  waiting for transfers between devices  74.2 us (36%)
  Pallas kernels  22.3 us (11%)
  local copies, waits for them, and re-layouts  12.8 us (6%)
  other arithmetic  6.91 us (3%)
  matrix products  2.32 us (1%)
    ppermute x33, starting transfers between devices, shift(): return lax.ppermute(value, axis, [(i, (i + by) % n) for i in range(n)])  52 us
    ppermute x33, waiting for transfers between devices, shift(): return lax.ppermute(value, axis, [(i, (i + by) % n) for i in range(n)])  34.7 us
    all_to_all x2, starting transfers between devices, exchange(): out = lax.all_to_all(value, axis, 0, 0, tiled=True)  13.2 us
    all_to_all x2, waiting for transfers between devices, exchange(): out = lax.all_to_all(value, axis, 0, 0, tiled=True)  12.3 us
    all_to_all x1, waiting for transfers between devices, shards(): lax.all_to_all(attended, GROUP, 0, 0, tiled=True)  10.1 us
    pallas_call x1, Pallas kernels, kv_project(): pl.pallas_call(kv_kernel, grid_spec=pltpu.PrefetchScalarGridSpec(num_scal...  7.98 us
    all_to_all x1, starting transfers between devices, shards(): queries = lax.all_to_all(queries, GROUP, 0, 0, tiled=True)  7.64 us
    all_to_all x1, waiting for transfers between devices, shards(): lax.all_to_all(active, 'z', 0, 0, tiled=True).reshape(all_rows, units)  6.99 us
  transfers between devices with their start and end apart: 39, of which 18 were waited for; matrix products, arithmetic and copies ran while one was open for 7% of the time, Pallas kernels for 7%

profile of v7, /device:TPU:1, one launch (start us, length us, event | category | flops | bytes accessed | tf_op | source)
XLA Modules:
  0.0 207.1 jit_solution(13968518198267930168)
XLA Ops:
  0.0 3.2 %collective-permute-start.1 = (bf16[1024,1024]{1,0:T(8,128)(2,1)}, bf16[1024,1024]{1,0:T(8,128)(2,1)S(1)}, u32[]{:S(2)}, u32[]{:S(2)}) collective-permute-start(bf16[1024,1024]{1,0:T(8,128)(2,1)} %k0.1), channel_id=1, source_target_pairs={{0,1},{1,0},{2,3},{3,2},{4,5},{5,4},{6,7},{7,6},{8,9},{9,8},{10,11... | collective-permute-start | bytes 6291464 | tf_op jit(solution)/shard_map/ppermute | solution.py:253
  5.8 9.5 %all-to-all-start = ((bf16[32,8,1024]{2,1,0:T(8,128)(2,1)}), bf16[32,8,1024]{2,1,0:T(8,128)(2,1)S(1)}, u32[]{:S(2)}, u32[]{:S(2)}) async-start(bf16[32,8,1024]{2,1,0:T(8,128)(2,1)} %fusion), calls=%async_computation | async-start | bytes 1048576 | tf_op jit(solution)/shard_map/all_to_all | solution.py:262
  17.2 8.0 %shard_map.163 = (bf16[320,256]{1,0:T(8,128)(2,1)}, bf16[320,256]{1,0:T(8,128)(2,1)}, bf16[640,256]{1,0:T(8,128)(2,1)}, bf16[640,256]{1,0:T(8,128)(2,1)}, bf16[640,256]{1,0:T(8,128)(2,1)}) custom-call(s32[2]{0:T(128)} %pad_add_fusion.place_ref, bf16[640,1024]{1,0:T(8,128)(2,1)} %x0.1, bf16[640,1024]{1,0:T(8,128)(2,1)} %collective-permute-done.x1, ...), custom_call_target="tpu_custom_call" | custom-call | tf_op jit(solution)/shard_map/pallas_call | solution.py:109
  28.6 3.0 %all-to-all-done.parts_ref = bf16[32,8,1024]{2,1,0:T(8,128)(2,1)S(1)} async-done(((bf16[32,8,1024]{2,1,0:T(8,128)(2,1)}), bf16[32,8,1024]{2,1,0:T(8,128)(2,1)S(1)}, u32[]{:S(2)}, u32[]{:S(2)}) %all-to-all-start) | async-done | bytes 524320 | tf_op jit(solution)/shard_map/all_to_all | solution.py:262
  37.6 7.6 %all-to-all-start.1 = ((bf16[32,8,512]{2,1,0:T(8,128)(2,1)}), bf16[32,8,512]{2,1,0:T(8,128)(2,1)S(1)}, u32[]{:S(2)}, u32[]{:S(2)}) async-start(bf16[32,8,512]{2,1,0:T(8,128)(2,1)} %bitcast.7), calls=%async_computation.1 | async-start | bytes 524288 | tf_op jit(solution)/shard_map/all_to_all | solution.py:356
  51.9 3.8 %all-to-all-done.1 = bf16[32,8,512]{2,1,0:T(8,128)(2,1)S(1)} async-done(((bf16[32,8,512]{2,1,0:T(8,128)(2,1)}), bf16[32,8,512]{2,1,0:T(8,128)(2,1)S(1)}, u32[]{:S(2)}, u32[]{:S(2)}) %all-to-all-start.1) | async-done | bytes 262176 | tf_op jit(solution)/shard_map/all_to_all | solution.py:356
  55.7 3.0 %shard_map.167 = bf16[256,640]{1,0:T(8,128)(2,1)} custom-call(s32[1]{0:T(128)} %bitcast.1.me_ref, s32[32,4]{1,0:T(8,128)S(1)} %copy.27.tiles_ref, bf16[640,256]{1,0:T(8,128)(2,1)S(1)} %copy-done.1, bf16[640,256]{1,0:T(8,128)(2,1)S(1)} %collective-permute-done.5.left_ref, bf16[640,256]{1,0:T(8,128)(2,1)S(1)} %collective-permute-done.6.right_ref, ...), custom_call_target="tpu_custom_call" | custom-call | tf_op jit(solution)/shard_map/pallas_call | solution.py:358
  58.7 4.3 %all-to-all-start.2 = ((bf16[32,8,640]{2,1,0:T(8,128)(2,1)}), bf16[32,8,640]{2,1,0:T(8,128)(2,1)S(1)}, u32[]{:S(2)}, u32[]{:S(2)}) async-start(bf16[32,8,640]{2,1,0:T(8,128)(2,1)} %bitcast.9), calls=%async_computation.2 | async-start | bytes 655360 | tf_op jit(solution)/shard_map/all_to_all | solution.py:374
  69.1 6.3 %all-to-all-done.2 = bf16[32,8,640]{2,1,0:T(8,128)(2,1)S(1)} async-done(((bf16[32,8,640]{2,1,0:T(8,128)(2,1)}), bf16[32,8,640]{2,1,0:T(8,128)(2,1)S(1)}, u32[]{:S(2)}, u32[]{:S(2)}) %all-to-all-start.2) | async-done | bytes 327712 | tf_op jit(solution)/shard_map/all_to_all | solution.py:374
  76.8 6.3 %all-to-all-start.3 = ((bf16[32,8,1024]{2,1,0:T(8,128)(2,1)}), bf16[32,8,1024]{2,1,0:T(8,128)(2,1)S(1)}, u32[]{:S(2)}, u32[]{:S(2)}) async-start(bf16[32,8,1024]{2,1,0:T(8,128)(2,1)} %shard_map.168), calls=%async_computation.3 | async-start | bytes 1048576 | tf_op jit(solution)/shard_map/all_to_all | solution.py:386
  85.8 10.1 %all-to-all-done.3 = bf16[32,8,1024]{2,1,0:T(8,128)(2,1)S(1)} async-done(((bf16[32,8,1024]{2,1,0:T(8,128)(2,1)}), bf16[32,8,1024]{2,1,0:T(8,128)(2,1)S(1)}, u32[]{:S(2)}, u32[]{:S(2)}) %all-to-all-start.3) | async-done | bytes 524320 | tf_op jit(solution)/shard_map/all_to_all | solution.py:386
  96.2 6.5 %collective-permute-start.9 = (bf16[256,256]{1,0:T(8,128)(2,1)S(1)}, bf16[256,256]{1,0:T(8,128)(2,1)S(1)}, u32[]{:S(2)}, u32[]{:S(2)}) collective-permute-start(bf16[256,256]{1,0:T(8,128)(2,1)S(1)} %convolution_convert_fusion.1), channel_id=1, source_target_pairs={{0,1},{1,0},{2,3},{3,2},{4,5},{5,4},{6,7},{7,6},{8,9},{9,8},{10,11... | collective-permute-start | bytes 393224 | tf_op jit(solution)/shard_map/ppermute | solution.py:253
  125.4 4.3 %shard_map.169 = bf16[256,1920]{1,0:T(8,128)(2,1)} custom-call(bf16[256,256]{1,0:T(8,128)(2,1)} %copy-done.8, bf16[256,256]{1,0:T(8,128)(2,1)} %copy-done.18, bf16[256,256]{1,0:T(8,128)(2,1)} %copy-done.19, bf16[256,256]{1,0:T(8,128)(2,1)} %copy-done.20, bf16[256,1792]{1,0:T(8,128)(2,1)} %get-tuple-element.72.w0, ...), custom_call_target="tpu_custom_call" | custom-call | tf_op jit(solution)/shard_map/pallas_call | solution.py:395
  129.7 3.7 %all-to-all-start.4 = ((bf16[8,32,1920]{2,1,0:T(8,128)(2,1)}), bf16[8,32,1920]{2,1,0:T(8,128)(2,1)S(1)}, u32[]{:S(2)}, u32[]{:S(2)}) async-start(bf16[8,32,1920]{2,1,0:T(8,128)(2,1)} %bitcast.24), calls=%async_computation.4 | async-start | bytes 1966080 | tf_op jit(solution)/shard_map/all_to_all | solution.py:262
  133.5 3.0 %collective-permute-start.21 = (bf16[896,256]{1,0:T(8,128)(2,1)S(1)}, bf16[896,256]{1,0:T(8,128)(2,1)}, u32[]{:S(2)}, u32[]{:S(2)}) collective-permute-start(bf16[896,256]{1,0:T(8,128)(2,1)S(1)} %get-tuple-element.53), channel_id=1, source_target_pairs={{0,24},{8,0},{16,8},{24,16},{1,25},{9,1},{17,9},{25,17},{2,26},{10... | collective-permute-start | bytes 1376264 | tf_op jit(solution)/shard_map/ppermute | solution.py:253
  139.2 10.0 %collective-permute-done.22 = bf16[448,256]{1,0:T(8,128)(2,1)S(1)} collective-permute-done((bf16[448,256]{1,0:T(8,128)(2,1)S(1)}, bf16[448,256]{1,0:T(8,128)(2,1)S(1)}, u32[]{:S(2)}, u32[]{:S(2)}) %collective-permute-start.22) | collective-permute-done | bytes 229408 | tf_op jit(solution)/shard_map/ppermute | solution.py:253
  150.0 9.3 %all-to-all-done.4.parts_ref = bf16[8,32,1920]{2,1,0:T(8,128)(2,1)S(1)} async-done(((bf16[8,32,1920]{2,1,0:T(8,128)(2,1)}), bf16[8,32,1920]{2,1,0:T(8,128)(2,1)S(1)}, u32[]{:S(2)}, u32[]{:S(2)}) %all-to-all-start.4) | async-done | bytes 983072 | tf_op jit(solution)/shard_map/all_to_all | solution.py:262
  160.3 3.5 %all-to-all-start.5 = ((bf16[8,32,896]{2,1,0:T(8,128)(2,1)}), bf16[8,32,896]{2,1,0:T(8,128)(2,1)S(1)}, u32[]{:S(2)}, u32[]{:S(2)}) async-start(bf16[8,32,896]{2,1,0:T(8,128)(2,1)} %shard_map.170), calls=%async_computation.5 | async-start | bytes 917504 | tf_op jit(solution)/shard_map/all_to_all | solution.py:415
  163.9 2.9 %collective-permute-start.25 = (bf16[448,256]{1,0:T(8,128)(2,1)S(1)}, bf16[448,256]{1,0:T(8,128)(2,1)S(1)}, u32[]{:S(2)}, u32[]{:S(2)}) collective-permute-start(bf16[448,256]{1,0:T(8,128)(2,1)S(1)} %copy-done.29), channel_id=1, source_target_pairs={{0,24},{8,0},{16,8},{24,16},{1,25},{9,1},{17,9},{25,17},{2,26},{10... | collective-permute-start | bytes 688136 | tf_op jit(solution)/shard_map/ppermute | solution.py:253
  166.8 3.3 %collective-permute-done.24.low2 = bf16[448,256]{1,0:T(8,128)(2,1)S(1)} collective-permute-done((bf16[448,256]{1,0:T(8,128)(2,1)S(1)}, bf16[448,256]{1,0:T(8,128)(2,1)S(1)}, u32[]{:S(2)}, u32[]{:S(2)}) %collective-permute-start.24) | collective-permute-done | bytes 229408 | tf_op jit(solution)/shard_map/ppermute | solution.py:253
  170.1 7.0 %all-to-all-done.5 = bf16[8,32,896]{2,1,0:T(8,128)(2,1)S(1)} async-done(((bf16[8,32,896]{2,1,0:T(8,128)(2,1)}), bf16[8,32,896]{2,1,0:T(8,128)(2,1)S(1)}, u32[]{:S(2)}, u32[]{:S(2)}) %all-to-all-start.5) | async-done | bytes 458784 | tf_op jit(solution)/shard_map/all_to_all | solution.py:415
  177.9 3.1 %shard_map.171 = (f32[256,256]{1,0:T(8,128)}, bf16[256,256]{1,0:T(8,128)(2,1)}, bf16[256,256]{1,0:T(8,128)(2,1)}, bf16[256,256]{1,0:T(8,128)(2,1)}) custom-call(bf16[256,896]{1,0:T(8,128)(2,1)} %bitcast.25, bf16[896,256]{1,0:T(8,128)(2,1)} %get-tuple-element.61.d0, bf16[896,256]{1,0:T(8,128)(2,1)} %copy-done.14, bf16[448,256]{1,0:T(8,128)(2,1)} %copy-done.15, ...), custom_call_target="tpu_custom_call" | custom-call | tf_op jit(solution)/shard_map/pallas_call | solution.py:416
  190.2 5.1 %collective-permute-start.29 = (bf16[256,256]{1,0:T(8,128)(2,1)S(1)}, bf16[256,256]{1,0:T(8,128)(2,1)S(1)}, u32[]{:S(2)}, u32[]{:S(2)}) collective-permute-start(bf16[256,256]{1,0:T(8,128)(2,1)S(1)} %add_convert_fusion.2), channel_id=1, source_target_pairs={{0,1},{1,0},{2,3},{3,2},{4,5},{5,4},{6,7},{7,6},{8,9},{9,8},{10,11... | collective-permute-start | bytes 393224 | tf_op jit(solution)/shard_map/ppermute | solution.py:253
  203.0 3.3 %collective-permute-done.31 = bf16[256,256]{1,0:T(8,128)(2,1)S(1)} collective-permute-done((bf16[256,256]{1,0:T(8,128)(2,1)S(1)}, bf16[256,256]{1,0:T(8,128)(2,1)S(1)}, u32[]{:S(2)}, u32[]{:S(2)}) %collective-permute-start.31) | collective-permute-done | bytes 131104 | tf_op jit(solution)/shard_map/ppermute | solution.py:253
  (148 shorter events, 75.3 us)
Async XLA Ops:
  0.0 15.8 %collective-permute-start.1 = (bf16[1024,1024]{1,0:T(8,128)(2,1)}, bf16[1024,1024]{1,0:T(8,128)(2,1)S(1)}, u32[]{:S(2)}, u32[]{:S(2)}) collective-permute-start(bf16[1024,1024]{1,0:T(8,128)(2,1)} %k0.1), channel_id=1, source_target_pairs={{0,1},{1,0},{2,3},{3,2},{4,5},{5,4},{6,7},{7,6},{8,9},{9,8},{10,11... | collective-permute-start | bytes 6291464 | tf_op jit(solution)/shard_map/ppermute | solution.py:253
  3.2 12.6 %collective-permute-start.2 = (bf16[1024,1024]{1,0:T(8,128)(2,1)}, bf16[1024,1024]{1,0:T(8,128)(2,1)}, u32[]{:S(2)}, u32[]{:S(2)}) collective-permute-start(bf16[1024,1024]{1,0:T(8,128)(2,1)} %v0.1), channel_id=1, source_target_pairs={{0,1},{1,0},{2,3},{3,2},{4,5},{5,4},{6,7},{7,6},{8,9},{9,8},{10,11... | collective-permute-start | bytes 6291464 | tf_op jit(solution)/shard_map/ppermute | solution.py:253
  3.2 12.6 %collective-permute-start = (bf16[640,1024]{1,0:T(8,128)(2,1)}, bf16[640,1024]{1,0:T(8,128)(2,1)}, u32[]{:S(2)}, u32[]{:S(2)}) collective-permute-start(bf16[640,1024]{1,0:T(8,128)(2,1)} %x0.1), channel_id=1, source_target_pairs={{0,1},{1,0},{2,3},{3,2},{4,5},{5,4},{6,7},{7,6},{8,9},{9,8},{10,11... | collective-permute-start | bytes 3932168 | tf_op jit(solution)/shard_map/ppermute | solution.py:253
  5.8 25.9 %all-to-all-start = ((bf16[32,8,1024]{2,1,0:T(8,128)(2,1)}), bf16[32,8,1024]{2,1,0:T(8,128)(2,1)S(1)}, u32[]{:S(2)}, u32[]{:S(2)}) async-start(bf16[32,8,1024]{2,1,0:T(8,128)(2,1)} %fusion), calls=%async_computation | async-start | bytes 1048576 | tf_op jit(solution)/shard_map/all_to_all | solution.py:262
  34.8 17.1 %collective-permute-start.5 = (bf16[640,256]{1,0:T(8,128)(2,1)S(1)}, bf16[640,256]{1,0:T(8,128)(2,1)S(1)}, u32[]{:S(2)}, u32[]{:S(2)}) collective-permute-start(bf16[640,256]{1,0:T(8,128)(2,1)S(1)} %get-tuple-element.38), channel_id=1, source_target_pairs={{0,2},{2,4},{4,6},{6,0},{1,3},{3,5},{5,7},{7,1},{8,10},{10,12},{12... | collective-permute-start | bytes 983048 | tf_op jit(solution)/shard_map/ppermute | solution.py:253
  36.1 15.8 %collective-permute-start.6 = (bf16[640,256]{1,0:T(8,128)(2,1)S(1)}, bf16[640,256]{1,0:T(8,128)(2,1)S(1)}, u32[]{:S(2)}, u32[]{:S(2)}) collective-permute-start(bf16[640,256]{1,0:T(8,128)(2,1)S(1)} %get-tuple-element.39), channel_id=1, source_target_pairs={{0,6},{2,0},{4,2},{6,4},{1,7},{3,1},{5,3},{7,5},{8,14},{10,8},{12,... | collective-permute-start | bytes 983048 | tf_op jit(solution)/shard_map/ppermute | solution.py:253
  37.6 18.1 %all-to-all-start.1 = ((bf16[32,8,512]{2,1,0:T(8,128)(2,1)}), bf16[32,8,512]{2,1,0:T(8,128)(2,1)S(1)}, u32[]{:S(2)}, u32[]{:S(2)}) async-start(bf16[32,8,512]{2,1,0:T(8,128)(2,1)} %bitcast.7), calls=%async_computation.1 | async-start | bytes 524288 | tf_op jit(solution)/shard_map/all_to_all | solution.py:356
  49.2 27.6 %collective-permute-start.7 = (bf16[256,1792]{1,0:T(8,128)(2,1)}, bf16[256,1792]{1,0:T(8,128)(2,1)}, u32[]{:S(2)}, u32[]{:S(2)}) collective-permute-start(bf16[256,1792]{1,0:T(8,128)(2,1)} %get-tuple-element.74), channel_id=1, source_target_pairs={{0,8},{8,16},{16,24},{24,0},{1,9},{9,17},{17,25},{25,1},{2,10},{10... | collective-permute-start | bytes 2752520 | tf_op jit(solution)/shard_map/ppermute | solution.py:253
  50.4 26.4 %collective-permute-start.8 = (bf16[256,1792]{1,0:T(8,128)(2,1)}, bf16[256,1792]{1,0:T(8,128)(2,1)}, u32[]{:S(2)}, u32[]{:S(2)}) collective-permute-start(bf16[256,1792]{1,0:T(8,128)(2,1)} %get-tuple-element.73), channel_id=1, source_target_pairs={{0,24},{8,0},{16,8},{24,16},{1,25},{9,1},{17,9},{25,17},{2,26},{10... | collective-permute-start | bytes 2752520 | tf_op jit(solution)/shard_map/ppermute | solution.py:253
  58.7 16.8 %all-to-all-start.2 = ((bf16[32,8,640]{2,1,0:T(8,128)(2,1)}), bf16[32,8,640]{2,1,0:T(8,128)(2,1)S(1)}, u32[]{:S(2)}, u32[]{:S(2)}) async-start(bf16[32,8,640]{2,1,0:T(8,128)(2,1)} %bitcast.9), calls=%async_computation.2 | async-start | bytes 655360 | tf_op jit(solution)/shard_map/all_to_all | solution.py:374
  76.8 19.2 %all-to-all-start.3 = ((bf16[32,8,1024]{2,1,0:T(8,128)(2,1)}), bf16[32,8,1024]{2,1,0:T(8,128)(2,1)S(1)}, u32[]{:S(2)}, u32[]{:S(2)}) async-start(bf16[32,8,1024]{2,1,0:T(8,128)(2,1)} %shard_map.168), calls=%async_computation.3 | async-start | bytes 1048576 | tf_op jit(solution)/shard_map/all_to_all | solution.py:386
  83.0 20.8 %collective-permute-start.10 = (bf16[256,896]{1,0:T(8,128)(2,1)}, bf16[256,896]{1,0:T(8,128)(2,1)}, u32[]{:S(2)}, u32[]{:S(2)}) collective-permute-start(bf16[256,896]{1,0:T(8,128)(2,1)} %get-tuple-element.76), channel_id=1, source_target_pairs={{0,8},{8,16},{16,24},{24,0},{1,9},{9,17},{17,25},{25,1},{2,10},{10... | collective-permute-start | bytes 1376264 | tf_op jit(solution)/shard_map/ppermute | solution.py:253
  84.3 19.5 %collective-permute-start.11 = (bf16[256,896]{1,0:T(8,128)(2,1)S(1)}, bf16[256,896]{1,0:T(8,128)(2,1)}, u32[]{:S(2)}, u32[]{:S(2)}) collective-permute-start(bf16[256,896]{1,0:T(8,128)(2,1)S(1)} %get-tuple-element.75), channel_id=1, source_target_pairs={{0,24},{8,0},{16,8},{24,16},{1,25},{9,1},{17,9},{25,17},{2,26},{10... | collective-permute-start | bytes 1376264 | tf_op jit(solution)/shard_map/ppermute | solution.py:253
  104.5 9.1 %collective-permute-start.13 = (bf16[256,256]{1,0:T(8,128)(2,1)S(1)}, bf16[256,256]{1,0:T(8,128)(2,1)S(1)}, u32[]{:S(2)}, u32[]{:S(2)}) collective-permute-start(bf16[256,256]{1,0:T(8,128)(2,1)S(1)} %add_convert_fusion.3), channel_id=1, source_target_pairs={{0,2},{2,4},{4,6},{6,0},{1,3},{3,5},{5,7},{7,1},{8,10},{10,12},{12... | collective-permute-start | bytes 393224 | tf_op jit(solution)/shard_map/ppermute | solution.py:253
  107.2 12.2 %collective-permute-start.18 = (bf16[256,896]{1,0:T(8,128)(2,1)}, bf16[256,896]{1,0:T(8,128)(2,1)S(1)}, u32[]{:S(2)}, u32[]{:S(2)}) collective-permute-start(bf16[256,896]{1,0:T(8,128)(2,1)} %collective-permute-done.10), channel_id=1, source_target_pairs={{0,8},{8,16},{16,24},{24,0},{1,9},{9,17},{17,25},{25,1},{2,10},{10... | collective-permute-start | bytes 1376264 | tf_op jit(solution)/shard_map/ppermute | solution.py:253
  107.4 12.0 %collective-permute-start.19 = (bf16[256,896]{1,0:T(8,128)(2,1)}, bf16[256,896]{1,0:T(8,128)(2,1)S(1)}, u32[]{:S(2)}, u32[]{:S(2)}) collective-permute-start(bf16[256,896]{1,0:T(8,128)(2,1)} %collective-permute-done.11), channel_id=1, source_target_pairs={{0,24},{8,0},{16,8},{24,16},{1,25},{9,1},{17,9},{25,17},{2,26},{10... | collective-permute-start | bytes 1376264 | tf_op jit(solution)/shard_map/ppermute | solution.py:253
  113.8 10.8 %collective-permute-start.16 = (bf16[256,256]{1,0:T(8,128)(2,1)S(1)}, bf16[256,256]{1,0:T(8,128)(2,1)S(1)}, u32[]{:S(2)}, u32[]{:S(2)}) collective-permute-start(bf16[256,256]{1,0:T(8,128)(2,1)S(1)} %fusion.3.m0), channel_id=1, source_target_pairs={{0,16},{8,24},{16,0},{24,8},{1,17},{9,25},{17,1},{25,9},{2,18},{10... | collective-permute-start | bytes 393224 | tf_op jit(solution)/shard_map/ppermute | solution.py:253
  129.7 29.5 %all-to-all-start.4 = ((bf16[8,32,1920]{2,1,0:T(8,128)(2,1)}), bf16[8,32,1920]{2,1,0:T(8,128)(2,1)S(1)}, u32[]{:S(2)}, u32[]{:S(2)}) async-start(bf16[8,32,1920]{2,1,0:T(8,128)(2,1)} %bitcast.24), calls=%async_computation.4 | async-start | bytes 1966080 | tf_op jit(solution)/shard_map/all_to_all | solution.py:262
  133.4 15.8 %collective-permute-start.20 = (bf16[896,256]{1,0:T(8,128)(2,1)S(1)}, bf16[896,256]{1,0:T(8,128)(2,1)S(1)}, u32[]{:S(2)}, u32[]{:S(2)}) collective-permute-start(bf16[896,256]{1,0:T(8,128)(2,1)S(1)} %get-tuple-element.52), channel_id=1, source_target_pairs={{0,8},{8,16},{16,24},{24,0},{1,9},{9,17},{17,25},{25,1},{2,10},{10... | collective-permute-start | bytes 1376264 | tf_op jit(solution)/shard_map/ppermute | solution.py:253
  133.5 16.5 %collective-permute-start.21 = (bf16[896,256]{1,0:T(8,128)(2,1)S(1)}, bf16[896,256]{1,0:T(8,128)(2,1)}, u32[]{:S(2)}, u32[]{:S(2)}) collective-permute-start(bf16[896,256]{1,0:T(8,128)(2,1)S(1)} %get-tuple-element.53), channel_id=1, source_target_pairs={{0,24},{8,0},{16,8},{24,16},{1,25},{9,1},{17,9},{25,17},{2,26},{10... | collective-permute-start | bytes 1376264 | tf_op jit(solution)/shard_map/ppermute | solution.py:253
  136.5 12.7 %collective-permute-start.22 = (bf16[448,256]{1,0:T(8,128)(2,1)S(1)}, bf16[448,256]{1,0:T(8,128)(2,1)S(1)}, u32[]{:S(2)}, u32[]{:S(2)}) collective-permute-start(bf16[448,256]{1,0:T(8,128)(2,1)S(1)} %copy-done.17), channel_id=1, source_target_pairs={{0,8},{8,16},{16,24},{24,0},{1,9},{9,17},{17,25},{25,1},{2,10},{10... | collective-permute-start | bytes 688136 | tf_op jit(solution)/shard_map/ppermute | solution.py:253
  136.5 12.7 %collective-permute-start.23 = (bf16[448,256]{1,0:T(8,128)(2,1)S(1)}, bf16[448,256]{1,0:T(8,128)(2,1)S(1)}, u32[]{:S(2)}, u32[]{:S(2)}) collective-permute-start(bf16[448,256]{1,0:T(8,128)(2,1)S(1)} %get-tuple-element.55), channel_id=1, source_target_pairs={{0,24},{8,0},{16,8},{24,16},{1,25},{9,1},{17,9},{25,17},{2,26},{10... | collective-permute-start | bytes 688136 | tf_op jit(solution)/shard_map/ppermute | solution.py:253
  160.3 16.8 %all-to-all-start.5 = ((bf16[8,32,896]{2,1,0:T(8,128)(2,1)}), bf16[8,32,896]{2,1,0:T(8,128)(2,1)S(1)}, u32[]{:S(2)}, u32[]{:S(2)}) async-start(bf16[8,32,896]{2,1,0:T(8,128)(2,1)} %shard_map.170), calls=%async_computation.5 | async-start | bytes 917504 | tf_op jit(solution)/shard_map/all_to_all | solution.py:415
  197.7 8.6 %collective-permute-start.31 = (bf16[256,256]{1,0:T(8,128)(2,1)S(1)}, bf16[256,256]{1,0:T(8,128)(2,1)S(1)}, u32[]{:S(2)}, u32[]{:S(2)}) collective-permute-start(bf16[256,256]{1,0:T(8,128)(2,1)S(1)} %add_convert_fusion.1), channel_id=1, source_target_pairs={{0,2},{2,4},{4,6},{6,0},{1,3},{3,5},{5,7},{7,1},{8,10},{10,12},{12... | collective-permute-start | bytes 393224 | tf_op jit(solution)/shard_map/ppermute | solution.py:253
  (45 other events, 435.7 us)

commit v8 on v7

--- a/solution.py
+++ b/solution.py
@@ -202,13 +202,34 @@
             out_ref[:, :, at : at + HEAD] = mixed
 
 
-def gate_up_kernel(m0, m1, m2, m3, w0, w1, gate2, up2, w3, out_ref):
+def core_rows(place_ref, rows):
+    return (
+        pl.ds(pl.multiple_of(place_ref[1] * rows, rows), rows),
+        pl.ds(pl.multiple_of((1 - place_ref[1]) * rows, rows), rows),
+    )
+
+
+def out_kernel(place_ref, a_ref, w_ref, mine_ref, theirs_ref):
+    mine, theirs = core_rows(place_ref, mine_ref.shape[0])
+    theirs_ref[...] = dot(a_ref[theirs, :], w_ref[...]).astype(BF)
+    mine_ref[...] = dot(a_ref[mine, :], w_ref[...])
+
+
+def gate_up_kernel(place_ref, own_ref, other_ref, w0, w1, gate2, up2, w3, out_ref, m_ref):
     units = gate2.shape[1]
     step = pl.program_id(0)
 
+    @pl.when(step == 0)
+    def _():
+        rows = own_ref.shape[0] // 4
+        mine, theirs = core_rows(place_ref, rows)
+        for d in range(4):
+            m_ref[d, mine, :] = own_ref[d * rows : (d + 1) * rows]
+            m_ref[d, theirs, :] = other_ref[d * rows : (d + 1) * rows]
+
     def product(w2):
-        total = dot(m0[...], w0[...]) + dot(m1[...], w1[...])
-        return (total + dot(m2[...], w2[...]) + dot(m3[...], w3[...])).astype(BF)
+        total = dot(m_ref[0], w0[...]) + dot(m_ref[1], w1[...])
+        return (total + dot(m_ref[2], w2[...]) + dot(m_ref[3], w3[...])).astype(BF)
 
     @pl.when(step == 0)
     def _():
@@ -217,24 +238,40 @@
     @pl.when(step == 1)
     def _():
         out_ref[:, units : 2 * units] = product(up2)
-        square = jnp.zeros((m0.shape[0], 1), F32)
-        for m in (m0, m1, m2, m3):
-            value = m[...].astype(F32)
+        square = jnp.zeros((m_ref.shape[1], 1), F32)
+        for d in range(4):
+            value = m_ref[d].astype(F32)
             square = square + jnp.sum(value * value, axis=1, keepdims=True)
         high = square.astype(BF).astype(F32)
-        lane = lax.broadcasted_iota(jnp.int32, (m0.shape[0], HEAD), 1)
+        lane = lax.broadcasted_iota(jnp.int32, (m_ref.shape[1], HEAD), 1)
         extra = jnp.where(lane == 0, high, jnp.where(lane == 1, square - high, 0.0))
         out_ref[:, 2 * units :] = extra.astype(BF)
 
 
-def down_kernel(a_ref, d0, d1, low2, high2, d3, own_ref, behind_ref, across_ref, ahead_ref):
+def down_kernel(place_ref, a_ref, d0, d1, low2, high2, d3, mine_ref, theirs_ref):
     active = a_ref[...]
     half = low2.shape[0]
-    total = dot(active[:, :half], low2[...]) + dot(active[:, half:], high2[...])
-    across_ref[...] = total.astype(BF)
-    behind_ref[...] = dot(active, d1[...]).astype(BF)
-    ahead_ref[...] = dot(active, d3[...]).astype(BF)
-    own_ref[...] = dot(active, d0[...])
+    rows = mine_ref.shape[1]
+
+    def store(d, total, keep_ref):
+        keep_ref[d] = total
+        theirs_ref[d] = keep_ref[d, core_rows(place_ref, rows)[1], :].astype(BF)
+        mine_ref[d] = keep_ref[d, core_rows(place_ref, rows)[0], :]
+
+    def run(keep_ref):
+        store(0, dot(active, d0[...]), keep_ref)
+        store(1, dot(active, d1[...]), keep_ref)
+        store(2, dot(active[:, :half], low2[...]) + dot(active[:, half:], high2[...]), keep_ref)
+        store(3, dot(active, d3[...]), keep_ref)
+
+    pl.run_scoped(run, pltpu.VMEM((4,) + active.shape[:1] + (d0.shape[1],), F32))
+
+
+def pair_kernel(mine_ref, theirs_ref, own_ref, behind_ref, across_ref, ahead_ref):
+    own_ref[...] = mine_ref[0] + theirs_ref[0].astype(F32)
+    behind_ref[...] = (mine_ref[1] + theirs_ref[1].astype(F32)).astype(BF)
+    across_ref[...] = (mine_ref[2] + theirs_ref[2].astype(F32)).astype(BF)
+    ahead_ref[...] = (mine_ref[3] + theirs_ref[3].astype(F32)).astype(BF)
 
 
 def active_kernel(full_width, parts_ref, out_ref):
@@ -263,12 +300,10 @@
     return out.reshape((n, value.shape[0] // n) + value.shape[1:])
 
 
-def tensor_sum(part, *others):
+def chip_sum(part):
     part = part.astype(BF)
-    pair = (part.astype(F32) + shift(part, "c", 1).astype(F32)).astype(BF)
-    pair = after(pair, *others)
-    ahead, behind, across = shift(pair, "x", 1), shift(pair, "x", -1), shift(pair, "x", 2)
-    return (pair.astype(F32) + across.astype(F32)) + (ahead.astype(F32) + behind.astype(F32))
+    ahead, behind, across = shift(part, "x", 1), shift(part, "x", -1), shift(part, "x", 2)
+    return (part.astype(F32) + across.astype(F32)) + (ahead.astype(F32) + behind.astype(F32))
 
 
 def shards(
@@ -384,22 +419,38 @@
     )(mixed, sel)
     attended = after(attended, wide_1, wide_3)
     attended = lax.all_to_all(attended, GROUP, 0, 0, tiled=True).reshape(all_rows, local_heads)
-    attn_sum = tensor_sum(dot(attended, o_weight), gate_2, up_2)
+    half_rows = all_rows // 2
+    first_row = lax.axis_index("c") * half_rows
+    half_f = lax.dynamic_slice_in_dim(hidden, first_row, half_rows, 0).astype(F32)
+    mine, theirs = pl.pallas_call(
+        out_kernel,
+        in_specs=[smem(), vmem(), vmem()],
+        out_specs=[vmem()] * 2,
+        out_shape=[
+            jax.ShapeDtypeStruct((half_rows, width_part), F32),
+            jax.ShapeDtypeStruct((half_rows, width_part), BF),
+        ],
+        compiler_params=params(),
+    )(place, attended, o_weight)
+    pair = (mine + shift(theirs, "c", 1).astype(F32)).astype(BF)
+    attn_sum = chip_sum(after(pair, gate_2, up_2))
     gate_2, up_2 = shift(gate_2, "y", 1), shift(up_2, "y", -1)
-    middle = (hidden_f + jnp.tanh(gate_logits[0]) * attn_sum).astype(BF)
+    middle = (half_f + jnp.tanh(gate_logits[0]) * attn_sum).astype(BF)
     middle_f = middle.astype(F32)
-    middles = [middle] + [shift(middle, "y", d) for d in (1, 2, 3)]
-    block = pl.BlockSpec((all_rows, width_part), lambda i: (0, 0))
+    own_rows_all = jnp.concatenate([middle] + [shift(middle, "y", d) for d in (1, 2, 3)], axis=0)
+    other_rows_all = shift(own_rows_all, "c", 1)
+    block = pl.BlockSpec((4 * half_rows, width_part), lambda i: (0, 0))
     direct = pl.BlockSpec((width_part, units), lambda i: (0, i))
     passed = pl.BlockSpec((width_part, units), lambda i: (0, 0))
     gate_up = pl.pallas_call(
         gate_up_kernel,
         grid=(2,),
-        in_specs=[block] * 4 + [direct] * 2 + [passed] * 2 + [direct],
+        in_specs=[smem()] + [block] * 2 + [direct] * 2 + [passed] * 2 + [direct],
         out_specs=pl.BlockSpec((all_rows, 2 * units + HEAD), lambda i: (0, 0)),
         out_shape=jax.ShapeDtypeStruct((all_rows, 2 * units + HEAD), BF),
+        scratch_shapes=[pltpu.VMEM((4, all_rows, width_part), BF)],
         compiler_params=params(LARGE_VMEM_BYTES),
-    )(*middles, wide_0, wide_1, gate_2, up_2, wide_3)
+    )(place, own_rows_all, other_rows_all, wide_0, wide_1, gate_2, up_2, wide_3)
     down_1, down_3, *down_2 = lax.optimization_barrier((down_1, down_3, *down_2, gate_up))[:4]
     down_1, down_3 = shift(down_1, "y", 1), shift(down_3, "y", -1)
     down_2 = shift(down_2[0], "y", 1), shift(down_2[1], "y", -1)
@@ -413,21 +464,33 @@
         compiler_params=params(),
     )(parts)
     active = lax.all_to_all(active, "z", 0, 0, tiled=True).reshape(all_rows, units)
+    mine, theirs = pl.pallas_call(
+        down_kernel,
+        in_specs=[smem()] + [vmem()] * 6,
+        out_specs=[vmem()] * 2,
+        out_shape=[
+            jax.ShapeDtypeStruct((4, half_rows, width_part), F32),
+            jax.ShapeDtypeStruct((4, half_rows, width_part), BF),
+        ],
+        compiler_params=params(LARGE_VMEM_BYTES),
+    )(place, active, down_0, down_1, *down_2, down_3)
     own_down, behind, across, ahead = pl.pallas_call(
-        down_kernel,
-        in_specs=[vmem()] * 6,
+        pair_kernel,
+        in_specs=[vmem()] * 2,
         out_specs=[vmem()] * 4,
-        out_shape=[jax.ShapeDtypeStruct((all_rows, width_part), F32)]
-        + [jax.ShapeDtypeStruct((all_rows, width_part), BF)] * 3,
-        compiler_params=params(LARGE_VMEM_BYTES),
-    )(active, down_0, down_1, *down_2, down_3)
+        out_shape=[jax.ShapeDtypeStruct((half_rows, width_part), F32)]
+        + [jax.ShapeDtypeStruct((half_rows, width_part), BF)] * 3,
+        compiler_params=params(),
+    )(mine, shift(theirs, "c", 1))
     across, behind, ahead = shift(across, "y", 2), shift(behind, "y", -1), shift(ahead, "y", 1)
-    down_part = own_down + across.astype(F32) + behind.astype(F32) + ahead.astype(F32)
-    down_sum = tensor_sum(down_part)
-    row_request = jnp.arange(all_rows, dtype=jnp.int32) // STEPS
+    down_sum = chip_sum(own_down + across.astype(F32) + behind.astype(F32) + ahead.astype(F32))
+    row_request = (jnp.arange(half_rows, dtype=jnp.int32) + first_row) // STEPS
     request_ids = (image_groups * (own_rows // STEPS) + image_requests).reshape(-1)
     has_image = jnp.any(row_request[:, None] == request_ids[None, :], axis=1).astype(F32)
-    return (middle_f + jnp.tanh(gate_logits[1]) * has_image[:, None] * down_sum).astype(BF)
+    output = (middle_f + jnp.tanh(gate_logits[1]) * has_image[:, None] * down_sum).astype(BF)
+    swapped = shift(output, "c", 1)
+    lower = lax.axis_index("c") == 0
+    return jnp.concatenate((jnp.where(lower, output, swapped), jnp.where(lower, swapped, output)), axis=0)
 
 
 def solution(mesh):

time: 208 us -> 208 us (level)
  waiting for transfers between devices: 74.2 us -> 70.1 us
  starting transfers between devices: 86.8 us -> 90.5 us
    ppermute x33 -> x35, starting transfers between devices: 52 us -> 55.7 us  [shift(): return lax.ppermute(value, axis, [(i, (i + by) % n) for i in range(n)])]
    all_to_all x2, waiting for transfers between devices: 12.3 us -> 9.72 us  [exchange(): out = lax.all_to_all(value, axis, 0, 0, tiled=True)]
    ppermute x33 -> x35, waiting for transfers between devices: 34.7 us -> 33.4 us  [shift(): return lax.ppermute(value, axis, [(i, (i + by) % n) for i in range(n)])]
    pallas_call x2 -> x4, Pallas kernels: 7.39 us -> 8.56 us  [the longest x1 4.33 us: shards(): pl.pallas_call(gate_up_kernel, grid=(2,), in_specs=[smem()] + [block] * 2...]
    unnamed x63 -> x61, local copies, waits for them, and re-layouts: 5.92 us -> 6.95 us
  transfers between devices with their start and end apart: 39 -> 41, of which waited for: 18 -> 19; matrix products, arithmetic and copies ran while one was open for 7% -> 7% of each run, Pallas kernels for 7% -> 7%
where the time goes in v8:
time: 208 us; the launch traced here: 207 us
  starting transfers between devices  90.5 us (44%)
  waiting for transfers between devices  70.1 us (34%)
  Pallas kernels  23.4 us (11%)
  local copies, waits for them, and re-layouts  13.9 us (7%)
  other arithmetic  5.84 us (3%)
    ppermute x35, starting transfers between devices, shift(): return lax.ppermute(value, axis, [(i, (i + by) % n) for i in range(n)])  55.7 us
    ppermute x35, waiting for transfers between devices, shift(): return lax.ppermute(value, axis, [(i, (i + by) % n) for i in range(n)])  33.4 us
    all_to_all x2, starting transfers between devices, exchange(): out = lax.all_to_all(value, axis, 0, 0, tiled=True)  13 us
    all_to_all x1, waiting for transfers between devices, shards(): lax.all_to_all(attended, GROUP, 0, 0, tiled=True)  10.1 us
    all_to_all x2, waiting for transfers between devices, exchange(): out = lax.all_to_all(value, axis, 0, 0, tiled=True)  9.72 us
    pallas_call x1, Pallas kernels, kv_project(): pl.pallas_call(kv_kernel, grid_spec=pltpu.PrefetchScalarGridSpec(num_scal...  7.97 us
    all_to_all x1, starting transfers between devices, shards(): queries = lax.all_to_all(queries, GROUP, 0, 0, tiled=True)  7.64 us
    unnamed x61, local copies, waits for them, and re-layouts  6.95 us
  transfers between devices with their start and end apart: 41, of which 19 were waited for; matrix products, arithmetic and copies ran while one was open for 7% of the time, Pallas kernels for 7%

profile of v8, /device:TPU:1, one launch (start us, length us, event | category | flops | bytes accessed | tf_op | source)
XLA Modules:
  0.0 207.5 jit_solution(13646202523457319062)
XLA Ops:
  0.0 3.2 %collective-permute-start.1 = (bf16[1024,1024]{1,0:T(8,128)(2,1)}, bf16[1024,1024]{1,0:T(8,128)(2,1)S(1)}, u32[]{:S(2)}, u32[]{:S(2)}) collective-permute-start(bf16[1024,1024]{1,0:T(8,128)(2,1)} %k0.1), channel_id=1, source_target_pairs={{0,1},{1,0},{2,3},{3,2},{4,5},{5,4},{6,7},{7,6},{8,9},{9,8},{10,11... | collective-permute-start | bytes 6291464 | tf_op jit(solution)/shard_map/ppermute | solution.py:290
  5.8 9.5 %all-to-all-start = ((bf16[32,8,1024]{2,1,0:T(8,128)(2,1)}), bf16[32,8,1024]{2,1,0:T(8,128)(2,1)S(1)}, u32[]{:S(2)}, u32[]{:S(2)}) async-start(bf16[32,8,1024]{2,1,0:T(8,128)(2,1)} %fusion), calls=%async_computation | async-start | bytes 1048576 | tf_op jit(solution)/shard_map/all_to_all | solution.py:299
  17.2 8.0 %shard_map.163 = (bf16[320,256]{1,0:T(8,128)(2,1)}, bf16[320,256]{1,0:T(8,128)(2,1)}, bf16[640,256]{1,0:T(8,128)(2,1)}, bf16[640,256]{1,0:T(8,128)(2,1)}, bf16[640,256]{1,0:T(8,128)(2,1)}) custom-call(s32[2]{0:T(128)} %pad_add_fusion.place_ref, bf16[640,1024]{1,0:T(8,128)(2,1)} %x0.1, bf16[640,1024]{1,0:T(8,128)(2,1)} %collective-permute-done.x1, ...), custom_call_target="tpu_custom_call" | custom-call | tf_op jit(solution)/shard_map/pallas_call | solution.py:109
  28.7 3.0 %all-to-all-done.parts_ref = bf16[32,8,1024]{2,1,0:T(8,128)(2,1)S(1)} async-done(((bf16[32,8,1024]{2,1,0:T(8,128)(2,1)}), bf16[32,8,1024]{2,1,0:T(8,128)(2,1)S(1)}, u32[]{:S(2)}, u32[]{:S(2)}) %all-to-all-start) | async-done | bytes 524320 | tf_op jit(solution)/shard_map/all_to_all | solution.py:299
  37.6 7.6 %all-to-all-start.1 = ((bf16[32,8,512]{2,1,0:T(8,128)(2,1)}), bf16[32,8,512]{2,1,0:T(8,128)(2,1)S(1)}, u32[]{:S(2)}, u32[]{:S(2)}) async-start(bf16[32,8,512]{2,1,0:T(8,128)(2,1)} %bitcast.7), calls=%async_computation.1 | async-start | bytes 524288 | tf_op jit(solution)/shard_map/all_to_all | solution.py:391
  52.0 3.7 %all-to-all-done.1 = bf16[32,8,512]{2,1,0:T(8,128)(2,1)S(1)} async-done(((bf16[32,8,512]{2,1,0:T(8,128)(2,1)}), bf16[32,8,512]{2,1,0:T(8,128)(2,1)S(1)}, u32[]{:S(2)}, u32[]{:S(2)}) %all-to-all-start.1) | async-done | bytes 262176 | tf_op jit(solution)/shard_map/all_to_all | solution.py:391
  55.7 3.0 %shard_map.167 = bf16[256,640]{1,0:T(8,128)(2,1)} custom-call(s32[1]{0:T(128)} %bitcast.3.me_ref, s32[32,4]{1,0:T(8,128)S(1)} %copy.27.tiles_ref, bf16[640,256]{1,0:T(8,128)(2,1)S(1)} %copy-done.3, bf16[640,256]{1,0:T(8,128)(2,1)S(1)} %collective-permute-done.5.left_ref, bf16[640,256]{1,0:T(8,128)(2,1)S(1)} %collective-permute-done.6.right_ref, ...), custom_call_target="tpu_custom_call" | custom-call | tf_op jit(solution)/shard_map/pallas_call | solution.py:393
  58.7 4.3 %all-to-all-start.2 = ((bf16[32,8,640]{2,1,0:T(8,128)(2,1)}), bf16[32,8,640]{2,1,0:T(8,128)(2,1)S(1)}, u32[]{:S(2)}, u32[]{:S(2)}) async-start(bf16[32,8,640]{2,1,0:T(8,128)(2,1)} %bitcast.9), calls=%async_computation.2 | async-start | bytes 655360 | tf_op jit(solution)/shard_map/all_to_all | solution.py:409
  69.2 6.3 %all-to-all-done.2 = bf16[32,8,640]{2,1,0:T(8,128)(2,1)S(1)} async-done(((bf16[32,8,640]{2,1,0:T(8,128)(2,1)}), bf16[32,8,640]{2,1,0:T(8,128)(2,1)S(1)}, u32[]{:S(2)}, u32[]{:S(2)}) %all-to-all-start.2) | async-done | bytes 327712 | tf_op jit(solution)/shard_map/all_to_all | solution.py:409
  76.8 6.2 %all-to-all-start.3 = ((bf16[32,8,1024]{2,1,0:T(8,128)(2,1)}), bf16[32,8,1024]{2,1,0:T(8,128)(2,1)S(1)}, u32[]{:S(2)}, u32[]{:S(2)}) async-start(bf16[32,8,1024]{2,1,0:T(8,128)(2,1)} %shard_map.168), calls=%async_computation.3 | async-start | bytes 1048576 | tf_op jit(solution)/shard_map/all_to_all | solution.py:421
  85.8 10.1 %all-to-all-done.3 = bf16[32,8,1024]{2,1,0:T(8,128)(2,1)S(1)} async-done(((bf16[32,8,1024]{2,1,0:T(8,128)(2,1)}), bf16[32,8,1024]{2,1,0:T(8,128)(2,1)S(1)}, u32[]{:S(2)}, u32[]{:S(2)}) %all-to-all-start.3) | async-done | bytes 524320 | tf_op jit(solution)/shard_map/all_to_all | solution.py:421
  96.7 6.5 %collective-permute-start.9 = (bf16[128,256]{1,0:T(8,128)(2,1)S(1)}, bf16[128,256]{1,0:T(8,128)(2,1)S(1)}, u32[]{:S(2)}, u32[]{:S(2)}) collective-permute-start(bf16[128,256]{1,0:T(8,128)(2,1)S(1)} %get-tuple-element.56), channel_id=1, source_target_pairs={{0,1},{1,0},{2,3},{3,2},{4,5},{5,4},{6,7},{7,6},{8,9},{9,8},{10,11... | collective-permute-start | bytes 196616 | tf_op jit(solution)/shard_map/ppermute | solution.py:290
  114.6 8.2 %collective-permute-done.15 = bf16[128,256]{1,0:T(8,128)(2,1)S(1)} collective-permute-done((bf16[128,256]{1,0:T(8,128)(2,1)S(1)}, bf16[128,256]{1,0:T(8,128)(2,1)S(1)}, u32[]{:S(2)}, u32[]{:S(2)}) %collective-permute-start.15) | collective-permute-done | bytes 65568 | tf_op jit(solution)/shard_map/ppermute | solution.py:290
  128.3 4.3 %shard_map.170 = bf16[256,1920]{1,0:T(8,128)(2,1)} custom-call(s32[2]{0:T(128)} %pad_add_fusion.place_ref, bf16[512,256]{1,0:T(8,128)(2,1)} %copy-done.11, bf16[512,256]{1,0:T(8,128)(2,1)} %copy-done.17, bf16[256,1792]{1,0:T(8,128)(2,1)} %get-tuple-element.82.w0, bf16[256,1792]{1,0:T(8,128)(2,1)} %collective-permute-done.7.w1, bf16[256,896]{1,0:T(8,128)(2,1)} %copy-done.14, ...), custom_call_target="tpu_custom_call" | custom-call | tf_op jit(solution)/shard_map/pallas_call | solution.py:445
  132.6 3.6 %all-to-all-start.4 = ((bf16[8,32,1920]{2,1,0:T(8,128)(2,1)}), bf16[8,32,1920]{2,1,0:T(8,128)(2,1)S(1)}, u32[]{:S(2)}, u32[]{:S(2)}) async-start(bf16[8,32,1920]{2,1,0:T(8,128)(2,1)} %bitcast.22), calls=%async_computation.4 | async-start | bytes 1966080 | tf_op jit(solution)/shard_map/all_to_all | solution.py:299
  136.4 2.8 %collective-permute-start.22 = (bf16[896,256]{1,0:T(8,128)(2,1)S(1)}, bf16[896,256]{1,0:T(8,128)(2,1)S(1)}, u32[]{:S(2)}, u32[]{:S(2)}) collective-permute-start(bf16[896,256]{1,0:T(8,128)(2,1)S(1)} %get-tuple-element.59), channel_id=1, source_target_pairs={{0,24},{8,0},{16,8},{24,16},{1,25},{9,1},{17,9},{25,17},{2,26},{10... | collective-permute-start | bytes 1376264 | tf_op jit(solution)/shard_map/ppermute | solution.py:290
  141.9 12.2 %collective-permute-done.23 = bf16[448,256]{1,0:T(8,128)(2,1)S(1)} collective-permute-done((bf16[448,256]{1,0:T(8,128)(2,1)}, bf16[448,256]{1,0:T(8,128)(2,1)S(1)}, u32[]{:S(2)}, u32[]{:S(2)}) %collective-permute-start.23) | collective-permute-done | bytes 229408 | tf_op jit(solution)/shard_map/ppermute | solution.py:290
  154.9 6.7 %all-to-all-done.4.parts_ref = bf16[8,32,1920]{2,1,0:T(8,128)(2,1)S(1)} async-done(((bf16[8,32,1920]{2,1,0:T(8,128)(2,1)}), bf16[8,32,1920]{2,1,0:T(8,128)(2,1)S(1)}, u32[]{:S(2)}, u32[]{:S(2)}) %all-to-all-start.4) | async-done | bytes 983072 | tf_op jit(solution)/shard_map/all_to_all | solution.py:299
  162.6 3.6 %all-to-all-start.5 = ((bf16[8,32,896]{2,1,0:T(8,128)(2,1)}), bf16[8,32,896]{2,1,0:T(8,128)(2,1)S(1)}, u32[]{:S(2)}, u32[]{:S(2)}) async-start(bf16[8,32,896]{2,1,0:T(8,128)(2,1)} %shard_map.171), calls=%async_computation.5 | async-start | bytes 917504 | tf_op jit(solution)/shard_map/all_to_all | solution.py:466
  169.1 3.3 %collective-permute-done.25.low2 = bf16[448,256]{1,0:T(8,128)(2,1)S(1)} collective-permute-done((bf16[448,256]{1,0:T(8,128)(2,1)S(1)}, bf16[448,256]{1,0:T(8,128)(2,1)S(1)}, u32[]{:S(2)}, u32[]{:S(2)}) %collective-permute-start.25) | collective-permute-done | bytes 229408 | tf_op jit(solution)/shard_map/ppermute | solution.py:290
  172.4 6.9 %all-to-all-done.5 = bf16[8,32,896]{2,1,0:T(8,128)(2,1)S(1)} async-done(((bf16[8,32,896]{2,1,0:T(8,128)(2,1)}), bf16[8,32,896]{2,1,0:T(8,128)(2,1)S(1)}, u32[]{:S(2)}, u32[]{:S(2)}) %all-to-all-start.5) | async-done | bytes 458784 | tf_op jit(solution)/shard_map/all_to_all | solution.py:466
  180.1 3.3 %shard_map.172 = (f32[4,128,256]{2,1,0:T(8,128)}, bf16[4,128,256]{2,1,0:T(8,128)(2,1)}) custom-call(s32[2]{0:T(128)} %pad_add_fusion.place_ref, bf16[256,896]{1,0:T(8,128)(2,1)} %bitcast.23, bf16[896,256]{1,0:T(8,128)(2,1)} %get-tuple-element.69.d0, bf16[896,256]{1,0:T(8,128)(2,1)} %copy-done.12, bf16[448,256]{1,0:T(8,128)(2,1)} %copy-done.18, ...), custom_call_target="tpu_custom_call" | custom-call | tf_op jit(solution)/shard_map/pallas_call | solution.py:467
  183.4 4.0 %collective-permute-start.27 = (bf16[4,128,256]{2,1,0:T(8,128)(2,1)}, bf16[4,128,256]{2,1,0:T(8,128)(2,1)S(1)}, u32[]{:S(2)}, u32[]{:S(2)}) collective-permute-start(bf16[4,128,256]{2,1,0:T(8,128)(2,1)} %get-tuple-element.64), channel_id=1, source_target_pairs={{0,1},{1,0},{2,3},{3,2},{4,5},{5,4},{6,7},{7,6},{8,9},{9,8},{10,11... | collective-permute-start | bytes 786440 | tf_op jit(solution)/shard_map/ppermute | solution.py:290
  202.6 3.3 %collective-permute-start.34 = (bf16[128,256]{1,0:T(8,128)(2,1)S(1)}, bf16[128,256]{1,0:T(8,128)(2,1)S(1)}, u32[]{:S(2)}, u32[]{:S(2)}) collective-permute-start(bf16[128,256]{1,0:T(8,128)(2,1)S(1)} %add_convert_fusion), channel_id=1, source_target_pairs={{0,1},{1,0},{2,3},{3,2},{4,5},{5,4},{6,7},{7,6},{8,9},{9,8},{10,11... | collective-permute-start | bytes 196616 | tf_op jit(solution)/shard_map/ppermute | solution.py:290
  (153 shorter events, 72.1 us)
Async XLA Ops:
  0.0 15.9 %collective-permute-start.1 = (bf16[1024,1024]{1,0:T(8,128)(2,1)}, bf16[1024,1024]{1,0:T(8,128)(2,1)S(1)}, u32[]{:S(2)}, u32[]{:S(2)}) collective-permute-start(bf16[1024,1024]{1,0:T(8,128)(2,1)} %k0.1), channel_id=1, source_target_pairs={{0,1},{1,0},{2,3},{3,2},{4,5},{5,4},{6,7},{7,6},{8,9},{9,8},{10,11... | collective-permute-start | bytes 6291464 | tf_op jit(solution)/shard_map/ppermute | solution.py:290
  3.2 12.6 %collective-permute-start.2 = (bf16[1024,1024]{1,0:T(8,128)(2,1)}, bf16[1024,1024]{1,0:T(8,128)(2,1)}, u32[]{:S(2)}, u32[]{:S(2)}) collective-permute-start(bf16[1024,1024]{1,0:T(8,128)(2,1)} %v0.1), channel_id=1, source_target_pairs={{0,1},{1,0},{2,3},{3,2},{4,5},{5,4},{6,7},{7,6},{8,9},{9,8},{10,11... | collective-permute-start | bytes 6291464 | tf_op jit(solution)/shard_map/ppermute | solution.py:290
  3.2 12.6 %collective-permute-start = (bf16[640,1024]{1,0:T(8,128)(2,1)}, bf16[640,1024]{1,0:T(8,128)(2,1)}, u32[]{:S(2)}, u32[]{:S(2)}) collective-permute-start(bf16[640,1024]{1,0:T(8,128)(2,1)} %x0.1), channel_id=1, source_target_pairs={{0,1},{1,0},{2,3},{3,2},{4,5},{5,4},{6,7},{7,6},{8,9},{9,8},{10,11... | collective-permute-start | bytes 3932168 | tf_op jit(solution)/shard_map/ppermute | solution.py:290
  5.8 25.9 %all-to-all-start = ((bf16[32,8,1024]{2,1,0:T(8,128)(2,1)}), bf16[32,8,1024]{2,1,0:T(8,128)(2,1)S(1)}, u32[]{:S(2)}, u32[]{:S(2)}) async-start(bf16[32,8,1024]{2,1,0:T(8,128)(2,1)} %fusion), calls=%async_computation | async-start | bytes 1048576 | tf_op jit(solution)/shard_map/all_to_all | solution.py:299
  34.9 17.1 %collective-permute-start.5 = (bf16[640,256]{1,0:T(8,128)(2,1)S(1)}, bf16[640,256]{1,0:T(8,128)(2,1)S(1)}, u32[]{:S(2)}, u32[]{:S(2)}) collective-permute-start(bf16[640,256]{1,0:T(8,128)(2,1)S(1)} %get-tuple-element.42), channel_id=1, source_target_pairs={{0,2},{2,4},{4,6},{6,0},{1,3},{3,5},{5,7},{7,1},{8,10},{10,12},{12... | collective-permute-start | bytes 983048 | tf_op jit(solution)/shard_map/ppermute | solution.py:290
  36.1 15.8 %collective-permute-start.6 = (bf16[640,256]{1,0:T(8,128)(2,1)S(1)}, bf16[640,256]{1,0:T(8,128)(2,1)S(1)}, u32[]{:S(2)}, u32[]{:S(2)}) collective-permute-start(bf16[640,256]{1,0:T(8,128)(2,1)S(1)} %get-tuple-element.43), channel_id=1, source_target_pairs={{0,6},{2,0},{4,2},{6,4},{1,7},{3,1},{5,3},{7,5},{8,14},{10,8},{12,... | collective-permute-start | bytes 983048 | tf_op jit(solution)/shard_map/ppermute | solution.py:290
  37.6 18.1 %all-to-all-start.1 = ((bf16[32,8,512]{2,1,0:T(8,128)(2,1)}), bf16[32,8,512]{2,1,0:T(8,128)(2,1)S(1)}, u32[]{:S(2)}, u32[]{:S(2)}) async-start(bf16[32,8,512]{2,1,0:T(8,128)(2,1)} %bitcast.7), calls=%async_computation.1 | async-start | bytes 524288 | tf_op jit(solution)/shard_map/all_to_all | solution.py:391
  49.2 27.6 %collective-permute-start.7 = (bf16[256,1792]{1,0:T(8,128)(2,1)}, bf16[256,1792]{1,0:T(8,128)(2,1)}, u32[]{:S(2)}, u32[]{:S(2)}) collective-permute-start(bf16[256,1792]{1,0:T(8,128)(2,1)} %get-tuple-element.84), channel_id=1, source_target_pairs={{0,8},{8,16},{16,24},{24,0},{1,9},{9,17},{17,25},{25,1},{2,10},{10... | collective-permute-start | bytes 2752520 | tf_op jit(solution)/shard_map/ppermute | solution.py:290
  50.4 26.4 %collective-permute-start.8 = (bf16[256,1792]{1,0:T(8,128)(2,1)}, bf16[256,1792]{1,0:T(8,128)(2,1)}, u32[]{:S(2)}, u32[]{:S(2)}) collective-permute-start(bf16[256,1792]{1,0:T(8,128)(2,1)} %get-tuple-element.83), channel_id=1, source_target_pairs={{0,24},{8,0},{16,8},{24,16},{1,25},{9,1},{17,9},{25,17},{2,26},{10... | collective-permute-start | bytes 2752520 | tf_op jit(solution)/shard_map/ppermute | solution.py:290
  58.7 16.8 %all-to-all-start.2 = ((bf16[32,8,640]{2,1,0:T(8,128)(2,1)}), bf16[32,8,640]{2,1,0:T(8,128)(2,1)S(1)}, u32[]{:S(2)}, u32[]{:S(2)}) async-start(bf16[32,8,640]{2,1,0:T(8,128)(2,1)} %bitcast.9), calls=%async_computation.2 | async-start | bytes 655360 | tf_op jit(solution)/shard_map/all_to_all | solution.py:409
  76.8 19.1 %all-to-all-start.3 = ((bf16[32,8,1024]{2,1,0:T(8,128)(2,1)}), bf16[32,8,1024]{2,1,0:T(8,128)(2,1)S(1)}, u32[]{:S(2)}, u32[]{:S(2)}) async-start(bf16[32,8,1024]{2,1,0:T(8,128)(2,1)} %shard_map.168), calls=%async_computation.3 | async-start | bytes 1048576 | tf_op jit(solution)/shard_map/all_to_all | solution.py:421
  83.0 21.1 %collective-permute-start.10 = (bf16[256,896]{1,0:T(8,128)(2,1)}, bf16[256,896]{1,0:T(8,128)(2,1)}, u32[]{:S(2)}, u32[]{:S(2)}) collective-permute-start(bf16[256,896]{1,0:T(8,128)(2,1)} %get-tuple-element.86), channel_id=1, source_target_pairs={{0,8},{8,16},{16,24},{24,0},{1,9},{9,17},{17,25},{25,1},{2,10},{10... | collective-permute-start | bytes 1376264 | tf_op jit(solution)/shard_map/ppermute | solution.py:290
  84.3 19.8 %collective-permute-start.11 = (bf16[256,896]{1,0:T(8,128)(2,1)S(1)}, bf16[256,896]{1,0:T(8,128)(2,1)}, u32[]{:S(2)}, u32[]{:S(2)}) collective-permute-start(bf16[256,896]{1,0:T(8,128)(2,1)S(1)} %get-tuple-element.85), channel_id=1, source_target_pairs={{0,24},{8,0},{16,8},{24,16},{1,25},{9,1},{17,9},{25,17},{2,26},{10... | collective-permute-start | bytes 1376264 | tf_op jit(solution)/shard_map/ppermute | solution.py:290
  109.0 17.4 %collective-permute-start.19 = (bf16[256,896]{1,0:T(8,128)(2,1)}, bf16[256,896]{1,0:T(8,128)(2,1)S(1)}, u32[]{:S(2)}, u32[]{:S(2)}) collective-permute-start(bf16[256,896]{1,0:T(8,128)(2,1)} %collective-permute-done.10), channel_id=1, source_target_pairs={{0,8},{8,16},{16,24},{24,0},{1,9},{9,17},{17,25},{25,1},{2,10},{10... | collective-permute-start | bytes 1376264 | tf_op jit(solution)/shard_map/ppermute | solution.py:290
  109.3 17.1 %collective-permute-start.20 = (bf16[256,896]{1,0:T(8,128)(2,1)}, bf16[256,896]{1,0:T(8,128)(2,1)S(1)}, u32[]{:S(2)}, u32[]{:S(2)}) collective-permute-start(bf16[256,896]{1,0:T(8,128)(2,1)} %collective-permute-done.11), channel_id=1, source_target_pairs={{0,24},{8,0},{16,8},{24,16},{1,25},{9,1},{17,9},{25,17},{2,26},{10... | collective-permute-start | bytes 1376264 | tf_op jit(solution)/shard_map/ppermute | solution.py:290
  111.9 11.0 %collective-permute-start.15 = (bf16[128,256]{1,0:T(8,128)(2,1)S(1)}, bf16[128,256]{1,0:T(8,128)(2,1)S(1)}, u32[]{:S(2)}, u32[]{:S(2)}) collective-permute-start(bf16[128,256]{1,0:T(8,128)(2,1)S(1)} %add_convert_fusion.2), channel_id=1, source_target_pairs={{0,8},{8,16},{16,24},{24,0},{1,9},{9,17},{17,25},{25,1},{2,10},{10... | collective-permute-start | bytes 196616 | tf_op jit(solution)/shard_map/ppermute | solution.py:290
  111.9 11.8 %collective-permute-start.16 = (bf16[128,256]{1,0:T(8,128)(2,1)S(1)}, bf16[128,256]{1,0:T(8,128)(2,1)S(1)}, u32[]{:S(2)}, u32[]{:S(2)}) collective-permute-start(bf16[128,256]{1,0:T(8,128)(2,1)S(1)} %add_convert_fusion.2), channel_id=1, source_target_pairs={{0,16},{8,24},{16,0},{24,8},{1,17},{9,25},{17,1},{25,9},{2,18},{10... | collective-permute-start | bytes 196616 | tf_op jit(solution)/shard_map/ppermute | solution.py:290
  113.3 10.5 %collective-permute-start.17 = (bf16[128,256]{1,0:T(8,128)(2,1)S(1)}, bf16[128,256]{1,0:T(8,128)(2,1)S(1)}, u32[]{:S(2)}, u32[]{:S(2)}) collective-permute-start(bf16[128,256]{1,0:T(8,128)(2,1)S(1)} %add_convert_fusion.2), channel_id=1, source_target_pairs={{0,24},{8,0},{16,8},{24,16},{1,25},{9,1},{17,9},{25,17},{2,26},{10... | collective-permute-start | bytes 196616 | tf_op jit(solution)/shard_map/ppermute | solution.py:290
  132.6 29.0 %all-to-all-start.4 = ((bf16[8,32,1920]{2,1,0:T(8,128)(2,1)}), bf16[8,32,1920]{2,1,0:T(8,128)(2,1)S(1)}, u32[]{:S(2)}, u32[]{:S(2)}) async-start(bf16[8,32,1920]{2,1,0:T(8,128)(2,1)} %bitcast.22), calls=%async_computation.4 | async-start | bytes 1966080 | tf_op jit(solution)/shard_map/all_to_all | solution.py:299
  136.1 17.9 %collective-permute-start.21 = (bf16[896,256]{1,0:T(8,128)(2,1)S(1)}, bf16[896,256]{1,0:T(8,128)(2,1)S(1)}, u32[]{:S(2)}, u32[]{:S(2)}) collective-permute-start(bf16[896,256]{1,0:T(8,128)(2,1)S(1)} %get-tuple-element.58), channel_id=1, source_target_pairs={{0,8},{8,16},{16,24},{24,0},{1,9},{9,17},{17,25},{25,1},{2,10},{10... | collective-permute-start | bytes 1376264 | tf_op jit(solution)/shard_map/ppermute | solution.py:290
  136.4 18.5 %collective-permute-start.22 = (bf16[896,256]{1,0:T(8,128)(2,1)S(1)}, bf16[896,256]{1,0:T(8,128)(2,1)S(1)}, u32[]{:S(2)}, u32[]{:S(2)}) collective-permute-start(bf16[896,256]{1,0:T(8,128)(2,1)S(1)} %get-tuple-element.59), channel_id=1, source_target_pairs={{0,24},{8,0},{16,8},{24,16},{1,25},{9,1},{17,9},{25,17},{2,26},{10... | collective-permute-start | bytes 1376264 | tf_op jit(solution)/shard_map/ppermute | solution.py:290
  139.2 14.9 %collective-permute-start.23 = (bf16[448,256]{1,0:T(8,128)(2,1)}, bf16[448,256]{1,0:T(8,128)(2,1)S(1)}, u32[]{:S(2)}, u32[]{:S(2)}) collective-permute-start(bf16[448,256]{1,0:T(8,128)(2,1)} %get-tuple-element.60), channel_id=1, source_target_pairs={{0,8},{8,16},{16,24},{24,0},{1,9},{9,17},{17,25},{25,1},{2,10},{10... | collective-permute-start | bytes 688136 | tf_op jit(solution)/shard_map/ppermute | solution.py:290
  139.2 14.9 %collective-permute-start.24 = (bf16[448,256]{1,0:T(8,128)(2,1)}, bf16[448,256]{1,0:T(8,128)(2,1)S(1)}, u32[]{:S(2)}, u32[]{:S(2)}) collective-permute-start(bf16[448,256]{1,0:T(8,128)(2,1)} %get-tuple-element.61), channel_id=1, source_target_pairs={{0,24},{8,0},{16,8},{24,16},{1,25},{9,1},{17,9},{25,17},{2,26},{10... | collective-permute-start | bytes 688136 | tf_op jit(solution)/shard_map/ppermute | solution.py:290
  162.6 16.7 %all-to-all-start.5 = ((bf16[8,32,896]{2,1,0:T(8,128)(2,1)}), bf16[8,32,896]{2,1,0:T(8,128)(2,1)S(1)}, u32[]{:S(2)}, u32[]{:S(2)}) async-start(bf16[8,32,896]{2,1,0:T(8,128)(2,1)} %shard_map.171), calls=%async_computation.5 | async-start | bytes 917504 | tf_op jit(solution)/shard_map/all_to_all | solution.py:466
  (46 other events, 399.9 us)

commit v9 on v8

--- a/solution.py
+++ b/solution.py
@@ -15,6 +15,7 @@
 SLOTS = 2
 STEPS = 2
 EPS = 1e-05
+QUARTERS_SENT = (1, 3, 2)
 VMEM_BYTES = 16 * 1024 * 1024
 LARGE_VMEM_BYTES = 60 * 1024 * 1024
 BF = jnp.bfloat16
@@ -215,6 +216,46 @@
     mine_ref[...] = dot(a_ref[mine, :], w_ref[...])
 
 
+def quarters_kernel(place_ref, gain_ref, *refs):
+    gain = gain_ref[...]
+    count = len(QUARTERS_SENT) * 2 if len(refs) > 4 else 2
+    inputs, outputs = refs[:count], refs[count:]
+    units = inputs[0].shape[1]
+    for pair in range(count // 2):
+        gate = (inputs[2 * pair][...].astype(F32) * gain).astype(BF)
+        up = (inputs[2 * pair + 1][...].astype(F32) * gain).astype(BF)
+        if pair < 2:
+            outputs[pair][:, :units] = gate
+            outputs[pair][:, units:] = up
+        else:
+            outputs[pair][...] = gate
+            outputs[pair + 1][...] = up
+
+
+def quarters(place, gain, gate_weight, up_weight, sent):
+    depth, width = gate_weight.shape
+    units, steps = width // 4, 4
+    rows = depth // steps
+    offsets = QUARTERS_SENT if sent else (0,)
+
+    def quarter(d):
+        return pl.BlockSpec((rows, units), lambda i, p: (i, lax.rem(p[2] + d, 4)))
+
+    widths = [2 * units, 2 * units, units, units] if sent else [2 * units]
+    return pl.pallas_call(
+        quarters_kernel,
+        grid_spec=pltpu.PrefetchScalarGridSpec(
+            num_scalar_prefetch=1,
+            grid=(steps,),
+            in_specs=[pl.BlockSpec((rows, 1), lambda i, p: (i, 0))]
+            + [spec for d in offsets for spec in (quarter(d), quarter(d))],
+            out_specs=[pl.BlockSpec((rows, n), lambda i, p: (i, 0)) for n in widths],
+        ),
+        out_shape=[jax.ShapeDtypeStruct((depth, n), BF) for n in widths],
+        compiler_params=params(LARGE_VMEM_BYTES),
+    )(place, gain, *[w for _ in offsets for w in (gate_weight, up_weight)])
+
+
 def gate_up_kernel(place_ref, own_ref, other_ref, w0, w1, gate2, up2, w3, out_ref, m_ref):
     units = gate2.shape[1]
     step = pl.program_id(0)
@@ -327,7 +368,7 @@
 ):
     groups = lax.axis_size("z") * lax.axis_size("y")
     me = (lax.axis_index("z") * lax.axis_size("y") + lax.axis_index("y")).astype(jnp.int32).reshape(1)
-    place = jnp.stack((lax.axis_index("x"), lax.axis_index("c"))).astype(jnp.int32)
+    place = jnp.stack((lax.axis_index("x"), lax.axis_index("c"), lax.axis_index("y"))).astype(jnp.int32)
     all_rows, width_part = hidden.shape
     own_rows = all_rows // groups
     full_width = width_part * groups
@@ -369,13 +410,6 @@
     half = units // 2
     gain = mlp_gain[:, None]
 
-    def columns(weight, d):
-        at = lax.rem(lax.axis_index("y") + d, chips_y) * units
-        return lax.dynamic_slice_in_dim(weight, at, units, 1).astype(F32)
-
-    def wide(*parts):
-        return (jnp.concatenate(parts, axis=1) * gain).astype(BF)
-
     queries = pl.pallas_call(
         query_kernel,
         in_specs=[vmem()] * 3,
@@ -384,10 +418,10 @@
         compiler_params=params(),
     )(q_parts, sel, q_gain.reshape(1, HEAD))
     queries = after(queries, forward, backward)
-    later_gate, later_up = lax.optimization_barrier((gate_weight, up_weight, queries))[:2]
-    wide_0 = wide(columns(later_gate, 0), columns(later_up, 0))
-    wide_1 = shift(wide(columns(later_gate, 1), columns(later_up, 1)), "y", 1)
-    wide_3 = shift(wide(columns(later_gate, 3), columns(later_up, 3)), "y", -1)
+    first_gate, first_up = lax.optimization_barrier((gate_weight, up_weight, queries))[:2]
+    wide_1, wide_3, gate_2, up_2 = quarters(place, gain, first_gate, first_up, True)
+    gate_2, up_2 = shift(gate_2, "y", 1), shift(up_2, "y", -1)
+    wide_1, wide_3 = shift(wide_1, "y", 1), shift(wide_3, "y", -1)
     queries = lax.all_to_all(queries, GROUP, 0, 0, tiled=True)
 
     mixed = pl.pallas_call(
@@ -398,7 +432,7 @@
         compiler_params=params(),
     )(me, image_tiles, own, kv_left, kv_right, k_gain.reshape(1, HEAD), queries, row_image)
     gate_weight, up_weight, down_weight = lax.optimization_barrier((gate_weight, up_weight, down_weight, mixed))[:3]
-    gate_2, up_2 = wide(columns(gate_weight, 2)), wide(columns(up_weight, 2))
+    (wide_0,) = quarters(place, gain, gate_weight, up_weight, False)
 
     def rows(d, start, size):
         at = lax.rem(lax.axis_index("y") + d, chips_y) * units + start
@@ -407,7 +441,7 @@
     down_0, down_1, down_3 = rows(0, 0, units), rows(1, 0, units), rows(3, 0, units)
     down_2 = rows(2, 0, half), rows(2, half, half)
     mixed = lax.all_to_all(mixed, GROUP, 0, 0, tiled=True)
-    mixed = after(mixed, gate_2, up_2, down_1, down_3, *down_2)
+    mixed = after(mixed, wide_0, down_1, down_3, *down_2)
     gate_2, up_2 = shift(gate_2, "y", 1), shift(up_2, "y", -1)
 
     attended = pl.pallas_call(
@@ -433,9 +467,9 @@
         compiler_params=params(),
     )(place, attended, o_weight)
     pair = (mine + shift(theirs, "c", 1).astype(F32)).astype(BF)
-    attn_sum = chip_sum(after(pair, gate_2, up_2))
-    gate_2, up_2 = shift(gate_2, "y", 1), shift(up_2, "y", -1)
+    attn_sum = chip_sum(pair)
     middle = (half_f + jnp.tanh(gate_logits[0]) * attn_sum).astype(BF)
+    middle = after(middle, gate_2, up_2)
     middle_f = middle.astype(F32)
     own_rows_all = jnp.concatenate([middle] + [shift(middle, "y", d) for d in (1, 2, 3)], axis=0)
     other_rows_all = shift(own_rows_all, "c", 1)
@@ -472,7 +506,7 @@
             jax.ShapeDtypeStruct((4, half_rows, width_part), F32),
             jax.ShapeDtypeStruct((4, half_rows, width_part), BF),
         ],
-        compiler_params=params(LARGE_VMEM_BYTES),
+        compiler_params=params(),
     )(place, active, down_0, down_1, *down_2, down_3)
     own_down, behind, across, ahead = pl.pallas_call(
         pair_kernel,

time: 208 us -> 209 us (level)
  Pallas kernels: 23.4 us -> 31.6 us
  waiting for transfers between devices: 70.1 us -> 64 us
  starting transfers between devices: 90.5 us -> 96.2 us
  other arithmetic: 5.84 us -> 1.76 us
  local copies, waits for them, and re-layouts: 13.9 us -> 10.9 us
    pallas_call x0 -> x2, Pallas kernels: none -> 9.46 us  [quarters(): pl.pallas_call(quarters_kernel, grid_spec=pltpu.PrefetchScalarGridSpec(nu...]
    convert_element_type x2 -> x0, other arithmetic: 4.14 us -> none  [wide(): return (jnp.concatenate(parts, axis=1) * gain).astype(BF)]
    all_to_all x1, waiting for transfers between devices: 6.26 us -> 2.19 us  [shards(): mixed = lax.all_to_all(mixed, GROUP, 0, 0, tiled=True)]
    all_to_all x1, starting transfers between devices: 4.3 us -> 8.18 us  [shards(): mixed = lax.all_to_all(mixed, GROUP, 0, 0, tiled=True)]
    all_to_all x1, waiting for transfers between devices: 3.73 us -> 0.01 us  [shards(): queries = lax.all_to_all(queries, GROUP, 0, 0, tiled=True)]
    ppermute x35, waiting for transfers between devices: 33.4 us -> 35.5 us  [shift(): return lax.ppermute(value, axis, [(i, (i + by) % n) for i in range(n)])]
    unnamed x61 -> x50, local copies, waits for them, and re-layouts: 6.95 us -> 5.11 us
  transfers between devices with their start and end apart: 41 -> 41, of which waited for: 19 -> 21; matrix products, arithmetic and copies ran while one was open for 7% -> 4% of each run, Pallas kernels for 7% -> 12%
where the time goes in v9:
time: 209 us; the launch traced here: 208 us
  starting transfers between devices  96.2 us (46%)
  waiting for transfers between devices  64 us (31%)
  Pallas kernels  31.6 us (15%)
  local copies, waits for them, and re-layouts  10.9 us (5%)
    ppermute x35, starting transfers between devices, shift(): return lax.ppermute(value, axis, [(i, (i + by) % n) for i in range(n)])  55.6 us
    ppermute x35, waiting for transfers between devices, shift(): return lax.ppermute(value, axis, [(i, (i + by) % n) for i in range(n)])  35.5 us
    all_to_all x2, starting transfers between devices, exchange(): out = lax.all_to_all(value, axis, 0, 0, tiled=True)  13.2 us
    all_to_all x1, waiting for transfers between devices, shards(): lax.all_to_all(attended, GROUP, 0, 0, tiled=True)  10.1 us
    pallas_call x2, Pallas kernels, quarters(): pl.pallas_call(quarters_kernel, grid_spec=pltpu.PrefetchScalarGridSpec(nu...  9.46 us
    all_to_all x2, waiting for transfers between devices, exchange(): out = lax.all_to_all(value, axis, 0, 0, tiled=True)  9.45 us
    all_to_all x1, starting transfers between devices, shards(): mixed = lax.all_to_all(mixed, GROUP, 0, 0, tiled=True)  8.18 us
    all_to_all x1, starting transfers between devices, shards(): lax.all_to_all(attended, GROUP, 0, 0, tiled=True)  7.95 us
  transfers between devices with their start and end apart: 41, of which 21 were waited for; matrix products, arithmetic and copies ran while one was open for 4% of the time, Pallas kernels for 12%

profile of v9, /device:TPU:1, one launch (start us, length us, event | category | flops | bytes accessed | tf_op | source)
XLA Modules:
  0.0 208.1 jit_solution(13891589015347627475)
XLA Ops:
  0.0 3.2 %collective-permute-start.1 = (bf16[1024,1024]{1,0:T(8,128)(2,1)}, bf16[1024,1024]{1,0:T(8,128)(2,1)S(1)}, u32[]{:S(2)}, u32[]{:S(2)}) collective-permute-start(bf16[1024,1024]{1,0:T(8,128)(2,1)} %k0.1), channel_id=1, source_target_pairs={{0,1},{1,0},{2,3},{3,2},{4,5},{5,4},{6,7},{7,6},{8,9},{9,8},{10,11... | collective-permute-start | bytes 6291464 | tf_op jit(solution)/shard_map/ppermute | solution.py:331
  5.8 9.5 %all-to-all-start = ((bf16[32,8,1024]{2,1,0:T(8,128)(2,1)}), bf16[32,8,1024]{2,1,0:T(8,128)(2,1)S(1)}, u32[]{:S(2)}, u32[]{:S(2)}) async-start(bf16[32,8,1024]{2,1,0:T(8,128)(2,1)} %fusion), calls=%async_computation | async-start | bytes 1048576 | tf_op jit(solution)/shard_map/all_to_all | solution.py:340
  17.3 7.9 %shard_map.163 = (bf16[320,256]{1,0:T(8,128)(2,1)}, bf16[320,256]{1,0:T(8,128)(2,1)}, bf16[640,256]{1,0:T(8,128)(2,1)}, bf16[640,256]{1,0:T(8,128)(2,1)}, bf16[640,256]{1,0:T(8,128)(2,1)}) custom-call(s32[3]{0:T(128)} %pad_add_fusion.place_ref, bf16[640,1024]{1,0:T(8,128)(2,1)} %x0.1, bf16[640,1024]{1,0:T(8,128)(2,1)} %collective-permute-done.x1, ...), custom_call_target="tpu_custom_call" | custom-call | tf_op jit(solution)/shard_map/pallas_call | solution.py:110
  28.7 2.9 %all-to-all-done.parts_ref = bf16[32,8,1024]{2,1,0:T(8,128)(2,1)S(1)} async-done(((bf16[32,8,1024]{2,1,0:T(8,128)(2,1)}), bf16[32,8,1024]{2,1,0:T(8,128)(2,1)S(1)}, u32[]{:S(2)}, u32[]{:S(2)}) %all-to-all-start) | async-done | bytes 524320 | tf_op jit(solution)/shard_map/all_to_all | solution.py:340
  34.8 7.7 %all-to-all-start.1 = ((bf16[32,8,512]{2,1,0:T(8,128)(2,1)}), bf16[32,8,512]{2,1,0:T(8,128)(2,1)S(1)}, u32[]{:S(2)}, u32[]{:S(2)}) async-start(bf16[32,8,512]{2,1,0:T(8,128)(2,1)} %bitcast.8), calls=%async_computation.1 | async-start | bytes 524288 | tf_op jit(solution)/shard_map/all_to_all | solution.py:425
  46.1 5.2 %shard_map.170 = (bf16[256,1792]{1,0:T(8,128)(2,1)}, bf16[256,1792]{1,0:T(8,128)(2,1)}, bf16[256,896]{1,0:T(8,128)(2,1)}, bf16[256,896]{1,0:T(8,128)(2,1)}) custom-call(s32[3]{0:T(128)} %pad_add_fusion.place_ref, f32[256,1]{1,0:T(8,128)} %copy.30.gain_ref, bf16[256,3584]{1,0:T(8,128)(2,1)} %refs_4_, bf16[256,3584]{1,0:T(8,128)(2,1)} %refs_5_, ...), custom_call_target="tpu_custom_call" | custom-call | tf_op jit(solution)/shard_map/pallas_call | solution.py:245
  54.2 2.9 %shard_map.167 = bf16[256,640]{1,0:T(8,128)(2,1)} custom-call(s32[1]{0:T(128)} %bitcast.4.me_ref, s32[32,4]{1,0:T(8,128)S(1)} %copy.29.tiles_ref, bf16[640,256]{1,0:T(8,128)(2,1)S(1)} %copy-done.2, bf16[640,256]{1,0:T(8,128)(2,1)S(1)} %collective-permute-done.5.left_ref, bf16[640,256]{1,0:T(8,128)(2,1)S(1)} %collective-permute-done.6.right_ref, ...), custom_call_target="tpu_custom_call" | custom-call | tf_op jit(solution)/shard_map/pallas_call | solution.py:427
  57.1 8.2 %all-to-all-start.2 = ((bf16[32,8,640]{2,1,0:T(8,128)(2,1)}), bf16[32,8,640]{2,1,0:T(8,128)(2,1)S(1)}, u32[]{:S(2)}, u32[]{:S(2)}) async-start(bf16[32,8,640]{2,1,0:T(8,128)(2,1)} %bitcast.10), calls=%async_computation.2 | async-start | bytes 655360 | tf_op jit(solution)/shard_map/all_to_all | solution.py:443
  65.3 4.2 %shard_map.168.w0 = bf16[256,1792]{1,0:T(8,128)(2,1)} custom-call(s32[3]{0:T(128)} %pad_add_fusion.place_ref, f32[256,1]{1,0:T(8,128)} %copy.30.gain_ref, bf16[256,3584]{1,0:T(8,128)(2,1)} %refs_4_, bf16[256,3584]{1,0:T(8,128)(2,1)} %refs_5_), custom_call_target="tpu_custom_call" | custom-call | tf_op jit(solution)/shard_map/pallas_call | solution.py:245
  77.1 7.9 %all-to-all-start.3 = ((bf16[32,8,1024]{2,1,0:T(8,128)(2,1)}), bf16[32,8,1024]{2,1,0:T(8,128)(2,1)S(1)}, u32[]{:S(2)}, u32[]{:S(2)}) async-start(bf16[32,8,1024]{2,1,0:T(8,128)(2,1)} %shard_map.169), calls=%async_computation.3 | async-start | bytes 1048576 | tf_op jit(solution)/shard_map/all_to_all | solution.py:455
  87.8 10.1 %all-to-all-done.3 = bf16[32,8,1024]{2,1,0:T(8,128)(2,1)S(1)} async-done(((bf16[32,8,1024]{2,1,0:T(8,128)(2,1)}), bf16[32,8,1024]{2,1,0:T(8,128)(2,1)S(1)}, u32[]{:S(2)}, u32[]{:S(2)}) %all-to-all-start.3) | async-done | bytes 524320 | tf_op jit(solution)/shard_map/all_to_all | solution.py:455
  98.8 6.4 %collective-permute-start.9 = (bf16[128,256]{1,0:T(8,128)(2,1)S(1)}, bf16[128,256]{1,0:T(8,128)(2,1)S(1)}, u32[]{:S(2)}, u32[]{:S(2)}) collective-permute-start(bf16[128,256]{1,0:T(8,128)(2,1)S(1)} %get-tuple-element.62), channel_id=1, source_target_pairs={{0,1},{1,0},{2,3},{3,2},{4,5},{5,4},{6,7},{7,6},{8,9},{9,8},{10,11... | collective-permute-start | bytes 196616 | tf_op jit(solution)/shard_map/ppermute | solution.py:331
  114.0 4.7 %collective-permute-done.14.gate2 = bf16[256,896]{1,0:T(8,128)(2,1)S(1)} collective-permute-done((bf16[256,896]{1,0:T(8,128)(2,1)}, bf16[256,896]{1,0:T(8,128)(2,1)S(1)}, u32[]{:S(2)}, u32[]{:S(2)}) %collective-permute-start.14) | collective-permute-done | bytes 458784 | tf_op jit(solution)/shard_map/ppermute | solution.py:331
  118.8 3.5 %collective-permute-start.18 = (bf16[128,256]{1,0:T(8,128)(2,1)S(1)}, bf16[128,256]{1,0:T(8,128)(2,1)S(1)}, u32[]{:S(2)}, u32[]{:S(2)}) collective-permute-start(bf16[128,256]{1,0:T(8,128)(2,1)S(1)} %add_convert_fusion.2), channel_id=1, source_target_pairs={{0,16},{8,24},{16,0},{24,8},{1,17},{9,25},{17,1},{25,9},{2,18},{10... | collective-permute-start | bytes 196616 | tf_op jit(solution)/shard_map/ppermute | solution.py:331
  130.2 4.3 %shard_map.172 = bf16[256,1920]{1,0:T(8,128)(2,1)} custom-call(s32[3]{0:T(128)} %pad_add_fusion.place_ref, bf16[512,256]{1,0:T(8,128)(2,1)} %copy-done.12, bf16[512,256]{1,0:T(8,128)(2,1)} %copy-done.14, bf16[256,1792]{1,0:T(8,128)(2,1)} %shard_map.168.w0, bf16[256,1792]{1,0:T(8,128)(2,1)} %collective-permute-done.7.w1, bf16[256,896]{1,0:T(8,128)(2,1)} %copy-done.10, ...), custom_call_target="tpu_custom_call" | custom-call | tf_op jit(solution)/shard_map/pallas_call | solution.py:479
  134.6 3.7 %all-to-all-start.4 = ((bf16[8,32,1920]{2,1,0:T(8,128)(2,1)}), bf16[8,32,1920]{2,1,0:T(8,128)(2,1)S(1)}, u32[]{:S(2)}, u32[]{:S(2)}) async-start(bf16[8,32,1920]{2,1,0:T(8,128)(2,1)} %bitcast.25), calls=%async_computation.4 | async-start | bytes 1966080 | tf_op jit(solution)/shard_map/all_to_all | solution.py:340
  143.7 12.7 %collective-permute-done.23 = bf16[448,256]{1,0:T(8,128)(2,1)S(1)} collective-permute-done((bf16[448,256]{1,0:T(8,128)(2,1)}, bf16[448,256]{1,0:T(8,128)(2,1)S(1)}, u32[]{:S(2)}, u32[]{:S(2)}) %collective-permute-start.23) | collective-permute-done | bytes 229408 | tf_op jit(solution)/shard_map/ppermute | solution.py:331
  157.2 6.5 %all-to-all-done.4.parts_ref = bf16[8,32,1920]{2,1,0:T(8,128)(2,1)S(1)} async-done(((bf16[8,32,1920]{2,1,0:T(8,128)(2,1)}), bf16[8,32,1920]{2,1,0:T(8,128)(2,1)S(1)}, u32[]{:S(2)}, u32[]{:S(2)}) %all-to-all-start.4) | async-done | bytes 983072 | tf_op jit(solution)/shard_map/all_to_all | solution.py:340
  164.8 3.6 %all-to-all-start.5 = ((bf16[8,32,896]{2,1,0:T(8,128)(2,1)}), bf16[8,32,896]{2,1,0:T(8,128)(2,1)S(1)}, u32[]{:S(2)}, u32[]{:S(2)}) async-start(bf16[8,32,896]{2,1,0:T(8,128)(2,1)} %shard_map.173), calls=%async_computation.5 | async-start | bytes 917504 | tf_op jit(solution)/shard_map/all_to_all | solution.py:500
  171.1 3.6 %collective-permute-done.25.low2 = bf16[448,256]{1,0:T(8,128)(2,1)S(1)} collective-permute-done((bf16[448,256]{1,0:T(8,128)(2,1)}, bf16[448,256]{1,0:T(8,128)(2,1)S(1)}, u32[]{:S(2)}, u32[]{:S(2)}) %collective-permute-start.25) | collective-permute-done | bytes 229408 | tf_op jit(solution)/shard_map/ppermute | solution.py:331
  174.7 6.8 %all-to-all-done.5 = bf16[8,32,896]{2,1,0:T(8,128)(2,1)S(1)} async-done(((bf16[8,32,896]{2,1,0:T(8,128)(2,1)}), bf16[8,32,896]{2,1,0:T(8,128)(2,1)S(1)}, u32[]{:S(2)}, u32[]{:S(2)}) %all-to-all-start.5) | async-done | bytes 458784 | tf_op jit(solution)/shard_map/all_to_all | solution.py:500
  183.5 4.0 %collective-permute-start.27 = (bf16[4,128,256]{2,1,0:T(8,128)(2,1)}, bf16[4,128,256]{2,1,0:T(8,128)(2,1)S(1)}, u32[]{:S(2)}, u32[]{:S(2)}) collective-permute-start(bf16[4,128,256]{2,1,0:T(8,128)(2,1)} %get-tuple-element.72), channel_id=1, source_target_pairs={{0,1},{1,0},{2,3},{3,2},{4,5},{5,4},{6,7},{7,6},{8,9},{9,8},{10,11... | collective-permute-start | bytes 786440 | tf_op jit(solution)/shard_map/ppermute | solution.py:331
  196.2 3.2 %collective-permute-start.32 = (bf16[128,256]{1,0:T(8,128)(2,1)S(1)}, bf16[128,256]{1,0:T(8,128)(2,1)S(1)}, u32[]{:S(2)}, u32[]{:S(2)}) collective-permute-start(bf16[128,256]{1,0:T(8,128)(2,1)S(1)} %add_convert_fusion.1), channel_id=1, source_target_pairs={{0,2},{2,4},{4,6},{6,0},{1,3},{3,5},{5,7},{7,1},{8,10},{10,12},{12... | collective-permute-start | bytes 196616 | tf_op jit(solution)/shard_map/ppermute | solution.py:331
  202.9 3.6 %collective-permute-start.34 = (bf16[128,256]{1,0:T(8,128)(2,1)S(1)}, bf16[128,256]{1,0:T(8,128)(2,1)S(1)}, u32[]{:S(2)}, u32[]{:S(2)}) collective-permute-start(bf16[128,256]{1,0:T(8,128)(2,1)S(1)} %add_convert_fusion), channel_id=1, source_target_pairs={{0,1},{1,0},{2,3},{3,2},{4,5},{5,4},{6,7},{7,6},{8,9},{9,8},{10,11... | collective-permute-start | bytes 196616 | tf_op jit(solution)/shard_map/ppermute | solution.py:331
  (142 shorter events, 70.0 us)
Async XLA Ops:
  0.0 15.9 %collective-permute-start.1 = (bf16[1024,1024]{1,0:T(8,128)(2,1)}, bf16[1024,1024]{1,0:T(8,128)(2,1)S(1)}, u32[]{:S(2)}, u32[]{:S(2)}) collective-permute-start(bf16[1024,1024]{1,0:T(8,128)(2,1)} %k0.1), channel_id=1, source_target_pairs={{0,1},{1,0},{2,3},{3,2},{4,5},{5,4},{6,7},{7,6},{8,9},{9,8},{10,11... | collective-permute-start | bytes 6291464 | tf_op jit(solution)/shard_map/ppermute | solution.py:331
  3.2 12.7 %collective-permute-start.2 = (bf16[1024,1024]{1,0:T(8,128)(2,1)}, bf16[1024,1024]{1,0:T(8,128)(2,1)}, u32[]{:S(2)}, u32[]{:S(2)}) collective-permute-start(bf16[1024,1024]{1,0:T(8,128)(2,1)} %v0.1), channel_id=1, source_target_pairs={{0,1},{1,0},{2,3},{3,2},{4,5},{5,4},{6,7},{7,6},{8,9},{9,8},{10,11... | collective-permute-start | bytes 6291464 | tf_op jit(solution)/shard_map/ppermute | solution.py:331
  3.2 12.7 %collective-permute-start = (bf16[640,1024]{1,0:T(8,128)(2,1)}, bf16[640,1024]{1,0:T(8,128)(2,1)}, u32[]{:S(2)}, u32[]{:S(2)}) collective-permute-start(bf16[640,1024]{1,0:T(8,128)(2,1)} %x0.1), channel_id=1, source_target_pairs={{0,1},{1,0},{2,3},{3,2},{4,5},{5,4},{6,7},{7,6},{8,9},{9,8},{10,11... | collective-permute-start | bytes 3932168 | tf_op jit(solution)/shard_map/ppermute | solution.py:331
  5.8 25.9 %all-to-all-start = ((bf16[32,8,1024]{2,1,0:T(8,128)(2,1)}), bf16[32,8,1024]{2,1,0:T(8,128)(2,1)S(1)}, u32[]{:S(2)}, u32[]{:S(2)}) async-start(bf16[32,8,1024]{2,1,0:T(8,128)(2,1)} %fusion), calls=%async_computation | async-start | bytes 1048576 | tf_op jit(solution)/shard_map/all_to_all | solution.py:340
  25.2 7.6 %collective-permute-start.3 = (bf16[320,256]{1,0:T(8,128)(2,1)}, bf16[320,256]{1,0:T(8,128)(2,1)S(1)}, u32[]{:S(2)}, u32[]{:S(2)}) collective-permute-start(bf16[320,256]{1,0:T(8,128)(2,1)} %get-tuple-element.44), channel_id=1, source_target_pairs={{0,2},{2,4},{4,6},{6,0},{1,3},{3,5},{5,7},{7,1},{8,10},{10,12},{12... | collective-permute-start | bytes 491528 | tf_op jit(solution)/shard_map/ppermute | solution.py:331
  26.5 6.3 %collective-permute-start.4 = (bf16[320,256]{1,0:T(8,128)(2,1)}, bf16[320,256]{1,0:T(8,128)(2,1)S(1)}, u32[]{:S(2)}, u32[]{:S(2)}) collective-permute-start(bf16[320,256]{1,0:T(8,128)(2,1)} %get-tuple-element.45), channel_id=1, source_target_pairs={{0,6},{2,0},{4,2},{6,4},{1,7},{3,1},{5,3},{7,5},{8,14},{10,8},{12,... | collective-permute-start | bytes 491528 | tf_op jit(solution)/shard_map/ppermute | solution.py:331
  34.8 19.3 %all-to-all-start.1 = ((bf16[32,8,512]{2,1,0:T(8,128)(2,1)}), bf16[32,8,512]{2,1,0:T(8,128)(2,1)S(1)}, u32[]{:S(2)}, u32[]{:S(2)}) async-start(bf16[32,8,512]{2,1,0:T(8,128)(2,1)} %bitcast.8), calls=%async_computation.1 | async-start | bytes 524288 | tf_op jit(solution)/shard_map/all_to_all | solution.py:425
  42.6 11.6 %collective-permute-start.5 = (bf16[640,256]{1,0:T(8,128)(2,1)S(1)}, bf16[640,256]{1,0:T(8,128)(2,1)S(1)}, u32[]{:S(2)}, u32[]{:S(2)}) collective-permute-start(bf16[640,256]{1,0:T(8,128)(2,1)S(1)} %get-tuple-element.46), channel_id=1, source_target_pairs={{0,2},{2,4},{4,6},{6,0},{1,3},{3,5},{5,7},{7,1},{8,10},{10,12},{12... | collective-permute-start | bytes 983048 | tf_op jit(solution)/shard_map/ppermute | solution.py:331
  43.7 10.5 %collective-permute-start.6 = (bf16[640,256]{1,0:T(8,128)(2,1)S(1)}, bf16[640,256]{1,0:T(8,128)(2,1)S(1)}, u32[]{:S(2)}, u32[]{:S(2)}) collective-permute-start(bf16[640,256]{1,0:T(8,128)(2,1)S(1)} %get-tuple-element.47), channel_id=1, source_target_pairs={{0,6},{2,0},{4,2},{6,4},{1,7},{3,1},{5,3},{7,5},{8,14},{10,8},{12,... | collective-permute-start | bytes 983048 | tf_op jit(solution)/shard_map/ppermute | solution.py:331
  51.3 25.8 %collective-permute-start.7 = (bf16[256,1792]{1,0:T(8,128)(2,1)}, bf16[256,1792]{1,0:T(8,128)(2,1)}, u32[]{:S(2)}, u32[]{:S(2)}) collective-permute-start(bf16[256,1792]{1,0:T(8,128)(2,1)} %get-tuple-element.58), channel_id=1, source_target_pairs={{0,8},{8,16},{16,24},{24,0},{1,9},{9,17},{17,25},{25,1},{2,10},{10... | collective-permute-start | bytes 2752520 | tf_op jit(solution)/shard_map/ppermute | solution.py:331
  52.6 24.5 %collective-permute-start.8 = (bf16[256,1792]{1,0:T(8,128)(2,1)}, bf16[256,1792]{1,0:T(8,128)(2,1)}, u32[]{:S(2)}, u32[]{:S(2)}) collective-permute-start(bf16[256,1792]{1,0:T(8,128)(2,1)} %get-tuple-element.59), channel_id=1, source_target_pairs={{0,24},{8,0},{16,8},{24,16},{1,25},{9,1},{17,9},{25,17},{2,26},{10... | collective-permute-start | bytes 2752520 | tf_op jit(solution)/shard_map/ppermute | solution.py:331
  57.1 18.7 %all-to-all-start.2 = ((bf16[32,8,640]{2,1,0:T(8,128)(2,1)}), bf16[32,8,640]{2,1,0:T(8,128)(2,1)S(1)}, u32[]{:S(2)}, u32[]{:S(2)}) async-start(bf16[32,8,640]{2,1,0:T(8,128)(2,1)} %bitcast.10), calls=%async_computation.2 | async-start | bytes 655360 | tf_op jit(solution)/shard_map/all_to_all | solution.py:443
  77.1 20.8 %all-to-all-start.3 = ((bf16[32,8,1024]{2,1,0:T(8,128)(2,1)}), bf16[32,8,1024]{2,1,0:T(8,128)(2,1)S(1)}, u32[]{:S(2)}, u32[]{:S(2)}) async-start(bf16[32,8,1024]{2,1,0:T(8,128)(2,1)} %shard_map.169), calls=%async_computation.3 | async-start | bytes 1048576 | tf_op jit(solution)/shard_map/all_to_all | solution.py:455
  85.1 20.1 %collective-permute-start.13 = (bf16[256,896]{1,0:T(8,128)(2,1)}, bf16[256,896]{1,0:T(8,128)(2,1)}, u32[]{:S(2)}, u32[]{:S(2)}) collective-permute-start(bf16[256,896]{1,0:T(8,128)(2,1)} %get-tuple-element.63), channel_id=1, source_target_pairs={{0,8},{8,16},{16,24},{24,0},{1,9},{9,17},{17,25},{25,1},{2,10},{10... | collective-permute-start | bytes 1376264 | tf_op jit(solution)/shard_map/ppermute | solution.py:331
  86.4 19.0 %collective-permute-start.15 = (bf16[256,896]{1,0:T(8,128)(2,1)}, bf16[256,896]{1,0:T(8,128)(2,1)}, u32[]{:S(2)}, u32[]{:S(2)}) collective-permute-start(bf16[256,896]{1,0:T(8,128)(2,1)} %get-tuple-element.64), channel_id=1, source_target_pairs={{0,24},{8,0},{16,8},{24,16},{1,25},{9,1},{17,9},{25,17},{2,26},{10... | collective-permute-start | bytes 1376264 | tf_op jit(solution)/shard_map/ppermute | solution.py:331
  98.8 9.1 %collective-permute-start.9 = (bf16[128,256]{1,0:T(8,128)(2,1)S(1)}, bf16[128,256]{1,0:T(8,128)(2,1)S(1)}, u32[]{:S(2)}, u32[]{:S(2)}) collective-permute-start(bf16[128,256]{1,0:T(8,128)(2,1)S(1)} %get-tuple-element.62), channel_id=1, source_target_pairs={{0,1},{1,0},{2,3},{3,2},{4,5},{5,4},{6,7},{7,6},{8,9},{9,8},{10,11... | collective-permute-start | bytes 196616 | tf_op jit(solution)/shard_map/ppermute | solution.py:331
  105.2 13.5 %collective-permute-start.14 = (bf16[256,896]{1,0:T(8,128)(2,1)}, bf16[256,896]{1,0:T(8,128)(2,1)S(1)}, u32[]{:S(2)}, u32[]{:S(2)}) collective-permute-start(bf16[256,896]{1,0:T(8,128)(2,1)} %collective-permute-done.13), channel_id=1, source_target_pairs={{0,8},{8,16},{16,24},{24,0},{1,9},{9,17},{17,25},{25,1},{2,10},{10... | collective-permute-start | bytes 1376264 | tf_op jit(solution)/shard_map/ppermute | solution.py:331
  105.3 13.4 %collective-permute-start.16 = (bf16[256,896]{1,0:T(8,128)(2,1)}, bf16[256,896]{1,0:T(8,128)(2,1)S(1)}, u32[]{:S(2)}, u32[]{:S(2)}) collective-permute-start(bf16[256,896]{1,0:T(8,128)(2,1)} %collective-permute-done.15), channel_id=1, source_target_pairs={{0,24},{8,0},{16,8},{24,16},{1,25},{9,1},{17,9},{25,17},{2,26},{10... | collective-permute-start | bytes 1376264 | tf_op jit(solution)/shard_map/ppermute | solution.py:331
  134.6 29.1 %all-to-all-start.4 = ((bf16[8,32,1920]{2,1,0:T(8,128)(2,1)}), bf16[8,32,1920]{2,1,0:T(8,128)(2,1)S(1)}, u32[]{:S(2)}, u32[]{:S(2)}) async-start(bf16[8,32,1920]{2,1,0:T(8,128)(2,1)} %bitcast.25), calls=%async_computation.4 | async-start | bytes 1966080 | tf_op jit(solution)/shard_map/all_to_all | solution.py:340
  138.3 18.2 %collective-permute-start.21 = (bf16[896,256]{1,0:T(8,128)(2,1)}, bf16[896,256]{1,0:T(8,128)(2,1)S(1)}, u32[]{:S(2)}, u32[]{:S(2)}) collective-permute-start(bf16[896,256]{1,0:T(8,128)(2,1)} %get-tuple-element.66), channel_id=1, source_target_pairs={{0,8},{8,16},{16,24},{24,0},{1,9},{9,17},{17,25},{25,1},{2,10},{10... | collective-permute-start | bytes 1376264 | tf_op jit(solution)/shard_map/ppermute | solution.py:331
  138.4 18.8 %collective-permute-start.22 = (bf16[896,256]{1,0:T(8,128)(2,1)S(1)}, bf16[896,256]{1,0:T(8,128)(2,1)S(1)}, u32[]{:S(2)}, u32[]{:S(2)}) collective-permute-start(bf16[896,256]{1,0:T(8,128)(2,1)S(1)} %get-tuple-element.67), channel_id=1, source_target_pairs={{0,24},{8,0},{16,8},{24,16},{1,25},{9,1},{17,9},{25,17},{2,26},{10... | collective-permute-start | bytes 1376264 | tf_op jit(solution)/shard_map/ppermute | solution.py:331
  141.0 15.4 %collective-permute-start.23 = (bf16[448,256]{1,0:T(8,128)(2,1)}, bf16[448,256]{1,0:T(8,128)(2,1)S(1)}, u32[]{:S(2)}, u32[]{:S(2)}) collective-permute-start(bf16[448,256]{1,0:T(8,128)(2,1)} %get-tuple-element.68), channel_id=1, source_target_pairs={{0,8},{8,16},{16,24},{24,0},{1,9},{9,17},{17,25},{25,1},{2,10},{10... | collective-permute-start | bytes 688136 | tf_op jit(solution)/shard_map/ppermute | solution.py:331
  141.0 15.4 %collective-permute-start.24 = (bf16[448,256]{1,0:T(8,128)(2,1)}, bf16[448,256]{1,0:T(8,128)(2,1)S(1)}, u32[]{:S(2)}, u32[]{:S(2)}) collective-permute-start(bf16[448,256]{1,0:T(8,128)(2,1)} %get-tuple-element.69), channel_id=1, source_target_pairs={{0,24},{8,0},{16,8},{24,16},{1,25},{9,1},{17,9},{25,17},{2,26},{10... | collective-permute-start | bytes 688136 | tf_op jit(solution)/shard_map/ppermute | solution.py:331
  164.8 16.7 %all-to-all-start.5 = ((bf16[8,32,896]{2,1,0:T(8,128)(2,1)}), bf16[8,32,896]{2,1,0:T(8,128)(2,1)S(1)}, u32[]{:S(2)}, u32[]{:S(2)}) async-start(bf16[8,32,896]{2,1,0:T(8,128)(2,1)} %shard_map.173), calls=%async_computation.5 | async-start | bytes 917504 | tf_op jit(solution)/shard_map/all_to_all | solution.py:500
  (39 other events, 376.8 us)

commit v10 on v8

--- a/solution.py
+++ b/solution.py
@@ -347,6 +347,7 @@
         compiler_params=params(),
     )(me, image_groups.reshape(groups, -1), image_requests.reshape(groups, -1))
 
+    hidden = after(hidden, place)
     hidden_f = hidden.astype(F32)
     normed = (hidden_f * attn_gain).astype(BF)
     q_part = dot(normed, q_weight).astype(BF)
@@ -359,7 +360,7 @@
         in_specs=[vmem()] * 4,
         out_specs=[vmem()] * 2,
         out_shape=[jax.ShapeDtypeStruct(ahead.shape, BF)] * 2,
-        compiler_params=params(),
+        compiler_params=params(LARGE_VMEM_BYTES),
     )(ahead, behind, shift(low, "x", 1), shift(high, "x", -1))
     kv_left = shift(forward, "x", 1)
     kv_right = shift(backward, "x", -1)
@@ -433,9 +434,10 @@
         compiler_params=params(),
     )(place, attended, o_weight)
     pair = (mine + shift(theirs, "c", 1).astype(F32)).astype(BF)
-    attn_sum = chip_sum(after(pair, gate_2, up_2))
+    attn_sum = chip_sum(pair)
     gate_2, up_2 = shift(gate_2, "y", 1), shift(up_2, "y", -1)
     middle = (half_f + jnp.tanh(gate_logits[0]) * attn_sum).astype(BF)
+    middle = after(middle, gate_2, up_2)
     middle_f = middle.astype(F32)
     own_rows_all = jnp.concatenate([middle] + [shift(middle, "y", d) for d in (1, 2, 3)], axis=0)
     other_rows_all = shift(own_rows_all, "c", 1)
@@ -472,7 +474,7 @@
             jax.ShapeDtypeStruct((4, half_rows, width_part), F32),
             jax.ShapeDtypeStruct((4, half_rows, width_part), BF),
         ],
-        compiler_params=params(LARGE_VMEM_BYTES),
+        compiler_params=params(),
     )(place, active, down_0, down_1, *down_2, down_3)
     own_down, behind, across, ahead = pl.pallas_call(
         pair_kernel,

time: 208 us -> 208 us (level)
  waiting for transfers between devices: 70.1 us -> 78.4 us
  starting transfers between devices: 90.5 us -> 85.1 us
  local copies, waits for them, and re-layouts: 13.9 us -> 10.4 us
    ppermute x35, starting transfers between devices: 55.7 us -> 51.2 us  [shift(): return lax.ppermute(value, axis, [(i, (i + by) % n) for i in range(n)])]
    all_to_all x2, waiting for transfers between devices: 9.72 us -> 13.2 us  [exchange(): out = lax.all_to_all(value, axis, 0, 0, tiled=True)]
    unnamed x61 -> x50, local copies, waits for them, and re-layouts: 6.95 us -> 3.84 us
    ppermute x35, waiting for transfers between devices: 33.4 us -> 36 us  [shift(): return lax.ppermute(value, axis, [(i, (i + by) % n) for i in range(n)])]
  transfers between devices with their start and end apart: 41 -> 41, of which waited for: 19 -> 20; matrix products, arithmetic and copies ran while one was open for 7% -> 7% of each run, Pallas kernels for 7% -> 7%
where the time goes in v10:
time: 208 us
  starting transfers between devices  85.1 us (41%)
  waiting for transfers between devices  78.4 us (38%)
  Pallas kernels  24.1 us (12%)
  local copies, waits for them, and re-layouts  10.4 us (5%)
  other arithmetic  5.98 us (3%)
    ppermute x35, starting transfers between devices, shift(): return lax.ppermute(value, axis, [(i, (i + by) % n) for i in range(n)])  51.2 us
    ppermute x35, waiting for transfers between devices, shift(): return lax.ppermute(value, axis, [(i, (i + by) % n) for i in range(n)])  36 us
    all_to_all x2, waiting for transfers between devices, exchange(): out = lax.all_to_all(value, axis, 0, 0, tiled=True)  13.2 us
    all_to_all x2, starting transfers between devices, exchange(): out = lax.all_to_all(value, axis, 0, 0, tiled=True)  13.2 us
    all_to_all x1, waiting for transfers between devices, shards(): lax.all_to_all(attended, GROUP, 0, 0, tiled=True)  10 us
    all_to_all x1, waiting for transfers between devices, shards(): lax.all_to_all(active, 'z', 0, 0, tiled=True).reshape(all_rows, units)  8.29 us
    pallas_call x1, Pallas kernels, kv_project(): pl.pallas_call(kv_kernel, grid_spec=pltpu.PrefetchScalarGridSpec(num_scal...  7.95 us
    all_to_all x1, starting transfers between devices, shards(): queries = lax.all_to_all(queries, GROUP, 0, 0, tiled=True)  7.13 us
  transfers between devices with their start and end apart: 41, of which 20 were waited for; matrix products, arithmetic and copies ran while one was open for 7% of the time, Pallas kernels for 7%

profile of v10, /device:TPU:1, one launch (start us, length us, event | category | flops | bytes accessed | tf_op | source)
XLA Modules:
  0.0 207.6 jit_solution(5874088174383001675)
XLA Ops:
  0.0 3.2 %collective-permute-start.1 = (bf16[1024,1024]{1,0:T(8,128)(2,1)}, bf16[1024,1024]{1,0:T(8,128)(2,1)}, u32[]{:S(2)}, u32[]{:S(2)}) collective-permute-start(bf16[1024,1024]{1,0:T(8,128)(2,1)} %k0.1), channel_id=1, source_target_pairs={{0,1},{1,0},{2,3},{3,2},{4,5},{5,4},{6,7},{7,6},{8,9},{9,8},{10,11... | collective-permute-start | bytes 6291464 | tf_op jit(solution)/shard_map/ppermute | solution.py:290
  6.4 9.5 %all-to-all-start = ((bf16[32,8,1024]{2,1,0:T(8,128)(2,1)}), bf16[32,8,1024]{2,1,0:T(8,128)(2,1)S(1)}, u32[]{:S(2)}, u32[]{:S(2)}) async-start(bf16[32,8,1024]{2,1,0:T(8,128)(2,1)} %fusion), calls=%async_computation | async-start | bytes 1048576 | tf_op jit(solution)/shard_map/all_to_all | solution.py:299
  17.0 8.0 %shard_map.163 = (bf16[320,256]{1,0:T(8,128)(2,1)}, bf16[320,256]{1,0:T(8,128)(2,1)}, bf16[640,256]{1,0:T(8,128)(2,1)}, bf16[640,256]{1,0:T(8,128)(2,1)}, bf16[640,256]{1,0:T(8,128)(2,1)}) custom-call(s32[2]{0:T(128)} %pad_add_fusion.place_ref, bf16[640,1024]{1,0:T(8,128)(2,1)} %x0.1, bf16[640,1024]{1,0:T(8,128)(2,1)} %copy-done.8, bf16[1024,1024]{1,0:T(8,128)(2,1)} %k0.1, ...), custom_call_target="tpu_custom_call" | custom-call | tf_op jit(solution)/shard_map/pallas_call | solution.py:109
  28.5 4.2 %all-to-all-done.parts_ref = bf16[32,8,1024]{2,1,0:T(8,128)(2,1)S(1)} async-done(((bf16[32,8,1024]{2,1,0:T(8,128)(2,1)}), bf16[32,8,1024]{2,1,0:T(8,128)(2,1)S(1)}, u32[]{:S(2)}, u32[]{:S(2)}) %all-to-all-start) | async-done | bytes 524320 | tf_op jit(solution)/shard_map/all_to_all | solution.py:299
  38.5 7.1 %all-to-all-start.1 = ((bf16[32,8,512]{2,1,0:T(8,128)(2,1)}), bf16[32,8,512]{2,1,0:T(8,128)(2,1)S(1)}, u32[]{:S(2)}, u32[]{:S(2)}) async-start(bf16[32,8,512]{2,1,0:T(8,128)(2,1)} %bitcast.7), calls=%async_computation.1 | async-start | bytes 524288 | tf_op jit(solution)/shard_map/all_to_all | solution.py:392
  51.9 4.1 %all-to-all-done.1 = bf16[32,8,512]{2,1,0:T(8,128)(2,1)S(1)} async-done(((bf16[32,8,512]{2,1,0:T(8,128)(2,1)}), bf16[32,8,512]{2,1,0:T(8,128)(2,1)S(1)}, u32[]{:S(2)}, u32[]{:S(2)}) %all-to-all-start.1) | async-done | bytes 262176 | tf_op jit(solution)/shard_map/all_to_all | solution.py:392
  56.1 3.0 %shard_map.167 = bf16[256,640]{1,0:T(8,128)(2,1)} custom-call(s32[1]{0:T(128)} %bitcast.3.me_ref, s32[32,4]{1,0:T(8,128)S(1)} %copy.27.tiles_ref, bf16[640,256]{1,0:T(8,128)(2,1)S(1)} %copy-done.2, bf16[640,256]{1,0:T(8,128)(2,1)S(1)} %collective-permute-done.5.left_ref, bf16[640,256]{1,0:T(8,128)(2,1)S(1)} %collective-permute-done.6.right_ref, ...), custom_call_target="tpu_custom_call" | custom-call | tf_op jit(solution)/shard_map/pallas_call | solution.py:394
  59.0 4.1 %all-to-all-start.2 = ((bf16[32,8,640]{2,1,0:T(8,128)(2,1)}), bf16[32,8,640]{2,1,0:T(8,128)(2,1)S(1)}, u32[]{:S(2)}, u32[]{:S(2)}) async-start(bf16[32,8,640]{2,1,0:T(8,128)(2,1)} %bitcast.9), calls=%async_computation.2 | async-start | bytes 655360 | tf_op jit(solution)/shard_map/all_to_all | solution.py:410
  69.5 6.8 %all-to-all-done.2 = bf16[32,8,640]{2,1,0:T(8,128)(2,1)S(1)} async-done(((bf16[32,8,640]{2,1,0:T(8,128)(2,1)}), bf16[32,8,640]{2,1,0:T(8,128)(2,1)S(1)}, u32[]{:S(2)}, u32[]{:S(2)}) %all-to-all-start.2) | async-done | bytes 327712 | tf_op jit(solution)/shard_map/all_to_all | solution.py:410
  78.5 6.0 %all-to-all-start.3 = ((bf16[32,8,1024]{2,1,0:T(8,128)(2,1)}), bf16[32,8,1024]{2,1,0:T(8,128)(2,1)S(1)}, u32[]{:S(2)}, u32[]{:S(2)}) async-start(bf16[32,8,1024]{2,1,0:T(8,128)(2,1)} %shard_map.168), calls=%async_computation.3 | async-start | bytes 1048576 | tf_op jit(solution)/shard_map/all_to_all | solution.py:422
  87.3 10.0 %all-to-all-done.3 = bf16[32,8,1024]{2,1,0:T(8,128)(2,1)S(1)} async-done(((bf16[32,8,1024]{2,1,0:T(8,128)(2,1)}), bf16[32,8,1024]{2,1,0:T(8,128)(2,1)S(1)}, u32[]{:S(2)}, u32[]{:S(2)}) %all-to-all-start.3) | async-done | bytes 524320 | tf_op jit(solution)/shard_map/all_to_all | solution.py:422
  98.2 6.5 %collective-permute-start.9 = (bf16[128,256]{1,0:T(8,128)(2,1)S(1)}, bf16[128,256]{1,0:T(8,128)(2,1)S(1)}, u32[]{:S(2)}, u32[]{:S(2)}) collective-permute-start(bf16[128,256]{1,0:T(8,128)(2,1)S(1)} %get-tuple-element.58), channel_id=1, source_target_pairs={{0,1},{1,0},{2,3},{3,2},{4,5},{5,4},{6,7},{7,6},{8,9},{9,8},{10,11... | collective-permute-start | bytes 196616 | tf_op jit(solution)/shard_map/ppermute | solution.py:290
  113.5 4.7 %collective-permute-done.14.gate2 = bf16[256,896]{1,0:T(8,128)(2,1)S(1)} collective-permute-done((bf16[256,896]{1,0:T(8,128)(2,1)}, bf16[256,896]{1,0:T(8,128)(2,1)S(1)}, u32[]{:S(2)}, u32[]{:S(2)}) %collective-permute-start.14) | collective-permute-done | bytes 458784 | tf_op jit(solution)/shard_map/ppermute | solution.py:290
  118.3 3.5 %collective-permute-start.18 = (bf16[128,256]{1,0:T(8,128)(2,1)S(1)}, bf16[128,256]{1,0:T(8,128)(2,1)S(1)}, u32[]{:S(2)}, u32[]{:S(2)}) collective-permute-start(bf16[128,256]{1,0:T(8,128)(2,1)S(1)} %add_convert_fusion.2), channel_id=1, source_target_pairs={{0,16},{8,24},{16,0},{24,8},{1,17},{9,25},{17,1},{25,9},{2,18},{10... | collective-permute-start | bytes 196616 | tf_op jit(solution)/shard_map/ppermute | solution.py:290
  129.7 4.3 %shard_map.170 = bf16[256,1920]{1,0:T(8,128)(2,1)} custom-call(s32[2]{0:T(128)} %pad_add_fusion.place_ref, bf16[512,256]{1,0:T(8,128)(2,1)} %copy-done.12, bf16[512,256]{1,0:T(8,128)(2,1)} %copy-done.14, bf16[256,1792]{1,0:T(8,128)(2,1)} %get-tuple-element.84.w0, bf16[256,1792]{1,0:T(8,128)(2,1)} %copy-done.9, bf16[256,896]{1,0:T(8,128)(2,1)} %copy-done.10, ...), custom_call_target="tpu_custom_call" | custom-call | tf_op jit(solution)/shard_map/pallas_call | solution.py:447
  134.1 3.7 %all-to-all-start.4 = ((bf16[8,32,1920]{2,1,0:T(8,128)(2,1)}), bf16[8,32,1920]{2,1,0:T(8,128)(2,1)S(1)}, u32[]{:S(2)}, u32[]{:S(2)}) async-start(bf16[8,32,1920]{2,1,0:T(8,128)(2,1)} %bitcast.23), calls=%async_computation.4 | async-start | bytes 1966080 | tf_op jit(solution)/shard_map/all_to_all | solution.py:299
  137.8 2.7 %collective-permute-start.22 = (bf16[896,256]{1,0:T(8,128)(2,1)S(1)}, bf16[896,256]{1,0:T(8,128)(2,1)S(1)}, u32[]{:S(2)}, u32[]{:S(2)}) collective-permute-start(bf16[896,256]{1,0:T(8,128)(2,1)S(1)} %get-tuple-element.61), channel_id=1, source_target_pairs={{0,24},{8,0},{16,8},{24,16},{1,25},{9,1},{17,9},{25,17},{2,26},{10... | collective-permute-start | bytes 1376264 | tf_op jit(solution)/shard_map/ppermute | solution.py:290
  140.5 2.7 %collective-permute-start.24 = (bf16[448,256]{1,0:T(8,128)(2,1)}, bf16[448,256]{1,0:T(8,128)(2,1)S(1)}, u32[]{:S(2)}, u32[]{:S(2)}) collective-permute-start(bf16[448,256]{1,0:T(8,128)(2,1)} %get-tuple-element.63), channel_id=1, source_target_pairs={{0,24},{8,0},{16,8},{24,16},{1,25},{9,1},{17,9},{25,17},{2,26},{10... | collective-permute-start | bytes 688136 | tf_op jit(solution)/shard_map/ppermute | solution.py:290
  143.2 12.5 %collective-permute-done.23 = bf16[448,256]{1,0:T(8,128)(2,1)S(1)} collective-permute-done((bf16[448,256]{1,0:T(8,128)(2,1)}, bf16[448,256]{1,0:T(8,128)(2,1)S(1)}, u32[]{:S(2)}, u32[]{:S(2)}) %collective-permute-start.23) | collective-permute-done | bytes 229408 | tf_op jit(solution)/shard_map/ppermute | solution.py:290
  156.5 9.1 %all-to-all-done.4.parts_ref = bf16[8,32,1920]{2,1,0:T(8,128)(2,1)S(1)} async-done(((bf16[8,32,1920]{2,1,0:T(8,128)(2,1)}), bf16[8,32,1920]{2,1,0:T(8,128)(2,1)S(1)}, u32[]{:S(2)}, u32[]{:S(2)}) %all-to-all-start.4) | async-done | bytes 983072 | tf_op jit(solution)/shard_map/all_to_all | solution.py:299
  166.6 3.5 %all-to-all-start.5 = ((bf16[8,32,896]{2,1,0:T(8,128)(2,1)}), bf16[8,32,896]{2,1,0:T(8,128)(2,1)S(1)}, u32[]{:S(2)}, u32[]{:S(2)}) async-start(bf16[8,32,896]{2,1,0:T(8,128)(2,1)} %shard_map.171), calls=%async_computation.5 | async-start | bytes 917504 | tf_op jit(solution)/shard_map/all_to_all | solution.py:468
  172.8 5.4 %collective-permute-done.25.low2 = bf16[448,256]{1,0:T(8,128)(2,1)S(1)} collective-permute-done((bf16[448,256]{1,0:T(8,128)(2,1)}, bf16[448,256]{1,0:T(8,128)(2,1)S(1)}, u32[]{:S(2)}, u32[]{:S(2)}) %collective-permute-start.25) | collective-permute-done | bytes 229408 | tf_op jit(solution)/shard_map/ppermute | solution.py:290
  178.2 8.3 %all-to-all-done.5 = bf16[8,32,896]{2,1,0:T(8,128)(2,1)S(1)} async-done(((bf16[8,32,896]{2,1,0:T(8,128)(2,1)}), bf16[8,32,896]{2,1,0:T(8,128)(2,1)S(1)}, u32[]{:S(2)}, u32[]{:S(2)}) %all-to-all-start.5) | async-done | bytes 458784 | tf_op jit(solution)/shard_map/all_to_all | solution.py:468
  202.2 3.8 %collective-permute-start.34 = (bf16[128,256]{1,0:T(8,128)(2,1)S(1)}, bf16[128,256]{1,0:T(8,128)(2,1)S(1)}, u32[]{:S(2)}, u32[]{:S(2)}) collective-permute-start(bf16[128,256]{1,0:T(8,128)(2,1)S(1)} %add_convert_fusion), channel_id=1, source_target_pairs={{0,1},{1,0},{2,3},{3,2},{4,5},{5,4},{6,7},{7,6},{8,9},{9,8},{10,11... | collective-permute-start | bytes 196616 | tf_op jit(solution)/shard_map/ppermute | solution.py:290
  (142 shorter events, 69.5 us)
Async XLA Ops:
  0.0 15.9 %collective-permute-start.1 = (bf16[1024,1024]{1,0:T(8,128)(2,1)}, bf16[1024,1024]{1,0:T(8,128)(2,1)}, u32[]{:S(2)}, u32[]{:S(2)}) collective-permute-start(bf16[1024,1024]{1,0:T(8,128)(2,1)} %k0.1), channel_id=1, source_target_pairs={{0,1},{1,0},{2,3},{3,2},{4,5},{5,4},{6,7},{7,6},{8,9},{9,8},{10,11... | collective-permute-start | bytes 6291464 | tf_op jit(solution)/shard_map/ppermute | solution.py:290
  3.2 12.7 %collective-permute-start.2 = (bf16[1024,1024]{1,0:T(8,128)(2,1)}, bf16[1024,1024]{1,0:T(8,128)(2,1)}, u32[]{:S(2)}, u32[]{:S(2)}) collective-permute-start(bf16[1024,1024]{1,0:T(8,128)(2,1)} %v0.1), channel_id=1, source_target_pairs={{0,1},{1,0},{2,3},{3,2},{4,5},{5,4},{6,7},{7,6},{8,9},{9,8},{10,11... | collective-permute-start | bytes 6291464 | tf_op jit(solution)/shard_map/ppermute | solution.py:290
  3.2 12.7 %collective-permute-start = (bf16[640,1024]{1,0:T(8,128)(2,1)}, bf16[640,1024]{1,0:T(8,128)(2,1)S(1)}, u32[]{:S(2)}, u32[]{:S(2)}) collective-permute-start(bf16[640,1024]{1,0:T(8,128)(2,1)} %x0.1), channel_id=1, source_target_pairs={{0,1},{1,0},{2,3},{3,2},{4,5},{5,4},{6,7},{7,6},{8,9},{9,8},{10,11... | collective-permute-start | bytes 3932168 | tf_op jit(solution)/shard_map/ppermute | solution.py:290
  6.4 26.3 %all-to-all-start = ((bf16[32,8,1024]{2,1,0:T(8,128)(2,1)}), bf16[32,8,1024]{2,1,0:T(8,128)(2,1)S(1)}, u32[]{:S(2)}, u32[]{:S(2)}) async-start(bf16[32,8,1024]{2,1,0:T(8,128)(2,1)} %fusion), calls=%async_computation | async-start | bytes 1048576 | tf_op jit(solution)/shard_map/all_to_all | solution.py:299
  25.0 8.8 %collective-permute-start.3 = (bf16[320,256]{1,0:T(8,128)(2,1)}, bf16[320,256]{1,0:T(8,128)(2,1)}, u32[]{:S(2)}, u32[]{:S(2)}) collective-permute-start(bf16[320,256]{1,0:T(8,128)(2,1)} %get-tuple-element.42), channel_id=1, source_target_pairs={{0,2},{2,4},{4,6},{6,0},{1,3},{3,5},{5,7},{7,1},{8,10},{10,12},{12... | collective-permute-start | bytes 491528 | tf_op jit(solution)/shard_map/ppermute | solution.py:290
  35.8 16.1 %collective-permute-start.5 = (bf16[640,256]{1,0:T(8,128)(2,1)}, bf16[640,256]{1,0:T(8,128)(2,1)S(1)}, u32[]{:S(2)}, u32[]{:S(2)}) collective-permute-start(bf16[640,256]{1,0:T(8,128)(2,1)} %get-tuple-element.44), channel_id=1, source_target_pairs={{0,2},{2,4},{4,6},{6,0},{1,3},{3,5},{5,7},{7,1},{8,10},{10,12},{12... | collective-permute-start | bytes 983048 | tf_op jit(solution)/shard_map/ppermute | solution.py:290
  37.1 14.9 %collective-permute-start.6 = (bf16[640,256]{1,0:T(8,128)(2,1)}, bf16[640,256]{1,0:T(8,128)(2,1)S(1)}, u32[]{:S(2)}, u32[]{:S(2)}) collective-permute-start(bf16[640,256]{1,0:T(8,128)(2,1)} %get-tuple-element.45), channel_id=1, source_target_pairs={{0,6},{2,0},{4,2},{6,4},{1,7},{3,1},{5,3},{7,5},{8,14},{10,8},{12,... | collective-permute-start | bytes 983048 | tf_op jit(solution)/shard_map/ppermute | solution.py:290
  38.5 17.6 %all-to-all-start.1 = ((bf16[32,8,512]{2,1,0:T(8,128)(2,1)}), bf16[32,8,512]{2,1,0:T(8,128)(2,1)S(1)}, u32[]{:S(2)}, u32[]{:S(2)}) async-start(bf16[32,8,512]{2,1,0:T(8,128)(2,1)} %bitcast.7), calls=%async_computation.1 | async-start | bytes 524288 | tf_op jit(solution)/shard_map/all_to_all | solution.py:392
  49.2 28.4 %collective-permute-start.7 = (bf16[256,1792]{1,0:T(8,128)(2,1)}, bf16[256,1792]{1,0:T(8,128)(2,1)S(1)}, u32[]{:S(2)}, u32[]{:S(2)}) collective-permute-start(bf16[256,1792]{1,0:T(8,128)(2,1)} %get-tuple-element.86), channel_id=1, source_target_pairs={{0,8},{8,16},{16,24},{24,0},{1,9},{9,17},{17,25},{25,1},{2,10},{10... | collective-permute-start | bytes 2752520 | tf_op jit(solution)/shard_map/ppermute | solution.py:290
  50.4 27.2 %collective-permute-start.8 = (bf16[256,1792]{1,0:T(8,128)(2,1)}, bf16[256,1792]{1,0:T(8,128)(2,1)}, u32[]{:S(2)}, u32[]{:S(2)}) collective-permute-start(bf16[256,1792]{1,0:T(8,128)(2,1)} %get-tuple-element.85), channel_id=1, source_target_pairs={{0,24},{8,0},{16,8},{24,16},{1,25},{9,1},{17,9},{25,17},{2,26},{10... | collective-permute-start | bytes 2752520 | tf_op jit(solution)/shard_map/ppermute | solution.py:290
  59.0 17.3 %all-to-all-start.2 = ((bf16[32,8,640]{2,1,0:T(8,128)(2,1)}), bf16[32,8,640]{2,1,0:T(8,128)(2,1)S(1)}, u32[]{:S(2)}, u32[]{:S(2)}) async-start(bf16[32,8,640]{2,1,0:T(8,128)(2,1)} %bitcast.9), calls=%async_computation.2 | async-start | bytes 655360 | tf_op jit(solution)/shard_map/all_to_all | solution.py:410
  78.5 18.8 %all-to-all-start.3 = ((bf16[32,8,1024]{2,1,0:T(8,128)(2,1)}), bf16[32,8,1024]{2,1,0:T(8,128)(2,1)S(1)}, u32[]{:S(2)}, u32[]{:S(2)}) async-start(bf16[32,8,1024]{2,1,0:T(8,128)(2,1)} %shard_map.168), calls=%async_computation.3 | async-start | bytes 1048576 | tf_op jit(solution)/shard_map/all_to_all | solution.py:422
  84.5 20.1 %collective-permute-start.13 = (bf16[256,896]{1,0:T(8,128)(2,1)}, bf16[256,896]{1,0:T(8,128)(2,1)}, u32[]{:S(2)}, u32[]{:S(2)}) collective-permute-start(bf16[256,896]{1,0:T(8,128)(2,1)} %get-tuple-element.88), channel_id=1, source_target_pairs={{0,8},{8,16},{16,24},{24,0},{1,9},{9,17},{17,25},{25,1},{2,10},{10... | collective-permute-start | bytes 1376264 | tf_op jit(solution)/shard_map/ppermute | solution.py:290
  85.9 19.0 %collective-permute-start.15 = (bf16[256,896]{1,0:T(8,128)(2,1)}, bf16[256,896]{1,0:T(8,128)(2,1)}, u32[]{:S(2)}, u32[]{:S(2)}) collective-permute-start(bf16[256,896]{1,0:T(8,128)(2,1)} %get-tuple-element.87), channel_id=1, source_target_pairs={{0,24},{8,0},{16,8},{24,16},{1,25},{9,1},{17,9},{25,17},{2,26},{10... | collective-permute-start | bytes 1376264 | tf_op jit(solution)/shard_map/ppermute | solution.py:290
  98.2 9.2 %collective-permute-start.9 = (bf16[128,256]{1,0:T(8,128)(2,1)S(1)}, bf16[128,256]{1,0:T(8,128)(2,1)S(1)}, u32[]{:S(2)}, u32[]{:S(2)}) collective-permute-start(bf16[128,256]{1,0:T(8,128)(2,1)S(1)} %get-tuple-element.58), channel_id=1, source_target_pairs={{0,1},{1,0},{2,3},{3,2},{4,5},{5,4},{6,7},{7,6},{8,9},{9,8},{10,11... | collective-permute-start | bytes 196616 | tf_op jit(solution)/shard_map/ppermute | solution.py:290
  104.7 13.5 %collective-permute-start.14 = (bf16[256,896]{1,0:T(8,128)(2,1)}, bf16[256,896]{1,0:T(8,128)(2,1)S(1)}, u32[]{:S(2)}, u32[]{:S(2)}) collective-permute-start(bf16[256,896]{1,0:T(8,128)(2,1)} %collective-permute-done.13), channel_id=1, source_target_pairs={{0,8},{8,16},{16,24},{24,0},{1,9},{9,17},{17,25},{25,1},{2,10},{10... | collective-permute-start | bytes 1376264 | tf_op jit(solution)/shard_map/ppermute | solution.py:290
  104.8 13.4 %collective-permute-start.16 = (bf16[256,896]{1,0:T(8,128)(2,1)}, bf16[256,896]{1,0:T(8,128)(2,1)S(1)}, u32[]{:S(2)}, u32[]{:S(2)}) collective-permute-start(bf16[256,896]{1,0:T(8,128)(2,1)} %collective-permute-done.15), channel_id=1, source_target_pairs={{0,24},{8,0},{16,8},{24,16},{1,25},{9,1},{17,9},{25,17},{2,26},{10... | collective-permute-start | bytes 1376264 | tf_op jit(solution)/shard_map/ppermute | solution.py:290
  134.1 31.5 %all-to-all-start.4 = ((bf16[8,32,1920]{2,1,0:T(8,128)(2,1)}), bf16[8,32,1920]{2,1,0:T(8,128)(2,1)S(1)}, u32[]{:S(2)}, u32[]{:S(2)}) async-start(bf16[8,32,1920]{2,1,0:T(8,128)(2,1)} %bitcast.23), calls=%async_computation.4 | async-start | bytes 1966080 | tf_op jit(solution)/shard_map/all_to_all | solution.py:299
  137.8 17.9 %collective-permute-start.21 = (bf16[896,256]{1,0:T(8,128)(2,1)}, bf16[896,256]{1,0:T(8,128)(2,1)S(1)}, u32[]{:S(2)}, u32[]{:S(2)}) collective-permute-start(bf16[896,256]{1,0:T(8,128)(2,1)} %get-tuple-element.60), channel_id=1, source_target_pairs={{0,8},{8,16},{16,24},{24,0},{1,9},{9,17},{17,25},{25,1},{2,10},{10... | collective-permute-start | bytes 1376264 | tf_op jit(solution)/shard_map/ppermute | solution.py:290
  137.8 18.6 %collective-permute-start.22 = (bf16[896,256]{1,0:T(8,128)(2,1)S(1)}, bf16[896,256]{1,0:T(8,128)(2,1)S(1)}, u32[]{:S(2)}, u32[]{:S(2)}) collective-permute-start(bf16[896,256]{1,0:T(8,128)(2,1)S(1)} %get-tuple-element.61), channel_id=1, source_target_pairs={{0,24},{8,0},{16,8},{24,16},{1,25},{9,1},{17,9},{25,17},{2,26},{10... | collective-permute-start | bytes 1376264 | tf_op jit(solution)/shard_map/ppermute | solution.py:290
  140.5 15.2 %collective-permute-start.23 = (bf16[448,256]{1,0:T(8,128)(2,1)}, bf16[448,256]{1,0:T(8,128)(2,1)S(1)}, u32[]{:S(2)}, u32[]{:S(2)}) collective-permute-start(bf16[448,256]{1,0:T(8,128)(2,1)} %get-tuple-element.62), channel_id=1, source_target_pairs={{0,8},{8,16},{16,24},{24,0},{1,9},{9,17},{17,25},{25,1},{2,10},{10... | collective-permute-start | bytes 688136 | tf_op jit(solution)/shard_map/ppermute | solution.py:290
  140.5 15.2 %collective-permute-start.24 = (bf16[448,256]{1,0:T(8,128)(2,1)}, bf16[448,256]{1,0:T(8,128)(2,1)S(1)}, u32[]{:S(2)}, u32[]{:S(2)}) collective-permute-start(bf16[448,256]{1,0:T(8,128)(2,1)} %get-tuple-element.63), channel_id=1, source_target_pairs={{0,24},{8,0},{16,8},{24,16},{1,25},{9,1},{17,9},{25,17},{2,26},{10... | collective-permute-start | bytes 688136 | tf_op jit(solution)/shard_map/ppermute | solution.py:290
  166.6 19.9 %all-to-all-start.5 = ((bf16[8,32,896]{2,1,0:T(8,128)(2,1)}), bf16[8,32,896]{2,1,0:T(8,128)(2,1)S(1)}, u32[]{:S(2)}, u32[]{:S(2)}) async-start(bf16[8,32,896]{2,1,0:T(8,128)(2,1)} %shard_map.171), calls=%async_computation.5 | async-start | bytes 917504 | tf_op jit(solution)/shard_map/all_to_all | solution.py:468
  170.1 8.2 %collective-permute-start.25 = (bf16[448,256]{1,0:T(8,128)(2,1)}, bf16[448,256]{1,0:T(8,128)(2,1)S(1)}, u32[]{:S(2)}, u32[]{:S(2)}) collective-permute-start(bf16[448,256]{1,0:T(8,128)(2,1)} %copy-done.20), channel_id=1, source_target_pairs={{0,8},{8,16},{16,24},{24,0},{1,9},{9,17},{17,25},{25,1},{2,10},{10... | collective-permute-start | bytes 688136 | tf_op jit(solution)/shard_map/ppermute | solution.py:290
  (39 other events, 396.3 us)

commit v11 on v10

--- a/solution.py
+++ b/solution.py
@@ -215,8 +215,8 @@
     mine_ref[...] = dot(a_ref[mine, :], w_ref[...])
 
 
-def gate_up_kernel(place_ref, own_ref, other_ref, w0, w1, gate2, up2, w3, out_ref, m_ref):
-    units = gate2.shape[1]
+def gate_up_kernel(place_ref, own_ref, other_ref, w0, w1, w2, w3, out_ref, m_ref):
+    units = w0.shape[1]
     step = pl.program_id(0)
 
     @pl.when(step == 0)
@@ -227,17 +227,17 @@
             m_ref[d, mine, :] = own_ref[d * rows : (d + 1) * rows]
             m_ref[d, theirs, :] = other_ref[d * rows : (d + 1) * rows]
 
-    def product(w2):
+    def product():
         total = dot(m_ref[0], w0[...]) + dot(m_ref[1], w1[...])
         return (total + dot(m_ref[2], w2[...]) + dot(m_ref[3], w3[...])).astype(BF)
 
     @pl.when(step == 0)
     def _():
-        out_ref[:, :units] = product(gate2)
+        out_ref[:, :units] = product()
 
     @pl.when(step == 1)
     def _():
-        out_ref[:, units : 2 * units] = product(up2)
+        out_ref[:, units : 2 * units] = product()
         square = jnp.zeros((m_ref.shape[1], 1), F32)
         for d in range(4):
             value = m_ref[d].astype(F32)
@@ -248,9 +248,8 @@
         out_ref[:, 2 * units :] = extra.astype(BF)
 
 
-def down_kernel(place_ref, a_ref, d0, d1, low2, high2, d3, mine_ref, theirs_ref):
+def down_kernel(place_ref, a_ref, d0, d1, d2, d3, mine_ref, theirs_ref):
     active = a_ref[...]
-    half = low2.shape[0]
     rows = mine_ref.shape[1]
 
     def store(d, total, keep_ref):
@@ -261,7 +260,7 @@
     def run(keep_ref):
         store(0, dot(active, d0[...]), keep_ref)
         store(1, dot(active, d1[...]), keep_ref)
-        store(2, dot(active[:, :half], low2[...]) + dot(active[:, half:], high2[...]), keep_ref)
+        store(2, dot(active, d2[...]), keep_ref)
         store(3, dot(active, d3[...]), keep_ref)
 
     pl.run_scoped(run, pltpu.VMEM((4,) + active.shape[:1] + (d0.shape[1],), F32))
@@ -367,7 +366,6 @@
 
     chips_y = lax.axis_size("y")
     units = hidden_part // chips_y
-    half = units // 2
     gain = mlp_gain[:, None]
 
     def columns(weight, d):
@@ -399,17 +397,16 @@
         compiler_params=params(),
     )(me, image_tiles, own, kv_left, kv_right, k_gain.reshape(1, HEAD), queries, row_image)
     gate_weight, up_weight, down_weight = lax.optimization_barrier((gate_weight, up_weight, down_weight, mixed))[:3]
-    gate_2, up_2 = wide(columns(gate_weight, 2)), wide(columns(up_weight, 2))
-
-    def rows(d, start, size):
-        at = lax.rem(lax.axis_index("y") + d, chips_y) * units + start
-        return lax.dynamic_slice_in_dim(down_weight, at, size, 0)
-
-    down_0, down_1, down_3 = rows(0, 0, units), rows(1, 0, units), rows(3, 0, units)
-    down_2 = rows(2, 0, half), rows(2, half, half)
+    wide_2 = wide(columns(gate_weight, 2), columns(up_weight, 2))
+
+    def rows(d):
+        at = lax.rem(lax.axis_index("y") + d, chips_y) * units
+        return lax.dynamic_slice_in_dim(down_weight, at, units, 0)
+
+    down_0, down_1, down_2, down_3 = rows(0), rows(1), rows(2), rows(3)
     mixed = lax.all_to_all(mixed, GROUP, 0, 0, tiled=True)
-    mixed = after(mixed, gate_2, up_2, down_1, down_3, *down_2)
-    gate_2, up_2 = shift(gate_2, "y", 1), shift(up_2, "y", -1)
+    mixed = after(mixed, wide_2, down_1, down_2, down_3)
+    wide_2 = shift(wide_2, "y", 2)
 
     attended = pl.pallas_call(
         combine_kernel,
@@ -435,29 +432,25 @@
     )(place, attended, o_weight)
     pair = (mine + shift(theirs, "c", 1).astype(F32)).astype(BF)
     attn_sum = chip_sum(pair)
-    gate_2, up_2 = shift(gate_2, "y", 1), shift(up_2, "y", -1)
     middle = (half_f + jnp.tanh(gate_logits[0]) * attn_sum).astype(BF)
-    middle = after(middle, gate_2, up_2)
+    middle = after(middle, wide_2)
     middle_f = middle.astype(F32)
     own_rows_all = jnp.concatenate([middle] + [shift(middle, "y", d) for d in (1, 2, 3)], axis=0)
     other_rows_all = shift(own_rows_all, "c", 1)
     block = pl.BlockSpec((4 * half_rows, width_part), lambda i: (0, 0))
     direct = pl.BlockSpec((width_part, units), lambda i: (0, i))
-    passed = pl.BlockSpec((width_part, units), lambda i: (0, 0))
     gate_up = pl.pallas_call(
         gate_up_kernel,
         grid=(2,),
-        in_specs=[smem()] + [block] * 2 + [direct] * 2 + [passed] * 2 + [direct],
+        in_specs=[smem()] + [block] * 2 + [direct] * 4,
         out_specs=pl.BlockSpec((all_rows, 2 * units + HEAD), lambda i: (0, 0)),
         out_shape=jax.ShapeDtypeStruct((all_rows, 2 * units + HEAD), BF),
         scratch_shapes=[pltpu.VMEM((4, all_rows, width_part), BF)],
         compiler_params=params(LARGE_VMEM_BYTES),
-    )(place, own_rows_all, other_rows_all, wide_0, wide_1, gate_2, up_2, wide_3)
-    down_1, down_3, *down_2 = lax.optimization_barrier((down_1, down_3, *down_2, gate_up))[:4]
-    down_1, down_3 = shift(down_1, "y", 1), shift(down_3, "y", -1)
-    down_2 = shift(down_2[0], "y", 1), shift(down_2[1], "y", -1)
-    parts = after(exchange(gate_up, "z"), down_1, down_3, *down_2)
-    down_2 = shift(down_2[0], "y", 1), shift(down_2[1], "y", -1)
+    )(place, own_rows_all, other_rows_all, wide_0, wide_1, wide_2, wide_3)
+    down_1, down_2, down_3 = lax.optimization_barrier((down_1, down_2, down_3, gate_up))[:3]
+    down_1, down_2, down_3 = shift(down_1, "y", 1), shift(down_2, "y", 2), shift(down_3, "y", -1)
+    parts = after(exchange(gate_up, "z"), down_1, down_2, down_3)
     active = pl.pallas_call(
         functools.partial(active_kernel, full_width),
         in_specs=[vmem()],
@@ -468,14 +461,14 @@
     active = lax.all_to_all(active, "z", 0, 0, tiled=True).reshape(all_rows, units)
     mine, theirs = pl.pallas_call(
         down_kernel,
-        in_specs=[smem()] + [vmem()] * 6,
+        in_specs=[smem()] + [vmem()] * 5,
         out_specs=[vmem()] * 2,
         out_shape=[
             jax.ShapeDtypeStruct((4, half_rows, width_part), F32),
             jax.ShapeDtypeStruct((4, half_rows, width_part), BF),
         ],
         compiler_params=params(),
-    )(place, active, down_0, down_1, *down_2, down_3)
+    )(place, active, down_0, down_1, down_2, down_3)
     own_down, behind, across, ahead = pl.pallas_call(
         pair_kernel,
         in_specs=[vmem()] * 2,

time: 208 us -> 223 us (1.072)
  blocking collectives: 0 us -> 15.9 us
  starting transfers between devices: 85.1 us -> 96.4 us
  waiting for transfers between devices: 78.4 us -> 68.6 us
    all_to_all x0 -> x1, blocking collectives: none -> 15.9 us  [shards(): lax.all_to_all(active, 'z', 0, 0, tiled=True).reshape(all_rows, units)]
    all_to_all x2, starting transfers between devices: 13.2 us -> 23 us  [exchange(): out = lax.all_to_all(value, axis, 0, 0, tiled=True)]
    all_to_all x1 -> x0, waiting for transfers between devices: 8.29 us -> none  [shards(): lax.all_to_all(active, 'z', 0, 0, tiled=True).reshape(all_rows, units)]
    all_to_all x2, waiting for transfers between devices: 13.2 us -> 7.44 us  [exchange(): out = lax.all_to_all(value, axis, 0, 0, tiled=True)]
    all_to_all x1, waiting for transfers between devices: 6.78 us -> 12.2 us  [shards(): mixed = lax.all_to_all(mixed, GROUP, 0, 0, tiled=True)]
    all_to_all x1 -> x0, starting transfers between devices: 3.47 us -> none  [shards(): lax.all_to_all(active, 'z', 0, 0, tiled=True).reshape(all_rows, units)]
    dynamic_slice x1 -> x2, local copies, waits for them, and re-layouts: 1.57 us -> 4.22 us  [columns(): return lax.dynamic_slice_in_dim(weight, at, units, 1).astype(F32)]
    all_to_all x1, waiting for transfers between devices: 4.11 us -> 1.49 us  [shards(): queries = lax.all_to_all(queries, GROUP, 0, 0, tiled=True)]
  transfers between devices with their start and end apart: 41 -> 34, of which waited for: 20 -> 22; matrix products, arithmetic and copies ran while one was open for 7% -> 4% of each run, Pallas kernels for 7% -> 5%
where the time goes in v11:
time: 223 us
  starting transfers between devices  96.4 us (43%)
  waiting for transfers between devices  68.6 us (31%)
  Pallas kernels  23.1 us (10%)
  blocking collectives  15.9 us (7%)
  local copies, waits for them, and re-layouts  10.7 us (5%)
  other arithmetic  4.05 us (2%)
    ppermute x29, starting transfers between devices, shift(): return lax.ppermute(value, axis, [(i, (i + by) % n) for i in range(n)])  52.9 us
    ppermute x29, waiting for transfers between devices, shift(): return lax.ppermute(value, axis, [(i, (i + by) % n) for i in range(n)])  37.2 us
    all_to_all x2, starting transfers between devices, exchange(): out = lax.all_to_all(value, axis, 0, 0, tiled=True)  23 us
    all_to_all x1, blocking collectives, shards(): lax.all_to_all(active, 'z', 0, 0, tiled=True).reshape(all_rows, units)  15.9 us
    all_to_all x1, waiting for transfers between devices, shards(): mixed = lax.all_to_all(mixed, GROUP, 0, 0, tiled=True)  12.2 us
    all_to_all x1, waiting for transfers between devices, shards(): lax.all_to_all(attended, GROUP, 0, 0, tiled=True)  10.3 us
    pallas_call x1, Pallas kernels, kv_project(): pl.pallas_call(kv_kernel, grid_spec=pltpu.PrefetchScalarGridSpec(num_scal...  7.93 us
    all_to_all x2, waiting for transfers between devices, exchange(): out = lax.all_to_all(value, axis, 0, 0, tiled=True)  7.44 us
  transfers between devices with their start and end apart: 34, of which 22 were waited for; matrix products, arithmetic and copies ran while one was open for 4% of the time, Pallas kernels for 5%

profile of v11, /device:TPU:1, one launch (start us, length us, event | category | flops | bytes accessed | tf_op | source)
XLA Modules:
  0.0 222.5 jit_solution(1713530183819344438)
XLA Ops:
  0.0 3.2 %collective-permute-start.1 = (bf16[1024,1024]{1,0:T(8,128)(2,1)}, bf16[1024,1024]{1,0:T(8,128)(2,1)}, u32[]{:S(2)}, u32[]{:S(2)}) collective-permute-start(bf16[1024,1024]{1,0:T(8,128)(2,1)} %k0.1), channel_id=1, source_target_pairs={{0,1},{1,0},{2,3},{3,2},{4,5},{5,4},{6,7},{7,6},{8,9},{9,8},{10,11... | collective-permute-start | bytes 6291464 | tf_op jit(solution)/shard_map/ppermute | solution.py:289
  6.4 9.5 %all-to-all-start = ((bf16[32,8,1024]{2,1,0:T(8,128)(2,1)}), bf16[32,8,1024]{2,1,0:T(8,128)(2,1)S(1)}, u32[]{:S(2)}, u32[]{:S(2)}) async-start(bf16[32,8,1024]{2,1,0:T(8,128)(2,1)} %fusion), calls=%async_computation | async-start | bytes 1048576 | tf_op jit(solution)/shard_map/all_to_all | solution.py:298
  17.0 7.9 %shard_map.163 = (bf16[320,256]{1,0:T(8,128)(2,1)}, bf16[320,256]{1,0:T(8,128)(2,1)}, bf16[640,256]{1,0:T(8,128)(2,1)}, bf16[640,256]{1,0:T(8,128)(2,1)}, bf16[640,256]{1,0:T(8,128)(2,1)}) custom-call(s32[2]{0:T(128)} %pad_add_fusion.place_ref, bf16[640,1024]{1,0:T(8,128)(2,1)} %x0.1, bf16[640,1024]{1,0:T(8,128)(2,1)} %copy-done.10, bf16[1024,1024]{1,0:T(8,128)(2,1)} %k0.1, ...), custom_call_target="tpu_custom_call" | custom-call | tf_op jit(solution)/shard_map/pallas_call | solution.py:109
  28.5 4.2 %all-to-all-done.parts_ref = bf16[32,8,1024]{2,1,0:T(8,128)(2,1)S(1)} async-done(((bf16[32,8,1024]{2,1,0:T(8,128)(2,1)}), bf16[32,8,1024]{2,1,0:T(8,128)(2,1)S(1)}, u32[]{:S(2)}, u32[]{:S(2)}) %all-to-all-start) | async-done | bytes 524320 | tf_op jit(solution)/shard_map/all_to_all | solution.py:298
  36.6 7.0 %all-to-all-start.1 = ((bf16[32,8,512]{2,1,0:T(8,128)(2,1)}), bf16[32,8,512]{2,1,0:T(8,128)(2,1)S(1)}, u32[]{:S(2)}, u32[]{:S(2)}) async-start(bf16[32,8,512]{2,1,0:T(8,128)(2,1)} %bitcast.7), calls=%async_computation.1 | async-start | bytes 524288 | tf_op jit(solution)/shard_map/all_to_all | solution.py:390
  46.4 3.0 %constant_dynamic-slice_fusion.1 = (bf16[256,896]{1,0:T(8,128)(2,1)S(1)}, bf16[256,896]{1,0:T(8,128)(2,1)S(1)}, bf16[256,896]{1,0:T(8,128)(2,1)S(1)}, bf16[256,8...) fusion(bf16[256,3584]{1,0:T(8,128)(2,1)} %param.29, s32[]{:T(128)S(6)} %select_n.50, ...), kind=kLoop, calls=%fused_computation.22 | loop fusion | bytes 5505036 | tf_op jit(solution)/shard_map/dynamic_slice | solution.py:373
  49.4 3.1 %collective-permute-done.5.left_ref = bf16[640,256]{1,0:T(8,128)(2,1)S(1)} collective-permute-done((bf16[640,256]{1,0:T(8,128)(2,1)}, bf16[640,256]{1,0:T(8,128)(2,1)S(1)}, u32[]{:S(2)}, u32[]{:S(2)}) %collective-permute-start.5) | collective-permute-done | bytes 327712 | tf_op jit(solution)/shard_map/ppermute | solution.py:289
  54.0 2.9 %shard_map.167 = bf16[256,640]{1,0:T(8,128)(2,1)} custom-call(s32[1]{0:T(128)} %bitcast.3.me_ref, s32[32,4]{1,0:T(8,128)S(1)} %copy.27.tiles_ref, bf16[640,256]{1,0:T(8,128)(2,1)S(1)} %copy-done.2, bf16[640,256]{1,0:T(8,128)(2,1)S(1)} %collective-permute-done.5.left_ref, bf16[640,256]{1,0:T(8,128)(2,1)S(1)} %collective-permute-done.6.right_ref, ...), custom_call_target="tpu_custom_call" | custom-call | tf_op jit(solution)/shard_map/pallas_call | solution.py:392
  63.2 6.4 %all-to-all-start.2 = ((bf16[32,8,640]{2,1,0:T(8,128)(2,1)}), bf16[32,8,640]{2,1,0:T(8,128)(2,1)S(1)}, u32[]{:S(2)}, u32[]{:S(2)}) async-start(bf16[32,8,640]{2,1,0:T(8,128)(2,1)} %bitcast.9), calls=%async_computation.2 | async-start | bytes 655360 | tf_op jit(solution)/shard_map/all_to_all | solution.py:407
  72.2 12.2 %all-to-all-done.2 = bf16[32,8,640]{2,1,0:T(8,128)(2,1)S(1)} async-done(((bf16[32,8,640]{2,1,0:T(8,128)(2,1)}), bf16[32,8,640]{2,1,0:T(8,128)(2,1)S(1)}, u32[]{:S(2)}, u32[]{:S(2)}) %all-to-all-start.2) | async-done | bytes 327712 | tf_op jit(solution)/shard_map/all_to_all | solution.py:407
  85.8 7.0 %all-to-all-start.3 = ((bf16[32,8,1024]{2,1,0:T(8,128)(2,1)}), bf16[32,8,1024]{2,1,0:T(8,128)(2,1)S(1)}, u32[]{:S(2)}, u32[]{:S(2)}) async-start(bf16[32,8,1024]{2,1,0:T(8,128)(2,1)} %shard_map.168), calls=%async_computation.3 | async-start | bytes 1048576 | tf_op jit(solution)/shard_map/all_to_all | solution.py:419
  92.8 2.8 %collective-permute-start.13 = (bf16[256,1792]{1,0:T(8,128)(2,1)}, bf16[256,1792]{1,0:T(8,128)(2,1)}, u32[]{:S(2)}, u32[]{:S(2)}) collective-permute-start(bf16[256,1792]{1,0:T(8,128)(2,1)} %get-tuple-element.84), channel_id=1, source_target_pairs={{0,16},{8,24},{16,0},{24,8},{1,17},{9,25},{17,1},{25,9},{2,18},{10... | collective-permute-start | bytes 2752520 | tf_op jit(solution)/shard_map/ppermute | solution.py:289
  95.6 10.3 %all-to-all-done.3 = bf16[32,8,1024]{2,1,0:T(8,128)(2,1)S(1)} async-done(((bf16[32,8,1024]{2,1,0:T(8,128)(2,1)}), bf16[32,8,1024]{2,1,0:T(8,128)(2,1)S(1)}, u32[]{:S(2)}, u32[]{:S(2)}) %all-to-all-start.3) | async-done | bytes 524320 | tf_op jit(solution)/shard_map/all_to_all | solution.py:419
  106.7 6.5 %collective-permute-start.9 = (bf16[128,256]{1,0:T(8,128)(2,1)S(1)}, bf16[128,256]{1,0:T(8,128)(2,1)S(1)}, u32[]{:S(2)}, u32[]{:S(2)}) collective-permute-start(bf16[128,256]{1,0:T(8,128)(2,1)S(1)} %get-tuple-element.57), channel_id=1, source_target_pairs={{0,1},{1,0},{2,3},{3,2},{4,5},{5,4},{6,7},{7,6},{8,9},{9,8},{10,11... | collective-permute-start | bytes 196616 | tf_op jit(solution)/shard_map/ppermute | solution.py:289
  126.6 4.7 %collective-permute-start.17 = (bf16[512,256]{1,0:T(8,128)(2,1)S(1)}, bf16[512,256]{1,0:T(8,128)(2,1)S(1)}, u32[]{:S(2)}, u32[]{:S(2)}) collective-permute-start(bf16[512,256]{1,0:T(8,128)(2,1)S(1)} %constant_dynamic-update-slice_fusion.own_ref), channel_id=1, source_target_pairs={{0,1},{1,0},{2,3},{3,2},{4,5},{5,4},{6,7},{7,6},{8,9},{9,8},{10,11... | collective-permute-start | bytes 786440 | tf_op jit(solution)/shard_map/ppermute | solution.py:289
  133.1 4.2 %shard_map.170 = bf16[256,1920]{1,0:T(8,128)(2,1)} custom-call(s32[2]{0:T(128)} %pad_add_fusion.place_ref, bf16[512,256]{1,0:T(8,128)(2,1)} %copy-done.11, bf16[512,256]{1,0:T(8,128)(2,1)} %copy-done.13, bf16[256,1792]{1,0:T(8,128)(2,1)} %get-tuple-element.81.w0, bf16[256,1792]{1,0:T(8,128)(2,1)} %collective-permute-done.7.w1, ...), custom_call_target="tpu_custom_call" | custom-call | tf_op jit(solution)/shard_map/pallas_call | solution.py:442
  137.4 13.5 %all-to-all-start.4 = ((bf16[8,32,1920]{2,1,0:T(8,128)(2,1)}), bf16[8,32,1920]{2,1,0:T(8,128)(2,1)S(1)}, u32[]{:S(2)}, u32[]{:S(2)}) async-start(bf16[8,32,1920]{2,1,0:T(8,128)(2,1)} %bitcast.23), calls=%async_computation.4 | async-start | bytes 1966080 | tf_op jit(solution)/shard_map/all_to_all | solution.py:298
  151.9 3.5 %collective-permute-start.19 = (bf16[896,256]{1,0:T(8,128)(2,1)}, bf16[896,256]{1,0:T(8,128)(2,1)S(1)}, u32[]{:S(2)}, u32[]{:S(2)}) collective-permute-start(bf16[896,256]{1,0:T(8,128)(2,1)} %get-tuple-element.60), channel_id=1, source_target_pairs={{0,16},{8,24},{16,0},{24,8},{1,17},{9,25},{17,1},{25,9},{2,18},{10... | collective-permute-start | bytes 1376264 | tf_op jit(solution)/shard_map/ppermute | solution.py:289
  155.5 9.3 %collective-permute-done.18.d1 = bf16[896,256]{1,0:T(8,128)(2,1)S(1)} collective-permute-done((bf16[896,256]{1,0:T(8,128)(2,1)}, bf16[896,256]{1,0:T(8,128)(2,1)S(1)}, u32[]{:S(2)}, u32[]{:S(2)}) %collective-permute-start.18) | collective-permute-done | bytes 458784 | tf_op jit(solution)/shard_map/ppermute | solution.py:289
  164.8 10.7 %collective-permute-done.19.d2 = bf16[896,256]{1,0:T(8,128)(2,1)S(1)} collective-permute-done((bf16[896,256]{1,0:T(8,128)(2,1)}, bf16[896,256]{1,0:T(8,128)(2,1)S(1)}, u32[]{:S(2)}, u32[]{:S(2)}) %collective-permute-start.19) | collective-permute-done | bytes 458784 | tf_op jit(solution)/shard_map/ppermute | solution.py:289
  175.5 3.3 %all-to-all-done.4.parts_ref = bf16[8,32,1920]{2,1,0:T(8,128)(2,1)S(1)} async-done(((bf16[8,32,1920]{2,1,0:T(8,128)(2,1)}), bf16[8,32,1920]{2,1,0:T(8,128)(2,1)S(1)}, u32[]{:S(2)}, u32[]{:S(2)}) %all-to-all-start.4) | async-done | bytes 983072 | tf_op jit(solution)/shard_map/all_to_all | solution.py:298
  179.0 15.9 %all_to_all.51 = bf16[8,32,896]{2,1,0:T(8,128)(2,1)S(1)} all-to-all(bf16[8,32,896]{2,1,0:T(8,128)(2,1)S(1)} %shard_map.171), channel_id=1, replica_groups=mesh['z'=8,'y'=4,'x'=4,'c'=2] {'z'}, dimensions={0} | all-to-all | bytes 917504 | tf_op jit(solution)/shard_map/all_to_all | solution.py:461
  197.0 4.0 %collective-permute-start.21 = (bf16[4,128,256]{2,1,0:T(8,128)(2,1)}, bf16[4,128,256]{2,1,0:T(8,128)(2,1)S(1)}, u32[]{:S(2)}, u32[]{:S(2)}) collective-permute-start(bf16[4,128,256]{2,1,0:T(8,128)(2,1)} %get-tuple-element.64), channel_id=1, source_target_pairs={{0,1},{1,0},{2,3},{3,2},{4,5},{5,4},{6,7},{7,6},{8,9},{9,8},{10,11... | collective-permute-start | bytes 786440 | tf_op jit(solution)/shard_map/ppermute | solution.py:289
  217.1 3.9 %collective-permute-start.28 = (bf16[128,256]{1,0:T(8,128)(2,1)S(1)}, bf16[128,256]{1,0:T(8,128)(2,1)S(1)}, u32[]{:S(2)}, u32[]{:S(2)}) collective-permute-start(bf16[128,256]{1,0:T(8,128)(2,1)S(1)} %add_convert_fusion), channel_id=1, source_target_pairs={{0,1},{1,0},{2,3},{3,2},{4,5},{5,4},{6,7},{7,6},{8,9},{9,8},{10,11... | collective-permute-start | bytes 196616 | tf_op jit(solution)/shard_map/ppermute | solution.py:289
  (126 shorter events, 61.7 us)
Async XLA Ops:
  0.0 16.0 %collective-permute-start.1 = (bf16[1024,1024]{1,0:T(8,128)(2,1)}, bf16[1024,1024]{1,0:T(8,128)(2,1)}, u32[]{:S(2)}, u32[]{:S(2)}) collective-permute-start(bf16[1024,1024]{1,0:T(8,128)(2,1)} %k0.1), channel_id=1, source_target_pairs={{0,1},{1,0},{2,3},{3,2},{4,5},{5,4},{6,7},{7,6},{8,9},{9,8},{10,11... | collective-permute-start | bytes 6291464 | tf_op jit(solution)/shard_map/ppermute | solution.py:289
  3.2 12.7 %collective-permute-start.2 = (bf16[1024,1024]{1,0:T(8,128)(2,1)}, bf16[1024,1024]{1,0:T(8,128)(2,1)}, u32[]{:S(2)}, u32[]{:S(2)}) collective-permute-start(bf16[1024,1024]{1,0:T(8,128)(2,1)} %v0.1), channel_id=1, source_target_pairs={{0,1},{1,0},{2,3},{3,2},{4,5},{5,4},{6,7},{7,6},{8,9},{9,8},{10,11... | collective-permute-start | bytes 6291464 | tf_op jit(solution)/shard_map/ppermute | solution.py:289
  3.2 12.7 %collective-permute-start = (bf16[640,1024]{1,0:T(8,128)(2,1)}, bf16[640,1024]{1,0:T(8,128)(2,1)S(1)}, u32[]{:S(2)}, u32[]{:S(2)}) collective-permute-start(bf16[640,1024]{1,0:T(8,128)(2,1)} %x0.1), channel_id=1, source_target_pairs={{0,1},{1,0},{2,3},{3,2},{4,5},{5,4},{6,7},{7,6},{8,9},{9,8},{10,11... | collective-permute-start | bytes 3932168 | tf_op jit(solution)/shard_map/ppermute | solution.py:289
  6.4 26.3 %all-to-all-start = ((bf16[32,8,1024]{2,1,0:T(8,128)(2,1)}), bf16[32,8,1024]{2,1,0:T(8,128)(2,1)S(1)}, u32[]{:S(2)}, u32[]{:S(2)}) async-start(bf16[32,8,1024]{2,1,0:T(8,128)(2,1)} %fusion), calls=%async_computation | async-start | bytes 1048576 | tf_op jit(solution)/shard_map/all_to_all | solution.py:298
  25.0 8.8 %collective-permute-start.3 = (bf16[320,256]{1,0:T(8,128)(2,1)}, bf16[320,256]{1,0:T(8,128)(2,1)S(1)}, u32[]{:S(2)}, u32[]{:S(2)}) collective-permute-start(bf16[320,256]{1,0:T(8,128)(2,1)} %get-tuple-element.41), channel_id=1, source_target_pairs={{0,2},{2,4},{4,6},{6,0},{1,3},{3,5},{5,7},{7,1},{8,10},{10,12},{12... | collective-permute-start | bytes 491528 | tf_op jit(solution)/shard_map/ppermute | solution.py:289
  26.3 7.5 %collective-permute-start.4 = (bf16[320,256]{1,0:T(8,128)(2,1)}, bf16[320,256]{1,0:T(8,128)(2,1)S(1)}, u32[]{:S(2)}, u32[]{:S(2)}) collective-permute-start(bf16[320,256]{1,0:T(8,128)(2,1)} %get-tuple-element.42), channel_id=1, source_target_pairs={{0,6},{2,0},{4,2},{6,4},{1,7},{3,1},{5,3},{7,5},{8,14},{10,8},{12,... | collective-permute-start | bytes 491528 | tf_op jit(solution)/shard_map/ppermute | solution.py:289
  36.6 17.4 %all-to-all-start.1 = ((bf16[32,8,512]{2,1,0:T(8,128)(2,1)}), bf16[32,8,512]{2,1,0:T(8,128)(2,1)S(1)}, u32[]{:S(2)}, u32[]{:S(2)}) async-start(bf16[32,8,512]{2,1,0:T(8,128)(2,1)} %bitcast.7), calls=%async_computation.1 | async-start | bytes 524288 | tf_op jit(solution)/shard_map/all_to_all | solution.py:390
  43.6 8.9 %collective-permute-start.5 = (bf16[640,256]{1,0:T(8,128)(2,1)}, bf16[640,256]{1,0:T(8,128)(2,1)S(1)}, u32[]{:S(2)}, u32[]{:S(2)}) collective-permute-start(bf16[640,256]{1,0:T(8,128)(2,1)} %get-tuple-element.43), channel_id=1, source_target_pairs={{0,2},{2,4},{4,6},{6,0},{1,3},{3,5},{5,7},{7,1},{8,10},{10,12},{12... | collective-permute-start | bytes 983048 | tf_op jit(solution)/shard_map/ppermute | solution.py:289
  44.5 8.0 %collective-permute-start.6 = (bf16[640,256]{1,0:T(8,128)(2,1)}, bf16[640,256]{1,0:T(8,128)(2,1)S(1)}, u32[]{:S(2)}, u32[]{:S(2)}) collective-permute-start(bf16[640,256]{1,0:T(8,128)(2,1)} %get-tuple-element.44), channel_id=1, source_target_pairs={{0,6},{2,0},{4,2},{6,4},{1,7},{3,1},{5,3},{7,5},{8,14},{10,8},{12,... | collective-permute-start | bytes 983048 | tf_op jit(solution)/shard_map/ppermute | solution.py:289
  60.5 25.2 %collective-permute-start.7 = (bf16[256,1792]{1,0:T(8,128)(2,1)}, bf16[256,1792]{1,0:T(8,128)(2,1)}, u32[]{:S(2)}, u32[]{:S(2)}) collective-permute-start(bf16[256,1792]{1,0:T(8,128)(2,1)} %get-tuple-element.82), channel_id=1, source_target_pairs={{0,8},{8,16},{16,24},{24,0},{1,9},{9,17},{17,25},{25,1},{2,10},{10... | collective-permute-start | bytes 2752520 | tf_op jit(solution)/shard_map/ppermute | solution.py:289
  60.5 25.2 %collective-permute-start.8 = (bf16[256,1792]{1,0:T(8,128)(2,1)}, bf16[256,1792]{1,0:T(8,128)(2,1)}, u32[]{:S(2)}, u32[]{:S(2)}) collective-permute-start(bf16[256,1792]{1,0:T(8,128)(2,1)} %get-tuple-element.83), channel_id=1, source_target_pairs={{0,24},{8,0},{16,8},{24,16},{1,25},{9,1},{17,9},{25,17},{2,26},{10... | collective-permute-start | bytes 2752520 | tf_op jit(solution)/shard_map/ppermute | solution.py:289
  63.2 21.3 %all-to-all-start.2 = ((bf16[32,8,640]{2,1,0:T(8,128)(2,1)}), bf16[32,8,640]{2,1,0:T(8,128)(2,1)S(1)}, u32[]{:S(2)}, u32[]{:S(2)}) async-start(bf16[32,8,640]{2,1,0:T(8,128)(2,1)} %bitcast.9), calls=%async_computation.2 | async-start | bytes 655360 | tf_op jit(solution)/shard_map/all_to_all | solution.py:407
  85.8 20.1 %all-to-all-start.3 = ((bf16[32,8,1024]{2,1,0:T(8,128)(2,1)}), bf16[32,8,1024]{2,1,0:T(8,128)(2,1)S(1)}, u32[]{:S(2)}, u32[]{:S(2)}) async-start(bf16[32,8,1024]{2,1,0:T(8,128)(2,1)} %shard_map.168), calls=%async_computation.3 | async-start | bytes 1048576 | tf_op jit(solution)/shard_map/all_to_all | solution.py:419
  92.8 28.1 %collective-permute-start.13 = (bf16[256,1792]{1,0:T(8,128)(2,1)}, bf16[256,1792]{1,0:T(8,128)(2,1)}, u32[]{:S(2)}, u32[]{:S(2)}) collective-permute-start(bf16[256,1792]{1,0:T(8,128)(2,1)} %get-tuple-element.84), channel_id=1, source_target_pairs={{0,16},{8,24},{16,0},{24,8},{1,17},{9,25},{17,1},{25,9},{2,18},{10... | collective-permute-start | bytes 2752520 | tf_op jit(solution)/shard_map/ppermute | solution.py:289
  106.7 7.4 %collective-permute-start.9 = (bf16[128,256]{1,0:T(8,128)(2,1)S(1)}, bf16[128,256]{1,0:T(8,128)(2,1)S(1)}, u32[]{:S(2)}, u32[]{:S(2)}) collective-permute-start(bf16[128,256]{1,0:T(8,128)(2,1)S(1)} %get-tuple-element.57), channel_id=1, source_target_pairs={{0,1},{1,0},{2,3},{3,2},{4,5},{5,4},{6,7},{7,6},{8,9},{9,8},{10,11... | collective-permute-start | bytes 196616 | tf_op jit(solution)/shard_map/ppermute | solution.py:289
  114.2 5.1 %collective-permute-start.10 = (bf16[128,256]{1,0:T(8,128)(2,1)S(1)}, bf16[128,256]{1,0:T(8,128)(2,1)S(1)}, u32[]{:S(2)}, u32[]{:S(2)}) collective-permute-start(bf16[128,256]{1,0:T(8,128)(2,1)S(1)} %add_convert_fusion.3), channel_id=1, source_target_pairs={{0,4},{2,6},{4,0},{6,2},{1,5},{3,7},{5,1},{7,3},{8,12},{10,14},{12... | collective-permute-start | bytes 196616 | tf_op jit(solution)/shard_map/ppermute | solution.py:289
  115.1 5.7 %collective-permute-start.11 = (bf16[128,256]{1,0:T(8,128)(2,1)S(1)}, bf16[128,256]{1,0:T(8,128)(2,1)S(1)}, u32[]{:S(2)}, u32[]{:S(2)}) collective-permute-start(bf16[128,256]{1,0:T(8,128)(2,1)S(1)} %add_convert_fusion.3), channel_id=1, source_target_pairs={{0,2},{2,4},{4,6},{6,0},{1,3},{3,5},{5,7},{7,1},{8,10},{10,12},{12... | collective-permute-start | bytes 196616 | tf_op jit(solution)/shard_map/ppermute | solution.py:289
  120.9 5.1 %collective-permute-start.14 = (bf16[128,256]{1,0:T(8,128)(2,1)S(1)}, bf16[128,256]{1,0:T(8,128)(2,1)S(1)}, u32[]{:S(2)}, u32[]{:S(2)}) collective-permute-start(bf16[128,256]{1,0:T(8,128)(2,1)S(1)} %add_convert_fusion.2), channel_id=1, source_target_pairs={{0,8},{8,16},{16,24},{24,0},{1,9},{9,17},{17,25},{25,1},{2,10},{10... | collective-permute-start | bytes 196616 | tf_op jit(solution)/shard_map/ppermute | solution.py:289
  126.6 5.8 %collective-permute-start.17 = (bf16[512,256]{1,0:T(8,128)(2,1)S(1)}, bf16[512,256]{1,0:T(8,128)(2,1)S(1)}, u32[]{:S(2)}, u32[]{:S(2)}) collective-permute-start(bf16[512,256]{1,0:T(8,128)(2,1)S(1)} %constant_dynamic-update-slice_fusion.own_ref), channel_id=1, source_target_pairs={{0,1},{1,0},{2,3},{3,2},{4,5},{5,4},{6,7},{7,6},{8,9},{9,8},{10,11... | collective-permute-start | bytes 786440 | tf_op jit(solution)/shard_map/ppermute | solution.py:289
  137.4 41.3 %all-to-all-start.4 = ((bf16[8,32,1920]{2,1,0:T(8,128)(2,1)}), bf16[8,32,1920]{2,1,0:T(8,128)(2,1)S(1)}, u32[]{:S(2)}, u32[]{:S(2)}) async-start(bf16[8,32,1920]{2,1,0:T(8,128)(2,1)} %bitcast.23), calls=%async_computation.4 | async-start | bytes 1966080 | tf_op jit(solution)/shard_map/all_to_all | solution.py:298
  150.9 13.8 %collective-permute-start.18 = (bf16[896,256]{1,0:T(8,128)(2,1)}, bf16[896,256]{1,0:T(8,128)(2,1)S(1)}, u32[]{:S(2)}, u32[]{:S(2)}) collective-permute-start(bf16[896,256]{1,0:T(8,128)(2,1)} %get-tuple-element.59), channel_id=1, source_target_pairs={{0,8},{8,16},{16,24},{24,0},{1,9},{9,17},{17,25},{25,1},{2,10},{10... | collective-permute-start | bytes 1376264 | tf_op jit(solution)/shard_map/ppermute | solution.py:289
  151.9 23.5 %collective-permute-start.19 = (bf16[896,256]{1,0:T(8,128)(2,1)}, bf16[896,256]{1,0:T(8,128)(2,1)S(1)}, u32[]{:S(2)}, u32[]{:S(2)}) collective-permute-start(bf16[896,256]{1,0:T(8,128)(2,1)} %get-tuple-element.60), channel_id=1, source_target_pairs={{0,16},{8,24},{16,0},{24,8},{1,17},{9,25},{17,1},{25,9},{2,18},{10... | collective-permute-start | bytes 1376264 | tf_op jit(solution)/shard_map/ppermute | solution.py:289
  155.5 20.0 %collective-permute-start.20 = (bf16[896,256]{1,0:T(8,128)(2,1)}, bf16[896,256]{1,0:T(8,128)(2,1)S(1)}, u32[]{:S(2)}, u32[]{:S(2)}) collective-permute-start(bf16[896,256]{1,0:T(8,128)(2,1)} %get-tuple-element.61), channel_id=1, source_target_pairs={{0,24},{8,0},{16,8},{24,16},{1,25},{9,1},{17,9},{25,17},{2,26},{10... | collective-permute-start | bytes 1376264 | tf_op jit(solution)/shard_map/ppermute | solution.py:289
  197.0 5.3 %collective-permute-start.21 = (bf16[4,128,256]{2,1,0:T(8,128)(2,1)}, bf16[4,128,256]{2,1,0:T(8,128)(2,1)S(1)}, u32[]{:S(2)}, u32[]{:S(2)}) collective-permute-start(bf16[4,128,256]{2,1,0:T(8,128)(2,1)} %get-tuple-element.64), channel_id=1, source_target_pairs={{0,1},{1,0},{2,3},{3,2},{4,5},{5,4},{6,7},{7,6},{8,9},{9,8},{10,11... | collective-permute-start | bytes 786440 | tf_op jit(solution)/shard_map/ppermute | solution.py:289
  (31 other events, 374.6 us)

commit v12 on v10

--- a/solution.py
+++ b/solution.py
@@ -215,8 +215,8 @@
     mine_ref[...] = dot(a_ref[mine, :], w_ref[...])
 
 
-def gate_up_kernel(place_ref, own_ref, other_ref, w0, w1, gate2, up2, w3, out_ref, m_ref):
-    units = gate2.shape[1]
+def gate_up_kernel(place_ref, own_ref, other_ref, w0, w1, w2, w3, out_ref, m_ref):
+    units = w0.shape[1]
     step = pl.program_id(0)
 
     @pl.when(step == 0)
@@ -227,17 +227,17 @@
             m_ref[d, mine, :] = own_ref[d * rows : (d + 1) * rows]
             m_ref[d, theirs, :] = other_ref[d * rows : (d + 1) * rows]
 
-    def product(w2):
+    def product():
         total = dot(m_ref[0], w0[...]) + dot(m_ref[1], w1[...])
         return (total + dot(m_ref[2], w2[...]) + dot(m_ref[3], w3[...])).astype(BF)
 
     @pl.when(step == 0)
     def _():
-        out_ref[:, :units] = product(gate2)
+        out_ref[:, :units] = product()
 
     @pl.when(step == 1)
     def _():
-        out_ref[:, units : 2 * units] = product(up2)
+        out_ref[:, units : 2 * units] = product()
         square = jnp.zeros((m_ref.shape[1], 1), F32)
         for d in range(4):
             value = m_ref[d].astype(F32)
@@ -388,6 +388,7 @@
     later_gate, later_up = lax.optimization_barrier((gate_weight, up_weight, queries))[:2]
     wide_0 = wide(columns(later_gate, 0), columns(later_up, 0))
     wide_1 = shift(wide(columns(later_gate, 1), columns(later_up, 1)), "y", 1)
+    wide_2 = wide(columns(later_gate, 2), columns(later_up, 2))
     wide_3 = shift(wide(columns(later_gate, 3), columns(later_up, 3)), "y", -1)
     queries = lax.all_to_all(queries, GROUP, 0, 0, tiled=True)
 
@@ -398,8 +399,7 @@
         out_shape=jax.ShapeDtypeStruct((slot_rows, local_heads // 2 + HEAD), BF),
         compiler_params=params(),
     )(me, image_tiles, own, kv_left, kv_right, k_gain.reshape(1, HEAD), queries, row_image)
-    gate_weight, up_weight, down_weight = lax.optimization_barrier((gate_weight, up_weight, down_weight, mixed))[:3]
-    gate_2, up_2 = wide(columns(gate_weight, 2)), wide(columns(up_weight, 2))
+    down_weight = after(down_weight, mixed)
 
     def rows(d, start, size):
         at = lax.rem(lax.axis_index("y") + d, chips_y) * units + start
@@ -408,8 +408,8 @@
     down_0, down_1, down_3 = rows(0, 0, units), rows(1, 0, units), rows(3, 0, units)
     down_2 = rows(2, 0, half), rows(2, half, half)
     mixed = lax.all_to_all(mixed, GROUP, 0, 0, tiled=True)
-    mixed = after(mixed, gate_2, up_2, down_1, down_3, *down_2)
-    gate_2, up_2 = shift(gate_2, "y", 1), shift(up_2, "y", -1)
+    mixed = after(mixed, down_1, down_3, *down_2)
+    wide_2 = shift(wide_2, "y", 2)
 
     attended = pl.pallas_call(
         combine_kernel,
@@ -435,24 +435,22 @@
     )(place, attended, o_weight)
     pair = (mine + shift(theirs, "c", 1).astype(F32)).astype(BF)
     attn_sum = chip_sum(pair)
-    gate_2, up_2 = shift(gate_2, "y", 1), shift(up_2, "y", -1)
     middle = (half_f + jnp.tanh(gate_logits[0]) * attn_sum).astype(BF)
-    middle = after(middle, gate_2, up_2)
+    middle = after(middle, wide_2)
     middle_f = middle.astype(F32)
     own_rows_all = jnp.concatenate([middle] + [shift(middle, "y", d) for d in (1, 2, 3)], axis=0)
     other_rows_all = shift(own_rows_all, "c", 1)
     block = pl.BlockSpec((4 * half_rows, width_part), lambda i: (0, 0))
     direct = pl.BlockSpec((width_part, units), lambda i: (0, i))
-    passed = pl.BlockSpec((width_part, units), lambda i: (0, 0))
     gate_up = pl.pallas_call(
         gate_up_kernel,
         grid=(2,),
-        in_specs=[smem()] + [block] * 2 + [direct] * 2 + [passed] * 2 + [direct],
+        in_specs=[smem()] + [block] * 2 + [direct] * 4,
         out_specs=pl.BlockSpec((all_rows, 2 * units + HEAD), lambda i: (0, 0)),
         out_shape=jax.ShapeDtypeStruct((all_rows, 2 * units + HEAD), BF),
         scratch_shapes=[pltpu.VMEM((4, all_rows, width_part), BF)],
         compiler_params=params(LARGE_VMEM_BYTES),
-    )(place, own_rows_all, other_rows_all, wide_0, wide_1, gate_2, up_2, wide_3)
+    )(place, own_rows_all, other_rows_all, wide_0, wide_1, wide_2, wide_3)
     down_1, down_3, *down_2 = lax.optimization_barrier((down_1, down_3, *down_2, gate_up))[:4]
     down_1, down_3 = shift(down_1, "y", 1), shift(down_3, "y", -1)
     down_2 = shift(down_2[0], "y", 1), shift(down_2[1], "y", -1)

time: 208 us -> 215 us (1.034)
  starting transfers between devices: 85.1 us -> 97.7 us
  waiting for transfers between devices: 78.4 us -> 73.1 us
    all_to_all x2, starting transfers between devices: 13.2 us -> 20.2 us  [exchange(): out = lax.all_to_all(value, axis, 0, 0, tiled=True)]
    ppermute x35 -> x32, starting transfers between devices: 51.2 us -> 54.8 us  [shift(): return lax.ppermute(value, axis, [(i, (i + by) % n) for i in range(n)])]
    ppermute x35 -> x32, waiting for transfers between devices: 36 us -> 32.6 us  [shift(): return lax.ppermute(value, axis, [(i, (i + by) % n) for i in range(n)])]
  transfers between devices with their start and end apart: 41 -> 38, of which waited for: 20 -> 22; matrix products, arithmetic and copies ran while one was open for 7% -> 6% of each run, Pallas kernels for 7% -> 7%
where the time goes in v12:
time: 215 us; the launch traced here: 214 us
  starting transfers between devices  97.7 us (45%)
  waiting for transfers between devices  73.1 us (34%)
  Pallas kernels  24 us (11%)
  local copies, waits for them, and re-layouts  11.4 us (5%)
  other arithmetic  4.07 us (2%)
    ppermute x32, starting transfers between devices, shift(): return lax.ppermute(value, axis, [(i, (i + by) % n) for i in range(n)])  54.8 us
    ppermute x32, waiting for transfers between devices, shift(): return lax.ppermute(value, axis, [(i, (i + by) % n) for i in range(n)])  32.6 us
    all_to_all x2, starting transfers between devices, exchange(): out = lax.all_to_all(value, axis, 0, 0, tiled=True)  20.2 us
    all_to_all x2, waiting for transfers between devices, exchange(): out = lax.all_to_all(value, axis, 0, 0, tiled=True)  12.2 us
    all_to_all x1, waiting for transfers between devices, shards(): lax.all_to_all(attended, GROUP, 0, 0, tiled=True)  10.2 us
    all_to_all x1, waiting for transfers between devices, shards(): mixed = lax.all_to_all(mixed, GROUP, 0, 0, tiled=True)  8.19 us
    pallas_call x1, Pallas kernels, kv_project(): pl.pallas_call(kv_kernel, grid_spec=pltpu.PrefetchScalarGridSpec(num_scal...  7.93 us
    all_to_all x1, starting transfers between devices, shards(): queries = lax.all_to_all(queries, GROUP, 0, 0, tiled=True)  7.2 us
  transfers between devices with their start and end apart: 38, of which 22 were waited for; matrix products, arithmetic and copies ran while one was open for 6% of the time, Pallas kernels for 7%

profile of v12, /device:TPU:1, one launch (start us, length us, event | category | flops | bytes accessed | tf_op | source)
XLA Modules:
  0.0 214.0 jit_solution(13334711629341703901)
XLA Ops:
  0.0 3.2 %collective-permute-start.1 = (bf16[1024,1024]{1,0:T(8,128)(2,1)}, bf16[1024,1024]{1,0:T(8,128)(2,1)S(1)}, u32[]{:S(2)}, u32[]{:S(2)}) collective-permute-start(bf16[1024,1024]{1,0:T(8,128)(2,1)} %k0.1), channel_id=1, source_target_pairs={{0,1},{1,0},{2,3},{3,2},{4,5},{5,4},{6,7},{7,6},{8,9},{9,8},{10,11... | collective-permute-start | bytes 6291464 | tf_op jit(solution)/shard_map/ppermute | solution.py:290
  6.4 9.5 %all-to-all-start = ((bf16[32,8,1024]{2,1,0:T(8,128)(2,1)}), bf16[32,8,1024]{2,1,0:T(8,128)(2,1)S(1)}, u32[]{:S(2)}, u32[]{:S(2)}) async-start(bf16[32,8,1024]{2,1,0:T(8,128)(2,1)} %fusion), calls=%async_computation | async-start | bytes 1048576 | tf_op jit(solution)/shard_map/all_to_all | solution.py:299
  17.3 7.9 %shard_map.163 = (bf16[320,256]{1,0:T(8,128)(2,1)}, bf16[320,256]{1,0:T(8,128)(2,1)}, bf16[640,256]{1,0:T(8,128)(2,1)}, bf16[640,256]{1,0:T(8,128)(2,1)}, bf16[640,256]{1,0:T(8,128)(2,1)}) custom-call(s32[2]{0:T(128)} %pad_add_fusion.place_ref, bf16[640,1024]{1,0:T(8,128)(2,1)} %x0.1, bf16[640,1024]{1,0:T(8,128)(2,1)} %collective-permute-done.x1, ...), custom_call_target="tpu_custom_call" | custom-call | tf_op jit(solution)/shard_map/pallas_call | solution.py:109
  28.7 4.0 %all-to-all-done.parts_ref = bf16[32,8,1024]{2,1,0:T(8,128)(2,1)S(1)} async-done(((bf16[32,8,1024]{2,1,0:T(8,128)(2,1)}), bf16[32,8,1024]{2,1,0:T(8,128)(2,1)S(1)}, u32[]{:S(2)}, u32[]{:S(2)}) %all-to-all-start) | async-done | bytes 524320 | tf_op jit(solution)/shard_map/all_to_all | solution.py:299
  39.3 7.2 %all-to-all-start.1 = ((bf16[32,8,512]{2,1,0:T(8,128)(2,1)}), bf16[32,8,512]{2,1,0:T(8,128)(2,1)S(1)}, u32[]{:S(2)}, u32[]{:S(2)}) async-start(bf16[32,8,512]{2,1,0:T(8,128)(2,1)} %bitcast.7), calls=%async_computation.1 | async-start | bytes 524288 | tf_op jit(solution)/shard_map/all_to_all | solution.py:393
  54.0 2.9 %all-to-all-done.1 = bf16[32,8,512]{2,1,0:T(8,128)(2,1)S(1)} async-done(((bf16[32,8,512]{2,1,0:T(8,128)(2,1)}), bf16[32,8,512]{2,1,0:T(8,128)(2,1)S(1)}, u32[]{:S(2)}, u32[]{:S(2)}) %all-to-all-start.1) | async-done | bytes 262176 | tf_op jit(solution)/shard_map/all_to_all | solution.py:393
  56.9 3.0 %shard_map.167 = bf16[256,640]{1,0:T(8,128)(2,1)} custom-call(s32[1]{0:T(128)} %bitcast.3.me_ref, s32[32,4]{1,0:T(8,128)S(1)} %copy.27.tiles_ref, bf16[640,256]{1,0:T(8,128)(2,1)S(1)} %copy-done.2, bf16[640,256]{1,0:T(8,128)(2,1)S(1)} %collective-permute-done.5.left_ref, bf16[640,256]{1,0:T(8,128)(2,1)S(1)} %collective-permute-done.6.right_ref, ...), custom_call_target="tpu_custom_call" | custom-call | tf_op jit(solution)/shard_map/pallas_call | solution.py:395
  59.9 5.2 %all-to-all-start.2 = ((bf16[32,8,640]{2,1,0:T(8,128)(2,1)}), bf16[32,8,640]{2,1,0:T(8,128)(2,1)S(1)}, u32[]{:S(2)}, u32[]{:S(2)}) async-start(bf16[32,8,640]{2,1,0:T(8,128)(2,1)} %bitcast.9), calls=%async_computation.2 | async-start | bytes 655360 | tf_op jit(solution)/shard_map/all_to_all | solution.py:410
  69.3 8.2 %all-to-all-done.2 = bf16[32,8,640]{2,1,0:T(8,128)(2,1)S(1)} async-done(((bf16[32,8,640]{2,1,0:T(8,128)(2,1)}), bf16[32,8,640]{2,1,0:T(8,128)(2,1)S(1)}, u32[]{:S(2)}, u32[]{:S(2)}) %all-to-all-start.2) | async-done | bytes 327712 | tf_op jit(solution)/shard_map/all_to_all | solution.py:410
  78.8 6.8 %all-to-all-start.3 = ((bf16[32,8,1024]{2,1,0:T(8,128)(2,1)}), bf16[32,8,1024]{2,1,0:T(8,128)(2,1)S(1)}, u32[]{:S(2)}, u32[]{:S(2)}) async-start(bf16[32,8,1024]{2,1,0:T(8,128)(2,1)} %shard_map.168), calls=%async_computation.3 | async-start | bytes 1048576 | tf_op jit(solution)/shard_map/all_to_all | solution.py:422
  85.6 2.8 %collective-permute-start.13 = (bf16[256,1792]{1,0:T(8,128)(2,1)}, bf16[256,1792]{1,0:T(8,128)(2,1)}, u32[]{:S(2)}, u32[]{:S(2)}) collective-permute-start(bf16[256,1792]{1,0:T(8,128)(2,1)} %get-tuple-element.84), channel_id=1, source_target_pairs={{0,16},{8,24},{16,0},{24,8},{1,17},{9,25},{17,1},{25,9},{2,18},{10... | collective-permute-start | bytes 2752520 | tf_op jit(solution)/shard_map/ppermute | solution.py:290
  88.4 10.2 %all-to-all-done.3 = bf16[32,8,1024]{2,1,0:T(8,128)(2,1)S(1)} async-done(((bf16[32,8,1024]{2,1,0:T(8,128)(2,1)}), bf16[32,8,1024]{2,1,0:T(8,128)(2,1)S(1)}, u32[]{:S(2)}, u32[]{:S(2)}) %all-to-all-start.3) | async-done | bytes 524320 | tf_op jit(solution)/shard_map/all_to_all | solution.py:422
  99.5 6.4 %collective-permute-start.9 = (bf16[128,256]{1,0:T(8,128)(2,1)S(1)}, bf16[128,256]{1,0:T(8,128)(2,1)S(1)}, u32[]{:S(2)}, u32[]{:S(2)}) collective-permute-start(bf16[128,256]{1,0:T(8,128)(2,1)S(1)} %get-tuple-element.54), channel_id=1, source_target_pairs={{0,1},{1,0},{2,3},{3,2},{4,5},{5,4},{6,7},{7,6},{8,9},{9,8},{10,11... | collective-permute-start | bytes 196616 | tf_op jit(solution)/shard_map/ppermute | solution.py:290
  113.8 2.5 %collective-permute-start.15 = (bf16[128,256]{1,0:T(8,128)(2,1)S(1)}, bf16[128,256]{1,0:T(8,128)(2,1)S(1)}, u32[]{:S(2)}, u32[]{:S(2)}) collective-permute-start(bf16[128,256]{1,0:T(8,128)(2,1)S(1)} %add_convert_fusion.2), channel_id=1, source_target_pairs={{0,16},{8,24},{16,0},{24,8},{1,17},{9,25},{17,1},{25,9},{2,18},{10... | collective-permute-start | bytes 196616 | tf_op jit(solution)/shard_map/ppermute | solution.py:290
  119.4 4.8 %collective-permute-start.17 = (bf16[512,256]{1,0:T(8,128)(2,1)S(1)}, bf16[512,256]{1,0:T(8,128)(2,1)S(1)}, u32[]{:S(2)}, u32[]{:S(2)}) collective-permute-start(bf16[512,256]{1,0:T(8,128)(2,1)S(1)} %constant_dynamic-update-slice_fusion.own_ref), channel_id=1, source_target_pairs={{0,1},{1,0},{2,3},{3,2},{4,5},{5,4},{6,7},{7,6},{8,9},{9,8},{10,11... | collective-permute-start | bytes 786440 | tf_op jit(solution)/shard_map/ppermute | solution.py:290
  126.1 4.2 %shard_map.170 = bf16[256,1920]{1,0:T(8,128)(2,1)} custom-call(s32[2]{0:T(128)} %pad_add_fusion.place_ref, bf16[512,256]{1,0:T(8,128)(2,1)} %copy-done.10, bf16[512,256]{1,0:T(8,128)(2,1)} %copy-done.12, bf16[256,1792]{1,0:T(8,128)(2,1)} %get-tuple-element.82.w0, bf16[256,1792]{1,0:T(8,128)(2,1)} %copy-done.8, bf16[256,1792]{1,0:T(8,128)(2,1)} %collective-permute-done.13.w2, ...), custom_call_target="tpu_custom_call" | custom-call | tf_op jit(solution)/shard_map/pallas_call | solution.py:445
  130.3 10.7 %all-to-all-start.4 = ((bf16[8,32,1920]{2,1,0:T(8,128)(2,1)}), bf16[8,32,1920]{2,1,0:T(8,128)(2,1)S(1)}, u32[]{:S(2)}, u32[]{:S(2)}) async-start(bf16[8,32,1920]{2,1,0:T(8,128)(2,1)} %bitcast.23), calls=%async_computation.4 | async-start | bytes 1966080 | tf_op jit(solution)/shard_map/all_to_all | solution.py:299
  144.5 2.7 %collective-permute-start.21 = (bf16[448,256]{1,0:T(8,128)(2,1)}, bf16[448,256]{1,0:T(8,128)(2,1)S(1)}, u32[]{:S(2)}, u32[]{:S(2)}) collective-permute-start(bf16[448,256]{1,0:T(8,128)(2,1)} %get-tuple-element.59), channel_id=1, source_target_pairs={{0,24},{8,0},{16,8},{24,16},{1,25},{9,1},{17,9},{25,17},{2,26},{10... | collective-permute-start | bytes 688136 | tf_op jit(solution)/shard_map/ppermute | solution.py:290
  147.2 12.7 %collective-permute-done.20 = bf16[448,256]{1,0:T(8,128)(2,1)} collective-permute-done((bf16[448,256]{1,0:T(8,128)(2,1)}, bf16[448,256]{1,0:T(8,128)(2,1)}, u32[]{:S(2)}, u32[]{:S(2)}) %collective-permute-start.20) | collective-permute-done | bytes 229408 | tf_op jit(solution)/shard_map/ppermute | solution.py:290
  160.6 8.3 %all-to-all-done.4.parts_ref = bf16[8,32,1920]{2,1,0:T(8,128)(2,1)S(1)} async-done(((bf16[8,32,1920]{2,1,0:T(8,128)(2,1)}), bf16[8,32,1920]{2,1,0:T(8,128)(2,1)S(1)}, u32[]{:S(2)}, u32[]{:S(2)}) %all-to-all-start.4) | async-done | bytes 983072 | tf_op jit(solution)/shard_map/all_to_all | solution.py:299
  169.9 3.5 %all-to-all-start.5 = ((bf16[8,32,896]{2,1,0:T(8,128)(2,1)}), bf16[8,32,896]{2,1,0:T(8,128)(2,1)S(1)}, u32[]{:S(2)}, u32[]{:S(2)}) async-start(bf16[8,32,896]{2,1,0:T(8,128)(2,1)} %shard_map.171), calls=%async_computation.5 | async-start | bytes 917504 | tf_op jit(solution)/shard_map/all_to_all | solution.py:466
  177.1 5.7 %collective-permute-done.22.low2 = bf16[448,256]{1,0:T(8,128)(2,1)S(1)} collective-permute-done((bf16[448,256]{1,0:T(8,128)(2,1)}, bf16[448,256]{1,0:T(8,128)(2,1)S(1)}, u32[]{:S(2)}, u32[]{:S(2)}) %collective-permute-start.22) | collective-permute-done | bytes 229408 | tf_op jit(solution)/shard_map/ppermute | solution.py:290
  182.8 7.1 %all-to-all-done.5 = bf16[8,32,896]{2,1,0:T(8,128)(2,1)S(1)} async-done(((bf16[8,32,896]{2,1,0:T(8,128)(2,1)}), bf16[8,32,896]{2,1,0:T(8,128)(2,1)S(1)}, u32[]{:S(2)}, u32[]{:S(2)}) %all-to-all-start.5) | async-done | bytes 458784 | tf_op jit(solution)/shard_map/all_to_all | solution.py:466
  208.9 3.5 %collective-permute-start.31 = (bf16[128,256]{1,0:T(8,128)(2,1)S(1)}, bf16[128,256]{1,0:T(8,128)(2,1)S(1)}, u32[]{:S(2)}, u32[]{:S(2)}) collective-permute-start(bf16[128,256]{1,0:T(8,128)(2,1)S(1)} %add_convert_fusion), channel_id=1, source_target_pairs={{0,1},{1,0},{2,3},{3,2},{4,5},{5,4},{6,7},{7,6},{8,9},{9,8},{10,11... | collective-permute-start | bytes 196616 | tf_op jit(solution)/shard_map/ppermute | solution.py:290
  (133 shorter events, 69.4 us)
Async XLA Ops:
  0.0 16.0 %collective-permute-start.1 = (bf16[1024,1024]{1,0:T(8,128)(2,1)}, bf16[1024,1024]{1,0:T(8,128)(2,1)S(1)}, u32[]{:S(2)}, u32[]{:S(2)}) collective-permute-start(bf16[1024,1024]{1,0:T(8,128)(2,1)} %k0.1), channel_id=1, source_target_pairs={{0,1},{1,0},{2,3},{3,2},{4,5},{5,4},{6,7},{7,6},{8,9},{9,8},{10,11... | collective-permute-start | bytes 6291464 | tf_op jit(solution)/shard_map/ppermute | solution.py:290
  3.2 12.7 %collective-permute-start.2 = (bf16[1024,1024]{1,0:T(8,128)(2,1)}, bf16[1024,1024]{1,0:T(8,128)(2,1)}, u32[]{:S(2)}, u32[]{:S(2)}) collective-permute-start(bf16[1024,1024]{1,0:T(8,128)(2,1)} %v0.1), channel_id=1, source_target_pairs={{0,1},{1,0},{2,3},{3,2},{4,5},{5,4},{6,7},{7,6},{8,9},{9,8},{10,11... | collective-permute-start | bytes 6291464 | tf_op jit(solution)/shard_map/ppermute | solution.py:290
  3.2 12.7 %collective-permute-start = (bf16[640,1024]{1,0:T(8,128)(2,1)}, bf16[640,1024]{1,0:T(8,128)(2,1)}, u32[]{:S(2)}, u32[]{:S(2)}) collective-permute-start(bf16[640,1024]{1,0:T(8,128)(2,1)} %x0.1), channel_id=1, source_target_pairs={{0,1},{1,0},{2,3},{3,2},{4,5},{5,4},{6,7},{7,6},{8,9},{9,8},{10,11... | collective-permute-start | bytes 3932168 | tf_op jit(solution)/shard_map/ppermute | solution.py:290
  6.4 26.3 %all-to-all-start = ((bf16[32,8,1024]{2,1,0:T(8,128)(2,1)}), bf16[32,8,1024]{2,1,0:T(8,128)(2,1)S(1)}, u32[]{:S(2)}, u32[]{:S(2)}) async-start(bf16[32,8,1024]{2,1,0:T(8,128)(2,1)} %fusion), calls=%async_computation | async-start | bytes 1048576 | tf_op jit(solution)/shard_map/all_to_all | solution.py:299
  25.2 8.5 %collective-permute-start.3 = (bf16[320,256]{1,0:T(8,128)(2,1)}, bf16[320,256]{1,0:T(8,128)(2,1)S(1)}, u32[]{:S(2)}, u32[]{:S(2)}) collective-permute-start(bf16[320,256]{1,0:T(8,128)(2,1)} %get-tuple-element.40), channel_id=1, source_target_pairs={{0,2},{2,4},{4,6},{6,0},{1,3},{3,5},{5,7},{7,1},{8,10},{10,12},{12... | collective-permute-start | bytes 491528 | tf_op jit(solution)/shard_map/ppermute | solution.py:290
  26.4 7.3 %collective-permute-start.4 = (bf16[320,256]{1,0:T(8,128)(2,1)}, bf16[320,256]{1,0:T(8,128)(2,1)S(1)}, u32[]{:S(2)}, u32[]{:S(2)}) collective-permute-start(bf16[320,256]{1,0:T(8,128)(2,1)} %get-tuple-element.41), channel_id=1, source_target_pairs={{0,6},{2,0},{4,2},{6,4},{1,7},{3,1},{5,3},{7,5},{8,14},{10,8},{12,... | collective-permute-start | bytes 491528 | tf_op jit(solution)/shard_map/ppermute | solution.py:290
  36.6 17.5 %collective-permute-start.5 = (bf16[640,256]{1,0:T(8,128)(2,1)}, bf16[640,256]{1,0:T(8,128)(2,1)S(1)}, u32[]{:S(2)}, u32[]{:S(2)}) collective-permute-start(bf16[640,256]{1,0:T(8,128)(2,1)} %get-tuple-element.42), channel_id=1, source_target_pairs={{0,2},{2,4},{4,6},{6,0},{1,3},{3,5},{5,7},{7,1},{8,10},{10,12},{12... | collective-permute-start | bytes 983048 | tf_op jit(solution)/shard_map/ppermute | solution.py:290
  37.8 16.2 %collective-permute-start.6 = (bf16[640,256]{1,0:T(8,128)(2,1)}, bf16[640,256]{1,0:T(8,128)(2,1)S(1)}, u32[]{:S(2)}, u32[]{:S(2)}) collective-permute-start(bf16[640,256]{1,0:T(8,128)(2,1)} %get-tuple-element.43), channel_id=1, source_target_pairs={{0,6},{2,0},{4,2},{6,4},{1,7},{3,1},{5,3},{7,5},{8,14},{10,8},{12,... | collective-permute-start | bytes 983048 | tf_op jit(solution)/shard_map/ppermute | solution.py:290
  39.3 17.6 %all-to-all-start.1 = ((bf16[32,8,512]{2,1,0:T(8,128)(2,1)}), bf16[32,8,512]{2,1,0:T(8,128)(2,1)S(1)}, u32[]{:S(2)}, u32[]{:S(2)}) async-start(bf16[32,8,512]{2,1,0:T(8,128)(2,1)} %bitcast.7), calls=%async_computation.1 | async-start | bytes 524288 | tf_op jit(solution)/shard_map/all_to_all | solution.py:393
  51.3 27.5 %collective-permute-start.7 = (bf16[256,1792]{1,0:T(8,128)(2,1)}, bf16[256,1792]{1,0:T(8,128)(2,1)S(1)}, u32[]{:S(2)}, u32[]{:S(2)}) collective-permute-start(bf16[256,1792]{1,0:T(8,128)(2,1)} %get-tuple-element.85), channel_id=1, source_target_pairs={{0,8},{8,16},{16,24},{24,0},{1,9},{9,17},{17,25},{25,1},{2,10},{10... | collective-permute-start | bytes 2752520 | tf_op jit(solution)/shard_map/ppermute | solution.py:290
  52.5 26.3 %collective-permute-start.8 = (bf16[256,1792]{1,0:T(8,128)(2,1)}, bf16[256,1792]{1,0:T(8,128)(2,1)}, u32[]{:S(2)}, u32[]{:S(2)}) collective-permute-start(bf16[256,1792]{1,0:T(8,128)(2,1)} %get-tuple-element.83), channel_id=1, source_target_pairs={{0,24},{8,0},{16,8},{24,16},{1,25},{9,1},{17,9},{25,17},{2,26},{10... | collective-permute-start | bytes 2752520 | tf_op jit(solution)/shard_map/ppermute | solution.py:290
  59.9 17.6 %all-to-all-start.2 = ((bf16[32,8,640]{2,1,0:T(8,128)(2,1)}), bf16[32,8,640]{2,1,0:T(8,128)(2,1)S(1)}, u32[]{:S(2)}, u32[]{:S(2)}) async-start(bf16[32,8,640]{2,1,0:T(8,128)(2,1)} %bitcast.9), calls=%async_computation.2 | async-start | bytes 655360 | tf_op jit(solution)/shard_map/all_to_all | solution.py:410
  78.8 19.9 %all-to-all-start.3 = ((bf16[32,8,1024]{2,1,0:T(8,128)(2,1)}), bf16[32,8,1024]{2,1,0:T(8,128)(2,1)S(1)}, u32[]{:S(2)}, u32[]{:S(2)}) async-start(bf16[32,8,1024]{2,1,0:T(8,128)(2,1)} %shard_map.168), calls=%async_computation.3 | async-start | bytes 1048576 | tf_op jit(solution)/shard_map/all_to_all | solution.py:422
  85.6 28.1 %collective-permute-start.13 = (bf16[256,1792]{1,0:T(8,128)(2,1)}, bf16[256,1792]{1,0:T(8,128)(2,1)}, u32[]{:S(2)}, u32[]{:S(2)}) collective-permute-start(bf16[256,1792]{1,0:T(8,128)(2,1)} %get-tuple-element.84), channel_id=1, source_target_pairs={{0,16},{8,24},{16,0},{24,8},{1,17},{9,25},{17,1},{25,9},{2,18},{10... | collective-permute-start | bytes 2752520 | tf_op jit(solution)/shard_map/ppermute | solution.py:290
  99.5 7.3 %collective-permute-start.9 = (bf16[128,256]{1,0:T(8,128)(2,1)S(1)}, bf16[128,256]{1,0:T(8,128)(2,1)S(1)}, u32[]{:S(2)}, u32[]{:S(2)}) collective-permute-start(bf16[128,256]{1,0:T(8,128)(2,1)S(1)} %get-tuple-element.54), channel_id=1, source_target_pairs={{0,1},{1,0},{2,3},{3,2},{4,5},{5,4},{6,7},{7,6},{8,9},{9,8},{10,11... | collective-permute-start | bytes 196616 | tf_op jit(solution)/shard_map/ppermute | solution.py:290
  107.6 6.0 %collective-permute-start.11 = (bf16[128,256]{1,0:T(8,128)(2,1)S(1)}, bf16[128,256]{1,0:T(8,128)(2,1)S(1)}, u32[]{:S(2)}, u32[]{:S(2)}) collective-permute-start(bf16[128,256]{1,0:T(8,128)(2,1)S(1)} %add_convert_fusion.3), channel_id=1, source_target_pairs={{0,2},{2,4},{4,6},{6,0},{1,3},{3,5},{5,7},{7,1},{8,10},{10,12},{12... | collective-permute-start | bytes 196616 | tf_op jit(solution)/shard_map/ppermute | solution.py:290
  130.3 38.5 %all-to-all-start.4 = ((bf16[8,32,1920]{2,1,0:T(8,128)(2,1)}), bf16[8,32,1920]{2,1,0:T(8,128)(2,1)S(1)}, u32[]{:S(2)}, u32[]{:S(2)}) async-start(bf16[8,32,1920]{2,1,0:T(8,128)(2,1)} %bitcast.23), calls=%async_computation.4 | async-start | bytes 1966080 | tf_op jit(solution)/shard_map/all_to_all | solution.py:299
  141.1 18.9 %collective-permute-start.18 = (bf16[896,256]{1,0:T(8,128)(2,1)}, bf16[896,256]{1,0:T(8,128)(2,1)S(1)}, u32[]{:S(2)}, u32[]{:S(2)}) collective-permute-start(bf16[896,256]{1,0:T(8,128)(2,1)} %get-tuple-element.56), channel_id=1, source_target_pairs={{0,8},{8,16},{16,24},{24,0},{1,9},{9,17},{17,25},{25,1},{2,10},{10... | collective-permute-start | bytes 1376264 | tf_op jit(solution)/shard_map/ppermute | solution.py:290
  142.1 18.5 %collective-permute-start.19 = (bf16[896,256]{1,0:T(8,128)(2,1)S(1)}, bf16[896,256]{1,0:T(8,128)(2,1)S(1)}, u32[]{:S(2)}, u32[]{:S(2)}) collective-permute-start(bf16[896,256]{1,0:T(8,128)(2,1)S(1)} %copy-done.9), channel_id=1, source_target_pairs={{0,24},{8,0},{16,8},{24,16},{1,25},{9,1},{17,9},{25,17},{2,26},{10... | collective-permute-start | bytes 1376264 | tf_op jit(solution)/shard_map/ppermute | solution.py:290
  144.5 15.4 %collective-permute-start.20 = (bf16[448,256]{1,0:T(8,128)(2,1)}, bf16[448,256]{1,0:T(8,128)(2,1)}, u32[]{:S(2)}, u32[]{:S(2)}) collective-permute-start(bf16[448,256]{1,0:T(8,128)(2,1)} %get-tuple-element.58), channel_id=1, source_target_pairs={{0,8},{8,16},{16,24},{24,0},{1,9},{9,17},{17,25},{25,1},{2,10},{10... | collective-permute-start | bytes 688136 | tf_op jit(solution)/shard_map/ppermute | solution.py:290
  144.5 15.4 %collective-permute-start.21 = (bf16[448,256]{1,0:T(8,128)(2,1)}, bf16[448,256]{1,0:T(8,128)(2,1)S(1)}, u32[]{:S(2)}, u32[]{:S(2)}) collective-permute-start(bf16[448,256]{1,0:T(8,128)(2,1)} %get-tuple-element.59), channel_id=1, source_target_pairs={{0,24},{8,0},{16,8},{24,16},{1,25},{9,1},{17,9},{25,17},{2,26},{10... | collective-permute-start | bytes 688136 | tf_op jit(solution)/shard_map/ppermute | solution.py:290
  169.9 19.9 %all-to-all-start.5 = ((bf16[8,32,896]{2,1,0:T(8,128)(2,1)}), bf16[8,32,896]{2,1,0:T(8,128)(2,1)S(1)}, u32[]{:S(2)}, u32[]{:S(2)}) async-start(bf16[8,32,896]{2,1,0:T(8,128)(2,1)} %shard_map.171), calls=%async_computation.5 | async-start | bytes 917504 | tf_op jit(solution)/shard_map/all_to_all | solution.py:466
  173.4 9.4 %collective-permute-start.22 = (bf16[448,256]{1,0:T(8,128)(2,1)}, bf16[448,256]{1,0:T(8,128)(2,1)S(1)}, u32[]{:S(2)}, u32[]{:S(2)}) collective-permute-start(bf16[448,256]{1,0:T(8,128)(2,1)} %collective-permute-done.20), channel_id=1, source_target_pairs={{0,8},{8,16},{16,24},{24,0},{1,9},{9,17},{17,25},{25,1},{2,10},{10... | collective-permute-start | bytes 688136 | tf_op jit(solution)/shard_map/ppermute | solution.py:290
  174.7 8.1 %collective-permute-start.23 = (bf16[448,256]{1,0:T(8,128)(2,1)}, bf16[448,256]{1,0:T(8,128)(2,1)S(1)}, u32[]{:S(2)}, u32[]{:S(2)}) collective-permute-start(bf16[448,256]{1,0:T(8,128)(2,1)} %copy-done.20), channel_id=1, source_target_pairs={{0,24},{8,0},{16,8},{24,16},{1,25},{9,1},{17,9},{25,17},{2,26},{10... | collective-permute-start | bytes 688136 | tf_op jit(solution)/shard_map/ppermute | solution.py:290
  (35 other events, 407.3 us)

commit v13 on v10

--- a/solution.py
+++ b/solution.py
@@ -209,41 +209,27 @@
     )
 
 
-def out_kernel(place_ref, a_ref, w_ref, mine_ref, theirs_ref):
-    mine, theirs = core_rows(place_ref, mine_ref.shape[0])
-    theirs_ref[...] = dot(a_ref[theirs, :], w_ref[...]).astype(BF)
-    mine_ref[...] = dot(a_ref[mine, :], w_ref[...])
-
-
-def gate_up_kernel(place_ref, own_ref, other_ref, w0, w1, gate2, up2, w3, out_ref, m_ref):
+def gate_up_kernel(m0, m1, m2, m3, w0, w1, gate2, up2, w3, out_ref):
     units = gate2.shape[1]
     step = pl.program_id(0)
 
+    def product(w2):
+        total = dot(m0[...], w0[...]) + dot(m1[...], w1[...])
+        return (total + dot(m2[...], w2[...]) + dot(m3[...], w3[...])).astype(BF)
+
     @pl.when(step == 0)
     def _():
-        rows = own_ref.shape[0] // 4
-        mine, theirs = core_rows(place_ref, rows)
-        for d in range(4):
-            m_ref[d, mine, :] = own_ref[d * rows : (d + 1) * rows]
-            m_ref[d, theirs, :] = other_ref[d * rows : (d + 1) * rows]
-
-    def product(w2):
-        total = dot(m_ref[0], w0[...]) + dot(m_ref[1], w1[...])
-        return (total + dot(m_ref[2], w2[...]) + dot(m_ref[3], w3[...])).astype(BF)
-
-    @pl.when(step == 0)
-    def _():
         out_ref[:, :units] = product(gate2)
 
     @pl.when(step == 1)
     def _():
         out_ref[:, units : 2 * units] = product(up2)
-        square = jnp.zeros((m_ref.shape[1], 1), F32)
-        for d in range(4):
-            value = m_ref[d].astype(F32)
+        square = jnp.zeros((m0.shape[0], 1), F32)
+        for m in (m0, m1, m2, m3):
+            value = m[...].astype(F32)
             square = square + jnp.sum(value * value, axis=1, keepdims=True)
         high = square.astype(BF).astype(F32)
-        lane = lax.broadcasted_iota(jnp.int32, (m_ref.shape[1], HEAD), 1)
+        lane = lax.broadcasted_iota(jnp.int32, (m0.shape[0], HEAD), 1)
         extra = jnp.where(lane == 0, high, jnp.where(lane == 1, square - high, 0.0))
         out_ref[:, 2 * units :] = extra.astype(BF)
 
@@ -422,37 +408,24 @@
     attended = lax.all_to_all(attended, GROUP, 0, 0, tiled=True).reshape(all_rows, local_heads)
     half_rows = all_rows // 2
     first_row = lax.axis_index("c") * half_rows
-    half_f = lax.dynamic_slice_in_dim(hidden, first_row, half_rows, 0).astype(F32)
-    mine, theirs = pl.pallas_call(
-        out_kernel,
-        in_specs=[smem(), vmem(), vmem()],
-        out_specs=[vmem()] * 2,
-        out_shape=[
-            jax.ShapeDtypeStruct((half_rows, width_part), F32),
-            jax.ShapeDtypeStruct((half_rows, width_part), BF),
-        ],
-        compiler_params=params(),
-    )(place, attended, o_weight)
-    pair = (mine + shift(theirs, "c", 1).astype(F32)).astype(BF)
-    attn_sum = chip_sum(pair)
+    part = dot(attended, o_weight).astype(BF)
+    pair = (part.astype(F32) + shift(part, "c", 1).astype(F32)).astype(BF)
+    attn_sum = chip_sum(after(pair, gate_2, up_2))
     gate_2, up_2 = shift(gate_2, "y", 1), shift(up_2, "y", -1)
-    middle = (half_f + jnp.tanh(gate_logits[0]) * attn_sum).astype(BF)
-    middle = after(middle, gate_2, up_2)
-    middle_f = middle.astype(F32)
-    own_rows_all = jnp.concatenate([middle] + [shift(middle, "y", d) for d in (1, 2, 3)], axis=0)
-    other_rows_all = shift(own_rows_all, "c", 1)
-    block = pl.BlockSpec((4 * half_rows, width_part), lambda i: (0, 0))
+    middle = (hidden_f + jnp.tanh(gate_logits[0]) * attn_sum).astype(BF)
+    middles = [middle] + [shift(middle, "y", d) for d in (1, 2, 3)]
+    middle_f = lax.dynamic_slice_in_dim(middle, first_row, half_rows, 0).astype(F32)
+    block = pl.BlockSpec((all_rows, width_part), lambda i: (0, 0))
     direct = pl.BlockSpec((width_part, units), lambda i: (0, i))
     passed = pl.BlockSpec((width_part, units), lambda i: (0, 0))
     gate_up = pl.pallas_call(
         gate_up_kernel,
         grid=(2,),
-        in_specs=[smem()] + [block] * 2 + [direct] * 2 + [passed] * 2 + [direct],
+        in_specs=[block] * 4 + [direct] * 2 + [passed] * 2 + [direct],
         out_specs=pl.BlockSpec((all_rows, 2 * units + HEAD), lambda i: (0, 0)),
         out_shape=jax.ShapeDtypeStruct((all_rows, 2 * units + HEAD), BF),
-        scratch_shapes=[pltpu.VMEM((4, all_rows, width_part), BF)],
         compiler_params=params(LARGE_VMEM_BYTES),
-    )(place, own_rows_all, other_rows_all, wide_0, wide_1, gate_2, up_2, wide_3)
+    )(*middles, wide_0, wide_1, gate_2, up_2, wide_3)
     down_1, down_3, *down_2 = lax.optimization_barrier((down_1, down_3, *down_2, gate_up))[:4]
     down_1, down_3 = shift(down_1, "y", 1), shift(down_3, "y", -1)
     down_2 = shift(down_2[0], "y", 1), shift(down_2[1], "y", -1)

time: 208 us -> 203 us (0.976)
  waiting for transfers between devices: 78.4 us -> 71.3 us
  starting transfers between devices: 85.1 us -> 88.6 us
    ppermute x35 -> x34, waiting for transfers between devices: 36 us -> 31.2 us  [shift(): return lax.ppermute(value, axis, [(i, (i + by) % n) for i in range(n)])]
    ppermute x35 -> x34, starting transfers between devices: 51.2 us -> 54.7 us  [shift(): return lax.ppermute(value, axis, [(i, (i + by) % n) for i in range(n)])]
    pallas_call x2 -> x1, Pallas kernels: 5.2 us -> 4.31 us  [shards(): pl.pallas_call(gate_up_kernel, grid=(2,), in_specs=[block] * 4 + [direct]...]
  transfers between devices with their start and end apart: 41 -> 40, of which waited for: 20 -> 20; matrix products, arithmetic and copies ran while one was open for 7% -> 7% of each run, Pallas kernels for 7% -> 7%
where the time goes in v13:
time: 203 us
  starting transfers between devices  88.6 us (44%)
  waiting for transfers between devices  71.3 us (35%)
  Pallas kernels  23.3 us (11%)
  local copies, waits for them, and re-layouts  9.49 us (5%)
  other arithmetic  6.01 us (3%)
  matrix products  2.33 us (1%)
    ppermute x34, starting transfers between devices, shift(): return lax.ppermute(value, axis, [(i, (i + by) % n) for i in range(n)])  54.7 us
    ppermute x34, waiting for transfers between devices, shift(): return lax.ppermute(value, axis, [(i, (i + by) % n) for i in range(n)])  31.2 us
    all_to_all x2, starting transfers between devices, exchange(): out = lax.all_to_all(value, axis, 0, 0, tiled=True)  13.2 us
    all_to_all x2, waiting for transfers between devices, exchange(): out = lax.all_to_all(value, axis, 0, 0, tiled=True)  13 us
    all_to_all x1, waiting for transfers between devices, shards(): lax.all_to_all(attended, GROUP, 0, 0, tiled=True)  10 us
    pallas_call x1, Pallas kernels, kv_project(): pl.pallas_call(kv_kernel, grid_spec=pltpu.PrefetchScalarGridSpec(num_scal...  7.95 us
    all_to_all x1, starting transfers between devices, shards(): queries = lax.all_to_all(queries, GROUP, 0, 0, tiled=True)  7.13 us
    all_to_all x1, waiting for transfers between devices, shards(): mixed = lax.all_to_all(mixed, GROUP, 0, 0, tiled=True)  6.6 us
  transfers between devices with their start and end apart: 40, of which 20 were waited for; matrix products, arithmetic and copies ran while one was open for 7% of the time, Pallas kernels for 7%

profile of v13, /device:TPU:1, one launch (start us, length us, event | category | flops | bytes accessed | tf_op | source)
XLA Modules:
  0.0 202.6 jit_solution(12958565763229055645)
XLA Ops:
  0.0 3.2 %collective-permute-start.1 = (bf16[1024,1024]{1,0:T(8,128)(2,1)}, bf16[1024,1024]{1,0:T(8,128)(2,1)}, u32[]{:S(2)}, u32[]{:S(2)}) collective-permute-start(bf16[1024,1024]{1,0:T(8,128)(2,1)} %k0.1), channel_id=1, source_target_pairs={{0,1},{1,0},{2,3},{3,2},{4,5},{5,4},{6,7},{7,6},{8,9},{9,8},{10,11... | collective-permute-start | bytes 6291464 | tf_op jit(solution)/shard_map/ppermute | solution.py:276
  6.4 9.5 %all-to-all-start = ((bf16[32,8,1024]{2,1,0:T(8,128)(2,1)}), bf16[32,8,1024]{2,1,0:T(8,128)(2,1)S(1)}, u32[]{:S(2)}, u32[]{:S(2)}) async-start(bf16[32,8,1024]{2,1,0:T(8,128)(2,1)} %fusion), calls=%async_computation | async-start | bytes 1048576 | tf_op jit(solution)/shard_map/all_to_all | solution.py:285
  17.0 8.0 %shard_map.163 = (bf16[320,256]{1,0:T(8,128)(2,1)}, bf16[320,256]{1,0:T(8,128)(2,1)}, bf16[640,256]{1,0:T(8,128)(2,1)}, bf16[640,256]{1,0:T(8,128)(2,1)}, bf16[640,256]{1,0:T(8,128)(2,1)}) custom-call(s32[2]{0:T(128)} %pad_add_fusion.place_ref, bf16[640,1024]{1,0:T(8,128)(2,1)} %x0.1, bf16[640,1024]{1,0:T(8,128)(2,1)} %copy-done.6, bf16[1024,1024]{1,0:T(8,128)(2,1)} %k0.1, ...), custom_call_target="tpu_custom_call" | custom-call | tf_op jit(solution)/shard_map/pallas_call | solution.py:109
  28.5 4.2 %all-to-all-done.parts_ref = bf16[32,8,1024]{2,1,0:T(8,128)(2,1)S(1)} async-done(((bf16[32,8,1024]{2,1,0:T(8,128)(2,1)}), bf16[32,8,1024]{2,1,0:T(8,128)(2,1)S(1)}, u32[]{:S(2)}, u32[]{:S(2)}) %all-to-all-start) | async-done | bytes 524320 | tf_op jit(solution)/shard_map/all_to_all | solution.py:285
  38.5 7.1 %all-to-all-start.1 = ((bf16[32,8,512]{2,1,0:T(8,128)(2,1)}), bf16[32,8,512]{2,1,0:T(8,128)(2,1)S(1)}, u32[]{:S(2)}, u32[]{:S(2)}) async-start(bf16[32,8,512]{2,1,0:T(8,128)(2,1)} %bitcast.7), calls=%async_computation.1 | async-start | bytes 524288 | tf_op jit(solution)/shard_map/all_to_all | solution.py:378
  51.9 4.1 %all-to-all-done.1 = bf16[32,8,512]{2,1,0:T(8,128)(2,1)S(1)} async-done(((bf16[32,8,512]{2,1,0:T(8,128)(2,1)}), bf16[32,8,512]{2,1,0:T(8,128)(2,1)S(1)}, u32[]{:S(2)}, u32[]{:S(2)}) %all-to-all-start.1) | async-done | bytes 262176 | tf_op jit(solution)/shard_map/all_to_all | solution.py:378
  56.0 3.0 %shard_map.167 = bf16[256,640]{1,0:T(8,128)(2,1)} custom-call(s32[1]{0:T(128)} %bitcast.3.me_ref, s32[32,4]{1,0:T(8,128)S(1)} %copy.27.tiles_ref, bf16[640,256]{1,0:T(8,128)(2,1)S(1)} %copy-done.1, bf16[640,256]{1,0:T(8,128)(2,1)S(1)} %collective-permute-done.5.left_ref, bf16[640,256]{1,0:T(8,128)(2,1)S(1)} %collective-permute-done.6.right_ref, ...), custom_call_target="tpu_custom_call" | custom-call | tf_op jit(solution)/shard_map/pallas_call | solution.py:380
  59.0 4.1 %all-to-all-start.2 = ((bf16[32,8,640]{2,1,0:T(8,128)(2,1)}), bf16[32,8,640]{2,1,0:T(8,128)(2,1)S(1)}, u32[]{:S(2)}, u32[]{:S(2)}) async-start(bf16[32,8,640]{2,1,0:T(8,128)(2,1)} %bitcast.9), calls=%async_computation.2 | async-start | bytes 655360 | tf_op jit(solution)/shard_map/all_to_all | solution.py:396
  69.7 6.6 %all-to-all-done.2 = bf16[32,8,640]{2,1,0:T(8,128)(2,1)S(1)} async-done(((bf16[32,8,640]{2,1,0:T(8,128)(2,1)}), bf16[32,8,640]{2,1,0:T(8,128)(2,1)S(1)}, u32[]{:S(2)}, u32[]{:S(2)}) %all-to-all-start.2) | async-done | bytes 327712 | tf_op jit(solution)/shard_map/all_to_all | solution.py:396
  77.6 6.1 %all-to-all-start.3 = ((bf16[32,8,1024]{2,1,0:T(8,128)(2,1)}), bf16[32,8,1024]{2,1,0:T(8,128)(2,1)S(1)}, u32[]{:S(2)}, u32[]{:S(2)}) async-start(bf16[32,8,1024]{2,1,0:T(8,128)(2,1)} %shard_map.168), calls=%async_computation.3 | async-start | bytes 1048576 | tf_op jit(solution)/shard_map/all_to_all | solution.py:408
  86.4 10.0 %all-to-all-done.3 = bf16[32,8,1024]{2,1,0:T(8,128)(2,1)S(1)} async-done(((bf16[32,8,1024]{2,1,0:T(8,128)(2,1)}), bf16[32,8,1024]{2,1,0:T(8,128)(2,1)S(1)}, u32[]{:S(2)}, u32[]{:S(2)}) %all-to-all-start.3) | async-done | bytes 524320 | tf_op jit(solution)/shard_map/all_to_all | solution.py:408
  96.7 6.5 %collective-permute-start.9 = (bf16[256,256]{1,0:T(8,128)(2,1)S(1)}, bf16[256,256]{1,0:T(8,128)(2,1)S(1)}, u32[]{:S(2)}, u32[]{:S(2)}) collective-permute-start(bf16[256,256]{1,0:T(8,128)(2,1)S(1)} %convolution_convert_fusion.1), channel_id=1, source_target_pairs={{0,1},{1,0},{2,3},{3,2},{4,5},{5,4},{6,7},{7,6},{8,9},{9,8},{10,11... | collective-permute-start | bytes 393224 | tf_op jit(solution)/shard_map/ppermute | solution.py:276
  120.2 3.0 %collective-permute-done.15.m1 = bf16[256,256]{1,0:T(8,128)(2,1)S(1)} collective-permute-done((bf16[256,256]{1,0:T(8,128)(2,1)S(1)}, bf16[256,256]{1,0:T(8,128)(2,1)S(1)}, u32[]{:S(2)}, u32[]{:S(2)}) %collective-permute-start.15) | collective-permute-done | bytes 131104 | tf_op jit(solution)/shard_map/ppermute | solution.py:276
  126.0 4.3 %shard_map.169 = bf16[256,1920]{1,0:T(8,128)(2,1)} custom-call(bf16[256,256]{1,0:T(8,128)(2,1)} %copy-done.8, bf16[256,256]{1,0:T(8,128)(2,1)} %copy-done.15, bf16[256,256]{1,0:T(8,128)(2,1)} %copy-done.16, bf16[256,256]{1,0:T(8,128)(2,1)} %copy-done.17, bf16[256,1792]{1,0:T(8,128)(2,1)} %get-tuple-element.80.w0, bf16[256,1792]{1,0:T(8,128)(2,1)} %copy-done.7, ...), custom_call_target="tpu_custom_call" | custom-call | tf_op jit(solution)/shard_map/pallas_call | solution.py:421
  130.3 3.7 %all-to-all-start.4 = ((bf16[8,32,1920]{2,1,0:T(8,128)(2,1)}), bf16[8,32,1920]{2,1,0:T(8,128)(2,1)S(1)}, u32[]{:S(2)}, u32[]{:S(2)}) async-start(bf16[8,32,1920]{2,1,0:T(8,128)(2,1)} %bitcast.25), calls=%async_computation.4 | async-start | bytes 1966080 | tf_op jit(solution)/shard_map/all_to_all | solution.py:285
  134.1 3.1 %collective-permute-start.21 = (bf16[896,256]{1,0:T(8,128)(2,1)S(1)}, bf16[896,256]{1,0:T(8,128)(2,1)S(1)}, u32[]{:S(2)}, u32[]{:S(2)}) collective-permute-start(bf16[896,256]{1,0:T(8,128)(2,1)S(1)} %copy-done.14), channel_id=1, source_target_pairs={{0,24},{8,0},{16,8},{24,16},{1,25},{9,1},{17,9},{25,17},{2,26},{10... | collective-permute-start | bytes 1376264 | tf_op jit(solution)/shard_map/ppermute | solution.py:276
  140.0 10.2 %collective-permute-done.22 = bf16[448,256]{1,0:T(8,128)(2,1)} collective-permute-done((bf16[448,256]{1,0:T(8,128)(2,1)}, bf16[448,256]{1,0:T(8,128)(2,1)}, u32[]{:S(2)}, u32[]{:S(2)}) %collective-permute-start.22) | collective-permute-done | bytes 229408 | tf_op jit(solution)/shard_map/ppermute | solution.py:276
  150.8 8.9 %all-to-all-done.4.parts_ref = bf16[8,32,1920]{2,1,0:T(8,128)(2,1)S(1)} async-done(((bf16[8,32,1920]{2,1,0:T(8,128)(2,1)}), bf16[8,32,1920]{2,1,0:T(8,128)(2,1)S(1)}, u32[]{:S(2)}, u32[]{:S(2)}) %all-to-all-start.4) | async-done | bytes 983072 | tf_op jit(solution)/shard_map/all_to_all | solution.py:285
  160.8 3.5 %all-to-all-start.5 = ((bf16[8,32,896]{2,1,0:T(8,128)(2,1)}), bf16[8,32,896]{2,1,0:T(8,128)(2,1)S(1)}, u32[]{:S(2)}, u32[]{:S(2)}) async-start(bf16[8,32,896]{2,1,0:T(8,128)(2,1)} %shard_map.170), calls=%async_computation.5 | async-start | bytes 917504 | tf_op jit(solution)/shard_map/all_to_all | solution.py:441
  164.4 3.2 %collective-permute-start.25 = (bf16[448,256]{1,0:T(8,128)(2,1)}, bf16[448,256]{1,0:T(8,128)(2,1)S(1)}, u32[]{:S(2)}, u32[]{:S(2)}) collective-permute-start(bf16[448,256]{1,0:T(8,128)(2,1)} %copy-done.23), channel_id=1, source_target_pairs={{0,24},{8,0},{16,8},{24,16},{1,25},{9,1},{17,9},{25,17},{2,26},{10... | collective-permute-start | bytes 688136 | tf_op jit(solution)/shard_map/ppermute | solution.py:276
  167.5 3.5 %collective-permute-done.24.low2 = bf16[448,256]{1,0:T(8,128)(2,1)S(1)} collective-permute-done((bf16[448,256]{1,0:T(8,128)(2,1)}, bf16[448,256]{1,0:T(8,128)(2,1)S(1)}, u32[]{:S(2)}, u32[]{:S(2)}) %collective-permute-start.24) | collective-permute-done | bytes 229408 | tf_op jit(solution)/shard_map/ppermute | solution.py:276
  171.1 6.3 %all-to-all-done.5 = bf16[8,32,896]{2,1,0:T(8,128)(2,1)S(1)} async-done(((bf16[8,32,896]{2,1,0:T(8,128)(2,1)}), bf16[8,32,896]{2,1,0:T(8,128)(2,1)S(1)}, u32[]{:S(2)}, u32[]{:S(2)}) %all-to-all-start.5) | async-done | bytes 458784 | tf_op jit(solution)/shard_map/all_to_all | solution.py:441
  179.5 3.8 %collective-permute-start.26 = (bf16[4,128,256]{2,1,0:T(8,128)(2,1)}, bf16[4,128,256]{2,1,0:T(8,128)(2,1)S(1)}, u32[]{:S(2)}, u32[]{:S(2)}) collective-permute-start(bf16[4,128,256]{2,1,0:T(8,128)(2,1)} %get-tuple-element.62), channel_id=1, source_target_pairs={{0,1},{1,0},{2,3},{3,2},{4,5},{5,4},{6,7},{7,6},{8,9},{9,8},{10,11... | collective-permute-start | bytes 786440 | tf_op jit(solution)/shard_map/ppermute | solution.py:276
  197.9 3.1 %collective-permute-start.33 = (bf16[128,256]{1,0:T(8,128)(2,1)S(1)}, bf16[128,256]{1,0:T(8,128)(2,1)S(1)}, u32[]{:S(2)}, u32[]{:S(2)}) collective-permute-start(bf16[128,256]{1,0:T(8,128)(2,1)S(1)} %add_convert_fusion.1), channel_id=1, source_target_pairs={{0,1},{1,0},{2,3},{3,2},{4,5},{5,4},{6,7},{7,6},{8,9},{9,8},{10,11... | collective-permute-start | bytes 196616 | tf_op jit(solution)/shard_map/ppermute | solution.py:276
  (140 shorter events, 72.0 us)
Async XLA Ops:
  0.0 15.9 %collective-permute-start.1 = (bf16[1024,1024]{1,0:T(8,128)(2,1)}, bf16[1024,1024]{1,0:T(8,128)(2,1)}, u32[]{:S(2)}, u32[]{:S(2)}) collective-permute-start(bf16[1024,1024]{1,0:T(8,128)(2,1)} %k0.1), channel_id=1, source_target_pairs={{0,1},{1,0},{2,3},{3,2},{4,5},{5,4},{6,7},{7,6},{8,9},{9,8},{10,11... | collective-permute-start | bytes 6291464 | tf_op jit(solution)/shard_map/ppermute | solution.py:276
  3.2 12.7 %collective-permute-start.2 = (bf16[1024,1024]{1,0:T(8,128)(2,1)}, bf16[1024,1024]{1,0:T(8,128)(2,1)}, u32[]{:S(2)}, u32[]{:S(2)}) collective-permute-start(bf16[1024,1024]{1,0:T(8,128)(2,1)} %v0.1), channel_id=1, source_target_pairs={{0,1},{1,0},{2,3},{3,2},{4,5},{5,4},{6,7},{7,6},{8,9},{9,8},{10,11... | collective-permute-start | bytes 6291464 | tf_op jit(solution)/shard_map/ppermute | solution.py:276
  3.2 12.6 %collective-permute-start = (bf16[640,1024]{1,0:T(8,128)(2,1)}, bf16[640,1024]{1,0:T(8,128)(2,1)S(1)}, u32[]{:S(2)}, u32[]{:S(2)}) collective-permute-start(bf16[640,1024]{1,0:T(8,128)(2,1)} %x0.1), channel_id=1, source_target_pairs={{0,1},{1,0},{2,3},{3,2},{4,5},{5,4},{6,7},{7,6},{8,9},{9,8},{10,11... | collective-permute-start | bytes 3932168 | tf_op jit(solution)/shard_map/ppermute | solution.py:276
  6.4 26.3 %all-to-all-start = ((bf16[32,8,1024]{2,1,0:T(8,128)(2,1)}), bf16[32,8,1024]{2,1,0:T(8,128)(2,1)S(1)}, u32[]{:S(2)}, u32[]{:S(2)}) async-start(bf16[32,8,1024]{2,1,0:T(8,128)(2,1)} %fusion), calls=%async_computation | async-start | bytes 1048576 | tf_op jit(solution)/shard_map/all_to_all | solution.py:285
  35.8 16.1 %collective-permute-start.5 = (bf16[640,256]{1,0:T(8,128)(2,1)}, bf16[640,256]{1,0:T(8,128)(2,1)S(1)}, u32[]{:S(2)}, u32[]{:S(2)}) collective-permute-start(bf16[640,256]{1,0:T(8,128)(2,1)} %get-tuple-element.42), channel_id=1, source_target_pairs={{0,2},{2,4},{4,6},{6,0},{1,3},{3,5},{5,7},{7,1},{8,10},{10,12},{12... | collective-permute-start | bytes 983048 | tf_op jit(solution)/shard_map/ppermute | solution.py:276
  37.0 14.9 %collective-permute-start.6 = (bf16[640,256]{1,0:T(8,128)(2,1)}, bf16[640,256]{1,0:T(8,128)(2,1)S(1)}, u32[]{:S(2)}, u32[]{:S(2)}) collective-permute-start(bf16[640,256]{1,0:T(8,128)(2,1)} %get-tuple-element.43), channel_id=1, source_target_pairs={{0,6},{2,0},{4,2},{6,4},{1,7},{3,1},{5,3},{7,5},{8,14},{10,8},{12,... | collective-permute-start | bytes 983048 | tf_op jit(solution)/shard_map/ppermute | solution.py:276
  38.5 17.6 %all-to-all-start.1 = ((bf16[32,8,512]{2,1,0:T(8,128)(2,1)}), bf16[32,8,512]{2,1,0:T(8,128)(2,1)S(1)}, u32[]{:S(2)}, u32[]{:S(2)}) async-start(bf16[32,8,512]{2,1,0:T(8,128)(2,1)} %bitcast.7), calls=%async_computation.1 | async-start | bytes 524288 | tf_op jit(solution)/shard_map/all_to_all | solution.py:378
  49.2 28.4 %collective-permute-start.7 = (bf16[256,1792]{1,0:T(8,128)(2,1)}, bf16[256,1792]{1,0:T(8,128)(2,1)S(1)}, u32[]{:S(2)}, u32[]{:S(2)}) collective-permute-start(bf16[256,1792]{1,0:T(8,128)(2,1)} %get-tuple-element.82), channel_id=1, source_target_pairs={{0,8},{8,16},{16,24},{24,0},{1,9},{9,17},{17,25},{25,1},{2,10},{10... | collective-permute-start | bytes 2752520 | tf_op jit(solution)/shard_map/ppermute | solution.py:276
  50.4 27.2 %collective-permute-start.8 = (bf16[256,1792]{1,0:T(8,128)(2,1)}, bf16[256,1792]{1,0:T(8,128)(2,1)}, u32[]{:S(2)}, u32[]{:S(2)}) collective-permute-start(bf16[256,1792]{1,0:T(8,128)(2,1)} %get-tuple-element.81), channel_id=1, source_target_pairs={{0,24},{8,0},{16,8},{24,16},{1,25},{9,1},{17,9},{25,17},{2,26},{10... | collective-permute-start | bytes 2752520 | tf_op jit(solution)/shard_map/ppermute | solution.py:276
  59.0 17.3 %all-to-all-start.2 = ((bf16[32,8,640]{2,1,0:T(8,128)(2,1)}), bf16[32,8,640]{2,1,0:T(8,128)(2,1)S(1)}, u32[]{:S(2)}, u32[]{:S(2)}) async-start(bf16[32,8,640]{2,1,0:T(8,128)(2,1)} %bitcast.9), calls=%async_computation.2 | async-start | bytes 655360 | tf_op jit(solution)/shard_map/all_to_all | solution.py:396
  77.6 18.9 %all-to-all-start.3 = ((bf16[32,8,1024]{2,1,0:T(8,128)(2,1)}), bf16[32,8,1024]{2,1,0:T(8,128)(2,1)S(1)}, u32[]{:S(2)}, u32[]{:S(2)}) async-start(bf16[32,8,1024]{2,1,0:T(8,128)(2,1)} %shard_map.168), calls=%async_computation.3 | async-start | bytes 1048576 | tf_op jit(solution)/shard_map/all_to_all | solution.py:408
  83.6 20.6 %collective-permute-start.10 = (bf16[256,896]{1,0:T(8,128)(2,1)}, bf16[256,896]{1,0:T(8,128)(2,1)}, u32[]{:S(2)}, u32[]{:S(2)}) collective-permute-start(bf16[256,896]{1,0:T(8,128)(2,1)} %get-tuple-element.84), channel_id=1, source_target_pairs={{0,8},{8,16},{16,24},{24,0},{1,9},{9,17},{17,25},{25,1},{2,10},{10... | collective-permute-start | bytes 1376264 | tf_op jit(solution)/shard_map/ppermute | solution.py:276
  84.9 19.3 %collective-permute-start.11 = (bf16[256,896]{1,0:T(8,128)(2,1)}, bf16[256,896]{1,0:T(8,128)(2,1)}, u32[]{:S(2)}, u32[]{:S(2)}) collective-permute-start(bf16[256,896]{1,0:T(8,128)(2,1)} %get-tuple-element.83), channel_id=1, source_target_pairs={{0,24},{8,0},{16,8},{24,16},{1,25},{9,1},{17,9},{25,17},{2,26},{10... | collective-permute-start | bytes 1376264 | tf_op jit(solution)/shard_map/ppermute | solution.py:276
  105.3 8.8 %collective-permute-start.13 = (bf16[256,256]{1,0:T(8,128)(2,1)S(1)}, bf16[256,256]{1,0:T(8,128)(2,1)S(1)}, u32[]{:S(2)}, u32[]{:S(2)}) collective-permute-start(bf16[256,256]{1,0:T(8,128)(2,1)S(1)} %add_convert_fusion), channel_id=1, source_target_pairs={{0,2},{2,4},{4,6},{6,0},{1,3},{3,5},{5,7},{7,1},{8,10},{10,12},{12... | collective-permute-start | bytes 393224 | tf_op jit(solution)/shard_map/ppermute | solution.py:276
  108.0 12.2 %collective-permute-start.18 = (bf16[256,896]{1,0:T(8,128)(2,1)}, bf16[256,896]{1,0:T(8,128)(2,1)S(1)}, u32[]{:S(2)}, u32[]{:S(2)}) collective-permute-start(bf16[256,896]{1,0:T(8,128)(2,1)} %collective-permute-done.10), channel_id=1, source_target_pairs={{0,8},{8,16},{16,24},{24,0},{1,9},{9,17},{17,25},{25,1},{2,10},{10... | collective-permute-start | bytes 1376264 | tf_op jit(solution)/shard_map/ppermute | solution.py:276
  108.0 12.2 %collective-permute-start.19 = (bf16[256,896]{1,0:T(8,128)(2,1)}, bf16[256,896]{1,0:T(8,128)(2,1)S(1)}, u32[]{:S(2)}, u32[]{:S(2)}) collective-permute-start(bf16[256,896]{1,0:T(8,128)(2,1)} %collective-permute-done.11), channel_id=1, source_target_pairs={{0,24},{8,0},{16,8},{24,16},{1,25},{9,1},{17,9},{25,17},{2,26},{10... | collective-permute-start | bytes 1376264 | tf_op jit(solution)/shard_map/ppermute | solution.py:276
  114.2 9.0 %collective-permute-start.15 = (bf16[256,256]{1,0:T(8,128)(2,1)S(1)}, bf16[256,256]{1,0:T(8,128)(2,1)S(1)}, u32[]{:S(2)}, u32[]{:S(2)}) collective-permute-start(bf16[256,256]{1,0:T(8,128)(2,1)S(1)} %fusion.3.m0), channel_id=1, source_target_pairs={{0,8},{8,16},{16,24},{24,0},{1,9},{9,17},{17,25},{25,1},{2,10},{10... | collective-permute-start | bytes 393224 | tf_op jit(solution)/shard_map/ppermute | solution.py:276
  114.4 10.9 %collective-permute-start.16 = (bf16[256,256]{1,0:T(8,128)(2,1)S(1)}, bf16[256,256]{1,0:T(8,128)(2,1)S(1)}, u32[]{:S(2)}, u32[]{:S(2)}) collective-permute-start(bf16[256,256]{1,0:T(8,128)(2,1)S(1)} %fusion.3.m0), channel_id=1, source_target_pairs={{0,16},{8,24},{16,0},{24,8},{1,17},{9,25},{17,1},{25,9},{2,18},{10... | collective-permute-start | bytes 393224 | tf_op jit(solution)/shard_map/ppermute | solution.py:276
  130.3 29.4 %all-to-all-start.4 = ((bf16[8,32,1920]{2,1,0:T(8,128)(2,1)}), bf16[8,32,1920]{2,1,0:T(8,128)(2,1)S(1)}, u32[]{:S(2)}, u32[]{:S(2)}) async-start(bf16[8,32,1920]{2,1,0:T(8,128)(2,1)} %bitcast.25), calls=%async_computation.4 | async-start | bytes 1966080 | tf_op jit(solution)/shard_map/all_to_all | solution.py:285
  134.0 16.1 %collective-permute-start.20 = (bf16[896,256]{1,0:T(8,128)(2,1)}, bf16[896,256]{1,0:T(8,128)(2,1)S(1)}, u32[]{:S(2)}, u32[]{:S(2)}) collective-permute-start(bf16[896,256]{1,0:T(8,128)(2,1)} %get-tuple-element.56), channel_id=1, source_target_pairs={{0,8},{8,16},{16,24},{24,0},{1,9},{9,17},{17,25},{25,1},{2,10},{10... | collective-permute-start | bytes 1376264 | tf_op jit(solution)/shard_map/ppermute | solution.py:276
  134.1 16.7 %collective-permute-start.21 = (bf16[896,256]{1,0:T(8,128)(2,1)S(1)}, bf16[896,256]{1,0:T(8,128)(2,1)S(1)}, u32[]{:S(2)}, u32[]{:S(2)}) collective-permute-start(bf16[896,256]{1,0:T(8,128)(2,1)S(1)} %copy-done.14), channel_id=1, source_target_pairs={{0,24},{8,0},{16,8},{24,16},{1,25},{9,1},{17,9},{25,17},{2,26},{10... | collective-permute-start | bytes 1376264 | tf_op jit(solution)/shard_map/ppermute | solution.py:276
  137.3 12.9 %collective-permute-start.22 = (bf16[448,256]{1,0:T(8,128)(2,1)}, bf16[448,256]{1,0:T(8,128)(2,1)}, u32[]{:S(2)}, u32[]{:S(2)}) collective-permute-start(bf16[448,256]{1,0:T(8,128)(2,1)} %get-tuple-element.58), channel_id=1, source_target_pairs={{0,8},{8,16},{16,24},{24,0},{1,9},{9,17},{17,25},{25,1},{2,10},{10... | collective-permute-start | bytes 688136 | tf_op jit(solution)/shard_map/ppermute | solution.py:276
  137.3 12.9 %collective-permute-start.23 = (bf16[448,256]{1,0:T(8,128)(2,1)}, bf16[448,256]{1,0:T(8,128)(2,1)S(1)}, u32[]{:S(2)}, u32[]{:S(2)}) collective-permute-start(bf16[448,256]{1,0:T(8,128)(2,1)} %get-tuple-element.59), channel_id=1, source_target_pairs={{0,24},{8,0},{16,8},{24,16},{1,25},{9,1},{17,9},{25,17},{2,26},{10... | collective-permute-start | bytes 688136 | tf_op jit(solution)/shard_map/ppermute | solution.py:276
  160.8 16.6 %all-to-all-start.5 = ((bf16[8,32,896]{2,1,0:T(8,128)(2,1)}), bf16[8,32,896]{2,1,0:T(8,128)(2,1)S(1)}, u32[]{:S(2)}, u32[]{:S(2)}) async-start(bf16[8,32,896]{2,1,0:T(8,128)(2,1)} %shard_map.170), calls=%async_computation.5 | async-start | bytes 917504 | tf_op jit(solution)/shard_map/all_to_all | solution.py:441
  (40 other events, 461.1 us)
